TPU v7x, 32 devices: a whole 2x2x4 slice. The times are simulated.
32 devices in a mesh: region: 16 (over z, y, x), split: 2 (over core).
Axes of the slice: x: 2, y: 2, z: 4, core: 2. Of those that a mesh axis runs over, the one named last changes fastest.
Arguments:
- features: bfloat16 [96, 16384], P(None, ('region', 'split')), may hold values from -6 to 6
- kernel_one: bfloat16 [27, 96, 96], replicated, may hold values from -0.125 to 0.125
- kernel_two: bfloat16 [27, 96, 192], replicated, may hold values from -0.125 to 0.125
- occupancy: int32 [32, 512], P(('region', 'split')), may hold values 0 or 1
- neighbors: int32 [32, 27], P(('region', 'split')), may hold values from -1 to 31, as said below
- cotangent: bfloat16 [192, 16384], P(None, ('region', 'split')), may hold values from -0.046875 to 0.046875
Outputs:
- output: bfloat16 [192, 16384], P(None, ('region', 'split'))
- grad_one: float32 [27, 96, 96], replicated
- grad_two: float32 [27, 96, 192], replicated
Inputs may be any that keep to these rules, and one draw needn't show every extreme that they name: `neighbors`: entry k = 9 (dx + 1) + 3 (dy + 1) + (dz + 1) of a block's row is the active block whose block coordinates differ by (dx, dy, dz), or -1 if there is none; entry 13 is the block itself. Blocks are numbered in device order. The blocks of region r have x coordinate r and y coordinate 0 or 1; the device of split index s holds the blocks with z coordinate s. So a neighbour in region r - 1 or r + 1 differs by dx = -1 or +1, and a neighbour on the other device of the same region lies across the z boundary between the two halves.
All inputs are finite; a program needn't handle non-finite values. No bound on the sum of `occupancy` on one device may be relied on, other than what follows from the above.
Results may differ from a plain program's by a relative error of at most 0.0049.
Values may be sent and summed in bfloat16 or wider, within the bound.
No kernel may reach another device: no remote copies, remote signals or barrier semaphores. Data moves between devices by JAX's collectives and lax.ppermute only.
A program may use at most 64 MiB of HBM per device.

v0:
```python
import jax
import jax.numpy as jnp
import numpy as np
from jax import lax
from jax.sharding import PartitionSpec as P


def swapped(value, axis, apart):
    mask = 2**apart
    pairs = [(source, source ^ mask) for source in range(lax.axis_size(axis))]
    return lax.ppermute(value, axis, pairs)


def from_behind(value, axis, steps):
    count = lax.axis_size(axis)
    first, last = (max(0, -steps), min(count, count - steps))
    return lax.ppermute(value, axis, [(source, source + steps) for source in range(first, last)])


def voxel_tables():
    voxels = np.arange(512)
    along_x = voxels // 64
    along_y = voxels // 8 % 8
    along_z = voxels % 8
    block_code = np.zeros((27, 512), np.int32)
    voxel_code = np.zeros((27, 512), np.int32)
    for offset in range(27):
        moved_x = along_x + offset // 9 - 1
        moved_y = along_y + offset // 3 % 3 - 1
        moved_z = along_z + offset % 3 - 1
        block_code[offset] = (moved_x // 8 + 1) * 9 + (moved_y // 8 + 1) * 3 + (moved_z // 8 + 1)
        voxel_code[offset] = moved_x % 8 * 64 + moved_y % 8 * 8 + moved_z % 8
    on_shell = (
        (along_x == 0)
        | (along_x == 7)
        | (along_y == 0)
        | (along_y == 7)
        | (along_z == 0)
        | (along_z == 7)
    )
    shell_voxels = voxels[on_shell].astype(np.int32)
    shell_slot = np.zeros(512, np.int32)
    shell_slot[shell_voxels] = np.arange(shell_voxels.shape[0], dtype=np.int32)
    return (block_code, voxel_code, shell_voxels, shell_slot)


def convolve(window_rows, lookup, kernel):

    def accumulate(offset, total):
        picked = jnp.take(
            window_rows, lax.dynamic_index_in_dim(lookup, offset, 0, keepdims=False), axis=0
        )
        weights = lax.dynamic_index_in_dim(kernel, offset, 0, keepdims=False)
        return total + jnp.dot(picked, weights, preferred_element_type=jnp.float32)

    return lax.fori_loop(
        0, 27, accumulate, jnp.zeros((lookup.shape[1], kernel.shape[2]), jnp.float32)
    )


def kernel_gradient(window_rows, lookup, gradient_rows):

    def accumulate(offset, total):
        picked = jnp.take(
            window_rows, lax.dynamic_index_in_dim(lookup, offset, 0, keepdims=False), axis=0
        )
        product = jnp.dot(picked.T, gradient_rows, preferred_element_type=jnp.float32)
        return lax.dynamic_update_index_in_dim(total, product, offset, 0)

    return lax.fori_loop(
        0,
        27,
        accumulate,
        jnp.zeros((27, window_rows.shape[1], gradient_rows.shape[1]), jnp.float32),
    )


def convolve_back(window_rows, lookup, kernel):

    def accumulate(offset, total):
        picked = jnp.take(
            window_rows, lax.dynamic_index_in_dim(lookup, 26 - offset, 0, keepdims=False), axis=0
        )
        weights = lax.dynamic_index_in_dim(kernel, offset, 0, keepdims=False)
        return total + jnp.dot(picked, weights.T, preferred_element_type=jnp.float32)

    return lax.fori_loop(
        0, 27, accumulate, jnp.zeros((lookup.shape[1], kernel.shape[1]), jnp.float32)
    )


def shards(features, kernel_one, kernel_two, occupancy, neighbors, cotangent):
    block_count = neighbors.shape[0]
    split_size = lax.axis_size("split")
    region_pos = lax.axis_index("region")
    split_pos = lax.axis_index("split")
    first_block = (region_pos * split_size + split_pos) * block_count
    block_code, voxel_code, shell_voxels, shell_slot = voxel_tables()
    block_ids = jnp.transpose(jnp.take(neighbors, jnp.asarray(block_code), axis=1), (1, 0, 2))
    voxel_target = jnp.asarray(voxel_code)[:, None, :]
    plane_cols = block_count * 64
    region_span = split_size * block_count
    region_first = region_pos * region_span
    partner_first = (region_pos * split_size + (1 - split_pos)) * block_count
    above_base = plane_cols + region_span * 64
    own_base = plane_cols + 2 * region_span * 64
    zero_col = own_base + block_count * 512
    slot_face_z = jnp.asarray(voxel_code // 8)[:, None, :]
    slot_face_x = jnp.asarray(voxel_code % 64)[:, None, :]
    owned = (block_ids >= first_block) & (block_ids < first_block + block_count)
    in_region = (block_ids >= region_first) & (block_ids < region_first + region_span)
    below = block_ids < region_first
    own_cols = own_base + (block_ids - first_block) * 512 + voxel_target
    partner_cols = (block_ids - partner_first) * 64 + slot_face_z
    below_cols = plane_cols + (block_ids - (region_first - region_span)) * 64 + slot_face_x
    above_cols = above_base + (block_ids - (region_first + region_span)) * 64 + slot_face_x
    lookup = jnp.where(
        block_ids < 0,
        zero_col,
        jnp.where(
            owned,
            own_cols,
            jnp.where(in_region, partner_cols, jnp.where(below, below_cols, above_cols)),
        ),
    )

    def spread(values):
        channels = values.shape[0]
        cubes = values.reshape(channels, block_count, 8, 8, 8)
        facing = lax.dynamic_index_in_dim(cubes, 7 * (1 - split_pos), 4, keepdims=False)
        facing = facing.reshape(channels, plane_cols)
        from_partner = swapped(facing, "split", 0)
        upper_plane = cubes[:, :, 7, :, :].reshape(channels, plane_cols)
        lower_plane = cubes[:, :, 0, :, :].reshape(channels, plane_cols)
        upper_all, lower_all = (
            lax.all_gather(upper_plane, "split", axis=1, tiled=True),
            lax.all_gather(lower_plane, "split", axis=1, tiled=True),
        )
        from_below = from_behind(upper_all, "region", 1)
        from_above = from_behind(lower_all, "region", -1)
        return jnp.concatenate(
            [from_partner, from_below, from_above, values, jnp.zeros((channels, 1), values.dtype)],
            axis=1,
        ).T

    lookup = lookup.reshape(27, -1).astype(jnp.int32)
    active = (occupancy.reshape(-1) > 0)[None, :]
    zero_value = jnp.zeros((), features.dtype)
    masked = jnp.where(active, features, zero_value)
    masked_window = spread(masked)
    hidden_pre = jnp.where(active, convolve(masked_window, lookup, kernel_one).T, 0.0)
    hidden = jnp.where(active, jax.nn.silu(hidden_pre), 0.0).astype(jnp.bfloat16)
    hidden_window = spread(hidden)
    output = jnp.where(active, convolve(hidden_window, lookup, kernel_two).T, 0.0)
    grad_out = jnp.where(active, cotangent, zero_value)
    grad_two = kernel_gradient(hidden_window, lookup, grad_out.T)
    back = convolve_back(spread(grad_out), lookup, kernel_two).T
    sigmoid_pre = jax.nn.sigmoid(hidden_pre)
    grad_pre = jnp.where(
        active, back * sigmoid_pre * (1.0 + hidden_pre * (1.0 - sigmoid_pre)), 0.0
    ).astype(jnp.bfloat16)
    grad_one = kernel_gradient(masked_window, lookup, grad_pre.T)
    grad_one, grad_two = lax.psum((grad_one, grad_two), ("region", "split"))
    return (output.astype(jnp.bfloat16), grad_one, grad_two)


def solution(mesh):
    in_specs = (
        P(None, ("region", "split")),
        P(),
        P(),
        P(("region", "split"), None),
        P(("region", "split"), None),
        P(None, ("region", "split")),
    )
    out_specs = (P(None, ("region", "split")), P(), P())
    return jax.shard_map(shards, mesh=mesh, in_specs=in_specs, out_specs=out_specs, check_vma=False)
```

profile of v0, /device:TPU:0, one launch (start us, length us, event | category | flops | bytes accessed | tf_op | source)
XLA Modules:
  0.0 561.1 jit_solution(613160817628008569)
XLA Ops:
  11.5 4.6 collective-permute-start.1
  22.6 4.5 collective-permute-start.7
  27.4 77.0 %gather_fusion.5 = s32[13824]{0:T(1024)S(1)} fusion(s32[27]{0:T(128)S(1)} %bitcast.104, s32[14336]{0:T(1024)S(1)} %pad_clamp_fusion.5), kind=kCustom, calls=%fused_computation.5 | custom fusion | bytes 165888 | tf_op jit(solution)/shard_map/jit(_take)/gather | solution.py:99
  108.0 67.2 %while.72 = (s32[]{:T(128)}, f32[512,96]{0,1:T(8,128)S(1)}, s32[27,512]{1,0:T(8,128)S(1)}, bf16[833,96]{1,0:T(8,128)(2,1)S(1)}, bf16[27,96,96]{2,1,0:T(8,128)(2,1)}, /*index=5*/s32[]{:T(128)}, s32[]{:T(128)}) while((s32[]{:T(128)}, f32[512,96]{0,1:T(8,128)S(1)}, s32[27,512]{1,0:T(8,128)S(1)}, bf16[833,96]{1,0:T(8,128)(2,1)S(1)}, ...), condition=%wide.region_1.3_spmd.clone, body=%wide.region_0.0_spmd.clone.sunk | while | flops 9590275 | bytes 732263 | solution.py:56
  177.6 4.9 collective-permute-start.4
  185.7 5.3 collective-permute-done.5
  191.6 85.4 %while.74 = (s32[]{:T(128)}, f32[512,96]{0,1:T(8,128)S(1)}, s32[27,512]{1,0:T(8,128)S(1)}, bf16[833,192]{1,0:T(8,128)(2,1)S(1)}, bf16[27,96,192]{2,1,0:T(8,128)(...) while((s32[]{:T(128)}, f32[512,96]{0,1:T(8,128)S(1)}, s32[27,512]{1,0:T(8,128)S(1)}, ...), condition=%wide.region_5.7_spmd.clone, body=%wide.region_4.6_spmd.clone.sunk | while | flops 19076616 | bytes 1049765 | solution.py:87
  191.6 2.0 gather_fusion.4
  194.8 2.0 gather_fusion.4
  198.0 2.0 gather_fusion.4
  201.1 2.0 gather_fusion.4
  204.3 2.0 gather_fusion.4
  207.5 2.0 gather_fusion.4
  210.6 2.0 gather_fusion.4
  213.8 2.0 gather_fusion.4
  217.0 2.0 gather_fusion.4
  220.1 2.0 gather_fusion.4
  223.3 2.0 gather_fusion.4
  226.4 2.0 gather_fusion.4
  229.6 2.0 gather_fusion.4
  232.8 2.0 gather_fusion.4
  235.9 2.0 gather_fusion.4
  239.1 2.0 gather_fusion.4
  242.3 2.0 gather_fusion.4
  245.4 2.0 gather_fusion.4
  258.1 2.0 gather_fusion.4
  264.4 2.0 gather_fusion.4
  277.3 63.1 %while.70 = (s32[]{:T(128)}, f32[27,96,96]{2,1,0:T(8,128)}, s32[27,512]{1,0:T(8,128)S(1)}, bf16[833,96]{1,0:T(8,128)(2,1)S(1)}, bf16[512,96]{1,0:T(8,128)(2,1)S(1)}, /*index=5*/s32[]{:T(128)}) while((s32[]{:T(128)}, f32[27,96,96]{2,1,0:T(8,128)}, s32[27,512]{1,0:T(8,128)S(1)}, bf16[833,96]{1,0:T(8,128)(2,1)S(1)}, ...), condition=%wide.region_7.9_spmd, body=%wide.region_6.8_spmd.sunk | while | flops 9491970 | bytes 461909 | solution.py:70
  340.5 63.7 %while.71 = (s32[]{:T(128)}, f32[27,96,192]{2,1,0:T(8,128)}, s32[27,512]{1,0:T(8,128)S(1)}, bf16[833,96]{1,0:T(8,128)(2,1)S(1)}, bf16[512,192]{1,0:T(8,128)(2,1)S(1)}, /*index=5*/s32[]{:T(128)}) while((s32[]{:T(128)}, f32[27,96,192]{2,1,0:T(8,128)}, s32[27,512]{1,0:T(8,128)S(1)}, bf16[833,96]{1,0:T(8,128)(2,1)S(1)}, ...), condition=%wide.region_10.12_spmd, body=%wide.region_9.11_spmd.sunk | while | flops 18929152 | bytes 609365 | solution.py:70
  404.2 69.9 %while.73 = (s32[]{:T(128)}, f32[512,192]{0,1:T(8,128)S(1)}, s32[27,512]{1,0:T(8,128)S(1)}, bf16[833,96]{1,0:T(8,128)(2,1)S(1)}, bf16[27,96,192]{2,1,0:T(8,128)(2,1)}, /*index=5*/s32[]{:T(128)}, s32[]{:T(128)}) while((s32[]{:T(128)}, f32[512,192]{0,1:T(8,128)S(1)}, s32[27,512]{1,0:T(8,128)S(1)}, bf16[833,96]{1,0:T(8,128)(2,1)S(1)}, ...), condition=%wide.region_3.5_spmd.clone, body=%wide.region_2.4_spmd.clone.sunk | while | flops 19125764 | bytes 1150055 | solution.py:56
  474.8 75.3 %all-reduce.3.cloned.1.call-done = (f32[27,96,96]{2,1,0:T(8,128)}, f32[27,96,192]{2,1,0:T(8,128)}) async-done(((f32[27,96,96]{2,1,0:T(8,128)}, f32[27,96,192]{2,1,0:T(8,128)}), (f32[27,96,96]{2,1,0:T(8,128)}, f32[27,96,192]{2,1,0:T(8,128)})) %all-reduce.3.cloned.1.call-update) | async-done | bytes 2986000 | tf_op jit(solution)/shard_map/psum | solution.py:163
  550.1 2.6 copy.88
  (844 shorter events, 326.9 us)
Async XLA Ops:
  7.2 20.2 %copy-start = (s32[1,27]{1,0:T(1,128)S(1)}, s32[1,27]{1,0:T(1,128)}, u32[]{:S(2)}) copy-start(s32[1,27]{1,0:T(1,128)} %param.26) | copy-start | bytes 328
  7.2 543.0 %all-reduce.3.cloned.1.call-start = ((), (), s32[]{:S(2)}) async-start(), calls=%async_computation | async-start | bytes 7962624 | tf_op jit(solution)/shard_map/psum | solution.py:163
  8.9 18.4 %copy-start.2 = (s32[13824]{0:T(1024)S(1)}, s32[13824]{0:T(1024)}, u32[]{:S(2)}) copy-start(s32[13824]{0:T(1024)} %constant.296) | copy-start | bytes 165892
  9.2 97.3 %collective-permute-start = (bf16[96,64]{0,1:T(8,128)(2,1)S(1)}, bf16[96,64]{0,1:T(8,128)(2,1)S(1)}, u32[]{:S(2)}, u32[]{:S(2)}) collective-permute-start(bf16[96,64]{0,1:T(8,128)(2,1)S(1)} %bitcast.125), channel_id=1, source_target_pairs={{0,1},{1,0},{2,3},{3,2},{4,5},{5,4},{6,7},{7,6},{8,9},{9,8},{10,11... | collective-permute-start | bytes 36872 | tf_op jit(solution)/shard_map/ppermute | solution.py:11
  11.5 96.2 %collective-permute-start.1 = (bf16[96,128]{0,1:T(8,128)(2,1)S(1)}, bf16[96,128]{0,1:T(8,128)(2,1)S(1)}, u32[]{:S(2)}, u32[]{:S(2)}) collective-permute-start(bf16[96,128]{0,1:T(8,128)(2,1)S(1)} %all_gather.18), channel_id=1, source_target_pairs={{0,2},{2,4},{4,6},{6,8},{8,10},{10,12},{12,14},{14,16},{16,18},{18... | collective-permute-start | bytes 73736 | tf_op jit(solution)/shard_map/ppermute | solution.py:17
  17.9 89.9 %collective-permute-start.2 = (bf16[96,128]{0,1:T(8,128)(2,1)S(1)}, bf16[96,128]{0,1:T(8,128)(2,1)S(1)}, u32[]{:S(2)}, u32[]{:S(2)}) collective-permute-start(bf16[96,128]{0,1:T(8,128)(2,1)S(1)} %all_gather.19), channel_id=1, source_target_pairs={{2,0},{4,2},{6,4},{8,6},{10,8},{12,10},{14,12},{16,14},{18,16},{20... | collective-permute-start | bytes 73736 | tf_op jit(solution)/shard_map/ppermute | solution.py:17
  20.5 163.9 %collective-permute-start.6 = (bf16[192,64]{0,1:T(8,128)(2,1)S(1)}, bf16[192,64]{0,1:T(8,128)(2,1)S(1)}, u32[]{:S(2)}, u32[]{:S(2)}) collective-permute-start(bf16[192,64]{0,1:T(8,128)(2,1)S(1)} %bitcast.124), channel_id=1, source_target_pairs={{0,1},{1,0},{2,3},{3,2},{4,5},{5,4},{6,7},{7,6},{8,9},{9,8},{10,11... | collective-permute-start | bytes 73736 | tf_op jit(solution)/shard_map/ppermute | solution.py:11
  22.6 168.8 %collective-permute-start.7 = (bf16[192,128]{0,1:T(8,128)(2,1)S(1)}, bf16[192,128]{0,1:T(8,128)(2,1)S(1)}, u32[]{:S(2)}, u32[]{:S(2)}) collective-permute-start(bf16[192,128]{0,1:T(8,128)(2,1)S(1)} %all_gather.22), channel_id=1, source_target_pairs={{0,2},{2,4},{4,6},{6,8},{8,10},{10,12},{12,14},{14,16},{16,18},{18... | collective-permute-start | bytes 147464 | tf_op jit(solution)/shard_map/ppermute | solution.py:17
  27.4 77.1 %copy-start.3 = (s32[13824]{0:T(1024)S(1)}, s32[13824]{0:T(1024)}, u32[]{:S(2)}) copy-start(s32[13824]{0:T(1024)} %constant.306) | copy-start | bytes 165892
  27.4 77.1 %copy-start.4 = (s32[13824]{0:T(1024)S(1)}, s32[13824]{0:T(1024)}, u32[]{:S(2)}) copy-start(s32[13824]{0:T(1024)} %constant.305) | copy-start | bytes 165892
  27.4 77.1 %copy-start.5 = (s32[13824]{0:T(1024)S(1)}, s32[13824]{0:T(1024)}, u32[]{:S(2)}) copy-start(s32[13824]{0:T(1024)} %constant.302) | copy-start | bytes 165892
  106.4 84.9 %collective-permute-start.8 = (bf16[192,128]{0,1:T(8,128)(2,1)S(1)}, bf16[192,128]{0,1:T(8,128)(2,1)S(1)}, u32[]{:S(2)}, u32[]{:S(2)}) collective-permute-start(bf16[192,128]{0,1:T(8,128)(2,1)S(1)} %all_gather.23), channel_id=1, source_target_pairs={{2,0},{4,2},{6,4},{8,6},{10,8},{12,10},{14,12},{16,14},{18,16},{20... | collective-permute-start | bytes 147464 | tf_op jit(solution)/shard_map/ppermute | solution.py:17
  175.6 10.1 %collective-permute-start.3 = (bf16[96,64]{0,1:T(8,128)(2,1)S(1)}, bf16[96,64]{0,1:T(8,128)(2,1)S(1)}, u32[]{:S(2)}, u32[]{:S(2)}) collective-permute-start(bf16[96,64]{0,1:T(8,128)(2,1)S(1)} %bitcast.126), channel_id=1, source_target_pairs={{0,1},{1,0},{2,3},{3,2},{4,5},{5,4},{6,7},{7,6},{8,9},{9,8},{10,11... | collective-permute-start | bytes 36872 | tf_op jit(solution)/shard_map/ppermute | solution.py:11
  177.6 8.1 %collective-permute-start.4 = (bf16[96,128]{0,1:T(8,128)(2,1)S(1)}, bf16[96,128]{0,1:T(8,128)(2,1)S(1)}, u32[]{:S(2)}, u32[]{:S(2)}) collective-permute-start(bf16[96,128]{0,1:T(8,128)(2,1)S(1)} %all_gather.20), channel_id=1, source_target_pairs={{0,2},{2,4},{4,6},{6,8},{8,10},{10,12},{12,14},{14,16},{16,18},{18... | collective-permute-start | bytes 73736 | tf_op jit(solution)/shard_map/ppermute | solution.py:17
  184.4 6.7 %collective-permute-start.5 = (bf16[96,128]{0,1:T(8,128)(2,1)S(1)}, bf16[96,128]{0,1:T(8,128)(2,1)S(1)}, u32[]{:S(2)}, u32[]{:S(2)}) collective-permute-start(bf16[96,128]{0,1:T(8,128)(2,1)S(1)} %all_gather.21), channel_id=1, source_target_pairs={{2,0},{4,2},{6,4},{8,6},{10,8},{12,10},{14,12},{16,14},{18,16},{20... | collective-permute-start | bytes 73736 | tf_op jit(solution)/shard_map/ppermute | solution.py:17
  550.1 2.6 copy-start.1
Sparse Core Ops, SparseCore 0:
  404.3 145.8 all-reduce.2
where the time goes:
time: 566 us; the launch traced here: 561 us
  local copies, waits for them, and re-layouts  282 us (50%)
  matrix products  142 us (25%)
  waiting for transfers between devices  80.7 us (14%)
  starting transfers between devices  18.9 us (3%)
  between operations  14.5 us (3%)
  blocking collectives  11 us (2%)
  loops' own time  6.28 us (1%)
    gather x108, local copies, waits for them, and re-layouts, accumulate(): jnp.take(window_rows, lax.dynamic_index_in_dim(lookup, offset, 0, keepdim...  145 us
    gather x1, local copies, waits for them, and re-layouts, shards(): jnp.take(neighbors, jnp.asarray(block_code), axis=1)  77 us
    psum x1, waiting for transfers between devices, shards(): grad_one, grad_two = lax.psum((grad_one, grad_two), ('region', 'split'))  75.3 us
    dot_general x54, matrix products, accumulate(): return total + jnp.dot(picked, weights, preferred_element_type=jnp.float32)  59.8 us
    gather x27, local copies, waits for them, and re-layouts, accumulate(): jnp.take(window_rows, lax.dynamic_index_in_dim(lookup, 26 - offset, 0, ke...  52.7 us
    dot_general x54, matrix products, accumulate(): jnp.dot(picked.T, gradient_rows, preferred_element_type=jnp.float32)  51.7 us
    dot_general x27, matrix products, accumulate(): jnp.dot(picked, weights.T, preferred_element_type=jnp.float32)  30.4 us
    ppermute x6, starting transfers between devices, from_behind(): lax.ppermute(value, axis, [(source, source + steps) for source in range(f...  17.8 us
  transfers between devices with their start and end apart: 10, of which 2 were waited for; matrix products, arithmetic and copies ran while one was open for 38% of the time, Pallas kernels for 0%

commit v1 on v0

v1 whole, which is shorter than its diff:
```python
import functools

import jax
import jax.numpy as jnp
from jax import lax
from jax.experimental import pallas as pl
from jax.experimental.pallas import tpu as pltpu
from jax.sharding import PartitionSpec as P

F32 = jnp.float32
BF16 = jnp.bfloat16
LANES = 128
VMEM_BYTES = 56 * 2**20


def up_to(value, step):
    return -(-value // step) * step


def whole(count):
    return [pl.BlockSpec(memory_space=pltpu.VMEM)] * count


def pack_kernel(features_ref, occupancy_ref, cotangent_ref, packed_ref):
    channels, voxels = features_ref.shape
    outs = cotangent_ref.shape[0]
    active = occupancy_ref[...] > 0
    masked = jnp.where(active, features_ref[...].astype(F32), 0.0)
    flag = jnp.where(active, 1.0, 0.0)
    row = lax.broadcasted_iota(jnp.int32, (LANES - channels, voxels), 0)
    tail = jnp.where(row == 0, jnp.broadcast_to(flag, row.shape), 0.0)
    packed_ref[:, :LANES] = jnp.concatenate([masked, tail], 0).T.astype(BF16)
    grad_out = jnp.where(active, cotangent_ref[...].astype(F32), 0.0)
    spare = up_to(outs, LANES) - outs
    grad_out = jnp.concatenate([grad_out, jnp.zeros((spare, voxels), F32)], 0)
    packed_ref[:, LANES:] = grad_out.T.astype(BF16)


def planes_kernel(position_ref, own_ref, partner_ref, first_ref, second_ref):
    odd = position_ref[0]
    for which, target in enumerate((first_ref, second_ref)):
        upper = 1 - odd if which == 0 else odd
        for source, block in enumerate((own_ref, partner_ref)):
            row = pl.multiple_of(upper * 384, 128)
            near = pl.multiple_of(upper * 448, 64)
            target[source, :, :LANES] = block[pl.ds(row, 128), :LANES]
            target[source, :64, LANES:] = block[pl.ds(near, 64), LANES : 2 * LANES]
            target[source, 64:, LANES:] = block[pl.ds(near, 64), 2 * LANES :]


def weights_kernel(one_ref, two_ref, one_pad_ref, two_pad_ref, two_turned_ref):
    offsets, channels, outs = two_ref.shape
    one_pad_ref[:, :channels, :] = one_ref[...]
    two_pad_ref[:, :channels, :] = two_ref[...]
    spare = LANES - channels
    one_pad_ref[:, channels:, :] = jnp.zeros((offsets, spare, one_ref.shape[2]), BF16)
    two_pad_ref[:, channels:, :] = jnp.zeros((offsets, spare, outs), BF16)
    two_turned_ref[:, outs:, :] = jnp.zeros((offsets, two_turned_ref.shape[1] - outs, channels), BF16)
    for offset in range(offsets):
        two_turned_ref[offset, :outs, :] = two_ref[offset].astype(F32).T.astype(BF16)


def tile_of(offset, offsets):
    group, place = divmod(offset, 4)
    return group, place


def store_gradient(total_ref, product, offset, first_row, rows, channels):
    group, place = tile_of(offset, 27)
    if place < 3:
        base = (3 * group + place) * rows + first_row
        total_ref[base : base + product.shape[0], :channels] = product[:, :channels]
    else:
        spare = LANES - channels
        for piece in range(3):
            base = (3 * group + piece) * rows + first_row
            total_ref[base : base + product.shape[0], channels:] = product[:, piece * spare : (piece + 1) * spare]


def main_kernel(
    position_ref, neighbors_ref, own_ref, partner_ref, first_ref, second_ref, cotangent_ref, occupancy_ref,
    one_ref, two_ref, turned_ref, output_ref, kept_ref, sent_ref, masked_w, grad_w, hidden_w, total,
):
    odd, split = position_ref[0], position_ref[1]
    channels = one_ref.shape[2]
    outs = two_ref.shape[2]
    wide = grad_w.shape[3]
    masked_w[:, 6:18] = jnp.zeros((12, 12, 24, LANES), F32)
    grad_w[:, 7:17] = jnp.zeros((10, 10, 24, wide), F32)

    own = own_ref[...].astype(F32).reshape(8, 8, 8, LANES + wide)
    masked_w[2:10, 8:16, 8:16, :] = own[..., :LANES]
    grad_w[1:9, 8:16, 8:16, :] = own[..., LANES:]

    def placed(step_x, step_z):
        found = [neighbors_ref[0, 9 * (step_x + 1) + 3 * step_y + step_z + 1] >= 0 for step_y in range(3)]
        y = jnp.where(found[0], 0, jnp.where(found[1], 1, 2))
        return found[0] | found[1] | found[2], pl.multiple_of(8 * y, 8)

    step_z = 1 - 2 * split
    valid, y = placed(0, step_z)
    z = pl.multiple_of(8 + 8 * step_z, 8)

    @pl.when(valid)
    def _():
        block = partner_ref[...].astype(F32).reshape(8, 8, 8, LANES + wide)
        masked_w[2:10, pl.ds(y, 8), pl.ds(z, 8), :] = block[..., :LANES]
        grad_w[1:9, pl.ds(y, 8), pl.ds(z, 8), :] = block[..., LANES:]

    for which, ref in enumerate((first_ref, second_ref)):
        step_x = 1 - 2 * odd if which == 0 else 2 * odd - 1
        for source in range(2):
            step_z = 0 if source == 0 else 1 - 2 * split
            valid, y = placed(step_x, step_z)
            z = pl.multiple_of(8 + 8 * step_z, 8)
            x_masked = jnp.where(step_x > 0, 10, 0)
            x_grad = jnp.where(step_x > 0, 9, 0)

            @pl.when(valid)
            def _():
                block = ref[source].astype(F32)
                masked_w[pl.ds(x_masked, 2), pl.ds(y, 8), pl.ds(z, 8), :] = block[:, :LANES].reshape(2, 8, 8, LANES)
                near = jnp.concatenate([block[:64, LANES:], block[64:, LANES:]], 1)
                grad_w[pl.ds(x_grad, 1), pl.ds(y, 8), pl.ds(z, 8), :] = near.reshape(1, 8, 8, wide)

    def weights(ref, code):
        return jnp.concatenate([ref[code], ref[9 + code], ref[18 + code]], 0)

    hidden_pre = None
    for code in range(9):
        dy, dz = divmod(code, 3)
        shifted = masked_w[:, 6 + dy : 16 + dy, 6 + dz : 22 + dz, :].reshape(12 * 160, LANES).astype(BF16)
        rows = jnp.concatenate([shifted[160 * dx : 160 * dx + 1600] for dx in range(3)], 1)
        term = jnp.dot(rows, weights(one_ref, code), preferred_element_type=F32)
        hidden_pre = term if hidden_pre is None else hidden_pre + term
    flags = masked_w[1:11, 7:17, 7:23, channels : channels + 1].reshape(1600, 1) > 0
    hidden_pre = jnp.where(flags, hidden_pre, 0.0)
    hidden = hidden_pre * jax.nn.sigmoid(hidden_pre)
    hidden_w[..., :channels] = hidden.reshape(10, 10, 16, channels)
    hidden_w[..., channels:] = jnp.zeros((10, 10, 16, LANES - channels), F32)
    own_pre = hidden_pre.reshape(10, 10, 16, channels)[1:9, 1:9, 1:9, :].reshape(512, channels)
    own_flag = masked_w[2:10, 8:16, 8:16, channels : channels + 1].reshape(512, 1) > 0

    rows_per_tile = outs + channels
    turned_out = jnp.where(occupancy_ref[...] > 0, cotangent_ref[...].astype(F32), 0.0).astype(BF16)
    output = None
    total[...] = jnp.zeros_like(total)
    for code in range(9):
        dy, dz = divmod(code, 3)
        shifted = hidden_w[:, dy : dy + 8, dz : dz + 8, :].reshape(640, LANES).astype(BF16)
        rows = jnp.concatenate([shifted[64 * dx : 64 * dx + 512] for dx in range(3)], 1)
        term = jnp.dot(rows, weights(two_ref, code), preferred_element_type=F32)
        output = term if output is None else output + term
        product = jnp.dot(turned_out, rows, preferred_element_type=F32)
        for dx in range(3):
            store_gradient(total, product[:, dx * LANES : (dx + 1) * LANES], 9 * dx + code, 0, rows_per_tile, channels)
    output_ref[...] = jnp.where(own_flag, output, 0.0).T.astype(BF16)

    back = None
    for code in range(9):
        dy, dz = divmod(code, 3)
        shifted = grad_w[:, 7 + dy : 15 + dy, 7 + dz : 15 + dz, :].reshape(640, wide).astype(BF16)
        rows = jnp.concatenate([shifted[64 * dx : 64 * dx + 512] for dx in range(3)], 1)
        kernel = jnp.concatenate([turned_ref[26 - code], turned_ref[17 - code], turned_ref[8 - code]], 0)
        term = jnp.dot(rows, kernel, preferred_element_type=F32)
        back = term if back is None else back + term
    gate = jax.nn.sigmoid(own_pre)
    grad_pre = jnp.where(own_flag, back * gate * (1.0 + own_pre * (1.0 - gate)), 0.0)
    turned_pre = grad_pre.T.astype(BF16)

    for code in range(9):
        dy, dz = divmod(code, 3)
        shifted = masked_w[1:11, 7 + dy : 15 + dy, 7 + dz : 15 + dz, :].reshape(640, LANES).astype(BF16)
        rows = jnp.concatenate([shifted[64 * dx : 64 * dx + 512] for dx in range(3)], 1)
        product = jnp.dot(turned_pre, rows, preferred_element_type=F32)
        for dx in range(3):
            store_gradient(
                total, product[:, dx * LANES : (dx + 1) * LANES], 9 * dx + code, outs, rows_per_tile, channels
            )

    half = kept_ref.shape[0]
    kept_ref[...] = total[pl.ds(pl.multiple_of(split * half, 16), half), :]
    sent_ref[...] = total[pl.ds(pl.multiple_of((1 - split) * half, 16), half), :].astype(BF16)


def unpack_kernel(sums_ref, one_ref, two_ref):
    count, channels, outs = two_ref.shape
    rows = outs + channels
    for place in range(3):
        tile = sums_ref[place * rows : (place + 1) * rows, :].astype(F32)
        for ref, part in ((two_ref, tile[:outs].T), (one_ref, tile[outs:].T)):
            spare = LANES - channels
            ref[place] = part[:channels]
            ref[3, place * spare : (place + 1) * spare, :] = part[channels:]


def call(kernel, out_shape, args, scalars=0, scratch=(), cost=None):
    specs = [pl.BlockSpec(memory_space=pltpu.SMEM)] * scalars + whole(len(args) - scalars)
    return pl.pallas_call(
        kernel,
        out_shape=out_shape,
        in_specs=specs,
        out_specs=jax.tree.map(lambda _: pl.BlockSpec(memory_space=pltpu.VMEM), out_shape),
        scratch_shapes=list(scratch),
        compiler_params=pltpu.CompilerParams(vmem_limit_bytes=VMEM_BYTES),
        cost_estimate=cost,
    )(*args)


def exchanged(value, axis, mask):
    return lax.ppermute(value, axis, [(i, i ^ mask) for i in range(lax.axis_size(axis))])


def halves(value, bit):
    half = value.shape[0] // 2
    return (
        lax.dynamic_slice_in_dim(value, bit * half, half, 0),
        lax.dynamic_slice_in_dim(value, (1 - bit) * half, half, 0),
    )


def shards(features, kernel_one, kernel_two, occupancy, neighbors, cotangent):
    channels, voxels = features.shape
    offsets, _, outs = kernel_two.shape
    regions = lax.axis_size("region")
    region = lax.axis_index("region").astype(jnp.int32)
    split = lax.axis_index("split").astype(jnp.int32)
    odd = region % 2
    position = jnp.stack([odd, split])
    wide = up_to(outs, LANES)
    struct = jax.ShapeDtypeStruct

    packed = call(pack_kernel, struct((voxels, LANES + wide), BF16), (features, occupancy, cotangent))
    partner = exchanged(packed, "split", 1)
    faces = struct((2, 128, 2 * LANES), BF16)
    first, second = call(planes_kernel, (faces, faces), (position, packed, partner), scalars=1)
    first = lax.ppermute(first, "region", [(i, i ^ 1) for i in range(regions)])
    pairs = [(i, i + 1) for i in range(1, regions - 1, 2)]
    second = lax.ppermute(second, "region", pairs + [(b, a) for a, b in pairs])
    weights = call(
        weights_kernel,
        (
            struct((offsets, LANES, channels), BF16),
            struct((offsets, LANES, outs), BF16),
            struct((offsets, wide, channels), BF16),
        ),
        (kernel_one, kernel_two),
        cost=pl.CostEstimate(flops=10**8, bytes_accessed=10**7, transcendentals=0),
    )

    groups = -(-offsets // 4)
    tile_rows = outs + channels
    rows = up_to(3 * groups * tile_rows, 2 * regions * 16)
    output, kept, sent = call(
        main_kernel,
        (struct((outs, voxels), BF16), struct((rows // 2, LANES), F32), struct((rows // 2, LANES), BF16)),
        (position, neighbors, packed, partner, first, second, cotangent, occupancy, *weights),
        scalars=2,
        scratch=(
            pltpu.VMEM((12, 24, 24, LANES), F32),
            pltpu.VMEM((10, 24, 24, wide), F32),
            pltpu.VMEM((10, 10, 16, LANES), F32),
            pltpu.VMEM((rows, LANES), F32),
        ),
    )

    total = kept + exchanged(sent, "split", 1).astype(F32)
    masks = [1 << i for i in range((regions - 1).bit_length())]
    for mask in masks:
        keep, give = halves(total, (region // mask) % 2)
        total = keep + exchanged(give.astype(BF16), "region", mask).astype(F32)
    total = total.astype(BF16)
    for axis, mask in [("region", mask) for mask in reversed(masks)] + [("split", 1)]:
        other = exchanged(total, axis, mask)
        bit = (region // mask) % 2 if axis == "region" else split
        total = jnp.where(bit == 0, jnp.concatenate([total, other], 0), jnp.concatenate([other, total], 0))

    grad_one, grad_two = pl.pallas_call(
        unpack_kernel,
        grid=(groups,),
        in_specs=[pl.BlockSpec((3 * tile_rows, LANES), lambda i: (i, 0))],
        out_specs=[
            pl.BlockSpec((4, channels, channels), lambda i: (i, 0, 0)),
            pl.BlockSpec((4, channels, outs), lambda i: (i, 0, 0)),
        ],
        out_shape=[struct((offsets, channels, channels), F32), struct((offsets, channels, outs), F32)],
    )(total)
    return output, grad_one, grad_two


def solution(mesh):
    rows = P(("region", "split"), None)
    columns = P(None, ("region", "split"))
    return jax.shard_map(
        shards,
        mesh=mesh,
        in_specs=(columns, P(), P(), rows, rows, columns),
        out_specs=(columns, P(), P()),
        check_vma=False,
    )
```

time: 566 us -> 102 us (0.18)
  local copies, waits for them, and re-layouts: 282 us -> 1.59 us
  matrix products: 142 us -> 0 us
  waiting for transfers between devices: 80.7 us -> 41.6 us
  Pallas kernels: 0 us -> 29.7 us
  between operations: 14.5 us -> 0.74 us
  blocking collectives: 11 us -> 0 us
  loops' own time: 6.28 us -> 0 us
    gather x136 -> x0, local copies, waits for them, and re-layouts: 275 us -> none  [the longest x108 145 us: accumulate(): jnp.take(window_rows, lax.dynamic_index_in_dim(lookup, offset, 0, keepdim...]
    dot_general x135 -> x0, matrix products: 142 us -> none  [the longest x54 59.8 us: accumulate(): return total + jnp.dot(picked, weights, preferred_element_type=jnp.float32)]
    psum x1 -> x0, waiting for transfers between devices: 75.3 us -> none  [shards(): grad_one, grad_two = lax.psum((grad_one, grad_two), ('region', 'split'))]
    ppermute x9 -> x13, waiting for transfers between devices: 5.37 us -> 41.6 us  [the longest x11 41.6 us: exchanged(): lax.ppermute(value, axis, [(i, i ^ mask) for i in range(lax.axis_size(axi...]
    pallas_call x0 -> x5, Pallas kernels: none -> 29.7 us  [the longest x4 23.7 us: call(): pl.pallas_call(kernel, out_shape=out_shape, in_specs=specs, out_specs=jax...]
    all_gather x6 -> x0, blocking collectives: 11 us -> none  [the longest x3 5.52 us: spread(): lax.all_gather(lower_plane, 'split', axis=1, tiled=True)]
    another operation x5 -> x0, loops' own time: 6.28 us -> none  [the longest x2 3.37 us: convolve(): lax.fori_loop(0, 27, accumulate, jnp.zeros((lookup.shape[1], kernel.shape...]
    ppermute x9 -> x13, starting transfers between devices: 18.8 us -> 23.9 us  [the longest x11 20.3 us: exchanged(): lax.ppermute(value, axis, [(i, i ^ mask) for i in range(lax.axis_size(axi...]
  transfers between devices with their start and end apart: 10 -> 13, of which waited for: 2 -> 11; matrix products, arithmetic and copies ran while one was open for 38% -> 1% of each run, Pallas kernels for 0% -> 4%
where the time goes in v1:
time: 102 us
  waiting for transfers between devices  41.6 us (41%)
  Pallas kernels  29.7 us (29%)
  starting transfers between devices  23.9 us (23%)
  other arithmetic  4.24 us (4%)
  local copies, waits for them, and re-layouts  1.59 us (2%)
    ppermute x11, waiting for transfers between devices, exchanged(): lax.ppermute(value, axis, [(i, i ^ mask) for i in range(lax.axis_size(axi...  41.6 us
    pallas_call x4, Pallas kernels, call(): pl.pallas_call(kernel, out_shape=out_shape, in_specs=specs, out_specs=jax...  23.7 us
    ppermute x11, starting transfers between devices, exchanged(): lax.ppermute(value, axis, [(i, i ^ mask) for i in range(lax.axis_size(axi...  20.3 us
    pallas_call x1, Pallas kernels, shards(): pl.pallas_call(unpack_kernel, grid=(groups,), in_specs=[pl.BlockSpec((3 *...  6.02 us
    ppermute x1, starting transfers between devices, shards(): first = lax.ppermute(first, 'region', [(i, i ^ 1) for i in range(regions)])  2.86 us
  transfers between devices with their start and end apart: 13, of which 11 were waited for; matrix products, arithmetic and copies ran while one was open for 1% of the time, Pallas kernels for 4%

profile of v1, /device:TPU:0, one launch (start us, length us, event | category | flops | bytes accessed | tf_op | source)
XLA Modules:
  0.0 101.7 jit_solution(10285173001916582955)
XLA Ops:
  0.6 1.9 %shard_map.85.own_ref = bf16[512,384]{1,0:T(8,128)(2,1)} custom-call(bf16[96,512]{1,0:T(8,128)(2,1)} %features_ref.1, s32[1,512]{1,0:T(1,128)} %occupancy_ref.3, bf16[192,512]{1,0:T(8,128)(2,1)} %cotangent_ref.3), custom_call_target="tpu_custom_call" | custom-call | tf_op jit(solution)/shard_map/pallas_call | solution.py:199
  2.6 0.5 collective-permute-start
  3.0 0.6 pad_add_fusion.position_ref
  3.6 1.0 collective-permute-done.partner_ref
  4.6 0.8 copy-done
  5.3 1.9 %shard_map.86 = (bf16[2,128,256]{2,1,0:T(8,128)(2,1)}, bf16[2,128,256]{2,1,0:T(8,128)(2,1)}) custom-call(s32[2]{0:T(128)} %pad_add_fusion.position_ref, bf16[512,384]{1,0:T(8,128)(2,1)} %shard_map.85.own_ref, bf16[512,384]{1,0:T(8,128)(2,1)} %copy-done), custom_call_target="tpu_custom_call" | custom-call | tf_op jit(solution)/shard_map/pallas_call | solution.py:199
  7.2 2.9 %collective-permute-start.1 = (bf16[2,128,256]{2,1,0:T(8,128)(2,1)}, bf16[2,128,256]{2,1,0:T(8,128)(2,1)S(1)}, u32[]{:S(2)}, u32[]{:S(2)}) collective-permute-start(bf16[2,128,256]{2,1,0:T(8,128)(2,1)} %get-tuple-element.13), channel_id=1, source_target_pairs={{0,2},{2,0},{4,6},{6,4},{8,10},{10,8},{12,14},{14,12},{16,18},{18,... | collective-permute-start | bytes 393224 | tf_op jit(solution)/shard_map/ppermute | solution.py:237
  10.1 0.7 collective-permute-start.2
  10.7 4.3 %shard_map.87 = (bf16[27,128,96]{2,1,0:T(8,128)(2,1)}, bf16[27,128,192]{2,1,0:T(8,128)(2,1)}, bf16[27,256,96]{2,1,0:T(8,128)(2,1)}) custom-call(bf16[27,96,96]{2,1,0:T(8,128)(2,1)} %one_ref.1, bf16[27,96,192]{2,1,0:T(8,128)(2,1)} %two_ref.1), custom_call_target="tpu_custom_call" | custom-call | flops 100000000 | bytes 10000000 | tf_op jit(solution)/shard_map/pallas_call | solution.py:199
  15.1 0.6 copy-done.1
  15.8 15.5 %shard_map.88 = (bf16[192,512]{1,0:T(8,128)(2,1)}, f32[3072,128]{1,0:T(8,128)}, bf16[3072,128]{1,0:T(8,128)(2,1)}) custom-call(s32[2]{0:T(128)} %pad_add_fusion.position_ref, s32[1,27]{1,0:T(1,128)} %neighbors_ref.1, bf16[512,384]{1,0:T(8,128)(2,1)} %shard_map.85.own_ref, bf16[512,384]{1,0:T(8,128)(2,1)} %copy-done, bf16[2,128,256]{2,1,0:T(8,128)(2,1)} %copy-done.1, ...), custom_call_target="tpu_custom_call" | custom-call | tf_op jit(solution)/shard_map/pallas_call | solution.py:199
  31.3 2.5 %collective-permute-done.3 = bf16[3072,128]{1,0:T(8,128)(2,1)S(1)} collective-permute-done((bf16[3072,128]{1,0:T(8,128)(2,1)}, bf16[3072,128]{1,0:T(8,128)(2,1)S(1)}, u32[]{:S(2)}, u32[]{:S(2)}) %collective-permute-start.3) | collective-permute-done | bytes 786464 | tf_op jit(solution)/shard_map/ppermute | solution.py:211
  33.8 1.5 %convert_add_fusion = f32[3072,128]{1,0:T(8,128)S(1)} fusion(f32[3072,128]{1,0:T(8,128)} %get-tuple-element.19, bf16[3072,128]{1,0:T(8,128)(2,1)S(1)} %collective-permute-done.3), kind=kLoop, calls=%fused_computation.1 | loop fusion | flops 786432 | bytes 3932160 | tf_op jit(solution)/shard_map/add | solution.py:267
  35.4 4.5 %collective-permute-start.4 = (bf16[1536,128]{1,0:T(8,128)(2,1)S(1)}, bf16[1536,128]{1,0:T(8,128)(2,1)S(1)}, u32[]{:S(2)}, u32[]{:S(2)}) collective-permute-start(bf16[1536,128]{1,0:T(8,128)(2,1)S(1)} %dynamic-slice_convert_fusion), channel_id=1, source_target_pairs={{0,2},{2,0},{4,6},{6,4},{8,10},{10,8},{12,14},{14,12},{16,18},{18,... | collective-permute-start | bytes 1179656 | tf_op jit(solution)/shard_map/ppermute | solution.py:211
  40.0 9.4 %collective-permute-done.4 = bf16[1536,128]{1,0:T(8,128)(2,1)S(1)} collective-permute-done((bf16[1536,128]{1,0:T(8,128)(2,1)S(1)}, bf16[1536,128]{1,0:T(8,128)(2,1)S(1)}, u32[]{:S(2)}, u32[]{:S(2)}) %collective-permute-start.4) | collective-permute-done | bytes 393248 | tf_op jit(solution)/shard_map/ppermute | solution.py:211
  49.5 2.1 %collective-permute-start.5 = (bf16[768,128]{1,0:T(8,128)(2,1)S(1)}, bf16[768,128]{1,0:T(8,128)(2,1)S(1)}, u32[]{:S(2)}, u32[]{:S(2)}) collective-permute-start(bf16[768,128]{1,0:T(8,128)(2,1)S(1)} %dynamic-slice_convert_fusion.1), channel_id=1, source_target_pairs={{0,4},{2,6},{4,0},{6,2},{8,12},{10,14},{12,8},{14,10},{16,20},{18,... | collective-permute-start | bytes 589832 | tf_op jit(solution)/shard_map/ppermute | solution.py:211
  51.5 4.4 %collective-permute-done.5 = bf16[768,128]{1,0:T(8,128)(2,1)S(1)} collective-permute-done((bf16[768,128]{1,0:T(8,128)(2,1)S(1)}, bf16[768,128]{1,0:T(8,128)(2,1)S(1)}, u32[]{:S(2)}, u32[]{:S(2)}) %collective-permute-start.5) | collective-permute-done | bytes 196640 | tf_op jit(solution)/shard_map/ppermute | solution.py:211
  56.0 2.7 %collective-permute-start.6 = (bf16[384,128]{1,0:T(8,128)(2,1)S(1)}, bf16[384,128]{1,0:T(8,128)(2,1)S(1)}, u32[]{:S(2)}, u32[]{:S(2)}) collective-permute-start(bf16[384,128]{1,0:T(8,128)(2,1)S(1)} %dynamic-slice_convert_fusion.2), channel_id=1, source_target_pairs={{0,8},{2,10},{4,12},{6,14},{8,0},{10,2},{12,4},{14,6},{16,24},{18,... | collective-permute-start | bytes 294920 | tf_op jit(solution)/shard_map/ppermute | solution.py:211
  58.7 2.6 %collective-permute-done.6 = bf16[384,128]{1,0:T(8,128)(2,1)S(1)} collective-permute-done((bf16[384,128]{1,0:T(8,128)(2,1)S(1)}, bf16[384,128]{1,0:T(8,128)(2,1)S(1)}, u32[]{:S(2)}, u32[]{:S(2)}) %collective-permute-start.6) | collective-permute-done | bytes 98336 | tf_op jit(solution)/shard_map/ppermute | solution.py:211
  61.4 3.3 %collective-permute-start.7 = (bf16[192,128]{1,0:T(8,128)(2,1)S(1)}, bf16[192,128]{1,0:T(8,128)(2,1)S(1)}, u32[]{:S(2)}, u32[]{:S(2)}) collective-permute-start(bf16[192,128]{1,0:T(8,128)(2,1)S(1)} %dynamic-slice_convert_fusion.3), channel_id=1, source_target_pairs={{0,16},{2,18},{4,20},{6,22},{8,24},{10,26},{12,28},{14,30},{16,0},... | collective-permute-start | bytes 147464 | tf_op jit(solution)/shard_map/ppermute | solution.py:211
  64.7 2.3 %collective-permute-done.7 = bf16[192,128]{1,0:T(8,128)(2,1)S(1)} collective-permute-done((bf16[192,128]{1,0:T(8,128)(2,1)S(1)}, bf16[192,128]{1,0:T(8,128)(2,1)S(1)}, u32[]{:S(2)}, u32[]{:S(2)}) %collective-permute-start.7) | collective-permute-done | bytes 49184 | tf_op jit(solution)/shard_map/ppermute | solution.py:211
  67.0 3.4 %collective-permute-start.8 = (bf16[192,128]{1,0:T(8,128)(2,1)S(1)}, bf16[192,128]{1,0:T(8,128)(2,1)S(1)}, u32[]{:S(2)}, u32[]{:S(2)}) collective-permute-start(bf16[192,128]{1,0:T(8,128)(2,1)S(1)} %add_convert_fusion), channel_id=1, source_target_pairs={{0,16},{2,18},{4,20},{6,22},{8,24},{10,26},{12,28},{14,30},{16,0},... | collective-permute-start | bytes 147464 | tf_op jit(solution)/shard_map/ppermute | solution.py:211
  70.3 2.1 %collective-permute-done.8 = bf16[192,128]{1,0:T(8,128)(2,1)S(1)} collective-permute-done((bf16[192,128]{1,0:T(8,128)(2,1)S(1)}, bf16[192,128]{1,0:T(8,128)(2,1)S(1)}, u32[]{:S(2)}, u32[]{:S(2)}) %collective-permute-start.8) | collective-permute-done | bytes 49184 | tf_op jit(solution)/shard_map/ppermute | solution.py:211
  72.4 2.8 %collective-permute-start.9 = (bf16[384,128]{1,0:T(8,128)(2,1)S(1)}, bf16[384,128]{1,0:T(8,128)(2,1)S(1)}, u32[]{:S(2)}, u32[]{:S(2)}) collective-permute-start(bf16[384,128]{1,0:T(8,128)(2,1)S(1)} %maximum_select_fusion.4), channel_id=1, source_target_pairs={{0,8},{2,10},{4,12},{6,14},{8,0},{10,2},{12,4},{14,6},{16,24},{18,... | collective-permute-start | bytes 294920 | tf_op jit(solution)/shard_map/ppermute | solution.py:211
  75.2 2.6 %collective-permute-done.9 = bf16[384,128]{1,0:T(8,128)(2,1)S(1)} collective-permute-done((bf16[384,128]{1,0:T(8,128)(2,1)S(1)}, bf16[384,128]{1,0:T(8,128)(2,1)S(1)}, u32[]{:S(2)}, u32[]{:S(2)}) %collective-permute-start.9) | collective-permute-done | bytes 98336 | tf_op jit(solution)/shard_map/ppermute | solution.py:211
  77.8 0.7 collective-permute-start.10
  78.5 5.1 %collective-permute-done.10 = bf16[768,128]{1,0:T(8,128)(2,1)S(1)} collective-permute-done((bf16[768,128]{1,0:T(8,128)(2,1)S(1)}, bf16[768,128]{1,0:T(8,128)(2,1)S(1)}, u32[]{:S(2)}, u32[]{:S(2)}) %collective-permute-start.10) | collective-permute-done | bytes 196640 | tf_op jit(solution)/shard_map/ppermute | solution.py:211
  83.7 0.4 collective-permute-start.11
  84.1 7.4 %collective-permute-done.11 = bf16[1536,128]{1,0:T(8,128)(2,1)S(1)} collective-permute-done((bf16[1536,128]{1,0:T(8,128)(2,1)S(1)}, bf16[1536,128]{1,0:T(8,128)(2,1)S(1)}, u32[]{:S(2)}, u32[]{:S(2)}) %collective-permute-start.11) | collective-permute-done | bytes 393248 | tf_op jit(solution)/shard_map/ppermute | solution.py:211
  91.8 2.3 %collective-permute-done.12 = bf16[3072,128]{1,0:T(8,128)(2,1)S(1)} collective-permute-done((bf16[3072,128]{1,0:T(8,128)(2,1)S(1)}, bf16[3072,128]{1,0:T(8,128)(2,1)S(1)}, u32[]{:S(2)}, u32[]{:S(2)}) %collective-permute-start.12) | collective-permute-done | bytes 786464 | tf_op jit(solution)/shard_map/ppermute | solution.py:211
  94.1 1.6 %maximum_select_fusion.sums_ref = bf16[6144,128]{1,0:T(8,128)(2,1)} fusion(bf16[3072,128]{1,0:T(8,128)(2,1)S(1)} %collective-permute-done.12, bf16[3072,128]{1,0:T(8,128)(2,1)S(1)} %maximum_select_fusion.1, pred[]{:T(512)S(6)} %eq.25), kind=kLoop, calls=%fused_computation | loop fusion | flops 7077888 | bytes 3145729 | tf_op jit(solution)/shard_map/jit(_where)/select_n | solution.py:276
  95.7 6.0 %shard_map.89 = (f32[27,96,96]{2,1,0:T(8,128)}, f32[27,96,192]{2,1,0:T(8,128)}) custom-call(bf16[6144,128]{1,0:T(8,128)(2,1)} %maximum_select_fusion.sums_ref), custom_call_target="tpu_custom_call" | custom-call | tf_op jit(solution)/shard_map/pallas_call | solution.py:278
  (20 shorter events, 0.8 us)
Async XLA Ops:
  2.6 2.0 %collective-permute-start = (bf16[512,384]{1,0:T(8,128)(2,1)}, bf16[512,384]{1,0:T(8,128)(2,1)S(1)}, u32[]{:S(2)}, u32[]{:S(2)}) collective-permute-start(bf16[512,384]{1,0:T(8,128)(2,1)} %shard_map.85.own_ref), channel_id=1, source_target_pairs={{0,1},{1,0},{2,3},{3,2},{4,5},{5,4},{6,7},{7,6},{8,9},{9,8},{10,11... | collective-permute-start | bytes 1179656 | tf_op jit(solution)/shard_map/ppermute | solution.py:211
  4.6 0.8 copy-start
  7.2 7.9 %collective-permute-start.1 = (bf16[2,128,256]{2,1,0:T(8,128)(2,1)}, bf16[2,128,256]{2,1,0:T(8,128)(2,1)S(1)}, u32[]{:S(2)}, u32[]{:S(2)}) collective-permute-start(bf16[2,128,256]{2,1,0:T(8,128)(2,1)} %get-tuple-element.13), channel_id=1, source_target_pairs={{0,2},{2,0},{4,6},{6,4},{8,10},{10,8},{12,14},{14,12},{16,18},{18,... | collective-permute-start | bytes 393224 | tf_op jit(solution)/shard_map/ppermute | solution.py:237
  10.1 5.0 %collective-permute-start.2 = (bf16[2,128,256]{2,1,0:T(8,128)(2,1)}, bf16[2,128,256]{2,1,0:T(8,128)(2,1)S(1)}, u32[]{:S(2)}, u32[]{:S(2)}) collective-permute-start(bf16[2,128,256]{2,1,0:T(8,128)(2,1)} %get-tuple-element.14), channel_id=1, source_target_pairs={{2,4},{6,8},{10,12},{14,16},{18,20},{22,24},{26,28},{4,2},{8,6},{1... | collective-permute-start | bytes 393224 | tf_op jit(solution)/shard_map/ppermute | solution.py:239
  15.1 0.6 copy-start.1
  15.1 0.7 copy-start.2
  31.3 2.5 %collective-permute-start.3 = (bf16[3072,128]{1,0:T(8,128)(2,1)}, bf16[3072,128]{1,0:T(8,128)(2,1)S(1)}, u32[]{:S(2)}, u32[]{:S(2)}) collective-permute-start(bf16[3072,128]{1,0:T(8,128)(2,1)} %get-tuple-element.20), channel_id=1, source_target_pairs={{0,1},{1,0},{2,3},{3,2},{4,5},{5,4},{6,7},{7,6},{8,9},{9,8},{10,11... | collective-permute-start | bytes 2359304 | tf_op jit(solution)/shard_map/ppermute | solution.py:211
  35.4 14.0 %collective-permute-start.4 = (bf16[1536,128]{1,0:T(8,128)(2,1)S(1)}, bf16[1536,128]{1,0:T(8,128)(2,1)S(1)}, u32[]{:S(2)}, u32[]{:S(2)}) collective-permute-start(bf16[1536,128]{1,0:T(8,128)(2,1)S(1)} %dynamic-slice_convert_fusion), channel_id=1, source_target_pairs={{0,2},{2,0},{4,6},{6,4},{8,10},{10,8},{12,14},{14,12},{16,18},{18,... | collective-permute-start | bytes 1179656 | tf_op jit(solution)/shard_map/ppermute | solution.py:211
  49.5 6.5 %collective-permute-start.5 = (bf16[768,128]{1,0:T(8,128)(2,1)S(1)}, bf16[768,128]{1,0:T(8,128)(2,1)S(1)}, u32[]{:S(2)}, u32[]{:S(2)}) collective-permute-start(bf16[768,128]{1,0:T(8,128)(2,1)S(1)} %dynamic-slice_convert_fusion.1), channel_id=1, source_target_pairs={{0,4},{2,6},{4,0},{6,2},{8,12},{10,14},{12,8},{14,10},{16,20},{18,... | collective-permute-start | bytes 589832 | tf_op jit(solution)/shard_map/ppermute | solution.py:211
  56.0 5.3 %collective-permute-start.6 = (bf16[384,128]{1,0:T(8,128)(2,1)S(1)}, bf16[384,128]{1,0:T(8,128)(2,1)S(1)}, u32[]{:S(2)}, u32[]{:S(2)}) collective-permute-start(bf16[384,128]{1,0:T(8,128)(2,1)S(1)} %dynamic-slice_convert_fusion.2), channel_id=1, source_target_pairs={{0,8},{2,10},{4,12},{6,14},{8,0},{10,2},{12,4},{14,6},{16,24},{18,... | collective-permute-start | bytes 294920 | tf_op jit(solution)/shard_map/ppermute | solution.py:211
  61.4 5.5 %collective-permute-start.7 = (bf16[192,128]{1,0:T(8,128)(2,1)S(1)}, bf16[192,128]{1,0:T(8,128)(2,1)S(1)}, u32[]{:S(2)}, u32[]{:S(2)}) collective-permute-start(bf16[192,128]{1,0:T(8,128)(2,1)S(1)} %dynamic-slice_convert_fusion.3), channel_id=1, source_target_pairs={{0,16},{2,18},{4,20},{6,22},{8,24},{10,26},{12,28},{14,30},{16,0},... | collective-permute-start | bytes 147464 | tf_op jit(solution)/shard_map/ppermute | solution.py:211
  67.0 5.4 %collective-permute-start.8 = (bf16[192,128]{1,0:T(8,128)(2,1)S(1)}, bf16[192,128]{1,0:T(8,128)(2,1)S(1)}, u32[]{:S(2)}, u32[]{:S(2)}) collective-permute-start(bf16[192,128]{1,0:T(8,128)(2,1)S(1)} %add_convert_fusion), channel_id=1, source_target_pairs={{0,16},{2,18},{4,20},{6,22},{8,24},{10,26},{12,28},{14,30},{16,0},... | collective-permute-start | bytes 147464 | tf_op jit(solution)/shard_map/ppermute | solution.py:211
  72.4 5.4 %collective-permute-start.9 = (bf16[384,128]{1,0:T(8,128)(2,1)S(1)}, bf16[384,128]{1,0:T(8,128)(2,1)S(1)}, u32[]{:S(2)}, u32[]{:S(2)}) collective-permute-start(bf16[384,128]{1,0:T(8,128)(2,1)S(1)} %maximum_select_fusion.4), channel_id=1, source_target_pairs={{0,8},{2,10},{4,12},{6,14},{8,0},{10,2},{12,4},{14,6},{16,24},{18,... | collective-permute-start | bytes 294920 | tf_op jit(solution)/shard_map/ppermute | solution.py:211
  77.8 5.7 %collective-permute-start.10 = (bf16[768,128]{1,0:T(8,128)(2,1)S(1)}, bf16[768,128]{1,0:T(8,128)(2,1)S(1)}, u32[]{:S(2)}, u32[]{:S(2)}) collective-permute-start(bf16[768,128]{1,0:T(8,128)(2,1)S(1)} %maximum_select_fusion.3), channel_id=1, source_target_pairs={{0,4},{2,6},{4,0},{6,2},{8,12},{10,14},{12,8},{14,10},{16,20},{18,... | collective-permute-start | bytes 589832 | tf_op jit(solution)/shard_map/ppermute | solution.py:211
  83.7 7.8 %collective-permute-start.11 = (bf16[1536,128]{1,0:T(8,128)(2,1)S(1)}, bf16[1536,128]{1,0:T(8,128)(2,1)S(1)}, u32[]{:S(2)}, u32[]{:S(2)}) collective-permute-start(bf16[1536,128]{1,0:T(8,128)(2,1)S(1)} %maximum_select_fusion.2), channel_id=1, source_target_pairs={{0,2},{2,0},{4,6},{6,4},{8,10},{10,8},{12,14},{14,12},{16,18},{18,... | collective-permute-start | bytes 1179656 | tf_op jit(solution)/shard_map/ppermute | solution.py:211
  91.7 2.4 %collective-permute-start.12 = (bf16[3072,128]{1,0:T(8,128)(2,1)S(1)}, bf16[3072,128]{1,0:T(8,128)(2,1)S(1)}, u32[]{:S(2)}, u32[]{:S(2)}) collective-permute-start(bf16[3072,128]{1,0:T(8,128)(2,1)S(1)} %maximum_select_fusion.1), channel_id=1, source_target_pairs={{0,1},{1,0},{2,3},{3,2},{4,5},{5,4},{6,7},{7,6},{8,9},{9,8},{10,11... | collective-permute-start | bytes 2359304 | tf_op jit(solution)/shard_map/ppermute | solution.py:211

commit v2 on v1

--- a/solution.py
+++ b/solution.py
@@ -1,5 +1,3 @@
-import functools
-
 import jax
 import jax.numpy as jnp
 from jax import lax
@@ -60,13 +58,8 @@
         two_turned_ref[offset, :outs, :] = two_ref[offset].astype(F32).T.astype(BF16)
 
 
-def tile_of(offset, offsets):
+def store_gradient(total_ref, product, offset, first_row, rows, channels):
     group, place = divmod(offset, 4)
-    return group, place
-
-
-def store_gradient(total_ref, product, offset, first_row, rows, channels):
-    group, place = tile_of(offset, 27)
     if place < 3:
         base = (3 * group + place) * rows + first_row
         total_ref[base : base + product.shape[0], :channels] = product[:, :channels]
@@ -141,7 +134,8 @@
     own_pre = hidden_pre.reshape(10, 10, 16, channels)[1:9, 1:9, 1:9, :].reshape(512, channels)
     own_flag = masked_w[2:10, 8:16, 8:16, channels : channels + 1].reshape(512, 1) > 0
 
-    rows_per_tile = outs + channels
+    third = kept_ref.shape[1]
+    first_one = 4 * third
     turned_out = jnp.where(occupancy_ref[...] > 0, cotangent_ref[...].astype(F32), 0.0).astype(BF16)
     output = None
     total[...] = jnp.zeros_like(total)
@@ -153,7 +147,7 @@
         output = term if output is None else output + term
         product = jnp.dot(turned_out, rows, preferred_element_type=F32)
         for dx in range(3):
-            store_gradient(total, product[:, dx * LANES : (dx + 1) * LANES], 9 * dx + code, 0, rows_per_tile, channels)
+            store_gradient(total, product[:, dx * LANES : (dx + 1) * LANES], 9 * dx + code, 0, outs, channels)
     output_ref[...] = jnp.where(own_flag, output, 0.0).T.astype(BF16)
 
     back = None
@@ -175,21 +169,21 @@
         product = jnp.dot(turned_pre, rows, preferred_element_type=F32)
         for dx in range(3):
             store_gradient(
-                total, product[:, dx * LANES : (dx + 1) * LANES], 9 * dx + code, outs, rows_per_tile, channels
+                total, product[:, dx * LANES : (dx + 1) * LANES], 9 * dx + code, first_one, channels, channels
             )
 
-    half = kept_ref.shape[0]
-    kept_ref[...] = total[pl.ds(pl.multiple_of(split * half, 16), half), :]
-    sent_ref[...] = total[pl.ds(pl.multiple_of((1 - split) * half, 16), half), :].astype(BF16)
-
-
-def unpack_kernel(sums_ref, one_ref, two_ref):
-    count, channels, outs = two_ref.shape
-    rows = outs + channels
-    for place in range(3):
-        tile = sums_ref[place * rows : (place + 1) * rows, :].astype(F32)
-        for ref, part in ((two_ref, tile[:outs].T), (one_ref, tile[outs:].T)):
-            spare = LANES - channels
+    for group in range(3):
+        start = 2 * third * group
+        kept_ref[group] = total[pl.ds(pl.multiple_of(start + split * third, 16), third), :]
+        sent_ref[group] = total[pl.ds(pl.multiple_of(start + (1 - split) * third, 16), third), :].astype(BF16)
+
+
+def unpack_kernel(two_sums_ref, one_sums_ref, one_ref, two_ref):
+    for sums, ref in ((two_sums_ref, two_ref), (one_sums_ref, one_ref)):
+        channels, outs = ref.shape[1:]
+        spare = LANES - channels
+        for place in range(3):
+            part = sums[place * outs : (place + 1) * outs, :].astype(F32).T
             ref[place] = part[:channels]
             ref[3, place * spare : (place + 1) * spare, :] = part[channels:]
 
@@ -248,43 +242,58 @@
         cost=pl.CostEstimate(flops=10**8, bytes_accessed=10**7, transcendentals=0),
     )
 
-    groups = -(-offsets // 4)
-    tile_rows = outs + channels
-    rows = up_to(3 * groups * tile_rows, 2 * regions * 16)
+    fours = -(-offsets // 4)
+    third = up_to(3 * fours * channels, 2 * regions * 8) // 2
     output, kept, sent = call(
         main_kernel,
-        (struct((outs, voxels), BF16), struct((rows // 2, LANES), F32), struct((rows // 2, LANES), BF16)),
+        (struct((outs, voxels), BF16), struct((3, third, LANES), F32), struct((3, third, LANES), BF16)),
         (position, neighbors, packed, partner, first, second, cotangent, occupancy, *weights),
         scalars=2,
         scratch=(
             pltpu.VMEM((12, 24, 24, LANES), F32),
             pltpu.VMEM((10, 24, 24, wide), F32),
             pltpu.VMEM((10, 10, 16, LANES), F32),
-            pltpu.VMEM((rows, LANES), F32),
+            pltpu.VMEM((6 * third, LANES), F32),
         ),
     )
 
-    total = kept + exchanged(sent, "split", 1).astype(F32)
-    masks = [1 << i for i in range((regions - 1).bit_length())]
-    for mask in masks:
-        keep, give = halves(total, (region // mask) % 2)
-        total = keep + exchanged(give.astype(BF16), "region", mask).astype(F32)
-    total = total.astype(BF16)
-    for axis, mask in [("region", mask) for mask in reversed(masks)] + [("split", 1)]:
-        other = exchanged(total, axis, mask)
-        bit = (region // mask) % 2 if axis == "region" else split
-        total = jnp.where(bit == 0, jnp.concatenate([total, other], 0), jnp.concatenate([other, total], 0))
+    received = exchanged(sent, "split", 1).astype(F32)
+    sums = [kept[part] + received[part] for part in range(3)]
+    bits = list(range((regions - 1).bit_length()))
+    orders = [bits, bits[1::-1] + bits[2:], bits[2:] + bits[:2]]
+
+    for step in range(len(bits) - 1):
+        for part, order in enumerate(orders):
+            mask = 1 << order[step]
+            keep, give = halves(sums[part], (region // mask) % 2)
+            sums[part] = keep + exchanged(give.astype(BF16), "region", mask).astype(F32)
+    for part, order in enumerate(orders):
+        own = sums[part].astype(BF16)
+        sums[part] = (own.astype(F32) + exchanged(own, "region", 1 << order[-1]).astype(F32)).astype(BF16)
+
+    def joined(own, other, bit):
+        return jnp.where(bit == 0, jnp.concatenate([own, other], 0), jnp.concatenate([other, own], 0))
+
+    for step in reversed(range(len(bits) - 1)):
+        for part, order in enumerate(orders):
+            mask = 1 << order[step]
+            sums[part] = joined(sums[part], exchanged(sums[part], "region", mask), (region // mask) % 2)
+    other = exchanged(jnp.stack(sums), "split", 1)
+    sums = [joined(sums[part], other[part], split) for part in range(3)]
 
     grad_one, grad_two = pl.pallas_call(
         unpack_kernel,
-        grid=(groups,),
-        in_specs=[pl.BlockSpec((3 * tile_rows, LANES), lambda i: (i, 0))],
+        grid=(fours,),
+        in_specs=[
+            pl.BlockSpec((3 * outs, LANES), lambda i: (i, 0)),
+            pl.BlockSpec((3 * channels, LANES), lambda i: (i, 0)),
+        ],
         out_specs=[
             pl.BlockSpec((4, channels, channels), lambda i: (i, 0, 0)),
             pl.BlockSpec((4, channels, outs), lambda i: (i, 0, 0)),
         ],
         out_shape=[struct((offsets, channels, channels), F32), struct((offsets, channels, outs), F32)],
-    )(total)
+    )(jnp.concatenate(sums[:2], 0), sums[2])
     return output, grad_one, grad_two
 
 

time: 102 us -> 89.2 us (0.87)
  waiting for transfers between devices: 41.6 us -> 15.9 us
  starting transfers between devices: 23.9 us -> 36.5 us
    ppermute x11 -> x24, waiting for transfers between devices: 41.6 us -> 15.9 us  [exchanged(): lax.ppermute(value, axis, [(i, i ^ mask) for i in range(lax.axis_size(axi...]
    ppermute x11 -> x24, starting transfers between devices: 20.3 us -> 33 us  [exchanged(): lax.ppermute(value, axis, [(i, i ^ mask) for i in range(lax.axis_size(axi...]
    add x4 -> x7, other arithmetic: 1.66 us -> 0.31 us  [the longest x1 0.19 us: shards(): sums = [kept[part] + received[part] for part in range(3)]]
    concatenate x0 -> x1, other arithmetic: none -> 1.05 us  [shards(): jnp.concatenate(sums[:2], 0)]
  transfers between devices with their start and end apart: 13 -> 26, of which waited for: 11 -> 11; matrix products, arithmetic and copies ran while one was open for 1% -> 2% of each run, Pallas kernels for 4% -> 5%
where the time goes in v2:
time: 89.2 us; the launch traced here: 88.9 us
  starting transfers between devices  36.5 us (41%)
  Pallas kernels  29.8 us (33%)
  waiting for transfers between devices  15.9 us (18%)
  other arithmetic  4.03 us (5%)
  local copies, waits for them, and re-layouts  1.67 us (2%)
  between operations  1.1 us (1%)
    ppermute x24, starting transfers between devices, exchanged(): lax.ppermute(value, axis, [(i, i ^ mask) for i in range(lax.axis_size(axi...  33 us
    pallas_call x4, Pallas kernels, call(): pl.pallas_call(kernel, out_shape=out_shape, in_specs=specs, out_specs=jax...  23.7 us
    ppermute x24, waiting for transfers between devices, exchanged(): lax.ppermute(value, axis, [(i, i ^ mask) for i in range(lax.axis_size(axi...  15.9 us
    pallas_call x1, Pallas kernels, shards(): pl.pallas_call(unpack_kernel, grid=(fours,), in_specs=[pl.BlockSpec((3 *...  6.11 us
    ppermute x1, starting transfers between devices, shards(): first = lax.ppermute(first, 'region', [(i, i ^ 1) for i in range(regions)])  2.86 us
    select_n x14, other arithmetic, joined(): jnp.where(bit == 0, jnp.concatenate([own, other], 0), jnp.concatenate([ot...  1.84 us
  transfers between devices with their start and end apart: 26, of which 11 were waited for; matrix products, arithmetic and copies ran while one was open for 2% of the time, Pallas kernels for 5%

profile of v2, /device:TPU:0, one launch (start us, length us, event | category | flops | bytes accessed | tf_op | source)
XLA Modules:
  0.0 88.9 jit_solution(15101355501321610810)
XLA Ops:
  0.6 1.9 %shard_map.85.own_ref = bf16[512,384]{1,0:T(8,128)(2,1)} custom-call(bf16[96,512]{1,0:T(8,128)(2,1)} %features_ref.1, s32[1,512]{1,0:T(1,128)} %occupancy_ref.3, bf16[192,512]{1,0:T(8,128)(2,1)} %cotangent_ref.3), custom_call_target="tpu_custom_call" | custom-call | tf_op jit(solution)/shard_map/pallas_call | solution.py:193
  3.6 1.0 %collective-permute-done.partner_ref = bf16[512,384]{1,0:T(8,128)(2,1)S(1)} collective-permute-done((bf16[512,384]{1,0:T(8,128)(2,1)}, bf16[512,384]{1,0:T(8,128)(2,1)S(1)}, u32[]{:S(2)}, u32[]{:S(2)}) %collective-permute-start) | collective-permute-done | bytes 393248 | tf_op jit(solution)/shard_map/ppermute | solution.py:205
  4.6 0.8 copy-done
  5.3 1.9 %shard_map.86 = (bf16[2,128,256]{2,1,0:T(8,128)(2,1)}, bf16[2,128,256]{2,1,0:T(8,128)(2,1)}) custom-call(s32[2]{0:T(128)} %pad_add_fusion.position_ref, bf16[512,384]{1,0:T(8,128)(2,1)} %shard_map.85.own_ref, bf16[512,384]{1,0:T(8,128)(2,1)} %copy-done), custom_call_target="tpu_custom_call" | custom-call | tf_op jit(solution)/shard_map/pallas_call | solution.py:193
  7.2 2.9 %collective-permute-start.1 = (bf16[2,128,256]{2,1,0:T(8,128)(2,1)}, bf16[2,128,256]{2,1,0:T(8,128)(2,1)S(1)}, u32[]{:S(2)}, u32[]{:S(2)}) collective-permute-start(bf16[2,128,256]{2,1,0:T(8,128)(2,1)} %get-tuple-element.13), channel_id=1, source_target_pairs={{0,2},{2,0},{4,6},{6,4},{8,10},{10,8},{12,14},{14,12},{16,18},{18,... | collective-permute-start | bytes 393224 | tf_op jit(solution)/shard_map/ppermute | solution.py:231
  10.7 4.3 %shard_map.87 = (bf16[27,128,96]{2,1,0:T(8,128)(2,1)}, bf16[27,128,192]{2,1,0:T(8,128)(2,1)}, bf16[27,256,96]{2,1,0:T(8,128)(2,1)}) custom-call(bf16[27,96,96]{2,1,0:T(8,128)(2,1)} %one_ref.1, bf16[27,96,192]{2,1,0:T(8,128)(2,1)} %two_ref.1), custom_call_target="tpu_custom_call" | custom-call | flops 100000000 | bytes 10000000 | tf_op jit(solution)/shard_map/pallas_call | solution.py:193
  15.8 15.5 %shard_map.88 = (bf16[192,512]{1,0:T(8,128)(2,1)}, f32[3,1024,128]{2,1,0:T(8,128)}, bf16[3,1024,128]{2,1,0:T(8,128)(2,1)}) custom-call(s32[2]{0:T(128)} %pad_add_fusion.position_ref, s32[1,27]{1,0:T(1,128)} %neighbors_ref.1, bf16[512,384]{1,0:T(8,128)(2,1)} %shard_map.85.own_ref, bf16[512,384]{1,0:T(8,128)(2,1)} %copy-done, bf16[2,128,256]{2,1,0:T(8,128)(2,1)} %copy-done.2, ...), custom_call_target="tpu_custom_call" | custom-call | tf_op jit(solution)/shard_map/pallas_call | solution.py:193
  31.5 2.3 %collective-permute-done.3 = bf16[3,1024,128]{2,1,0:T(8,128)(2,1)S(1)} collective-permute-done((bf16[3,1024,128]{2,1,0:T(8,128)(2,1)}, bf16[3,1024,128]{2,1,0:T(8,128)(2,1)S(1)}, u32[]{:S(2)}, u32[]{:S(2)}) %collective-permute-start.3) | collective-permute-done | bytes 786464 | tf_op jit(solution)/shard_map/ppermute | solution.py:205
  34.2 5.7 %collective-permute-start.18 = (bf16[512,128]{1,0:T(8,128)(2,1)S(1)}, bf16[512,128]{1,0:T(8,128)(2,1)S(1)}, u32[]{:S(2)}, u32[]{:S(2)}) collective-permute-start(bf16[512,128]{1,0:T(8,128)(2,1)S(1)} %fusion.2), channel_id=1, source_target_pairs={{0,8},{2,10},{4,12},{6,14},{8,0},{10,2},{12,4},{14,6},{16,24},{18,... | collective-permute-start | bytes 393224 | tf_op jit(solution)/shard_map/ppermute | solution.py:205
  40.4 1.8 %collective-permute-start.11 = (bf16[512,128]{1,0:T(8,128)(2,1)S(1)}, bf16[512,128]{1,0:T(8,128)(2,1)S(1)}, u32[]{:S(2)}, u32[]{:S(2)}) collective-permute-start(bf16[512,128]{1,0:T(8,128)(2,1)S(1)} %fusion.1), channel_id=1, source_target_pairs={{0,4},{2,6},{4,0},{6,2},{8,12},{10,14},{12,8},{14,10},{16,20},{18,... | collective-permute-start | bytes 393224 | tf_op jit(solution)/shard_map/ppermute | solution.py:205
  42.1 1.6 %collective-permute-done.18 = bf16[512,128]{1,0:T(8,128)(2,1)S(1)} collective-permute-done((bf16[512,128]{1,0:T(8,128)(2,1)S(1)}, bf16[512,128]{1,0:T(8,128)(2,1)S(1)}, u32[]{:S(2)}, u32[]{:S(2)}) %collective-permute-start.18) | collective-permute-done | bytes 131104 | tf_op jit(solution)/shard_map/ppermute | solution.py:205
  43.8 2.8 %collective-permute-start.19 = (bf16[256,128]{1,0:T(8,128)(2,1)S(1)}, bf16[256,128]{1,0:T(8,128)(2,1)S(1)}, u32[]{:S(2)}, u32[]{:S(2)}) collective-permute-start(bf16[256,128]{1,0:T(8,128)(2,1)S(1)} %dynamic-slice_convert_fusion.3), channel_id=1, source_target_pairs={{0,16},{2,18},{4,20},{6,22},{8,24},{10,26},{12,28},{14,30},{16,0},... | collective-permute-start | bytes 196616 | tf_op jit(solution)/shard_map/ppermute | solution.py:205
  47.4 1.5 %collective-permute-start.12 = (bf16[256,128]{1,0:T(8,128)(2,1)S(1)}, bf16[256,128]{1,0:T(8,128)(2,1)S(1)}, u32[]{:S(2)}, u32[]{:S(2)}) collective-permute-start(bf16[256,128]{1,0:T(8,128)(2,1)S(1)} %dynamic-slice_convert_fusion.4), channel_id=1, source_target_pairs={{0,2},{2,0},{4,6},{6,4},{8,10},{10,8},{12,14},{14,12},{16,18},{18,... | collective-permute-start | bytes 196616 | tf_op jit(solution)/shard_map/ppermute | solution.py:205
  49.7 1.3 %collective-permute-done.5 = bf16[256,128]{1,0:T(8,128)(2,1)S(1)} collective-permute-done((bf16[256,128]{1,0:T(8,128)(2,1)S(1)}, bf16[256,128]{1,0:T(8,128)(2,1)S(1)}, u32[]{:S(2)}, u32[]{:S(2)}) %collective-permute-start.5) | collective-permute-done | bytes 65568 | tf_op jit(solution)/shard_map/ppermute | solution.py:205
  51.0 1.6 %collective-permute-start.6 = (bf16[128,128]{1,0:T(8,128)(2,1)S(1)}, bf16[128,128]{1,0:T(8,128)(2,1)S(1)}, u32[]{:S(2)}, u32[]{:S(2)}) collective-permute-start(bf16[128,128]{1,0:T(8,128)(2,1)S(1)} %dynamic-slice_convert_fusion.8), channel_id=1, source_target_pairs={{0,8},{2,10},{4,12},{6,14},{8,0},{10,2},{12,4},{14,6},{16,24},{18,... | collective-permute-start | bytes 98312 | tf_op jit(solution)/shard_map/ppermute | solution.py:205
  53.4 1.5 %collective-permute-start.21 = (bf16[128,128]{1,0:T(8,128)(2,1)S(1)}, bf16[128,128]{1,0:T(8,128)(2,1)S(1)}, u32[]{:S(2)}, u32[]{:S(2)}) collective-permute-start(bf16[128,128]{1,0:T(8,128)(2,1)S(1)} %add_convert_fusion.1), channel_id=1, source_target_pairs={{0,4},{2,6},{4,0},{6,2},{8,12},{10,14},{12,8},{14,10},{16,20},{18,... | collective-permute-start | bytes 98312 | tf_op jit(solution)/shard_map/ppermute | solution.py:205
  55.0 1.6 %collective-permute-start.7 = (bf16[128,128]{1,0:T(8,128)(2,1)S(1)}, bf16[128,128]{1,0:T(8,128)(2,1)S(1)}, u32[]{:S(2)}, u32[]{:S(2)}) collective-permute-start(bf16[128,128]{1,0:T(8,128)(2,1)S(1)} %add_convert_fusion.5), channel_id=1, source_target_pairs={{0,16},{2,18},{4,20},{6,22},{8,24},{10,26},{12,28},{14,30},{16,0},... | collective-permute-start | bytes 98312 | tf_op jit(solution)/shard_map/ppermute | solution.py:205
  56.7 1.9 %collective-permute-start.14 = (bf16[128,128]{1,0:T(8,128)(2,1)S(1)}, bf16[128,128]{1,0:T(8,128)(2,1)S(1)}, u32[]{:S(2)}, u32[]{:S(2)}) collective-permute-start(bf16[128,128]{1,0:T(8,128)(2,1)S(1)} %add_convert_fusion.3), channel_id=1, source_target_pairs={{0,16},{2,18},{4,20},{6,22},{8,24},{10,26},{12,28},{14,30},{16,0},... | collective-permute-start | bytes 98312 | tf_op jit(solution)/shard_map/ppermute | solution.py:205
  58.6 1.7 %collective-permute-start.22 = (bf16[128,128]{1,0:T(8,128)(2,1)S(1)}, bf16[128,128]{1,0:T(8,128)(2,1)S(1)}, u32[]{:S(2)}, u32[]{:S(2)}) collective-permute-start(bf16[128,128]{1,0:T(8,128)(2,1)S(1)} %add_convert_fusion), channel_id=1, source_target_pairs={{0,2},{2,0},{4,6},{6,4},{8,10},{10,8},{12,14},{14,12},{16,18},{18,... | collective-permute-start | bytes 98312 | tf_op jit(solution)/shard_map/ppermute | solution.py:205
  60.4 1.5 %collective-permute-start.8 = (bf16[128,128]{1,0:T(8,128)(2,1)S(1)}, bf16[128,128]{1,0:T(8,128)(2,1)S(1)}, u32[]{:S(2)}, u32[]{:S(2)}) collective-permute-start(bf16[128,128]{1,0:T(8,128)(2,1)S(1)} %add_convert_fusion.4), channel_id=1, source_target_pairs={{0,8},{2,10},{4,12},{6,14},{8,0},{10,2},{12,4},{14,6},{16,24},{18,... | collective-permute-start | bytes 98312 | tf_op jit(solution)/shard_map/ppermute | solution.py:205
  61.9 1.9 %collective-permute-start.15 = (bf16[128,128]{1,0:T(8,128)(2,1)S(1)}, bf16[128,128]{1,0:T(8,128)(2,1)S(1)}, u32[]{:S(2)}, u32[]{:S(2)}) collective-permute-start(bf16[128,128]{1,0:T(8,128)(2,1)S(1)} %add_convert_fusion.2), channel_id=1, source_target_pairs={{0,8},{2,10},{4,12},{6,14},{8,0},{10,2},{12,4},{14,6},{16,24},{18,... | collective-permute-start | bytes 98312 | tf_op jit(solution)/shard_map/ppermute | solution.py:205
  63.8 2.5 %collective-permute-start.23 = (bf16[256,128]{1,0:T(8,128)(2,1)S(1)}, bf16[256,128]{1,0:T(8,128)(2,1)S(1)}, u32[]{:S(2)}, u32[]{:S(2)}) collective-permute-start(bf16[256,128]{1,0:T(8,128)(2,1)S(1)} %maximum_select_fusion.14), channel_id=1, source_target_pairs={{0,16},{2,18},{4,20},{6,22},{8,24},{10,26},{12,28},{14,30},{16,0},... | collective-permute-start | bytes 196616 | tf_op jit(solution)/shard_map/ppermute | solution.py:205
  66.4 1.0 %collective-permute-start.16 = (bf16[256,128]{1,0:T(8,128)(2,1)S(1)}, bf16[256,128]{1,0:T(8,128)(2,1)S(1)}, u32[]{:S(2)}, u32[]{:S(2)}) collective-permute-start(bf16[256,128]{1,0:T(8,128)(2,1)S(1)} %maximum_select_fusion.13), channel_id=1, source_target_pairs={{0,2},{2,0},{4,6},{6,4},{8,10},{10,8},{12,14},{14,12},{16,18},{18,... | collective-permute-start | bytes 196616 | tf_op jit(solution)/shard_map/ppermute | solution.py:205
  67.4 3.2 %collective-permute-done.9 = bf16[256,128]{1,0:T(8,128)(2,1)S(1)} collective-permute-done((bf16[256,128]{1,0:T(8,128)(2,1)S(1)}, bf16[256,128]{1,0:T(8,128)(2,1)S(1)}, u32[]{:S(2)}, u32[]{:S(2)}) %collective-permute-start.9) | collective-permute-done | bytes 65568 | tf_op jit(solution)/shard_map/ppermute | solution.py:205
  70.8 2.0 %collective-permute-start.17 = (bf16[512,128]{1,0:T(8,128)(2,1)S(1)}, bf16[512,128]{1,0:T(8,128)(2,1)S(1)}, u32[]{:S(2)}, u32[]{:S(2)}) collective-permute-start(bf16[512,128]{1,0:T(8,128)(2,1)S(1)} %maximum_select_fusion.10), channel_id=1, source_target_pairs={{0,4},{2,6},{4,0},{6,2},{8,12},{10,14},{12,8},{14,10},{16,20},{18,... | collective-permute-start | bytes 393224 | tf_op jit(solution)/shard_map/ppermute | solution.py:205
  72.9 1.0 %collective-permute-start.24 = (bf16[512,128]{1,0:T(8,128)(2,1)S(1)}, bf16[512,128]{1,0:T(8,128)(2,1)S(1)}, u32[]{:S(2)}, u32[]{:S(2)}) collective-permute-start(bf16[512,128]{1,0:T(8,128)(2,1)S(1)} %maximum_select_fusion.11), channel_id=1, source_target_pairs={{0,8},{2,10},{4,12},{6,14},{8,0},{10,2},{12,4},{14,6},{16,24},{18,... | collective-permute-start | bytes 393224 | tf_op jit(solution)/shard_map/ppermute | solution.py:205
  73.9 1.9 %collective-permute-done.10 = bf16[512,128]{1,0:T(8,128)(2,1)S(1)} collective-permute-done((bf16[512,128]{1,0:T(8,128)(2,1)S(1)}, bf16[512,128]{1,0:T(8,128)(2,1)S(1)}, u32[]{:S(2)}, u32[]{:S(2)}) %collective-permute-start.10) | collective-permute-done | bytes 131104 | tf_op jit(solution)/shard_map/ppermute | solution.py:205
  75.9 2.0 %collective-permute-done.24 = bf16[512,128]{1,0:T(8,128)(2,1)S(1)} collective-permute-done((bf16[512,128]{1,0:T(8,128)(2,1)S(1)}, bf16[512,128]{1,0:T(8,128)(2,1)S(1)}, u32[]{:S(2)}, u32[]{:S(2)}) %collective-permute-start.24) | collective-permute-done | bytes 131104 | tf_op jit(solution)/shard_map/ppermute | solution.py:205
  78.5 2.0 %collective-permute-done.25 = bf16[3,1024,128]{2,1,0:T(8,128)(2,1)S(1)} collective-permute-done((bf16[3,1024,128]{2,1,0:T(8,128)(2,1)S(1)}, bf16[3,1024,128]{2,1,0:T(8,128)(2,1)S(1)}, u32[]{:S(2)}, u32[]{:S(2)}) %collective-permute-start.25) | collective-permute-done | bytes 786464 | tf_op jit(solution)/shard_map/ppermute | solution.py:205
  80.5 0.9 %maximum_select_fusion.2.one_sums_ref = bf16[2048,128]{1,0:T(8,128)(2,1)} fusion(bf16[1024,128]{1,0:T(8,128)(2,1)S(1)} %get-tuple-element.26, bf16[1024,128]{1,0:T(8,128)(2,1)S(1)} %maximum_select_fusion.8, pred[]{:T(512)S(6)} %eq.42), kind=kLoop, calls=%fused_computation.7 | loop fusion | flops 2359296 | bytes 1048577 | tf_op jit(solution)/shard_map/jit(_where)/select_n | solution.py:275
  81.7 1.0 %pad_maximum_fusion.two_sums_ref = bf16[4096,128]{1,0:T(8,128)(2,1)} fusion(bf16[2048,128]{1,0:T(8,128)(2,1)S(1)} %get-tuple-element.30, bf16[2048,128]{1,0:T(8,128)(2,1)S(1)} %get-tuple-element.29), kind=kLoop, calls=%fused_computation | loop fusion | flops 2097152 | bytes 2097152 | tf_op jit(solution)/shard_map/concatenate | solution.py:296
  82.8 6.1 %shard_map.89 = (f32[27,96,96]{2,1,0:T(8,128)}, f32[27,96,192]{2,1,0:T(8,128)}) custom-call(bf16[4096,128]{1,0:T(8,128)(2,1)} %pad_maximum_fusion.two_sums_ref, bf16[2048,128]{1,0:T(8,128)(2,1)} %maximum_select_fusion.2.one_sums_ref), custom_call_target="tpu_custom_call" | custom-call | tf_op jit(solution)/shard_map/pallas_call | solution.py:284
  (74 shorter events, 7.1 us)
Async XLA Ops:
  2.6 2.0 %collective-permute-start = (bf16[512,384]{1,0:T(8,128)(2,1)}, bf16[512,384]{1,0:T(8,128)(2,1)S(1)}, u32[]{:S(2)}, u32[]{:S(2)}) collective-permute-start(bf16[512,384]{1,0:T(8,128)(2,1)} %shard_map.85.own_ref), channel_id=1, source_target_pairs={{0,1},{1,0},{2,3},{3,2},{4,5},{5,4},{6,7},{7,6},{8,9},{9,8},{10,11... | collective-permute-start | bytes 1179656 | tf_op jit(solution)/shard_map/ppermute | solution.py:205
  4.6 0.8 copy-start
  7.2 7.9 %collective-permute-start.1 = (bf16[2,128,256]{2,1,0:T(8,128)(2,1)}, bf16[2,128,256]{2,1,0:T(8,128)(2,1)S(1)}, u32[]{:S(2)}, u32[]{:S(2)}) collective-permute-start(bf16[2,128,256]{2,1,0:T(8,128)(2,1)} %get-tuple-element.13), channel_id=1, source_target_pairs={{0,2},{2,0},{4,6},{6,4},{8,10},{10,8},{12,14},{14,12},{16,18},{18,... | collective-permute-start | bytes 393224 | tf_op jit(solution)/shard_map/ppermute | solution.py:231
  10.1 5.0 %collective-permute-start.2 = (bf16[2,128,256]{2,1,0:T(8,128)(2,1)}, bf16[2,128,256]{2,1,0:T(8,128)(2,1)S(1)}, u32[]{:S(2)}, u32[]{:S(2)}) collective-permute-start(bf16[2,128,256]{2,1,0:T(8,128)(2,1)} %get-tuple-element.14), channel_id=1, source_target_pairs={{2,4},{6,8},{10,12},{14,16},{18,20},{22,24},{26,28},{4,2},{8,6},{1... | collective-permute-start | bytes 393224 | tf_op jit(solution)/shard_map/ppermute | solution.py:233
  15.1 0.7 copy-start.2
  15.1 0.7 copy-start.3
  31.3 2.6 %copy-start.1 = (f32[3,1024,128]{2,1,0:T(8,128)S(1)}, f32[3,1024,128]{2,1,0:T(8,128)}, u32[]{:S(2)}) copy-start(f32[3,1024,128]{2,1,0:T(8,128)} %get-tuple-element.19) | copy-start | bytes 4718596
  31.3 2.5 %collective-permute-start.3 = (bf16[3,1024,128]{2,1,0:T(8,128)(2,1)}, bf16[3,1024,128]{2,1,0:T(8,128)(2,1)S(1)}, u32[]{:S(2)}, u32[]{:S(2)}) collective-permute-start(bf16[3,1024,128]{2,1,0:T(8,128)(2,1)} %get-tuple-element.20), channel_id=1, source_target_pairs={{0,1},{1,0},{2,3},{3,2},{4,5},{5,4},{6,7},{7,6},{8,9},{9,8},{10,11... | collective-permute-start | bytes 2359304 | tf_op jit(solution)/shard_map/ppermute | solution.py:205
  34.2 9.5 %collective-permute-start.18 = (bf16[512,128]{1,0:T(8,128)(2,1)S(1)}, bf16[512,128]{1,0:T(8,128)(2,1)S(1)}, u32[]{:S(2)}, u32[]{:S(2)}) collective-permute-start(bf16[512,128]{1,0:T(8,128)(2,1)S(1)} %fusion.2), channel_id=1, source_target_pairs={{0,8},{2,10},{4,12},{6,14},{8,0},{10,2},{12,4},{14,6},{16,24},{18,... | collective-permute-start | bytes 393224 | tf_op jit(solution)/shard_map/ppermute | solution.py:205
  39.9 6.7 %collective-permute-start.4 = (bf16[512,128]{1,0:T(8,128)(2,1)S(1)}, bf16[512,128]{1,0:T(8,128)(2,1)S(1)}, u32[]{:S(2)}, u32[]{:S(2)}) collective-permute-start(bf16[512,128]{1,0:T(8,128)(2,1)S(1)} %fusion), channel_id=1, source_target_pairs={{0,2},{2,0},{4,6},{6,4},{8,10},{10,8},{12,14},{14,12},{16,18},{18,... | collective-permute-start | bytes 393224 | tf_op jit(solution)/shard_map/ppermute | solution.py:205
  40.4 7.0 %collective-permute-start.11 = (bf16[512,128]{1,0:T(8,128)(2,1)S(1)}, bf16[512,128]{1,0:T(8,128)(2,1)S(1)}, u32[]{:S(2)}, u32[]{:S(2)}) collective-permute-start(bf16[512,128]{1,0:T(8,128)(2,1)S(1)} %fusion.1), channel_id=1, source_target_pairs={{0,4},{2,6},{4,0},{6,2},{8,12},{10,14},{12,8},{14,10},{16,20},{18,... | collective-permute-start | bytes 393224 | tf_op jit(solution)/shard_map/ppermute | solution.py:205
  43.8 5.4 %collective-permute-start.19 = (bf16[256,128]{1,0:T(8,128)(2,1)S(1)}, bf16[256,128]{1,0:T(8,128)(2,1)S(1)}, u32[]{:S(2)}, u32[]{:S(2)}) collective-permute-start(bf16[256,128]{1,0:T(8,128)(2,1)S(1)} %dynamic-slice_convert_fusion.3), channel_id=1, source_target_pairs={{0,16},{2,18},{4,20},{6,22},{8,24},{10,26},{12,28},{14,30},{16,0},... | collective-permute-start | bytes 196616 | tf_op jit(solution)/shard_map/ppermute | solution.py:205
  46.6 4.3 %collective-permute-start.5 = (bf16[256,128]{1,0:T(8,128)(2,1)S(1)}, bf16[256,128]{1,0:T(8,128)(2,1)S(1)}, u32[]{:S(2)}, u32[]{:S(2)}) collective-permute-start(bf16[256,128]{1,0:T(8,128)(2,1)S(1)} %dynamic-slice_convert_fusion.5), channel_id=1, source_target_pairs={{0,4},{2,6},{4,0},{6,2},{8,12},{10,14},{12,8},{14,10},{16,20},{18,... | collective-permute-start | bytes 196616 | tf_op jit(solution)/shard_map/ppermute | solution.py:205
  47.4 5.3 %collective-permute-start.12 = (bf16[256,128]{1,0:T(8,128)(2,1)S(1)}, bf16[256,128]{1,0:T(8,128)(2,1)S(1)}, u32[]{:S(2)}, u32[]{:S(2)}) collective-permute-start(bf16[256,128]{1,0:T(8,128)(2,1)S(1)} %dynamic-slice_convert_fusion.4), channel_id=1, source_target_pairs={{0,2},{2,0},{4,6},{6,4},{8,10},{10,8},{12,14},{14,12},{16,18},{18,... | collective-permute-start | bytes 196616 | tf_op jit(solution)/shard_map/ppermute | solution.py:205
  49.2 4.2 %collective-permute-start.20 = (bf16[128,128]{1,0:T(8,128)(2,1)S(1)}, bf16[128,128]{1,0:T(8,128)(2,1)S(1)}, u32[]{:S(2)}, u32[]{:S(2)}) collective-permute-start(bf16[128,128]{1,0:T(8,128)(2,1)S(1)} %dynamic-slice_convert_fusion.6), channel_id=1, source_target_pairs={{0,2},{2,0},{4,6},{6,4},{8,10},{10,8},{12,14},{14,12},{16,18},{18,... | collective-permute-start | bytes 98312 | tf_op jit(solution)/shard_map/ppermute | solution.py:205
  51.0 4.0 %collective-permute-start.6 = (bf16[128,128]{1,0:T(8,128)(2,1)S(1)}, bf16[128,128]{1,0:T(8,128)(2,1)S(1)}, u32[]{:S(2)}, u32[]{:S(2)}) collective-permute-start(bf16[128,128]{1,0:T(8,128)(2,1)S(1)} %dynamic-slice_convert_fusion.8), channel_id=1, source_target_pairs={{0,8},{2,10},{4,12},{6,14},{8,0},{10,2},{12,4},{14,6},{16,24},{18,... | collective-permute-start | bytes 98312 | tf_op jit(solution)/shard_map/ppermute | solution.py:205
  52.7 4.0 %collective-permute-start.13 = (bf16[128,128]{1,0:T(8,128)(2,1)S(1)}, bf16[128,128]{1,0:T(8,128)(2,1)S(1)}, u32[]{:S(2)}, u32[]{:S(2)}) collective-permute-start(bf16[128,128]{1,0:T(8,128)(2,1)S(1)} %dynamic-slice_convert_fusion.7), channel_id=1, source_target_pairs={{0,8},{2,10},{4,12},{6,14},{8,0},{10,2},{12,4},{14,6},{16,24},{18,... | collective-permute-start | bytes 98312 | tf_op jit(solution)/shard_map/ppermute | solution.py:205
  53.4 5.2 %collective-permute-start.21 = (bf16[128,128]{1,0:T(8,128)(2,1)S(1)}, bf16[128,128]{1,0:T(8,128)(2,1)S(1)}, u32[]{:S(2)}, u32[]{:S(2)}) collective-permute-start(bf16[128,128]{1,0:T(8,128)(2,1)S(1)} %add_convert_fusion.1), channel_id=1, source_target_pairs={{0,4},{2,6},{4,0},{6,2},{8,12},{10,14},{12,8},{14,10},{16,20},{18,... | collective-permute-start | bytes 98312 | tf_op jit(solution)/shard_map/ppermute | solution.py:205
  55.0 5.3 %collective-permute-start.7 = (bf16[128,128]{1,0:T(8,128)(2,1)S(1)}, bf16[128,128]{1,0:T(8,128)(2,1)S(1)}, u32[]{:S(2)}, u32[]{:S(2)}) collective-permute-start(bf16[128,128]{1,0:T(8,128)(2,1)S(1)} %add_convert_fusion.5), channel_id=1, source_target_pairs={{0,16},{2,18},{4,20},{6,22},{8,24},{10,26},{12,28},{14,30},{16,0},... | collective-permute-start | bytes 98312 | tf_op jit(solution)/shard_map/ppermute | solution.py:205
  56.7 5.2 %collective-permute-start.14 = (bf16[128,128]{1,0:T(8,128)(2,1)S(1)}, bf16[128,128]{1,0:T(8,128)(2,1)S(1)}, u32[]{:S(2)}, u32[]{:S(2)}) collective-permute-start(bf16[128,128]{1,0:T(8,128)(2,1)S(1)} %add_convert_fusion.3), channel_id=1, source_target_pairs={{0,16},{2,18},{4,20},{6,22},{8,24},{10,26},{12,28},{14,30},{16,0},... | collective-permute-start | bytes 98312 | tf_op jit(solution)/shard_map/ppermute | solution.py:205
  58.6 5.2 %collective-permute-start.22 = (bf16[128,128]{1,0:T(8,128)(2,1)S(1)}, bf16[128,128]{1,0:T(8,128)(2,1)S(1)}, u32[]{:S(2)}, u32[]{:S(2)}) collective-permute-start(bf16[128,128]{1,0:T(8,128)(2,1)S(1)} %add_convert_fusion), channel_id=1, source_target_pairs={{0,2},{2,0},{4,6},{6,4},{8,10},{10,8},{12,14},{14,12},{16,18},{18,... | collective-permute-start | bytes 98312 | tf_op jit(solution)/shard_map/ppermute | solution.py:205
  60.4 6.0 %collective-permute-start.8 = (bf16[128,128]{1,0:T(8,128)(2,1)S(1)}, bf16[128,128]{1,0:T(8,128)(2,1)S(1)}, u32[]{:S(2)}, u32[]{:S(2)}) collective-permute-start(bf16[128,128]{1,0:T(8,128)(2,1)S(1)} %add_convert_fusion.4), channel_id=1, source_target_pairs={{0,8},{2,10},{4,12},{6,14},{8,0},{10,2},{12,4},{14,6},{16,24},{18,... | collective-permute-start | bytes 98312 | tf_op jit(solution)/shard_map/ppermute | solution.py:205
  61.9 4.5 %collective-permute-start.15 = (bf16[128,128]{1,0:T(8,128)(2,1)S(1)}, bf16[128,128]{1,0:T(8,128)(2,1)S(1)}, u32[]{:S(2)}, u32[]{:S(2)}) collective-permute-start(bf16[128,128]{1,0:T(8,128)(2,1)S(1)} %add_convert_fusion.2), channel_id=1, source_target_pairs={{0,8},{2,10},{4,12},{6,14},{8,0},{10,2},{12,4},{14,6},{16,24},{18,... | collective-permute-start | bytes 98312 | tf_op jit(solution)/shard_map/ppermute | solution.py:205
  63.8 9.0 %collective-permute-start.23 = (bf16[256,128]{1,0:T(8,128)(2,1)S(1)}, bf16[256,128]{1,0:T(8,128)(2,1)S(1)}, u32[]{:S(2)}, u32[]{:S(2)}) collective-permute-start(bf16[256,128]{1,0:T(8,128)(2,1)S(1)} %maximum_select_fusion.14), channel_id=1, source_target_pairs={{0,16},{2,18},{4,20},{6,22},{8,24},{10,26},{12,28},{14,30},{16,0},... | collective-permute-start | bytes 196616 | tf_op jit(solution)/shard_map/ppermute | solution.py:205
  66.3 4.3 %collective-permute-start.9 = (bf16[256,128]{1,0:T(8,128)(2,1)S(1)}, bf16[256,128]{1,0:T(8,128)(2,1)S(1)}, u32[]{:S(2)}, u32[]{:S(2)}) collective-permute-start(bf16[256,128]{1,0:T(8,128)(2,1)S(1)} %maximum_select_fusion.12), channel_id=1, source_target_pairs={{0,4},{2,6},{4,0},{6,2},{8,12},{10,14},{12,8},{14,10},{16,20},{18,... | collective-permute-start | bytes 196616 | tf_op jit(solution)/shard_map/ppermute | solution.py:205
  66.4 4.3 %collective-permute-start.16 = (bf16[256,128]{1,0:T(8,128)(2,1)S(1)}, bf16[256,128]{1,0:T(8,128)(2,1)S(1)}, u32[]{:S(2)}, u32[]{:S(2)}) collective-permute-start(bf16[256,128]{1,0:T(8,128)(2,1)S(1)} %maximum_select_fusion.13), channel_id=1, source_target_pairs={{0,2},{2,0},{4,6},{6,4},{8,10},{10,8},{12,14},{14,12},{16,18},{18,... | collective-permute-start | bytes 196616 | tf_op jit(solution)/shard_map/ppermute | solution.py:205
  70.7 5.0 %collective-permute-start.10 = (bf16[512,128]{1,0:T(8,128)(2,1)S(1)}, bf16[512,128]{1,0:T(8,128)(2,1)S(1)}, u32[]{:S(2)}, u32[]{:S(2)}) collective-permute-start(bf16[512,128]{1,0:T(8,128)(2,1)S(1)} %maximum_select_fusion.9), channel_id=1, source_target_pairs={{0,2},{2,0},{4,6},{6,4},{8,10},{10,8},{12,14},{14,12},{16,18},{18,... | collective-permute-start | bytes 393224 | tf_op jit(solution)/shard_map/ppermute | solution.py:205
  70.8 5.0 %collective-permute-start.17 = (bf16[512,128]{1,0:T(8,128)(2,1)S(1)}, bf16[512,128]{1,0:T(8,128)(2,1)S(1)}, u32[]{:S(2)}, u32[]{:S(2)}) collective-permute-start(bf16[512,128]{1,0:T(8,128)(2,1)S(1)} %maximum_select_fusion.10), channel_id=1, source_target_pairs={{0,4},{2,6},{4,0},{6,2},{8,12},{10,14},{12,8},{14,10},{16,20},{18,... | collective-permute-start | bytes 393224 | tf_op jit(solution)/shard_map/ppermute | solution.py:205
  72.9 5.0 %collective-permute-start.24 = (bf16[512,128]{1,0:T(8,128)(2,1)S(1)}, bf16[512,128]{1,0:T(8,128)(2,1)S(1)}, u32[]{:S(2)}, u32[]{:S(2)}) collective-permute-start(bf16[512,128]{1,0:T(8,128)(2,1)S(1)} %maximum_select_fusion.11), channel_id=1, source_target_pairs={{0,8},{2,10},{4,12},{6,14},{8,0},{10,2},{12,4},{14,6},{16,24},{18,... | collective-permute-start | bytes 393224 | tf_op jit(solution)/shard_map/ppermute | solution.py:205
  78.1 2.4 %collective-permute-start.25 = (bf16[3,1024,128]{2,1,0:T(8,128)(2,1)S(1)}, bf16[3,1024,128]{2,1,0:T(8,128)(2,1)S(1)}, u32[]{:S(2)}, u32[]{:S(2)}) collective-permute-start(bf16[3,1024,128]{2,1,0:T(8,128)(2,1)S(1)} %pad_maximum_fusion.1), channel_id=1, source_target_pairs={{0,1},{1,0},{2,3},{3,2},{4,5},{5,4},{6,7},{7,6},{8,9},{9,8},{10,11... | collective-permute-start | bytes 2359304 | tf_op jit(solution)/shard_map/ppermute | solution.py:205

commit v3 on v2

--- a/solution.py
+++ b/solution.py
@@ -8,7 +8,7 @@
 F32 = jnp.float32
 BF16 = jnp.bfloat16
 LANES = 128
-VMEM_BYTES = 56 * 2**20
+VMEM_BYTES = 32 * 2**20
 
 
 def up_to(value, step):
@@ -19,7 +19,7 @@
     return [pl.BlockSpec(memory_space=pltpu.VMEM)] * count
 
 
-def pack_kernel(features_ref, occupancy_ref, cotangent_ref, packed_ref):
+def pack_kernel(position_ref, features_ref, occupancy_ref, cotangent_ref, packed_ref, first_ref, second_ref):
     channels, voxels = features_ref.shape
     outs = cotangent_ref.shape[0]
     active = occupancy_ref[...] > 0
@@ -32,52 +32,54 @@
     spare = up_to(outs, LANES) - outs
     grad_out = jnp.concatenate([grad_out, jnp.zeros((spare, voxels), F32)], 0)
     packed_ref[:, LANES:] = grad_out.T.astype(BF16)
-
-
-def planes_kernel(position_ref, own_ref, partner_ref, first_ref, second_ref):
     odd = position_ref[0]
-    for which, target in enumerate((first_ref, second_ref)):
-        upper = 1 - odd if which == 0 else odd
-        for source, block in enumerate((own_ref, partner_ref)):
-            row = pl.multiple_of(upper * 384, 128)
-            near = pl.multiple_of(upper * 448, 64)
-            target[source, :, :LANES] = block[pl.ds(row, 128), :LANES]
-            target[source, :64, LANES:] = block[pl.ds(near, 64), LANES : 2 * LANES]
-            target[source, 64:, LANES:] = block[pl.ds(near, 64), 2 * LANES :]
-
-
-def weights_kernel(one_ref, two_ref, one_pad_ref, two_pad_ref, two_turned_ref):
+    for target, upper in ((first_ref, 1 - odd), (second_ref, odd)):
+        row = pl.multiple_of(upper * 384, 128)
+        near = pl.multiple_of(upper * 448, 64)
+        target[:, :LANES] = packed_ref[pl.ds(row, 128), :LANES]
+        target[:64, LANES:] = packed_ref[pl.ds(near, 64), LANES : 2 * LANES]
+        target[64:, LANES:] = packed_ref[pl.ds(near, 64), 2 * LANES :]
+
+
+def weights_kernel(one_ref, two_ref, one_pad_ref, two_pad_ref):
     offsets, channels, outs = two_ref.shape
+    spare = LANES - channels
     one_pad_ref[:, :channels, :] = one_ref[...]
-    two_pad_ref[:, :channels, :] = two_ref[...]
+    one_pad_ref[:, channels:, :] = jnp.zeros((offsets, spare, one_ref.shape[2]), BF16)
+    two_pad_ref[:, :channels, :outs] = two_ref[...]
+    two_pad_ref[:, :channels, outs:] = jnp.zeros((offsets, channels, two_pad_ref.shape[2] - outs), BF16)
+    two_pad_ref[:, channels:, :] = jnp.zeros((offsets, spare, two_pad_ref.shape[2]), BF16)
+
+
+def store_two(total_ref, product, offset):
+    rows, outs = product.shape
+    spare = outs - LANES
+    pair, place = divmod(offset, 2)
+    total_ref[pl.ds((3 * pair + place) * rows, rows), :] = product[:, :LANES]
+    total_ref[pl.ds((3 * pair + 2) * rows, rows), place * spare : (place + 1) * spare] = product[:, LANES:]
+
+
+def store_one(total_ref, product, offset, first_row):
+    rows, channels = product.shape
     spare = LANES - channels
-    one_pad_ref[:, channels:, :] = jnp.zeros((offsets, spare, one_ref.shape[2]), BF16)
-    two_pad_ref[:, channels:, :] = jnp.zeros((offsets, spare, outs), BF16)
-    two_turned_ref[:, outs:, :] = jnp.zeros((offsets, two_turned_ref.shape[1] - outs, channels), BF16)
-    for offset in range(offsets):
-        two_turned_ref[offset, :outs, :] = two_ref[offset].astype(F32).T.astype(BF16)
-
-
-def store_gradient(total_ref, product, offset, first_row, rows, channels):
     group, place = divmod(offset, 4)
     if place < 3:
-        base = (3 * group + place) * rows + first_row
-        total_ref[base : base + product.shape[0], :channels] = product[:, :channels]
+        total_ref[pl.ds(first_row + (3 * group + place) * rows, rows), :channels] = product
     else:
-        spare = LANES - channels
         for piece in range(3):
-            base = (3 * group + piece) * rows + first_row
-            total_ref[base : base + product.shape[0], channels:] = product[:, piece * spare : (piece + 1) * spare]
+            base = first_row + (3 * group + piece) * rows
+            total_ref[pl.ds(base, rows), channels:] = product[:, piece * spare : (piece + 1) * spare]
 
 
 def main_kernel(
-    position_ref, neighbors_ref, own_ref, partner_ref, first_ref, second_ref, cotangent_ref, occupancy_ref,
-    one_ref, two_ref, turned_ref, output_ref, kept_ref, sent_ref, masked_w, grad_w, hidden_w, total,
+    position_ref, neighbors_ref, own_ref, partner_ref, first_ref, second_ref, first_far_ref, second_far_ref,
+    one_ref, two_ref, output_ref, kept_ref, sent_ref, masked_w, grad_w, hidden_w, total,
 ):
     odd, split = position_ref[0], position_ref[1]
     channels = one_ref.shape[2]
-    outs = two_ref.shape[2]
+    outs = output_ref.shape[0]
     wide = grad_w.shape[3]
+    over = (((0,), (0,)), ((), ()))
     masked_w[:, 6:18] = jnp.zeros((12, 12, 24, LANES), F32)
     grad_w[:, 7:17] = jnp.zeros((10, 10, 24, wide), F32)
 
@@ -100,9 +102,9 @@
         masked_w[2:10, pl.ds(y, 8), pl.ds(z, 8), :] = block[..., :LANES]
         grad_w[1:9, pl.ds(y, 8), pl.ds(z, 8), :] = block[..., LANES:]
 
-    for which, ref in enumerate((first_ref, second_ref)):
+    for which, refs in enumerate(((first_ref, first_far_ref), (second_ref, second_far_ref))):
         step_x = 1 - 2 * odd if which == 0 else 2 * odd - 1
-        for source in range(2):
+        for source, ref in enumerate(refs):
             step_z = 0 if source == 0 else 1 - 2 * split
             valid, y = placed(step_x, step_z)
             z = pl.multiple_of(8 + 8 * step_z, 8)
@@ -111,7 +113,7 @@
 
             @pl.when(valid)
             def _():
-                block = ref[source].astype(F32)
+                block = ref[...].astype(F32)
                 masked_w[pl.ds(x_masked, 2), pl.ds(y, 8), pl.ds(z, 8), :] = block[:, :LANES].reshape(2, 8, 8, LANES)
                 near = jnp.concatenate([block[:64, LANES:], block[64:, LANES:]], 1)
                 grad_w[pl.ds(x_grad, 1), pl.ds(y, 8), pl.ds(z, 8), :] = near.reshape(1, 8, 8, wide)
@@ -135,19 +137,18 @@
     own_flag = masked_w[2:10, 8:16, 8:16, channels : channels + 1].reshape(512, 1) > 0
 
     third = kept_ref.shape[1]
-    first_one = 4 * third
-    turned_out = jnp.where(occupancy_ref[...] > 0, cotangent_ref[...].astype(F32), 0.0).astype(BF16)
+    grad_out = own_ref[:, LANES : LANES + outs]
     output = None
     total[...] = jnp.zeros_like(total)
     for code in range(9):
         dy, dz = divmod(code, 3)
         shifted = hidden_w[:, dy : dy + 8, dz : dz + 8, :].reshape(640, LANES).astype(BF16)
         rows = jnp.concatenate([shifted[64 * dx : 64 * dx + 512] for dx in range(3)], 1)
-        term = jnp.dot(rows, weights(two_ref, code), preferred_element_type=F32)
+        term = jnp.dot(rows, weights(two_ref, code)[:, :outs], preferred_element_type=F32)
         output = term if output is None else output + term
-        product = jnp.dot(turned_out, rows, preferred_element_type=F32)
+        product = lax.dot_general(rows, grad_out, over, preferred_element_type=F32)
         for dx in range(3):
-            store_gradient(total, product[:, dx * LANES : (dx + 1) * LANES], 9 * dx + code, 0, outs, channels)
+            store_two(total, product[dx * LANES : dx * LANES + channels], 9 * dx + code)
     output_ref[...] = jnp.where(own_flag, output, 0.0).T.astype(BF16)
 
     back = None
@@ -155,22 +156,20 @@
         dy, dz = divmod(code, 3)
         shifted = grad_w[:, 7 + dy : 15 + dy, 7 + dz : 15 + dz, :].reshape(640, wide).astype(BF16)
         rows = jnp.concatenate([shifted[64 * dx : 64 * dx + 512] for dx in range(3)], 1)
-        kernel = jnp.concatenate([turned_ref[26 - code], turned_ref[17 - code], turned_ref[8 - code]], 0)
-        term = jnp.dot(rows, kernel, preferred_element_type=F32)
+        kernel = jnp.concatenate([two_ref[26 - code], two_ref[17 - code], two_ref[8 - code]], 1)
+        term = lax.dot_general(rows, kernel, (((1,), (1,)), ((), ())), preferred_element_type=F32)
         back = term if back is None else back + term
+    back = back[:, :channels]
     gate = jax.nn.sigmoid(own_pre)
-    grad_pre = jnp.where(own_flag, back * gate * (1.0 + own_pre * (1.0 - gate)), 0.0)
-    turned_pre = grad_pre.T.astype(BF16)
+    grad_pre = jnp.where(own_flag, back * gate * (1.0 + own_pre * (1.0 - gate)), 0.0).astype(BF16)
 
     for code in range(9):
         dy, dz = divmod(code, 3)
         shifted = masked_w[1:11, 7 + dy : 15 + dy, 7 + dz : 15 + dz, :].reshape(640, LANES).astype(BF16)
         rows = jnp.concatenate([shifted[64 * dx : 64 * dx + 512] for dx in range(3)], 1)
-        product = jnp.dot(turned_pre, rows, preferred_element_type=F32)
+        product = lax.dot_general(rows, grad_pre, over, preferred_element_type=F32)
         for dx in range(3):
-            store_gradient(
-                total, product[:, dx * LANES : (dx + 1) * LANES], 9 * dx + code, first_one, channels, channels
-            )
+            store_one(total, product[dx * LANES : dx * LANES + channels], 9 * dx + code, 4 * third)
 
     for group in range(3):
         start = 2 * third * group
@@ -178,14 +177,32 @@
         sent_ref[group] = total[pl.ds(pl.multiple_of(start + (1 - split) * third, 16), third), :].astype(BF16)
 
 
-def unpack_kernel(two_sums_ref, one_sums_ref, one_ref, two_ref):
-    for sums, ref in ((two_sums_ref, two_ref), (one_sums_ref, one_ref)):
-        channels, outs = ref.shape[1:]
+def unpack_kernel(position_ref, own_ref, other_ref, one_ref, two_ref, sums):
+    split = position_ref[1]
+    offsets, channels, outs = two_ref.shape
+    third = own_ref.shape[1]
+    for part in range(3):
+        for place, ref in ((split, own_ref), (1 - split, other_ref)):
+            sums[pl.ds(pl.multiple_of((2 * part + place) * third, 16), third), :] = ref[part]
+    for offset in range(offsets):
+        pair, place = divmod(offset, 2)
+        base = 3 * pair * channels
+        spare = outs - LANES
+        two_ref[offset, :, :LANES] = sums[pl.ds(base + place * channels, channels), :].astype(F32)
+        two_ref[offset, :, LANES:] = sums[pl.ds(base + 2 * channels, channels), :].astype(F32)[
+            :, place * spare : (place + 1) * spare
+        ]
+    for offset in range(offsets):
+        group, place = divmod(offset, 4)
+        base = 4 * third + 3 * group * channels
         spare = LANES - channels
-        for place in range(3):
-            part = sums[place * outs : (place + 1) * outs, :].astype(F32).T
-            ref[place] = part[:channels]
-            ref[3, place * spare : (place + 1) * spare, :] = part[channels:]
+        if place < 3:
+            one_ref[offset] = sums[pl.ds(base + place * channels, channels), :].astype(F32)[:, :channels]
+        else:
+            for piece in range(3):
+                one_ref[offset, :, piece * spare : (piece + 1) * spare] = sums[
+                    pl.ds(base + piece * channels, channels), :
+                ].astype(F32)[:, channels:]
 
 
 def call(kernel, out_shape, args, scalars=0, scratch=(), cost=None):
@@ -224,20 +241,21 @@
     wide = up_to(outs, LANES)
     struct = jax.ShapeDtypeStruct
 
-    packed = call(pack_kernel, struct((voxels, LANES + wide), BF16), (features, occupancy, cotangent))
+    planes = struct((128, 2 * LANES), BF16)
+    packed, first, second = call(
+        pack_kernel,
+        (struct((voxels, LANES + wide), BF16), planes, planes),
+        (position, features, occupancy, cotangent),
+        scalars=1,
+    )
     partner = exchanged(packed, "split", 1)
-    faces = struct((2, 128, 2 * LANES), BF16)
-    first, second = call(planes_kernel, (faces, faces), (position, packed, partner), scalars=1)
     first = lax.ppermute(first, "region", [(i, i ^ 1) for i in range(regions)])
     pairs = [(i, i + 1) for i in range(1, regions - 1, 2)]
     second = lax.ppermute(second, "region", pairs + [(b, a) for a, b in pairs])
+    first_far, second_far = exchanged(first, "split", 1), exchanged(second, "split", 1)
     weights = call(
         weights_kernel,
-        (
-            struct((offsets, LANES, channels), BF16),
-            struct((offsets, LANES, outs), BF16),
-            struct((offsets, wide, channels), BF16),
-        ),
+        (struct((offsets, LANES, channels), BF16), struct((offsets, LANES, wide), BF16)),
         (kernel_one, kernel_two),
         cost=pl.CostEstimate(flops=10**8, bytes_accessed=10**7, transcendentals=0),
     )
@@ -247,7 +265,7 @@
     output, kept, sent = call(
         main_kernel,
         (struct((outs, voxels), BF16), struct((3, third, LANES), F32), struct((3, third, LANES), BF16)),
-        (position, neighbors, packed, partner, first, second, cotangent, occupancy, *weights),
+        (position, neighbors, packed, partner, first, second, first_far, second_far, *weights),
         scalars=2,
         scratch=(
             pltpu.VMEM((12, 24, 24, LANES), F32),
@@ -278,22 +296,14 @@
         for part, order in enumerate(orders):
             mask = 1 << order[step]
             sums[part] = joined(sums[part], exchanged(sums[part], "region", mask), (region // mask) % 2)
-    other = exchanged(jnp.stack(sums), "split", 1)
-    sums = [joined(sums[part], other[part], split) for part in range(3)]
-
-    grad_one, grad_two = pl.pallas_call(
+    own = jnp.stack(sums)
+    grad_one, grad_two = call(
         unpack_kernel,
-        grid=(fours,),
-        in_specs=[
-            pl.BlockSpec((3 * outs, LANES), lambda i: (i, 0)),
-            pl.BlockSpec((3 * channels, LANES), lambda i: (i, 0)),
-        ],
-        out_specs=[
-            pl.BlockSpec((4, channels, channels), lambda i: (i, 0, 0)),
-            pl.BlockSpec((4, channels, outs), lambda i: (i, 0, 0)),
-        ],
-        out_shape=[struct((offsets, channels, channels), F32), struct((offsets, channels, outs), F32)],
-    )(jnp.concatenate(sums[:2], 0), sums[2])
+        (struct((offsets, channels, channels), F32), struct((offsets, channels, outs), F32)),
+        (position, own, exchanged(own, "split", 1)),
+        scalars=1,
+        scratch=(pltpu.VMEM((6 * third, LANES), BF16),),
+    )
     return output, grad_one, grad_two
 
 

time: 89.2 us -> 79 us (0.89)
  Pallas kernels: 29.8 us -> 17.2 us
  local copies, waits for them, and re-layouts: 1.67 us -> 5.06 us
  other arithmetic: 4.03 us -> 1.04 us
  starting transfers between devices: 36.5 us -> 37.6 us
  waiting for transfers between devices: 15.9 us -> 16.9 us
    pallas_call x4, Pallas kernels: 23.7 us -> 17.2 us  [call(): pl.pallas_call(kernel, out_shape=out_shape, in_specs=specs, out_specs=jax...]
    pallas_call x1 -> x0, Pallas kernels: 6.11 us -> none  [shards(): pl.pallas_call(unpack_kernel, grid=(fours,), in_specs=[pl.BlockSpec((3 *...]
    unnamed x8 -> x12, local copies, waits for them, and re-layouts: 1.47 us -> 4.92 us
    ppermute x1, waiting for transfers between devices: 0.01 us -> 2.03 us  [shards(): first = lax.ppermute(first, 'region', [(i, i ^ 1) for i in range(regions)])]
    select_n x14 -> x9, other arithmetic: 1.84 us -> 0.39 us  [joined(): jnp.where(bit == 0, jnp.concatenate([own, other], 0), jnp.concatenate([ot...]
    ppermute x24 -> x26, starting transfers between devices: 33 us -> 34.4 us  [exchanged(): lax.ppermute(value, axis, [(i, i ^ mask) for i in range(lax.axis_size(axi...]
    concatenate x1 -> x0, other arithmetic: 1.05 us -> none  [shards(): jnp.concatenate(sums[:2], 0)]
    ppermute x24 -> x26, waiting for transfers between devices: 15.9 us -> 14.8 us  [exchanged(): lax.ppermute(value, axis, [(i, i ^ mask) for i in range(lax.axis_size(axi...]
  transfers between devices with their start and end apart: 26 -> 28, of which waited for: 11 -> 13; matrix products, arithmetic and copies ran while one was open for 2% -> 1% of each run, Pallas kernels for 5% -> 0%
where the time goes in v3:
time: 79 us; the launch traced here: 78.7 us
  starting transfers between devices  37.6 us (48%)
  Pallas kernels  17.2 us (22%)
  waiting for transfers between devices  16.9 us (21%)
  local copies, waits for them, and re-layouts  5.06 us (6%)
  other arithmetic  1.04 us (1%)
  between operations  0.9 us (1%)
    ppermute x26, starting transfers between devices, exchanged(): lax.ppermute(value, axis, [(i, i ^ mask) for i in range(lax.axis_size(axi...  34.4 us
    pallas_call x4, Pallas kernels, call(): pl.pallas_call(kernel, out_shape=out_shape, in_specs=specs, out_specs=jax...  17.2 us
    ppermute x26, waiting for transfers between devices, exchanged(): lax.ppermute(value, axis, [(i, i ^ mask) for i in range(lax.axis_size(axi...  14.8 us
    unnamed x12, local copies, waits for them, and re-layouts  4.92 us
    ppermute x1, starting transfers between devices, shards(): first = lax.ppermute(first, 'region', [(i, i ^ 1) for i in range(regions)])  2.56 us
    ppermute x1, waiting for transfers between devices, shards(): first = lax.ppermute(first, 'region', [(i, i ^ 1) for i in range(regions)])  2.03 us
  transfers between devices with their start and end apart: 28, of which 13 were waited for; matrix products, arithmetic and copies ran while one was open for 1% of the time, Pallas kernels for 0%

profile of v3, /device:TPU:0, one launch (start us, length us, event | category | flops | bytes accessed | tf_op | source)
XLA Modules:
  0.0 78.7 jit_solution(8583414719041687467)
XLA Ops:
  0.7 0.9 %copy-done.2 = bf16[192,512]{1,0:T(8,128)(2,1)S(1)} copy-done((bf16[192,512]{1,0:T(8,128)(2,1)S(1)}, bf16[192,512]{1,0:T(8,128)(2,1)}, u32[]{:S(2)}) %copy-start.2) | copy-done | bytes 196632
  1.7 0.9 %copy-done.3 = bf16[96,512]{1,0:T(8,128)(2,1)S(1)} copy-done((bf16[96,512]{1,0:T(8,128)(2,1)S(1)}, bf16[96,512]{1,0:T(8,128)(2,1)}, u32[]{:S(2)}) %copy-start.3) | copy-done | bytes 98328
  4.5 2.6 %collective-permute-start.1 = (bf16[128,256]{1,0:T(8,128)(2,1)S(1)}, bf16[128,256]{1,0:T(8,128)(2,1)S(1)}, u32[]{:S(2)}, u32[]{:S(2)}) collective-permute-start(bf16[128,256]{1,0:T(8,128)(2,1)S(1)} %get-tuple-element.14), channel_id=1, source_target_pairs={{0,2},{2,0},{4,6},{6,4},{8,10},{10,8},{12,14},{14,12},{16,18},{18,... | collective-permute-start | bytes 196616 | tf_op jit(solution)/shard_map/ppermute | solution.py:252
  7.7 2.0 %collective-permute-done.1.first_ref = bf16[128,256]{1,0:T(8,128)(2,1)S(1)} collective-permute-done((bf16[128,256]{1,0:T(8,128)(2,1)S(1)}, bf16[128,256]{1,0:T(8,128)(2,1)S(1)}, u32[]{:S(2)}, u32[]{:S(2)}) %collective-permute-start.1) | collective-permute-done | bytes 65568 | tf_op jit(solution)/shard_map/ppermute | solution.py:252
  10.3 1.3 %copy-done = bf16[27,96,192]{2,1,0:T(8,128)(2,1)S(1)} copy-done((bf16[27,96,192]{2,1,0:T(8,128)(2,1)S(1)}, bf16[27,96,192]{2,1,0:T(8,128)(2,1)}, u32[]{:S(2)}) %copy-start) | copy-done | bytes 995352
  11.6 1.1 %copy-done.1 = bf16[27,96,96]{2,1,0:T(8,128)(2,1)S(1)} copy-done((bf16[27,96,96]{2,1,0:T(8,128)(2,1)S(1)}, bf16[27,96,96]{2,1,0:T(8,128)(2,1)}, u32[]{:S(2)}) %copy-start.1) | copy-done | bytes 497688
  13.1 13.2 %shard_map.87 = (bf16[192,512]{1,0:T(8,128)(2,1)}, f32[3,1024,128]{2,1,0:T(8,128)S(1)}, bf16[3,1024,128]{2,1,0:T(8,128)(2,1)S(1)}) custom-call(s32[2]{0:T(128)S(1)} %pad_add_fusion.position_ref, s32[1,27]{1,0:T(1,128)S(1)} %copy-done.5, bf16[512,384]{1,0:T(8,128)(2,1)S(1)} %get-tuple-element.13.own_ref, ...), custom_call_target="tpu_custom_call" | custom-call | tf_op jit(solution)/shard_map/pallas_call | solution.py:210
  26.3 2.3 %collective-permute-done.5 = bf16[3,1024,128]{2,1,0:T(8,128)(2,1)S(1)} collective-permute-done((bf16[3,1024,128]{2,1,0:T(8,128)(2,1)S(1)}, bf16[3,1024,128]{2,1,0:T(8,128)(2,1)S(1)}, u32[]{:S(2)}, u32[]{:S(2)}) %collective-permute-start.5) | collective-permute-done | bytes 786464 | tf_op jit(solution)/shard_map/ppermute | solution.py:222
  28.9 4.3 %collective-permute-start.6 = (bf16[512,128]{1,0:T(8,128)(2,1)S(1)}, bf16[512,128]{1,0:T(8,128)(2,1)S(1)}, u32[]{:S(2)}, u32[]{:S(2)}) collective-permute-start(bf16[512,128]{1,0:T(8,128)(2,1)S(1)} %fusion), channel_id=1, source_target_pairs={{0,2},{2,0},{4,6},{6,4},{8,10},{10,8},{12,14},{14,12},{16,18},{18,... | collective-permute-start | bytes 393224 | tf_op jit(solution)/shard_map/ppermute | solution.py:222
  33.2 2.8 %collective-permute-start.13 = (bf16[512,128]{1,0:T(8,128)(2,1)S(1)}, bf16[512,128]{1,0:T(8,128)(2,1)S(1)}, u32[]{:S(2)}, u32[]{:S(2)}) collective-permute-start(bf16[512,128]{1,0:T(8,128)(2,1)S(1)} %fusion.1), channel_id=1, source_target_pairs={{0,4},{2,6},{4,0},{6,2},{8,12},{10,14},{12,8},{14,10},{16,20},{18,... | collective-permute-start | bytes 393224 | tf_op jit(solution)/shard_map/ppermute | solution.py:222
  36.0 1.6 %collective-permute-start.20 = (bf16[512,128]{1,0:T(8,128)(2,1)S(1)}, bf16[512,128]{1,0:T(8,128)(2,1)S(1)}, u32[]{:S(2)}, u32[]{:S(2)}) collective-permute-start(bf16[512,128]{1,0:T(8,128)(2,1)S(1)} %fusion.2), channel_id=1, source_target_pairs={{0,8},{2,10},{4,12},{6,14},{8,0},{10,2},{12,4},{14,6},{16,24},{18,... | collective-permute-start | bytes 393224 | tf_op jit(solution)/shard_map/ppermute | solution.py:222
  37.7 2.6 %collective-permute-start.7 = (bf16[256,128]{1,0:T(8,128)(2,1)S(1)}, bf16[256,128]{1,0:T(8,128)(2,1)S(1)}, u32[]{:S(2)}, u32[]{:S(2)}) collective-permute-start(bf16[256,128]{1,0:T(8,128)(2,1)S(1)} %dynamic-slice_convert_fusion.5), channel_id=1, source_target_pairs={{0,4},{2,6},{4,0},{6,2},{8,12},{10,14},{12,8},{14,10},{16,20},{18,... | collective-permute-start | bytes 196616 | tf_op jit(solution)/shard_map/ppermute | solution.py:222
  40.4 1.5 %collective-permute-start.14 = (bf16[256,128]{1,0:T(8,128)(2,1)S(1)}, bf16[256,128]{1,0:T(8,128)(2,1)S(1)}, u32[]{:S(2)}, u32[]{:S(2)}) collective-permute-start(bf16[256,128]{1,0:T(8,128)(2,1)S(1)} %dynamic-slice_convert_fusion.4), channel_id=1, source_target_pairs={{0,2},{2,0},{4,6},{6,4},{8,10},{10,8},{12,14},{14,12},{16,18},{18,... | collective-permute-start | bytes 196616 | tf_op jit(solution)/shard_map/ppermute | solution.py:222
  42.0 2.7 %collective-permute-start.21 = (bf16[256,128]{1,0:T(8,128)(2,1)S(1)}, bf16[256,128]{1,0:T(8,128)(2,1)S(1)}, u32[]{:S(2)}, u32[]{:S(2)}) collective-permute-start(bf16[256,128]{1,0:T(8,128)(2,1)S(1)} %dynamic-slice_convert_fusion.3), channel_id=1, source_target_pairs={{0,16},{2,18},{4,20},{6,22},{8,24},{10,26},{12,28},{14,30},{16,0},... | collective-permute-start | bytes 196616 | tf_op jit(solution)/shard_map/ppermute | solution.py:222
  44.7 1.3 %collective-permute-start.8 = (bf16[128,128]{1,0:T(8,128)(2,1)S(1)}, bf16[128,128]{1,0:T(8,128)(2,1)S(1)}, u32[]{:S(2)}, u32[]{:S(2)}) collective-permute-start(bf16[128,128]{1,0:T(8,128)(2,1)S(1)} %dynamic-slice_convert_fusion.8), channel_id=1, source_target_pairs={{0,8},{2,10},{4,12},{6,14},{8,0},{10,2},{12,4},{14,6},{16,24},{18,... | collective-permute-start | bytes 98312 | tf_op jit(solution)/shard_map/ppermute | solution.py:222
  46.0 0.9 %collective-permute-start.15 = (bf16[128,128]{1,0:T(8,128)(2,1)S(1)}, bf16[128,128]{1,0:T(8,128)(2,1)S(1)}, u32[]{:S(2)}, u32[]{:S(2)}) collective-permute-start(bf16[128,128]{1,0:T(8,128)(2,1)S(1)} %dynamic-slice_convert_fusion.7), channel_id=1, source_target_pairs={{0,8},{2,10},{4,12},{6,14},{8,0},{10,2},{12,4},{14,6},{16,24},{18,... | collective-permute-start | bytes 98312 | tf_op jit(solution)/shard_map/ppermute | solution.py:222
  48.7 2.3 %collective-permute-start.9 = (bf16[128,128]{1,0:T(8,128)(2,1)S(1)}, bf16[128,128]{1,0:T(8,128)(2,1)S(1)}, u32[]{:S(2)}, u32[]{:S(2)}) collective-permute-start(bf16[128,128]{1,0:T(8,128)(2,1)S(1)} %add_convert_fusion.5), channel_id=1, source_target_pairs={{0,16},{2,18},{4,20},{6,22},{8,24},{10,26},{12,28},{14,30},{16,0},... | collective-permute-start | bytes 98312 | tf_op jit(solution)/shard_map/ppermute | solution.py:222
  51.0 1.4 %collective-permute-start.16 = (bf16[128,128]{1,0:T(8,128)(2,1)S(1)}, bf16[128,128]{1,0:T(8,128)(2,1)S(1)}, u32[]{:S(2)}, u32[]{:S(2)}) collective-permute-start(bf16[128,128]{1,0:T(8,128)(2,1)S(1)} %add_convert_fusion.3), channel_id=1, source_target_pairs={{0,16},{2,18},{4,20},{6,22},{8,24},{10,26},{12,28},{14,30},{16,0},... | collective-permute-start | bytes 98312 | tf_op jit(solution)/shard_map/ppermute | solution.py:222
  52.4 1.0 %collective-permute-start.23 = (bf16[128,128]{1,0:T(8,128)(2,1)S(1)}, bf16[128,128]{1,0:T(8,128)(2,1)S(1)}, u32[]{:S(2)}, u32[]{:S(2)}) collective-permute-start(bf16[128,128]{1,0:T(8,128)(2,1)S(1)} %add_convert_fusion.1), channel_id=1, source_target_pairs={{0,4},{2,6},{4,0},{6,2},{8,12},{10,14},{12,8},{14,10},{16,20},{18,... | collective-permute-start | bytes 98312 | tf_op jit(solution)/shard_map/ppermute | solution.py:222
  53.9 1.0 %collective-permute-start.10 = (bf16[128,128]{1,0:T(8,128)(2,1)S(1)}, bf16[128,128]{1,0:T(8,128)(2,1)S(1)}, u32[]{:S(2)}, u32[]{:S(2)}) collective-permute-start(bf16[128,128]{1,0:T(8,128)(2,1)S(1)} %add_convert_fusion.4), channel_id=1, source_target_pairs={{0,8},{2,10},{4,12},{6,14},{8,0},{10,2},{12,4},{14,6},{16,24},{18,... | collective-permute-start | bytes 98312 | tf_op jit(solution)/shard_map/ppermute | solution.py:222
  54.9 0.9 %collective-permute-done.16 = bf16[128,128]{1,0:T(8,128)(2,1)S(1)} collective-permute-done((bf16[128,128]{1,0:T(8,128)(2,1)S(1)}, bf16[128,128]{1,0:T(8,128)(2,1)S(1)}, u32[]{:S(2)}, u32[]{:S(2)}) %collective-permute-start.16) | collective-permute-done | bytes 32800 | tf_op jit(solution)/shard_map/ppermute | solution.py:222
  55.8 2.0 %collective-permute-start.17 = (bf16[128,128]{1,0:T(8,128)(2,1)S(1)}, bf16[128,128]{1,0:T(8,128)(2,1)S(1)}, u32[]{:S(2)}, u32[]{:S(2)}) collective-permute-start(bf16[128,128]{1,0:T(8,128)(2,1)S(1)} %add_convert_fusion.2), channel_id=1, source_target_pairs={{0,8},{2,10},{4,12},{6,14},{8,0},{10,2},{12,4},{14,6},{16,24},{18,... | collective-permute-start | bytes 98312 | tf_op jit(solution)/shard_map/ppermute | solution.py:222
  57.9 1.1 %collective-permute-start.24 = (bf16[128,128]{1,0:T(8,128)(2,1)S(1)}, bf16[128,128]{1,0:T(8,128)(2,1)S(1)}, u32[]{:S(2)}, u32[]{:S(2)}) collective-permute-start(bf16[128,128]{1,0:T(8,128)(2,1)S(1)} %add_convert_fusion), channel_id=1, source_target_pairs={{0,2},{2,0},{4,6},{6,4},{8,10},{10,8},{12,14},{14,12},{16,18},{18,... | collective-permute-start | bytes 98312 | tf_op jit(solution)/shard_map/ppermute | solution.py:222
  59.8 1.6 %collective-permute-start.18 = (bf16[256,128]{1,0:T(8,128)(2,1)S(1)}, bf16[256,128]{1,0:T(8,128)(2,1)S(1)}, u32[]{:S(2)}, u32[]{:S(2)}) collective-permute-start(bf16[256,128]{1,0:T(8,128)(2,1)S(1)} %maximum_select_fusion.7), channel_id=1, source_target_pairs={{0,2},{2,0},{4,6},{6,4},{8,10},{10,8},{12,14},{14,12},{16,18},{18,... | collective-permute-start | bytes 196616 | tf_op jit(solution)/shard_map/ppermute | solution.py:222
  62.2 1.3 %collective-permute-start.25 = (bf16[256,128]{1,0:T(8,128)(2,1)S(1)}, bf16[256,128]{1,0:T(8,128)(2,1)S(1)}, u32[]{:S(2)}, u32[]{:S(2)}) collective-permute-start(bf16[256,128]{1,0:T(8,128)(2,1)S(1)} %maximum_select_fusion.8), channel_id=1, source_target_pairs={{0,16},{2,18},{4,20},{6,22},{8,24},{10,26},{12,28},{14,30},{16,0},... | collective-permute-start | bytes 196616 | tf_op jit(solution)/shard_map/ppermute | solution.py:222
  63.6 1.1 %collective-permute-start.12 = (bf16[512,128]{1,0:T(8,128)(2,1)S(1)}, bf16[512,128]{1,0:T(8,128)(2,1)S(1)}, u32[]{:S(2)}, u32[]{:S(2)}) collective-permute-start(bf16[512,128]{1,0:T(8,128)(2,1)S(1)} %maximum_select_fusion.3), channel_id=1, source_target_pairs={{0,2},{2,0},{4,6},{6,4},{8,10},{10,8},{12,14},{14,12},{16,18},{18,... | collective-permute-start | bytes 393224 | tf_op jit(solution)/shard_map/ppermute | solution.py:222
  64.8 1.0 %collective-permute-start.19 = (bf16[512,128]{1,0:T(8,128)(2,1)S(1)}, bf16[512,128]{1,0:T(8,128)(2,1)S(1)}, u32[]{:S(2)}, u32[]{:S(2)}) collective-permute-start(bf16[512,128]{1,0:T(8,128)(2,1)S(1)} %maximum_select_fusion.4), channel_id=1, source_target_pairs={{0,4},{2,6},{4,0},{6,2},{8,12},{10,14},{12,8},{14,10},{16,20},{18,... | collective-permute-start | bytes 393224 | tf_op jit(solution)/shard_map/ppermute | solution.py:222
  65.8 2.3 %collective-permute-done.25 = bf16[256,128]{1,0:T(8,128)(2,1)S(1)} collective-permute-done((bf16[256,128]{1,0:T(8,128)(2,1)S(1)}, bf16[256,128]{1,0:T(8,128)(2,1)S(1)}, u32[]{:S(2)}, u32[]{:S(2)}) %collective-permute-start.25) | collective-permute-done | bytes 65568 | tf_op jit(solution)/shard_map/ppermute | solution.py:222
  68.8 1.1 %collective-permute-done.19 = bf16[512,128]{1,0:T(8,128)(2,1)S(1)} collective-permute-done((bf16[512,128]{1,0:T(8,128)(2,1)S(1)}, bf16[512,128]{1,0:T(8,128)(2,1)S(1)}, u32[]{:S(2)}, u32[]{:S(2)}) %collective-permute-start.19) | collective-permute-done | bytes 131104 | tf_op jit(solution)/shard_map/ppermute | solution.py:222
  69.9 3.3 %collective-permute-done.26 = bf16[512,128]{1,0:T(8,128)(2,1)S(1)} collective-permute-done((bf16[512,128]{1,0:T(8,128)(2,1)S(1)}, bf16[512,128]{1,0:T(8,128)(2,1)S(1)}, u32[]{:S(2)}, u32[]{:S(2)}) %collective-permute-start.26) | collective-permute-done | bytes 131104 | tf_op jit(solution)/shard_map/ppermute | solution.py:222
  73.5 2.3 %collective-permute-done.27.other_ref = bf16[3,1024,128]{2,1,0:T(8,128)(2,1)S(1)} collective-permute-done((bf16[3,1024,128]{2,1,0:T(8,128)(2,1)S(1)}, bf16[3,1024,128]{2,1,0:T(8,128)(2,1)S(1)}, u32[]{:S(2)}, u32[]{:S(2)}) %collective-permute-start.27) | collective-permute-done | bytes 786464 | tf_op jit(solution)/shard_map/ppermute | solution.py:222
  75.8 2.9 %shard_map.88 = (f32[27,96,96]{2,1,0:T(8,128)}, f32[27,96,192]{2,1,0:T(8,128)}) custom-call(s32[2]{0:T(128)S(1)} %pad_add_fusion.position_ref, bf16[3,1024,128]{2,1,0:T(8,128)(2,1)S(1)} %pad_maximum_fusion.own_ref, bf16[3,1024,128]{2,1,0:T(8,128)(2,1)S(1)} %collective-permute-done.27.other_ref), custom_call_target="tpu_custom_call" | custom-call | tf_op jit(solution)/shard_map/pallas_call | solution.py:210
  (74 shorter events, 8.9 us)
Async XLA Ops:
  0.6 12.4 %copy-start.5 = (s32[1,27]{1,0:T(1,128)S(1)}, s32[1,27]{1,0:T(1,128)}, u32[]{:S(2)}) copy-start(s32[1,27]{1,0:T(1,128)} %neighbors_ref.1) | copy-start | bytes 328
  0.7 0.9 %copy-start.2 = (bf16[192,512]{1,0:T(8,128)(2,1)S(1)}, bf16[192,512]{1,0:T(8,128)(2,1)}, u32[]{:S(2)}) copy-start(bf16[192,512]{1,0:T(8,128)(2,1)} %cotangent_ref.1) | copy-start | bytes 589828
  4.0 9.1 %collective-permute-start = (bf16[512,384]{1,0:T(8,128)(2,1)S(1)}, bf16[512,384]{1,0:T(8,128)(2,1)S(1)}, u32[]{:S(2)}, u32[]{:S(2)}) collective-permute-start(bf16[512,384]{1,0:T(8,128)(2,1)S(1)} %get-tuple-element.13.own_ref), channel_id=1, source_target_pairs={{0,1},{1,0},{2,3},{3,2},{4,5},{5,4},{6,7},{7,6},{8,9},{9,8},{10,11... | collective-permute-start | bytes 1179656 | tf_op jit(solution)/shard_map/ppermute | solution.py:222
  4.5 5.3 %collective-permute-start.1 = (bf16[128,256]{1,0:T(8,128)(2,1)S(1)}, bf16[128,256]{1,0:T(8,128)(2,1)S(1)}, u32[]{:S(2)}, u32[]{:S(2)}) collective-permute-start(bf16[128,256]{1,0:T(8,128)(2,1)S(1)} %get-tuple-element.14), channel_id=1, source_target_pairs={{0,2},{2,0},{4,6},{6,4},{8,10},{10,8},{12,14},{14,12},{16,18},{18,... | collective-permute-start | bytes 196616 | tf_op jit(solution)/shard_map/ppermute | solution.py:252
  7.1 2.7 %collective-permute-start.2 = (bf16[128,256]{1,0:T(8,128)(2,1)S(1)}, bf16[128,256]{1,0:T(8,128)(2,1)S(1)}, u32[]{:S(2)}, u32[]{:S(2)}) collective-permute-start(bf16[128,256]{1,0:T(8,128)(2,1)S(1)} %get-tuple-element.15), channel_id=1, source_target_pairs={{2,4},{6,8},{10,12},{14,16},{18,20},{22,24},{26,28},{4,2},{8,6},{1... | collective-permute-start | bytes 196616 | tf_op jit(solution)/shard_map/ppermute | solution.py:254
  9.7 3.3 %collective-permute-start.3 = (bf16[128,256]{1,0:T(8,128)(2,1)S(1)}, bf16[128,256]{1,0:T(8,128)(2,1)S(1)}, u32[]{:S(2)}, u32[]{:S(2)}) collective-permute-start(bf16[128,256]{1,0:T(8,128)(2,1)S(1)} %collective-permute-done.1.first_ref), channel_id=1, source_target_pairs={{0,1},{1,0},{2,3},{3,2},{4,5},{5,4},{6,7},{7,6},{8,9},{9,8},{10,11... | collective-permute-start | bytes 196616 | tf_op jit(solution)/shard_map/ppermute | solution.py:222
  9.8 3.3 %collective-permute-start.4 = (bf16[128,256]{1,0:T(8,128)(2,1)S(1)}, bf16[128,256]{1,0:T(8,128)(2,1)S(1)}, u32[]{:S(2)}, u32[]{:S(2)}) collective-permute-start(bf16[128,256]{1,0:T(8,128)(2,1)S(1)} %collective-permute-done.2.second_ref), channel_id=1, source_target_pairs={{0,1},{1,0},{2,3},{3,2},{4,5},{5,4},{6,7},{7,6},{8,9},{9,8},{10,11... | collective-permute-start | bytes 196616 | tf_op jit(solution)/shard_map/ppermute | solution.py:222
  10.3 1.3 %copy-start = (bf16[27,96,192]{2,1,0:T(8,128)(2,1)S(1)}, bf16[27,96,192]{2,1,0:T(8,128)(2,1)}, u32[]{:S(2)}) copy-start(bf16[27,96,192]{2,1,0:T(8,128)(2,1)} %two_ref.1) | copy-start | bytes 2985988
  11.6 1.1 %copy-start.1 = (bf16[27,96,96]{2,1,0:T(8,128)(2,1)S(1)}, bf16[27,96,96]{2,1,0:T(8,128)(2,1)}, u32[]{:S(2)}) copy-start(bf16[27,96,96]{2,1,0:T(8,128)(2,1)} %one_ref.1) | copy-start | bytes 1492996
  26.3 2.3 %collective-permute-start.5 = (bf16[3,1024,128]{2,1,0:T(8,128)(2,1)S(1)}, bf16[3,1024,128]{2,1,0:T(8,128)(2,1)S(1)}, u32[]{:S(2)}, u32[]{:S(2)}) collective-permute-start(bf16[3,1024,128]{2,1,0:T(8,128)(2,1)S(1)} %get-tuple-element.20), channel_id=1, source_target_pairs={{0,1},{1,0},{2,3},{3,2},{4,5},{5,4},{6,7},{7,6},{8,9},{9,8},{10,11... | collective-permute-start | bytes 2359304 | tf_op jit(solution)/shard_map/ppermute | solution.py:222
  28.9 8.8 %collective-permute-start.6 = (bf16[512,128]{1,0:T(8,128)(2,1)S(1)}, bf16[512,128]{1,0:T(8,128)(2,1)S(1)}, u32[]{:S(2)}, u32[]{:S(2)}) collective-permute-start(bf16[512,128]{1,0:T(8,128)(2,1)S(1)} %fusion), channel_id=1, source_target_pairs={{0,2},{2,0},{4,6},{6,4},{8,10},{10,8},{12,14},{14,12},{16,18},{18,... | collective-permute-start | bytes 393224 | tf_op jit(solution)/shard_map/ppermute | solution.py:222
  33.2 7.1 %collective-permute-start.13 = (bf16[512,128]{1,0:T(8,128)(2,1)S(1)}, bf16[512,128]{1,0:T(8,128)(2,1)S(1)}, u32[]{:S(2)}, u32[]{:S(2)}) collective-permute-start(bf16[512,128]{1,0:T(8,128)(2,1)S(1)} %fusion.1), channel_id=1, source_target_pairs={{0,4},{2,6},{4,0},{6,2},{8,12},{10,14},{12,8},{14,10},{16,20},{18,... | collective-permute-start | bytes 393224 | tf_op jit(solution)/shard_map/ppermute | solution.py:222
  36.0 5.9 %collective-permute-start.20 = (bf16[512,128]{1,0:T(8,128)(2,1)S(1)}, bf16[512,128]{1,0:T(8,128)(2,1)S(1)}, u32[]{:S(2)}, u32[]{:S(2)}) collective-permute-start(bf16[512,128]{1,0:T(8,128)(2,1)S(1)} %fusion.2), channel_id=1, source_target_pairs={{0,8},{2,10},{4,12},{6,14},{8,0},{10,2},{12,4},{14,6},{16,24},{18,... | collective-permute-start | bytes 393224 | tf_op jit(solution)/shard_map/ppermute | solution.py:222
  37.7 6.9 %collective-permute-start.7 = (bf16[256,128]{1,0:T(8,128)(2,1)S(1)}, bf16[256,128]{1,0:T(8,128)(2,1)S(1)}, u32[]{:S(2)}, u32[]{:S(2)}) collective-permute-start(bf16[256,128]{1,0:T(8,128)(2,1)S(1)} %dynamic-slice_convert_fusion.5), channel_id=1, source_target_pairs={{0,4},{2,6},{4,0},{6,2},{8,12},{10,14},{12,8},{14,10},{16,20},{18,... | collective-permute-start | bytes 196616 | tf_op jit(solution)/shard_map/ppermute | solution.py:222
  40.4 5.6 %collective-permute-start.14 = (bf16[256,128]{1,0:T(8,128)(2,1)S(1)}, bf16[256,128]{1,0:T(8,128)(2,1)S(1)}, u32[]{:S(2)}, u32[]{:S(2)}) collective-permute-start(bf16[256,128]{1,0:T(8,128)(2,1)S(1)} %dynamic-slice_convert_fusion.4), channel_id=1, source_target_pairs={{0,2},{2,0},{4,6},{6,4},{8,10},{10,8},{12,14},{14,12},{16,18},{18,... | collective-permute-start | bytes 196616 | tf_op jit(solution)/shard_map/ppermute | solution.py:222
  42.0 5.2 %collective-permute-start.21 = (bf16[256,128]{1,0:T(8,128)(2,1)S(1)}, bf16[256,128]{1,0:T(8,128)(2,1)S(1)}, u32[]{:S(2)}, u32[]{:S(2)}) collective-permute-start(bf16[256,128]{1,0:T(8,128)(2,1)S(1)} %dynamic-slice_convert_fusion.3), channel_id=1, source_target_pairs={{0,16},{2,18},{4,20},{6,22},{8,24},{10,26},{12,28},{14,30},{16,0},... | collective-permute-start | bytes 196616 | tf_op jit(solution)/shard_map/ppermute | solution.py:222
  44.7 4.0 %collective-permute-start.8 = (bf16[128,128]{1,0:T(8,128)(2,1)S(1)}, bf16[128,128]{1,0:T(8,128)(2,1)S(1)}, u32[]{:S(2)}, u32[]{:S(2)}) collective-permute-start(bf16[128,128]{1,0:T(8,128)(2,1)S(1)} %dynamic-slice_convert_fusion.8), channel_id=1, source_target_pairs={{0,8},{2,10},{4,12},{6,14},{8,0},{10,2},{12,4},{14,6},{16,24},{18,... | collective-permute-start | bytes 98312 | tf_op jit(solution)/shard_map/ppermute | solution.py:222
  46.0 4.9 %collective-permute-start.15 = (bf16[128,128]{1,0:T(8,128)(2,1)S(1)}, bf16[128,128]{1,0:T(8,128)(2,1)S(1)}, u32[]{:S(2)}, u32[]{:S(2)}) collective-permute-start(bf16[128,128]{1,0:T(8,128)(2,1)S(1)} %dynamic-slice_convert_fusion.7), channel_id=1, source_target_pairs={{0,8},{2,10},{4,12},{6,14},{8,0},{10,2},{12,4},{14,6},{16,24},{18,... | collective-permute-start | bytes 98312 | tf_op jit(solution)/shard_map/ppermute | solution.py:222
  47.3 5.1 %collective-permute-start.22 = (bf16[128,128]{1,0:T(8,128)(2,1)S(1)}, bf16[128,128]{1,0:T(8,128)(2,1)S(1)}, u32[]{:S(2)}, u32[]{:S(2)}) collective-permute-start(bf16[128,128]{1,0:T(8,128)(2,1)S(1)} %dynamic-slice_convert_fusion.6), channel_id=1, source_target_pairs={{0,2},{2,0},{4,6},{6,4},{8,10},{10,8},{12,14},{14,12},{16,18},{18,... | collective-permute-start | bytes 98312 | tf_op jit(solution)/shard_map/ppermute | solution.py:222
  48.7 5.2 %collective-permute-start.9 = (bf16[128,128]{1,0:T(8,128)(2,1)S(1)}, bf16[128,128]{1,0:T(8,128)(2,1)S(1)}, u32[]{:S(2)}, u32[]{:S(2)}) collective-permute-start(bf16[128,128]{1,0:T(8,128)(2,1)S(1)} %add_convert_fusion.5), channel_id=1, source_target_pairs={{0,16},{2,18},{4,20},{6,22},{8,24},{10,26},{12,28},{14,30},{16,0},... | collective-permute-start | bytes 98312 | tf_op jit(solution)/shard_map/ppermute | solution.py:222
  51.0 4.9 %collective-permute-start.16 = (bf16[128,128]{1,0:T(8,128)(2,1)S(1)}, bf16[128,128]{1,0:T(8,128)(2,1)S(1)}, u32[]{:S(2)}, u32[]{:S(2)}) collective-permute-start(bf16[128,128]{1,0:T(8,128)(2,1)S(1)} %add_convert_fusion.3), channel_id=1, source_target_pairs={{0,16},{2,18},{4,20},{6,22},{8,24},{10,26},{12,28},{14,30},{16,0},... | collective-permute-start | bytes 98312 | tf_op jit(solution)/shard_map/ppermute | solution.py:222
  52.4 5.5 %collective-permute-start.23 = (bf16[128,128]{1,0:T(8,128)(2,1)S(1)}, bf16[128,128]{1,0:T(8,128)(2,1)S(1)}, u32[]{:S(2)}, u32[]{:S(2)}) collective-permute-start(bf16[128,128]{1,0:T(8,128)(2,1)S(1)} %add_convert_fusion.1), channel_id=1, source_target_pairs={{0,4},{2,6},{4,0},{6,2},{8,12},{10,14},{12,8},{14,10},{16,20},{18,... | collective-permute-start | bytes 98312 | tf_op jit(solution)/shard_map/ppermute | solution.py:222
  53.9 5.1 %collective-permute-start.10 = (bf16[128,128]{1,0:T(8,128)(2,1)S(1)}, bf16[128,128]{1,0:T(8,128)(2,1)S(1)}, u32[]{:S(2)}, u32[]{:S(2)}) collective-permute-start(bf16[128,128]{1,0:T(8,128)(2,1)S(1)} %add_convert_fusion.4), channel_id=1, source_target_pairs={{0,8},{2,10},{4,12},{6,14},{8,0},{10,2},{12,4},{14,6},{16,24},{18,... | collective-permute-start | bytes 98312 | tf_op jit(solution)/shard_map/ppermute | solution.py:222
  55.8 4.0 %collective-permute-start.17 = (bf16[128,128]{1,0:T(8,128)(2,1)S(1)}, bf16[128,128]{1,0:T(8,128)(2,1)S(1)}, u32[]{:S(2)}, u32[]{:S(2)}) collective-permute-start(bf16[128,128]{1,0:T(8,128)(2,1)S(1)} %add_convert_fusion.2), channel_id=1, source_target_pairs={{0,8},{2,10},{4,12},{6,14},{8,0},{10,2},{12,4},{14,6},{16,24},{18,... | collective-permute-start | bytes 98312 | tf_op jit(solution)/shard_map/ppermute | solution.py:222
  57.9 4.3 %collective-permute-start.24 = (bf16[128,128]{1,0:T(8,128)(2,1)S(1)}, bf16[128,128]{1,0:T(8,128)(2,1)S(1)}, u32[]{:S(2)}, u32[]{:S(2)}) collective-permute-start(bf16[128,128]{1,0:T(8,128)(2,1)S(1)} %add_convert_fusion), channel_id=1, source_target_pairs={{0,2},{2,0},{4,6},{6,4},{8,10},{10,8},{12,14},{14,12},{16,18},{18,... | collective-permute-start | bytes 98312 | tf_op jit(solution)/shard_map/ppermute | solution.py:222
  59.0 4.6 %collective-permute-start.11 = (bf16[256,128]{1,0:T(8,128)(2,1)S(1)}, bf16[256,128]{1,0:T(8,128)(2,1)S(1)}, u32[]{:S(2)}, u32[]{:S(2)}) collective-permute-start(bf16[256,128]{1,0:T(8,128)(2,1)S(1)} %maximum_select_fusion.6), channel_id=1, source_target_pairs={{0,4},{2,6},{4,0},{6,2},{8,12},{10,14},{12,8},{14,10},{16,20},{18,... | collective-permute-start | bytes 196616 | tf_op jit(solution)/shard_map/ppermute | solution.py:222
  59.8 4.9 %collective-permute-start.18 = (bf16[256,128]{1,0:T(8,128)(2,1)S(1)}, bf16[256,128]{1,0:T(8,128)(2,1)S(1)}, u32[]{:S(2)}, u32[]{:S(2)}) collective-permute-start(bf16[256,128]{1,0:T(8,128)(2,1)S(1)} %maximum_select_fusion.7), channel_id=1, source_target_pairs={{0,2},{2,0},{4,6},{6,4},{8,10},{10,8},{12,14},{14,12},{16,18},{18,... | collective-permute-start | bytes 196616 | tf_op jit(solution)/shard_map/ppermute | solution.py:222
  62.2 5.9 %collective-permute-start.25 = (bf16[256,128]{1,0:T(8,128)(2,1)S(1)}, bf16[256,128]{1,0:T(8,128)(2,1)S(1)}, u32[]{:S(2)}, u32[]{:S(2)}) collective-permute-start(bf16[256,128]{1,0:T(8,128)(2,1)S(1)} %maximum_select_fusion.8), channel_id=1, source_target_pairs={{0,16},{2,18},{4,20},{6,22},{8,24},{10,26},{12,28},{14,30},{16,0},... | collective-permute-start | bytes 196616 | tf_op jit(solution)/shard_map/ppermute | solution.py:222
  63.6 5.0 %collective-permute-start.12 = (bf16[512,128]{1,0:T(8,128)(2,1)S(1)}, bf16[512,128]{1,0:T(8,128)(2,1)S(1)}, u32[]{:S(2)}, u32[]{:S(2)}) collective-permute-start(bf16[512,128]{1,0:T(8,128)(2,1)S(1)} %maximum_select_fusion.3), channel_id=1, source_target_pairs={{0,2},{2,0},{4,6},{6,4},{8,10},{10,8},{12,14},{14,12},{16,18},{18,... | collective-permute-start | bytes 393224 | tf_op jit(solution)/shard_map/ppermute | solution.py:222
  64.8 5.0 %collective-permute-start.19 = (bf16[512,128]{1,0:T(8,128)(2,1)S(1)}, bf16[512,128]{1,0:T(8,128)(2,1)S(1)}, u32[]{:S(2)}, u32[]{:S(2)}) collective-permute-start(bf16[512,128]{1,0:T(8,128)(2,1)S(1)} %maximum_select_fusion.4), channel_id=1, source_target_pairs={{0,4},{2,6},{4,0},{6,2},{8,12},{10,14},{12,8},{14,10},{16,20},{18,... | collective-permute-start | bytes 393224 | tf_op jit(solution)/shard_map/ppermute | solution.py:222
  68.2 5.0 %collective-permute-start.26 = (bf16[512,128]{1,0:T(8,128)(2,1)S(1)}, bf16[512,128]{1,0:T(8,128)(2,1)S(1)}, u32[]{:S(2)}, u32[]{:S(2)}) collective-permute-start(bf16[512,128]{1,0:T(8,128)(2,1)S(1)} %maximum_select_fusion.5), channel_id=1, source_target_pairs={{0,8},{2,10},{4,12},{6,14},{8,0},{10,2},{12,4},{14,6},{16,24},{18,... | collective-permute-start | bytes 393224 | tf_op jit(solution)/shard_map/ppermute | solution.py:222
  73.4 2.4 %collective-permute-start.27 = (bf16[3,1024,128]{2,1,0:T(8,128)(2,1)S(1)}, bf16[3,1024,128]{2,1,0:T(8,128)(2,1)S(1)}, u32[]{:S(2)}, u32[]{:S(2)}) collective-permute-start(bf16[3,1024,128]{2,1,0:T(8,128)(2,1)S(1)} %pad_maximum_fusion.own_ref), channel_id=1, source_target_pairs={{0,1},{1,0},{2,3},{3,2},{4,5},{5,4},{6,7},{7,6},{8,9},{9,8},{10,11... | collective-permute-start | bytes 2359304 | tf_op jit(solution)/shard_map/ppermute | solution.py:222
  (2 other events, 1.6 us)

commit v4 on v3

v4 whole, which is shorter than its diff:
```python
import jax
import jax.numpy as jnp
from jax import lax
from jax.experimental import pallas as pl
from jax.experimental.pallas import tpu as pltpu
from jax.sharding import PartitionSpec as P

F32 = jnp.float32
BF16 = jnp.bfloat16
LANES = 128
VMEM_BYTES = 32 * 2**20


def up_to(value, step):
    return -(-value // step) * step


def fetched(pairs, sems):
    copies = [pltpu.make_async_copy(source, target, sems.at[place]) for place, (source, target) in enumerate(pairs)]
    for copy in copies:
        copy.start()
    return copies


def pack_kernel(
    position_ref, features_hbm, occupancy_hbm, cotangent_hbm, packed_ref, first_ref, second_ref, turned_ref,
    features_ref, occupancy_ref, cotangent_ref, sems,
):
    copies = fetched(
        ((occupancy_hbm, occupancy_ref), (features_hbm, features_ref), (cotangent_hbm, cotangent_ref)), sems
    )
    channels, voxels = features_ref.shape
    outs = cotangent_ref.shape[0]
    copies[0].wait()
    copies[1].wait()
    active = occupancy_ref[...] > 0
    masked = jnp.where(active, features_ref[...].astype(F32), 0.0)
    flag = jnp.where(active, 1.0, 0.0)
    row = lax.broadcasted_iota(jnp.int32, (LANES - channels, voxels), 0)
    tail = jnp.where(row == 0, jnp.broadcast_to(flag, row.shape), 0.0)
    packed_ref[:, :LANES] = jnp.concatenate([masked, tail], 0).T.astype(BF16)
    copies[2].wait()
    grad_out = jnp.where(active, cotangent_ref[...].astype(F32), 0.0)
    turned_ref[...] = grad_out.astype(BF16)
    spare = up_to(outs, LANES) - outs
    grad_out = jnp.concatenate([grad_out, jnp.zeros((spare, voxels), F32)], 0)
    packed_ref[:, LANES:] = grad_out.T.astype(BF16)
    odd = position_ref[0]
    for target, upper in ((first_ref, 1 - odd), (second_ref, odd)):
        row = pl.multiple_of(upper * 384, 128)
        near = pl.multiple_of(upper * 448, 64)
        target[:, :LANES] = packed_ref[pl.ds(row, 128), :LANES]
        target[:64, LANES:] = packed_ref[pl.ds(near, 64), LANES : 2 * LANES]
        target[64:, LANES:] = packed_ref[pl.ds(near, 64), 2 * LANES :]


def weights_kernel(one_hbm, two_hbm, one_pad_ref, two_pad_ref, one_ref, two_ref, sems):
    copies = fetched(((one_hbm, one_ref), (two_hbm, two_ref)), sems)
    offsets, channels, outs = two_ref.shape
    spare = LANES - channels
    one_pad_ref[:, channels:, :] = jnp.zeros((offsets, spare, one_ref.shape[2]), BF16)
    copies[0].wait()
    one_pad_ref[:, :channels, :] = one_ref[...]
    copies[1].wait()
    two_pad_ref[:, :channels, :outs] = two_ref[...]
    two_pad_ref[:, :channels, outs:] = jnp.zeros((offsets, channels, two_pad_ref.shape[2] - outs), BF16)
    two_pad_ref[:, channels:, :] = jnp.zeros((offsets, spare, two_pad_ref.shape[2]), BF16)


def store_turned(total_ref, product, offset, first_row, channels):
    rows = product.shape[0]
    spare = LANES - channels
    group, place = divmod(offset, 4)
    if place < 3:
        base = first_row + (3 * group + place) * rows
        total_ref[pl.ds(base, rows), :channels] = product[:, :channels]
    else:
        for piece in range(3):
            base = first_row + (3 * group + piece) * rows
            total_ref[pl.ds(base, rows), channels:] = product[:, piece * spare : (piece + 1) * spare]


def main_kernel(
    position_ref, neighbors_ref, own_ref, partner_ref, first_ref, second_ref, first_far_ref, second_far_ref,
    turned_ref, one_ref, two_ref, output_ref, kept_p_ref, kept_q_ref, sent_p_ref, sent_q_ref, masked_w, grad_w, hidden_w, total, masked_s, plane_s, hidden_s, grad_s,
):
    odd, split = position_ref[0], position_ref[1]
    channels = one_ref.shape[2]
    outs = output_ref.shape[0]
    wide = grad_w.shape[3]
    masked_w[:, 6:18] = jnp.zeros((12, 12, 24, LANES), F32)
    grad_w[:, 7:17] = jnp.zeros((10, 10, 24, wide), F32)

    own = own_ref[...].astype(F32).reshape(8, 8, 8, LANES + wide)
    masked_w[2:10, 8:16, 8:16, :] = own[..., :LANES]
    grad_w[1:9, 8:16, 8:16, :] = own[..., LANES:]

    def placed(step_x, step_z):
        found = [neighbors_ref[0, 9 * (step_x + 1) + 3 * step_y + step_z + 1] >= 0 for step_y in range(3)]
        y = jnp.where(found[0], 0, jnp.where(found[1], 1, 2))
        return found[0] | found[1] | found[2], pl.multiple_of(8 * y, 8)

    step_z = 1 - 2 * split
    valid, y = placed(0, step_z)
    z = pl.multiple_of(8 + 8 * step_z, 8)

    @pl.when(valid)
    def _():
        block = partner_ref[...].astype(F32).reshape(8, 8, 8, LANES + wide)
        masked_w[2:10, pl.ds(y, 8), pl.ds(z, 8), :] = block[..., :LANES]
        grad_w[1:9, pl.ds(y, 8), pl.ds(z, 8), :] = block[..., LANES:]

    for which, refs in enumerate(((first_ref, first_far_ref), (second_ref, second_far_ref))):
        step_x = 1 - 2 * odd if which == 0 else 2 * odd - 1
        for source, ref in enumerate(refs):
            step_z = 0 if source == 0 else 1 - 2 * split
            valid, y = placed(step_x, step_z)
            z = pl.multiple_of(8 + 8 * step_z, 8)
            x_masked = jnp.where(step_x > 0, 10, 0)
            x_grad = jnp.where(step_x > 0, 9, 0)

            @pl.when(valid)
            def _():
                block = ref[...].astype(F32)
                masked_w[pl.ds(x_masked, 2), pl.ds(y, 8), pl.ds(z, 8), :] = block[:, :LANES].reshape(2, 8, 8, LANES)
                near = jnp.concatenate([block[:64, LANES:], block[64:, LANES:]], 1)
                grad_w[pl.ds(x_grad, 1), pl.ds(y, 8), pl.ds(z, 8), :] = near.reshape(1, 8, 8, wide)

    def stage(target, source, first_x, first_y, first_z):
        count_x, rows = target.shape[2:4]
        lanes = target.shape[4]
        for dz in range(3):
            block = source[
                first_x : first_x + count_x, first_y : first_y + rows // 8, first_z + dz : first_z + dz + 8, :
            ]
            target[dz, 0] = block.reshape(count_x, rows, lanes).astype(BF16)
            target[dz, 1, :, : rows - 16] = block[:, 1 : rows // 8 - 1].reshape(count_x, rows - 16, lanes).astype(BF16)

    def staged(target, tap, count, more=0):
        code, dx = divmod(tap, 3)
        dy, dz = divmod(code, 3)
        row = 16 * ((dy + more) // 2)
        first = dx + more
        block = target[dz, (dy + more) % 2, first : first + count, row : row + 8 * count, :]
        return block.reshape(8 * count * count, target.shape[4])

    taps = range(27)
    chunks = [taps[first : first + 6] for first in range(0, 27, 6)]

    def offset_of(tap):
        return 9 * (tap % 3) + tap // 3

    beside = 16 - 9 * split
    stage(masked_s, masked_w, 0, 6, 7)
    for dz in range(3):
        plane = masked_w[:, 6:24, pl.ds(beside - 1 + dz, 1), :].reshape(12, 18, LANES)
        for dy in range(3):
            plane_s[dz, dy] = plane[:, dy : dy + 16, :].astype(BF16)
        if dz == 1:
            plane_flag = plane[1:11, 1:17, channels : channels + 1].reshape(160, 1) > 0

    def plane_rows(tap):
        code, dx = divmod(tap, 3)
        dy, dz = divmod(code, 3)
        return plane_s[dz, dy, dx : dx + 10].reshape(160, LANES)

    hidden_pre = None
    for chunk in chunks:
        rows = jnp.concatenate(
            [jnp.concatenate([staged(masked_s, tap, 10), plane_rows(tap)], 0) for tap in chunk], 1
        )
        kernel = jnp.concatenate([one_ref[offset_of(tap)] for tap in chunk], 0)
        term = jnp.dot(rows, kernel, preferred_element_type=F32)
        hidden_pre = term if hidden_pre is None else hidden_pre + term
    flags = masked_w[1:11, 7:17, 8:16, channels : channels + 1].reshape(800, 1) > 0
    hidden_pre = jnp.where(jnp.concatenate([flags, plane_flag], 0), hidden_pre, 0.0)
    hidden = hidden_pre * jax.nn.sigmoid(hidden_pre)
    hidden = jnp.concatenate([hidden, jnp.zeros((960, LANES - channels), F32)], 1)
    hidden_w[:, :, 8:16, :] = hidden[:800].reshape(10, 10, 8, LANES)
    hidden_w[:, :, 0:8, :] = jnp.zeros((10, 10, 8, LANES), F32)
    hidden_w[:, :, 16:24, :] = jnp.zeros((10, 10, 8, LANES), F32)
    hidden_w[:, :, pl.ds(beside, 1), :] = hidden[800:].reshape(10, 16, LANES)[:, :10].reshape(10, 10, 1, LANES)
    own_pre = hidden_pre[:800].reshape(10, 10, 8, channels)[1:9, 1:9].reshape(512, channels)
    own_flag = masked_w[2:10, 8:16, 8:16, channels : channels + 1].reshape(512, 1) > 0

    first_one = 3 * (-(-27 // 4)) * outs
    turned_out = turned_ref[...]
    stage(hidden_s, hidden_w, 0, 0, 7)
    output = None
    for chunk in chunks:
        rows = jnp.concatenate([staged(hidden_s, tap, 8) for tap in chunk], 1)
        kernel = jnp.concatenate([two_ref[offset_of(tap)] for tap in chunk], 0)[:, :outs]
        term = jnp.dot(rows, kernel, preferred_element_type=F32)
        output = term if output is None else output + term
        product = jnp.dot(turned_out, rows, preferred_element_type=F32)
        for place, tap in enumerate(chunk):
            store_turned(total, product[:, place * LANES : (place + 1) * LANES], offset_of(tap), 0, channels)
    output_ref[...] = jnp.where(own_flag, output, 0.0).T.astype(BF16)

    stage(grad_s, grad_w, 0, 7, 7)
    back = None
    for chunk in chunks:
        rows = jnp.concatenate([staged(grad_s, tap, 8) for tap in chunk], 1)
        kernel = jnp.concatenate([two_ref[26 - offset_of(tap)] for tap in chunk], 1)
        term = lax.dot_general(rows, kernel, (((1,), (1,)), ((), ())), preferred_element_type=F32)
        back = term if back is None else back + term
    back = back[:, :channels]
    gate = jax.nn.sigmoid(own_pre)
    grad_pre = jnp.where(own_flag, back * gate * (1.0 + own_pre * (1.0 - gate)), 0.0)
    turned_pre = grad_pre.T.astype(BF16)

    for chunk in chunks:
        rows = jnp.concatenate([staged(masked_s, tap, 8, 1) for tap in chunk], 1)
        product = jnp.dot(turned_pre, rows, preferred_element_type=F32)
        for place, tap in enumerate(chunk):
            store_turned(
                total, product[:, place * LANES : (place + 1) * LANES], offset_of(tap), first_one, channels
            )

    half = kept_p_ref.shape[0]
    for start, kept_ref, sent_ref in ((0, kept_p_ref, sent_p_ref), (2 * half, kept_q_ref, sent_q_ref)):
        kept_ref[...] = total[pl.ds(pl.multiple_of(start + split * half, 16), half), :]
        sent_ref[...] = total[pl.ds(pl.multiple_of(start + (1 - split) * half, 16), half), :].astype(BF16)


def unpack_kernel(position_ref, own_p_ref, other_p_ref, own_q_ref, other_q_ref, one_ref, two_ref, sums):
    split = position_ref[1]
    offsets, channels, outs = two_ref.shape
    half = own_p_ref.shape[0]
    for start, own_ref, other_ref in ((0, own_p_ref, other_p_ref), (2 * half, own_q_ref, other_q_ref)):
        sums[pl.ds(pl.multiple_of(start + split * half, 16), half), :] = own_ref[...]
        sums[pl.ds(pl.multiple_of(start + (1 - split) * half, 16), half), :] = other_ref[...]
    row = lax.broadcasted_iota(jnp.int32, (LANES, LANES), 0)
    unit = jnp.where(row == lax.broadcasted_iota(jnp.int32, (LANES, LANES), 1), 1.0, 0.0).astype(BF16)
    spare = LANES - channels
    for ref, first, rows in ((two_ref, 0, outs), (one_ref, 3 * (-(-offsets // 4)) * outs, channels)):
        for tile in range(3 * (-(-offsets // 4))):
            group, place = divmod(tile, 3)
            part = sums[pl.ds(first + tile * rows, rows), :]
            part = lax.dot_general(unit, part, (((1,), (1,)), ((), ())), preferred_element_type=F32)
            ref[4 * group + place] = part[:channels]
            if 4 * group + 3 < offsets:
                ref[4 * group + 3, place * spare : (place + 1) * spare, :] = part[channels:]


def call(kernel, out_shape, args, scalars=0, scratch=(), cost=None, fetch=0, vmem=VMEM_BYTES):
    spaces = [pltpu.SMEM] * scalars + [pltpu.HBM] * fetch + [pltpu.VMEM] * (len(args) - scalars - fetch)
    return pl.pallas_call(
        kernel,
        out_shape=out_shape,
        in_specs=[pl.BlockSpec(memory_space=space) for space in spaces],
        out_specs=jax.tree.map(lambda _: pl.BlockSpec(memory_space=pltpu.VMEM), out_shape),
        scratch_shapes=list(scratch),
        compiler_params=pltpu.CompilerParams(vmem_limit_bytes=vmem),
        cost_estimate=cost,
    )(*args)


def exchanged(value, axis, mask):
    return lax.ppermute(value, axis, [(i, i ^ mask) for i in range(lax.axis_size(axis))])


def halves(value, bit):
    half = value.shape[0] // 2
    return (
        lax.dynamic_slice_in_dim(value, bit * half, half, 0),
        lax.dynamic_slice_in_dim(value, (1 - bit) * half, half, 0),
    )


def shards(features, kernel_one, kernel_two, occupancy, neighbors, cotangent):
    channels, voxels = features.shape
    offsets, _, outs = kernel_two.shape
    regions = lax.axis_size("region")
    region = lax.axis_index("region").astype(jnp.int32)
    split = lax.axis_index("split").astype(jnp.int32)
    odd = region % 2
    position = jnp.stack([odd, split])
    wide = up_to(outs, LANES)
    struct = jax.ShapeDtypeStruct

    planes = struct((128, 2 * LANES), BF16)
    packed, first, second, turned = call(
        pack_kernel,
        (struct((voxels, LANES + wide), BF16), planes, planes, struct((outs, voxels), BF16)),
        (position, features, occupancy, cotangent),
        scalars=1,
        fetch=3,
        vmem=56 * 2**20,
        scratch=(
            pltpu.VMEM(features.shape, BF16),
            pltpu.VMEM(occupancy.shape, occupancy.dtype),
            pltpu.VMEM(cotangent.shape, BF16),
            pltpu.SemaphoreType.DMA((3,)),
        ),
    )
    pairs = [(i, i + 1) for i in range(1, regions - 1, 2)]
    second = lax.ppermute(second, "region", pairs + [(b, a) for a, b in pairs])
    first = lax.ppermute(first, "region", [(i, i ^ 1) for i in range(regions)])
    partner = exchanged(packed, "split", 1)
    weights = call(
        weights_kernel,
        (struct((offsets, LANES, channels), BF16), struct((offsets, LANES, wide), BF16)),
        (kernel_one, kernel_two),
        fetch=2,
        scratch=(
            pltpu.VMEM(kernel_one.shape, BF16),
            pltpu.VMEM(kernel_two.shape, BF16),
            pltpu.SemaphoreType.DMA((2,)),
        ),
        cost=pl.CostEstimate(flops=10**8, bytes_accessed=10**7, transcendentals=0),
    )
    first, second, *weights = lax.optimization_barrier((first, second, *weights))
    first_far, second_far = exchanged(first, "split", 1), exchanged(second, "split", 1)

    tile_rows = 3 * -(-offsets // 4) * (outs + channels)
    half = up_to(tile_rows, 4 * regions * 8) // 4
    kept, sent = struct((half, LANES), F32), struct((half, LANES), BF16)
    output, *sums = call(
        main_kernel,
        (struct((outs, voxels), BF16), kept, kept, sent, sent),
        (position, neighbors, packed, partner, first, second, first_far, second_far, turned, *weights),
        scalars=2,
        scratch=(
            pltpu.VMEM((12, 24, 24, LANES), F32),
            pltpu.VMEM((10, 24, 24, wide), F32),
            pltpu.VMEM((10, 10, 24, LANES), F32),
            pltpu.VMEM((4 * half, LANES), F32),
            pltpu.VMEM((3, 2, 12, 96, LANES), BF16),
            pltpu.VMEM((3, 3, 12, 16, LANES), BF16),
            pltpu.VMEM((3, 2, 10, 80, LANES), BF16),
            pltpu.VMEM((3, 2, 10, 80, wide), BF16),
        ),
    )

    sums = [sums[part] + exchanged(sums[2 + part], "split", 1).astype(F32) for part in range(2)]
    bits = list(range((regions - 1).bit_length()))
    orders = [bits, bits[1::-1] + bits[2:]]

    for step in range(len(bits) - 1):
        for part, order in enumerate(orders):
            mask = 1 << order[step]
            keep, give = halves(sums[part], (region // mask) % 2)
            sums[part] = keep + exchanged(give.astype(BF16), "region", mask).astype(F32)
    for part, order in enumerate(orders):
        own = sums[part].astype(BF16)
        sums[part] = (own.astype(F32) + exchanged(own, "region", 1 << order[-1]).astype(F32)).astype(BF16)

    def joined(own, other, bit):
        return jnp.where(bit == 0, jnp.concatenate([own, other], 0), jnp.concatenate([other, own], 0))

    for step in reversed(range(len(bits) - 1)):
        for part, order in enumerate(orders):
            mask = 1 << order[step]
            sums[part] = joined(sums[part], exchanged(sums[part], "region", mask), (region // mask) % 2)
    ends = [value for own in sums for value in (own, exchanged(own, "split", 1))]
    grad_one, grad_two = call(
        unpack_kernel,
        (struct((offsets, channels, channels), F32), struct((offsets, channels, outs), F32)),
        (position, *ends),
        scalars=1,
        scratch=(pltpu.VMEM((4 * half, LANES), BF16),),
    )
    return output, grad_one, grad_two


def solution(mesh):
    rows = P(("region", "split"), None)
    columns = P(None, ("region", "split"))
    return jax.shard_map(
        shards,
        mesh=mesh,
        in_specs=(columns, P(), P(), rows, rows, columns),
        out_specs=(columns, P(), P()),
        check_vma=False,
    )
```

time: 79 us -> 72.2 us (0.914)
  starting transfers between devices: 37.6 us -> 27.7 us
  waiting for transfers between devices: 16.9 us -> 23.5 us
  local copies, waits for them, and re-layouts: 5.06 us -> 2.55 us
  Pallas kernels: 17.2 us -> 16.1 us
    ppermute x26 -> x21, starting transfers between devices: 34.4 us -> 24.4 us  [exchanged(): lax.ppermute(value, axis, [(i, i ^ mask) for i in range(lax.axis_size(axi...]
    ppermute x26 -> x21, waiting for transfers between devices: 14.8 us -> 23.5 us  [exchanged(): lax.ppermute(value, axis, [(i, i ^ mask) for i in range(lax.axis_size(axi...]
    unnamed x12, local copies, waits for them, and re-layouts: 4.92 us -> 2.42 us
    ppermute x1, waiting for transfers between devices: 2.03 us -> 0.01 us  [shards(): first = lax.ppermute(first, 'region', [(i, i ^ 1) for i in range(regions)])]
    pallas_call x4, Pallas kernels: 17.2 us -> 16.1 us  [call(): pl.pallas_call(kernel, out_shape=out_shape, in_specs=[pl.BlockSpec(memory...]
  transfers between devices with their start and end apart: 28 -> 23, of which waited for: 13 -> 15; matrix products, arithmetic and copies ran while one was open for 1% -> 1% of each run, Pallas kernels for 0% -> 1%
where the time goes in v4:
time: 72.2 us; the launch traced here: 71.9 us
  starting transfers between devices  27.7 us (38%)
  waiting for transfers between devices  23.5 us (33%)
  Pallas kernels  16.1 us (22%)
  local copies, waits for them, and re-layouts  2.55 us (4%)
  other arithmetic  1.33 us (2%)
  between operations  0.86 us (1%)
    ppermute x21, starting transfers between devices, exchanged(): lax.ppermute(value, axis, [(i, i ^ mask) for i in range(lax.axis_size(axi...  24.4 us
    ppermute x21, waiting for transfers between devices, exchanged(): lax.ppermute(value, axis, [(i, i ^ mask) for i in range(lax.axis_size(axi...  23.5 us
    pallas_call x4, Pallas kernels, call(): pl.pallas_call(kernel, out_shape=out_shape, in_specs=[pl.BlockSpec(memory...  16.1 us
    ppermute x1, starting transfers between devices, shards(): first = lax.ppermute(first, 'region', [(i, i ^ 1) for i in range(regions)])  2.56 us
    unnamed x12, local copies, waits for them, and re-layouts  2.42 us
  transfers between devices with their start and end apart: 23, of which 15 were waited for; matrix products, arithmetic and copies ran while one was open for 1% of the time, Pallas kernels for 1%

profile of v4, /device:TPU:0, one launch (start us, length us, event | category | flops | bytes accessed | tf_op | source)
XLA Modules:
  0.0 71.9 jit_solution(6325019244265536278)
XLA Ops:
  0.7 0.7 pad_add_fusion.position_ref
  1.3 2.7 %shard_map.85 = (bf16[512,384]{1,0:T(8,128)(2,1)}, bf16[128,256]{1,0:T(8,128)(2,1)}, bf16[128,256]{1,0:T(8,128)(2,1)}, bf16[192,512]{1,0:T(8,128)(2,1)}) custom-call(s32[2]{0:T(128)} %pad_add_fusion.position_ref, bf16[96,512]{1,0:T(8,128)(2,1)} %features_hbm.1, s32[1,512]{1,0:T(1,128)} %occupancy_hbm.1, bf16[192,512]{1,0:T(8,128)(2,1)} %cotangent_hbm.1), custom_call_target="tpu_custom_call" | custom-call | tf_op jit(solution)/shard_map/pallas_call | solution.py:248
  4.5 2.6 %collective-permute-start.1 = (bf16[128,256]{1,0:T(8,128)(2,1)}, bf16[128,256]{1,0:T(8,128)(2,1)S(1)}, u32[]{:S(2)}, u32[]{:S(2)}) collective-permute-start(bf16[128,256]{1,0:T(8,128)(2,1)} %get-tuple-element.21), channel_id=1, source_target_pairs={{0,2},{2,0},{4,6},{6,4},{8,10},{10,8},{12,14},{14,12},{16,18},{18,... | collective-permute-start | bytes 196616 | tf_op jit(solution)/shard_map/ppermute | solution.py:299
  7.1 0.7 collective-permute-start.2
  7.8 1.3 %copy-done = bf16[27,96,192]{2,1,0:T(8,128)(2,1)S(1)} copy-done((bf16[27,96,192]{2,1,0:T(8,128)(2,1)S(1)}, bf16[27,96,192]{2,1,0:T(8,128)(2,1)}, u32[]{:S(2)}) %copy-start) | copy-done | bytes 995352
  9.1 1.1 %copy-done.1 = bf16[27,96,96]{2,1,0:T(8,128)(2,1)S(1)} copy-done((bf16[27,96,96]{2,1,0:T(8,128)(2,1)S(1)}, bf16[27,96,96]{2,1,0:T(8,128)(2,1)}, u32[]{:S(2)}) %copy-start.1) | copy-done | bytes 497688
  10.2 0.7 shard_map.86
  11.5 0.7 %collective-permute-done.3.first_far_ref = bf16[128,256]{1,0:T(8,128)(2,1)S(1)} collective-permute-done((bf16[128,256]{1,0:T(8,128)(2,1)S(1)}, bf16[128,256]{1,0:T(8,128)(2,1)S(1)}, u32[]{:S(2)}, u32[]{:S(2)}) %collective-permute-start.3) | collective-permute-done | bytes 65568 | tf_op jit(solution)/shard_map/ppermute | solution.py:260
  12.4 9.2 %shard_map.87 = (bf16[192,512]{1,0:T(8,128)(2,1)}, f32[1536,128]{1,0:T(8,128)S(1)}, f32[1536,128]{1,0:T(8,128)S(1)}, bf16[1536,128]{1,0:T(8,128)(2,1)S(1)}, bf16[1536,128]{1,0:T(8,128)(2,1)S(1)}) custom-call(s32[2]{0:T(128)S(1)} %copy-done.4, s32[1,27]{1,0:T(1,128)S(1)} %copy-done.5, bf16[512,384]{1,0:T(8,128)(2,1)S(1)} %copy-done.2, ...), custom_call_target="tpu_custom_call" | custom-call | tf_op jit(solution)/shard_map/pallas_call | solution.py:248
  22.1 1.2 %collective-permute-done.14 = bf16[1536,128]{1,0:T(8,128)(2,1)S(1)} collective-permute-done((bf16[1536,128]{1,0:T(8,128)(2,1)S(1)}, bf16[1536,128]{1,0:T(8,128)(2,1)S(1)}, u32[]{:S(2)}, u32[]{:S(2)}) %collective-permute-start.14) | collective-permute-done | bytes 393248 | tf_op jit(solution)/shard_map/ppermute | solution.py:260
  23.4 5.0 %collective-permute-start.15 = (bf16[768,128]{1,0:T(8,128)(2,1)S(1)}, bf16[768,128]{1,0:T(8,128)(2,1)S(1)}, u32[]{:S(2)}, u32[]{:S(2)}) collective-permute-start(bf16[768,128]{1,0:T(8,128)(2,1)S(1)} %dynamic-slice_convert_fusion), channel_id=1, source_target_pairs={{0,4},{2,6},{4,0},{6,2},{8,12},{10,14},{12,8},{14,10},{16,20},{18,... | collective-permute-start | bytes 589832 | tf_op jit(solution)/shard_map/ppermute | solution.py:260
  28.5 1.5 %collective-permute-start.6 = (bf16[768,128]{1,0:T(8,128)(2,1)S(1)}, bf16[768,128]{1,0:T(8,128)(2,1)S(1)}, u32[]{:S(2)}, u32[]{:S(2)}) collective-permute-start(bf16[768,128]{1,0:T(8,128)(2,1)S(1)} %dynamic-slice_convert_fusion.1), channel_id=1, source_target_pairs={{0,2},{2,0},{4,6},{6,4},{8,10},{10,8},{12,14},{14,12},{16,18},{18,... | collective-permute-start | bytes 589832 | tf_op jit(solution)/shard_map/ppermute | solution.py:260
  30.0 3.8 %collective-permute-done.15 = bf16[768,128]{1,0:T(8,128)(2,1)S(1)} collective-permute-done((bf16[768,128]{1,0:T(8,128)(2,1)S(1)}, bf16[768,128]{1,0:T(8,128)(2,1)S(1)}, u32[]{:S(2)}, u32[]{:S(2)}) %collective-permute-start.15) | collective-permute-done | bytes 196640 | tf_op jit(solution)/shard_map/ppermute | solution.py:260
  33.9 1.5 %collective-permute-start.16 = (bf16[384,128]{1,0:T(8,128)(2,1)S(1)}, bf16[384,128]{1,0:T(8,128)(2,1)S(1)}, u32[]{:S(2)}, u32[]{:S(2)}) collective-permute-start(bf16[384,128]{1,0:T(8,128)(2,1)S(1)} %dynamic-slice_convert_fusion.2), channel_id=1, source_target_pairs={{0,2},{2,0},{4,6},{6,4},{8,10},{10,8},{12,14},{14,12},{16,18},{18,... | collective-permute-start | bytes 294920 | tf_op jit(solution)/shard_map/ppermute | solution.py:260
  35.5 1.7 %collective-permute-start.7 = (bf16[384,128]{1,0:T(8,128)(2,1)S(1)}, bf16[384,128]{1,0:T(8,128)(2,1)S(1)}, u32[]{:S(2)}, u32[]{:S(2)}) collective-permute-start(bf16[384,128]{1,0:T(8,128)(2,1)S(1)} %dynamic-slice_convert_fusion.3), channel_id=1, source_target_pairs={{0,4},{2,6},{4,0},{6,2},{8,12},{10,14},{12,8},{14,10},{16,20},{18,... | collective-permute-start | bytes 294920 | tf_op jit(solution)/shard_map/ppermute | solution.py:260
  37.2 1.3 %collective-permute-done.16 = bf16[384,128]{1,0:T(8,128)(2,1)S(1)} collective-permute-done((bf16[384,128]{1,0:T(8,128)(2,1)S(1)}, bf16[384,128]{1,0:T(8,128)(2,1)S(1)}, u32[]{:S(2)}, u32[]{:S(2)}) %collective-permute-start.16) | collective-permute-done | bytes 98336 | tf_op jit(solution)/shard_map/ppermute | solution.py:260
  38.6 2.8 %collective-permute-start.17 = (bf16[192,128]{1,0:T(8,128)(2,1)S(1)}, bf16[192,128]{1,0:T(8,128)(2,1)S(1)}, u32[]{:S(2)}, u32[]{:S(2)}) collective-permute-start(bf16[192,128]{1,0:T(8,128)(2,1)S(1)} %dynamic-slice_convert_fusion.4), channel_id=1, source_target_pairs={{0,8},{2,10},{4,12},{6,14},{8,0},{10,2},{12,4},{14,6},{16,24},{18,... | collective-permute-start | bytes 147464 | tf_op jit(solution)/shard_map/ppermute | solution.py:260
  41.9 1.5 %collective-permute-done.17 = bf16[192,128]{1,0:T(8,128)(2,1)S(1)} collective-permute-done((bf16[192,128]{1,0:T(8,128)(2,1)S(1)}, bf16[192,128]{1,0:T(8,128)(2,1)S(1)}, u32[]{:S(2)}, u32[]{:S(2)}) %collective-permute-start.17) | collective-permute-done | bytes 49184 | tf_op jit(solution)/shard_map/ppermute | solution.py:260
  43.4 3.3 %collective-permute-start.18 = (bf16[192,128]{1,0:T(8,128)(2,1)S(1)}, bf16[192,128]{1,0:T(8,128)(2,1)S(1)}, u32[]{:S(2)}, u32[]{:S(2)}) collective-permute-start(bf16[192,128]{1,0:T(8,128)(2,1)S(1)} %add_convert_fusion.1), channel_id=1, source_target_pairs={{0,16},{2,18},{4,20},{6,22},{8,24},{10,26},{12,28},{14,30},{16,0},... | collective-permute-start | bytes 147464 | tf_op jit(solution)/shard_map/ppermute | solution.py:260
  46.8 1.4 %collective-permute-start.9 = (bf16[192,128]{1,0:T(8,128)(2,1)S(1)}, bf16[192,128]{1,0:T(8,128)(2,1)S(1)}, u32[]{:S(2)}, u32[]{:S(2)}) collective-permute-start(bf16[192,128]{1,0:T(8,128)(2,1)S(1)} %add_convert_fusion.3), channel_id=1, source_target_pairs={{0,16},{2,18},{4,20},{6,22},{8,24},{10,26},{12,28},{14,30},{16,0},... | collective-permute-start | bytes 147464 | tf_op jit(solution)/shard_map/ppermute | solution.py:260
  48.2 0.9 %collective-permute-done.18 = bf16[192,128]{1,0:T(8,128)(2,1)S(1)} collective-permute-done((bf16[192,128]{1,0:T(8,128)(2,1)S(1)}, bf16[192,128]{1,0:T(8,128)(2,1)S(1)}, u32[]{:S(2)}, u32[]{:S(2)}) %collective-permute-start.18) | collective-permute-done | bytes 49184 | tf_op jit(solution)/shard_map/ppermute | solution.py:260
  49.1 1.5 %collective-permute-start.19 = (bf16[192,128]{1,0:T(8,128)(2,1)S(1)}, bf16[192,128]{1,0:T(8,128)(2,1)S(1)}, u32[]{:S(2)}, u32[]{:S(2)}) collective-permute-start(bf16[192,128]{1,0:T(8,128)(2,1)S(1)} %add_convert_fusion), channel_id=1, source_target_pairs={{0,8},{2,10},{4,12},{6,14},{8,0},{10,2},{12,4},{14,6},{16,24},{18,... | collective-permute-start | bytes 147464 | tf_op jit(solution)/shard_map/ppermute | solution.py:260
  50.6 1.3 %collective-permute-done.9 = bf16[192,128]{1,0:T(8,128)(2,1)S(1)} collective-permute-done((bf16[192,128]{1,0:T(8,128)(2,1)S(1)}, bf16[192,128]{1,0:T(8,128)(2,1)S(1)}, u32[]{:S(2)}, u32[]{:S(2)}) %collective-permute-start.9) | collective-permute-done | bytes 49184 | tf_op jit(solution)/shard_map/ppermute | solution.py:260
  51.9 1.4 %collective-permute-start.10 = (bf16[192,128]{1,0:T(8,128)(2,1)S(1)}, bf16[192,128]{1,0:T(8,128)(2,1)S(1)}, u32[]{:S(2)}, u32[]{:S(2)}) collective-permute-start(bf16[192,128]{1,0:T(8,128)(2,1)S(1)} %add_convert_fusion.2), channel_id=1, source_target_pairs={{0,8},{2,10},{4,12},{6,14},{8,0},{10,2},{12,4},{14,6},{16,24},{18,... | collective-permute-start | bytes 147464 | tf_op jit(solution)/shard_map/ppermute | solution.py:260
  54.0 2.1 %collective-permute-done.10 = bf16[192,128]{1,0:T(8,128)(2,1)S(1)} collective-permute-done((bf16[192,128]{1,0:T(8,128)(2,1)S(1)}, bf16[192,128]{1,0:T(8,128)(2,1)S(1)}, u32[]{:S(2)}, u32[]{:S(2)}) %collective-permute-start.10) | collective-permute-done | bytes 49184 | tf_op jit(solution)/shard_map/ppermute | solution.py:260
  56.5 2.5 %collective-permute-done.20 = bf16[384,128]{1,0:T(8,128)(2,1)S(1)} collective-permute-done((bf16[384,128]{1,0:T(8,128)(2,1)S(1)}, bf16[384,128]{1,0:T(8,128)(2,1)S(1)}, u32[]{:S(2)}, u32[]{:S(2)}) %collective-permute-start.20) | collective-permute-done | bytes 98336 | tf_op jit(solution)/shard_map/ppermute | solution.py:260
  59.1 0.7 collective-permute-start.21
  59.8 1.0 %collective-permute-done.11 = bf16[384,128]{1,0:T(8,128)(2,1)S(1)} collective-permute-done((bf16[384,128]{1,0:T(8,128)(2,1)S(1)}, bf16[384,128]{1,0:T(8,128)(2,1)S(1)}, u32[]{:S(2)}, u32[]{:S(2)}) %collective-permute-start.11) | collective-permute-done | bytes 98336 | tf_op jit(solution)/shard_map/ppermute | solution.py:260
  61.1 3.8 %collective-permute-done.21 = bf16[768,128]{1,0:T(8,128)(2,1)S(1)} collective-permute-done((bf16[768,128]{1,0:T(8,128)(2,1)S(1)}, bf16[768,128]{1,0:T(8,128)(2,1)S(1)}, u32[]{:S(2)}, u32[]{:S(2)}) %collective-permute-start.21) | collective-permute-done | bytes 196640 | tf_op jit(solution)/shard_map/ppermute | solution.py:260
  65.0 1.5 %collective-permute-done.12 = bf16[768,128]{1,0:T(8,128)(2,1)S(1)} collective-permute-done((bf16[768,128]{1,0:T(8,128)(2,1)S(1)}, bf16[768,128]{1,0:T(8,128)(2,1)S(1)}, u32[]{:S(2)}, u32[]{:S(2)}) %collective-permute-start.12) | collective-permute-done | bytes 196640 | tf_op jit(solution)/shard_map/ppermute | solution.py:260
  66.7 1.7 %collective-permute-done.13.other_p_ref = bf16[1536,128]{1,0:T(8,128)(2,1)S(1)} collective-permute-done((bf16[1536,128]{1,0:T(8,128)(2,1)S(1)}, bf16[1536,128]{1,0:T(8,128)(2,1)S(1)}, u32[]{:S(2)}, u32[]{:S(2)}) %collective-permute-start.13) | collective-permute-done | bytes 393248 | tf_op jit(solution)/shard_map/ppermute | solution.py:260
  68.4 3.5 %shard_map.88 = (f32[27,96,96]{2,1,0:T(8,128)}, f32[27,96,192]{2,1,0:T(8,128)}) custom-call(s32[2]{0:T(128)S(1)} %copy-done.4, bf16[1536,128]{1,0:T(8,128)(2,1)S(1)} %maximum_select_fusion.own_p_ref, bf16[1536,128]{1,0:T(8,128)(2,1)S(1)} %collective-permute-done.13.other_p_ref, bf16[1536,128]{1,0:T(8,128)(2,1)S(1)} %maximum_select_fusion.1.own_q_ref, ...), custom_call_target="tpu_custom_call" | custom-call | tf_op jit(solution)/shard_map/pallas_call | solution.py:248
  (53 shorter events, 4.7 us)
Async XLA Ops:
  0.6 11.8 %copy-start.5 = (s32[1,27]{1,0:T(1,128)S(1)}, s32[1,27]{1,0:T(1,128)}, u32[]{:S(2)}) copy-start(s32[1,27]{1,0:T(1,128)} %neighbors_ref.1) | copy-start | bytes 328
  1.3 11.1 %copy-start.4 = (s32[2]{0:T(128)S(1)}, s32[2]{0:T(128)}, u32[]{:S(2)}) copy-start(s32[2]{0:T(128)} %pad_add_fusion.position_ref) | copy-start | bytes 28
  4.0 8.4 %collective-permute-start = (bf16[512,384]{1,0:T(8,128)(2,1)}, bf16[512,384]{1,0:T(8,128)(2,1)S(1)}, u32[]{:S(2)}, u32[]{:S(2)}) collective-permute-start(bf16[512,384]{1,0:T(8,128)(2,1)} %get-tuple-element.20.own_ref), channel_id=1, source_target_pairs={{0,1},{1,0},{2,3},{3,2},{4,5},{5,4},{6,7},{7,6},{8,9},{9,8},{10,11... | collective-permute-start | bytes 1179656 | tf_op jit(solution)/shard_map/ppermute | solution.py:260
  4.5 6.3 %collective-permute-start.1 = (bf16[128,256]{1,0:T(8,128)(2,1)}, bf16[128,256]{1,0:T(8,128)(2,1)S(1)}, u32[]{:S(2)}, u32[]{:S(2)}) collective-permute-start(bf16[128,256]{1,0:T(8,128)(2,1)} %get-tuple-element.21), channel_id=1, source_target_pairs={{0,2},{2,0},{4,6},{6,4},{8,10},{10,8},{12,14},{14,12},{16,18},{18,... | collective-permute-start | bytes 196616 | tf_op jit(solution)/shard_map/ppermute | solution.py:299
  7.1 3.8 %collective-permute-start.2 = (bf16[128,256]{1,0:T(8,128)(2,1)}, bf16[128,256]{1,0:T(8,128)(2,1)S(1)}, u32[]{:S(2)}, u32[]{:S(2)}) collective-permute-start(bf16[128,256]{1,0:T(8,128)(2,1)} %get-tuple-element.22), channel_id=1, source_target_pairs={{2,4},{6,8},{10,12},{14,16},{18,20},{22,24},{26,28},{4,2},{8,6},{1... | collective-permute-start | bytes 196616 | tf_op jit(solution)/shard_map/ppermute | solution.py:298
  7.8 1.3 %copy-start = (bf16[27,96,192]{2,1,0:T(8,128)(2,1)S(1)}, bf16[27,96,192]{2,1,0:T(8,128)(2,1)}, u32[]{:S(2)}) copy-start(bf16[27,96,192]{2,1,0:T(8,128)(2,1)} %two_hbm.1) | copy-start | bytes 2985988
  9.1 1.1 %copy-start.1 = (bf16[27,96,96]{2,1,0:T(8,128)(2,1)S(1)}, bf16[27,96,96]{2,1,0:T(8,128)(2,1)}, u32[]{:S(2)}) copy-start(bf16[27,96,96]{2,1,0:T(8,128)(2,1)} %one_hbm.1) | copy-start | bytes 1492996
  10.2 2.2 %copy-start.2 = (bf16[512,384]{1,0:T(8,128)(2,1)S(1)}, bf16[512,384]{1,0:T(8,128)(2,1)}, u32[]{:S(2)}) copy-start(bf16[512,384]{1,0:T(8,128)(2,1)} %get-tuple-element.20.own_ref) | copy-start | bytes 1179652
  10.2 2.2 %copy-start.3 = (bf16[192,512]{1,0:T(8,128)(2,1)S(1)}, bf16[192,512]{1,0:T(8,128)(2,1)}, u32[]{:S(2)}) copy-start(bf16[192,512]{1,0:T(8,128)(2,1)} %get-tuple-element.27.turned_ref) | copy-start | bytes 589828
  10.9 1.3 %collective-permute-start.3 = (bf16[128,256]{1,0:T(8,128)(2,1)S(1)}, bf16[128,256]{1,0:T(8,128)(2,1)S(1)}, u32[]{:S(2)}, u32[]{:S(2)}) collective-permute-start(bf16[128,256]{1,0:T(8,128)(2,1)S(1)} %collective-permute-done.1.first_ref), channel_id=1, source_target_pairs={{0,1},{1,0},{2,3},{3,2},{4,5},{5,4},{6,7},{7,6},{8,9},{9,8},{10,11... | collective-permute-start | bytes 196616 | tf_op jit(solution)/shard_map/ppermute | solution.py:260
  11.1 1.3 %collective-permute-start.4 = (bf16[128,256]{1,0:T(8,128)(2,1)S(1)}, bf16[128,256]{1,0:T(8,128)(2,1)S(1)}, u32[]{:S(2)}, u32[]{:S(2)}) collective-permute-start(bf16[128,256]{1,0:T(8,128)(2,1)S(1)} %collective-permute-done.2.second_ref), channel_id=1, source_target_pairs={{0,1},{1,0},{2,3},{3,2},{4,5},{5,4},{6,7},{7,6},{8,9},{9,8},{10,11... | collective-permute-start | bytes 196616 | tf_op jit(solution)/shard_map/ppermute | solution.py:260
  21.6 1.7 %collective-permute-start.14 = (bf16[1536,128]{1,0:T(8,128)(2,1)S(1)}, bf16[1536,128]{1,0:T(8,128)(2,1)S(1)}, u32[]{:S(2)}, u32[]{:S(2)}) collective-permute-start(bf16[1536,128]{1,0:T(8,128)(2,1)S(1)} %get-tuple-element.34), channel_id=1, source_target_pairs={{0,1},{1,0},{2,3},{3,2},{4,5},{5,4},{6,7},{7,6},{8,9},{9,8},{10,11... | collective-permute-start | bytes 1179656 | tf_op jit(solution)/shard_map/ppermute | solution.py:260
  21.9 6.5 %collective-permute-start.5 = (bf16[1536,128]{1,0:T(8,128)(2,1)S(1)}, bf16[1536,128]{1,0:T(8,128)(2,1)S(1)}, u32[]{:S(2)}, u32[]{:S(2)}) collective-permute-start(bf16[1536,128]{1,0:T(8,128)(2,1)S(1)} %get-tuple-element.32), channel_id=1, source_target_pairs={{0,1},{1,0},{2,3},{3,2},{4,5},{5,4},{6,7},{7,6},{8,9},{9,8},{10,11... | collective-permute-start | bytes 1179656 | tf_op jit(solution)/shard_map/ppermute | solution.py:260
  23.4 10.4 %collective-permute-start.15 = (bf16[768,128]{1,0:T(8,128)(2,1)S(1)}, bf16[768,128]{1,0:T(8,128)(2,1)S(1)}, u32[]{:S(2)}, u32[]{:S(2)}) collective-permute-start(bf16[768,128]{1,0:T(8,128)(2,1)S(1)} %dynamic-slice_convert_fusion), channel_id=1, source_target_pairs={{0,4},{2,6},{4,0},{6,2},{8,12},{10,14},{12,8},{14,10},{16,20},{18,... | collective-permute-start | bytes 589832 | tf_op jit(solution)/shard_map/ppermute | solution.py:260
  28.5 6.9 %collective-permute-start.6 = (bf16[768,128]{1,0:T(8,128)(2,1)S(1)}, bf16[768,128]{1,0:T(8,128)(2,1)S(1)}, u32[]{:S(2)}, u32[]{:S(2)}) collective-permute-start(bf16[768,128]{1,0:T(8,128)(2,1)S(1)} %dynamic-slice_convert_fusion.1), channel_id=1, source_target_pairs={{0,2},{2,0},{4,6},{6,4},{8,10},{10,8},{12,14},{14,12},{16,18},{18,... | collective-permute-start | bytes 589832 | tf_op jit(solution)/shard_map/ppermute | solution.py:260
  33.9 4.7 %collective-permute-start.16 = (bf16[384,128]{1,0:T(8,128)(2,1)S(1)}, bf16[384,128]{1,0:T(8,128)(2,1)S(1)}, u32[]{:S(2)}, u32[]{:S(2)}) collective-permute-start(bf16[384,128]{1,0:T(8,128)(2,1)S(1)} %dynamic-slice_convert_fusion.2), channel_id=1, source_target_pairs={{0,2},{2,0},{4,6},{6,4},{8,10},{10,8},{12,14},{14,12},{16,18},{18,... | collective-permute-start | bytes 294920 | tf_op jit(solution)/shard_map/ppermute | solution.py:260
  35.5 5.9 %collective-permute-start.7 = (bf16[384,128]{1,0:T(8,128)(2,1)S(1)}, bf16[384,128]{1,0:T(8,128)(2,1)S(1)}, u32[]{:S(2)}, u32[]{:S(2)}) collective-permute-start(bf16[384,128]{1,0:T(8,128)(2,1)S(1)} %dynamic-slice_convert_fusion.3), channel_id=1, source_target_pairs={{0,4},{2,6},{4,0},{6,2},{8,12},{10,14},{12,8},{14,10},{16,20},{18,... | collective-permute-start | bytes 294920 | tf_op jit(solution)/shard_map/ppermute | solution.py:260
  38.6 4.8 %collective-permute-start.17 = (bf16[192,128]{1,0:T(8,128)(2,1)S(1)}, bf16[192,128]{1,0:T(8,128)(2,1)S(1)}, u32[]{:S(2)}, u32[]{:S(2)}) collective-permute-start(bf16[192,128]{1,0:T(8,128)(2,1)S(1)} %dynamic-slice_convert_fusion.4), channel_id=1, source_target_pairs={{0,8},{2,10},{4,12},{6,14},{8,0},{10,2},{12,4},{14,6},{16,24},{18,... | collective-permute-start | bytes 147464 | tf_op jit(solution)/shard_map/ppermute | solution.py:260
  41.4 5.4 %collective-permute-start.8 = (bf16[192,128]{1,0:T(8,128)(2,1)S(1)}, bf16[192,128]{1,0:T(8,128)(2,1)S(1)}, u32[]{:S(2)}, u32[]{:S(2)}) collective-permute-start(bf16[192,128]{1,0:T(8,128)(2,1)S(1)} %dynamic-slice_convert_fusion.5), channel_id=1, source_target_pairs={{0,8},{2,10},{4,12},{6,14},{8,0},{10,2},{12,4},{14,6},{16,24},{18,... | collective-permute-start | bytes 147464 | tf_op jit(solution)/shard_map/ppermute | solution.py:260
  43.4 5.7 %collective-permute-start.18 = (bf16[192,128]{1,0:T(8,128)(2,1)S(1)}, bf16[192,128]{1,0:T(8,128)(2,1)S(1)}, u32[]{:S(2)}, u32[]{:S(2)}) collective-permute-start(bf16[192,128]{1,0:T(8,128)(2,1)S(1)} %add_convert_fusion.1), channel_id=1, source_target_pairs={{0,16},{2,18},{4,20},{6,22},{8,24},{10,26},{12,28},{14,30},{16,0},... | collective-permute-start | bytes 147464 | tf_op jit(solution)/shard_map/ppermute | solution.py:260
  46.8 5.1 %collective-permute-start.9 = (bf16[192,128]{1,0:T(8,128)(2,1)S(1)}, bf16[192,128]{1,0:T(8,128)(2,1)S(1)}, u32[]{:S(2)}, u32[]{:S(2)}) collective-permute-start(bf16[192,128]{1,0:T(8,128)(2,1)S(1)} %add_convert_fusion.3), channel_id=1, source_target_pairs={{0,16},{2,18},{4,20},{6,22},{8,24},{10,26},{12,28},{14,30},{16,0},... | collective-permute-start | bytes 147464 | tf_op jit(solution)/shard_map/ppermute | solution.py:260
  49.1 4.2 %collective-permute-start.19 = (bf16[192,128]{1,0:T(8,128)(2,1)S(1)}, bf16[192,128]{1,0:T(8,128)(2,1)S(1)}, u32[]{:S(2)}, u32[]{:S(2)}) collective-permute-start(bf16[192,128]{1,0:T(8,128)(2,1)S(1)} %add_convert_fusion), channel_id=1, source_target_pairs={{0,8},{2,10},{4,12},{6,14},{8,0},{10,2},{12,4},{14,6},{16,24},{18,... | collective-permute-start | bytes 147464 | tf_op jit(solution)/shard_map/ppermute | solution.py:260
  51.9 4.2 %collective-permute-start.10 = (bf16[192,128]{1,0:T(8,128)(2,1)S(1)}, bf16[192,128]{1,0:T(8,128)(2,1)S(1)}, u32[]{:S(2)}, u32[]{:S(2)}) collective-permute-start(bf16[192,128]{1,0:T(8,128)(2,1)S(1)} %add_convert_fusion.2), channel_id=1, source_target_pairs={{0,8},{2,10},{4,12},{6,14},{8,0},{10,2},{12,4},{14,6},{16,24},{18,... | collective-permute-start | bytes 147464 | tf_op jit(solution)/shard_map/ppermute | solution.py:260
  53.3 5.7 %collective-permute-start.20 = (bf16[384,128]{1,0:T(8,128)(2,1)S(1)}, bf16[384,128]{1,0:T(8,128)(2,1)S(1)}, u32[]{:S(2)}, u32[]{:S(2)}) collective-permute-start(bf16[384,128]{1,0:T(8,128)(2,1)S(1)} %maximum_select_fusion.5), channel_id=1, source_target_pairs={{0,2},{2,0},{4,6},{6,4},{8,10},{10,8},{12,14},{14,12},{16,18},{18,... | collective-permute-start | bytes 294920 | tf_op jit(solution)/shard_map/ppermute | solution.py:260
  56.1 4.7 %collective-permute-start.11 = (bf16[384,128]{1,0:T(8,128)(2,1)S(1)}, bf16[384,128]{1,0:T(8,128)(2,1)S(1)}, u32[]{:S(2)}, u32[]{:S(2)}) collective-permute-start(bf16[384,128]{1,0:T(8,128)(2,1)S(1)} %maximum_select_fusion.4), channel_id=1, source_target_pairs={{0,4},{2,6},{4,0},{6,2},{8,12},{10,14},{12,8},{14,10},{16,20},{18,... | collective-permute-start | bytes 294920 | tf_op jit(solution)/shard_map/ppermute | solution.py:260
  59.1 5.7 %collective-permute-start.21 = (bf16[768,128]{1,0:T(8,128)(2,1)S(1)}, bf16[768,128]{1,0:T(8,128)(2,1)S(1)}, u32[]{:S(2)}, u32[]{:S(2)}) collective-permute-start(bf16[768,128]{1,0:T(8,128)(2,1)S(1)} %maximum_select_fusion.3), channel_id=1, source_target_pairs={{0,4},{2,6},{4,0},{6,2},{8,12},{10,14},{12,8},{14,10},{16,20},{18,... | collective-permute-start | bytes 589832 | tf_op jit(solution)/shard_map/ppermute | solution.py:260
  60.8 5.7 %collective-permute-start.12 = (bf16[768,128]{1,0:T(8,128)(2,1)S(1)}, bf16[768,128]{1,0:T(8,128)(2,1)S(1)}, u32[]{:S(2)}, u32[]{:S(2)}) collective-permute-start(bf16[768,128]{1,0:T(8,128)(2,1)S(1)} %maximum_select_fusion.2), channel_id=1, source_target_pairs={{0,2},{2,0},{4,6},{6,4},{8,10},{10,8},{12,14},{14,12},{16,18},{18,... | collective-permute-start | bytes 589832 | tf_op jit(solution)/shard_map/ppermute | solution.py:260
  64.9 1.8 %collective-permute-start.22 = (bf16[1536,128]{1,0:T(8,128)(2,1)S(1)}, bf16[1536,128]{1,0:T(8,128)(2,1)S(1)}, u32[]{:S(2)}, u32[]{:S(2)}) collective-permute-start(bf16[1536,128]{1,0:T(8,128)(2,1)S(1)} %maximum_select_fusion.1.own_q_ref), channel_id=1, source_target_pairs={{0,1},{1,0},{2,3},{3,2},{4,5},{5,4},{6,7},{7,6},{8,9},{9,8},{10,11... | collective-permute-start | bytes 1179656 | tf_op jit(solution)/shard_map/ppermute | solution.py:260
  66.6 1.8 %collective-permute-start.13 = (bf16[1536,128]{1,0:T(8,128)(2,1)S(1)}, bf16[1536,128]{1,0:T(8,128)(2,1)S(1)}, u32[]{:S(2)}, u32[]{:S(2)}) collective-permute-start(bf16[1536,128]{1,0:T(8,128)(2,1)S(1)} %maximum_select_fusion.own_p_ref), channel_id=1, source_target_pairs={{0,1},{1,0},{2,3},{3,2},{4,5},{5,4},{6,7},{7,6},{8,9},{9,8},{10,11... | collective-permute-start | bytes 1179656 | tf_op jit(solution)/shard_map/ppermute | solution.py:260

commit v5 on v4

v5 whole, which is shorter than its diff:
```python
import functools

import jax
import jax.numpy as jnp
from jax import lax
from jax.experimental import pallas as pl
from jax.experimental.pallas import tpu as pltpu
from jax.sharding import PartitionSpec as P

F32 = jnp.float32
BF16 = jnp.bfloat16
LANES = 128
VMEM_BYTES = 32 * 2**20


def up_to(value, step):
    return -(-value // step) * step


def store_planes(target_ref, rows, upper):
    row = pl.multiple_of(upper * 384, 128)
    near = pl.multiple_of(upper * 448, 64)
    target_ref[:, :LANES] = rows[pl.ds(row, 128), :LANES]
    target_ref[:64, LANES:] = rows[pl.ds(near, 64), LANES : 2 * LANES]
    target_ref[64:, LANES:] = rows[pl.ds(near, 64), 2 * LANES :]


def pack_kernel(stack_ref, packed_ref, first_ref, second_ref):
    packed_ref[...] = stack_ref[...].astype(F32).T.astype(BF16)
    odd = lax.axis_index("region") % 2
    store_planes(first_ref, packed_ref, 1 - odd)
    store_planes(second_ref, packed_ref, odd)


def store_turned(total_ref, product, offset, first_row, channels):
    rows = product.shape[0]
    spare = LANES - channels
    group, place = divmod(offset, 4)
    if place < 3:
        base = first_row + (3 * group + place) * rows
        total_ref[pl.ds(base, rows), :channels] = product[:, :channels]
    else:
        for piece in range(3):
            base = first_row + (3 * group + piece) * rows
            total_ref[pl.ds(base, rows), channels:] = product[:, piece * spare : (piece + 1) * spare]


TAPS = range(27)
CHUNKS = [TAPS[first : first + 6] for first in range(0, 27, 6)]


def offset_of(tap):
    return 9 * (tap % 3) + tap // 3


def staged(target, tap, count, more=0):
    code, dx = divmod(tap, 3)
    dy, dz = divmod(code, 3)
    row = 16 * ((dy + more) // 2)
    first = dx + more
    block = target[dz, (dy + more) % 2, first : first + count, row : row + 8 * count, :]
    return block.reshape(8 * count * count, target.shape[4])


def second_layer_kernel(occupancy_ref, hidden_s, two_ref, output_ref):
    outs = output_ref.shape[0]
    output = None
    for chunk in CHUNKS:
        rows = jnp.concatenate([staged(hidden_s, tap, 8) for tap in chunk], 1)
        kernel = jnp.concatenate([two_ref[offset_of(tap)] for tap in chunk], 0)[:, :outs]
        term = jnp.dot(rows, kernel, preferred_element_type=F32)
        output = term if output is None else output + term
    output_ref[...] = jnp.where(occupancy_ref[...] > 0, output.T, 0.0).astype(BF16)


def main_kernel(
    outs, neighbors_ref, own_ref, partner_ref, first_ref, second_ref, first_far_ref, second_far_ref,
    stack_ref, one_ref, two_ref, kept_p_ref, kept_q_ref, sent_p_ref, sent_q_ref, hidden_s,
    masked_w, grad_w, hidden_w, total, masked_s, plane_s, grad_s,
):
    odd, split = lax.axis_index("region") % 2, lax.axis_index("split")
    channels = one_ref.shape[2]
    wide = grad_w.shape[3]
    masked_w[:, 6:18] = jnp.zeros((12, 12, 24, LANES), F32)
    grad_w[:, 7:17] = jnp.zeros((10, 10, 24, wide), F32)

    own = own_ref[...].astype(F32).reshape(8, 8, 8, LANES + wide)
    masked_w[2:10, 8:16, 8:16, :] = own[..., :LANES]
    grad_w[1:9, 8:16, 8:16, :] = own[..., LANES:]

    def placed(step_x, step_z):
        found = [neighbors_ref[0, 9 * (step_x + 1) + 3 * step_y + step_z + 1] >= 0 for step_y in range(3)]
        y = jnp.where(found[0], 0, jnp.where(found[1], 1, 2))
        return found[0] | found[1] | found[2], pl.multiple_of(8 * y, 8)

    step_z = 1 - 2 * split
    valid, y = placed(0, step_z)
    z = pl.multiple_of(8 + 8 * step_z, 8)

    @pl.when(valid)
    def _():
        block = partner_ref[...].astype(F32).reshape(8, 8, 8, LANES + wide)
        masked_w[2:10, pl.ds(y, 8), pl.ds(z, 8), :] = block[..., :LANES]
        grad_w[1:9, pl.ds(y, 8), pl.ds(z, 8), :] = block[..., LANES:]

    for which, refs in enumerate(((first_ref, first_far_ref), (second_ref, second_far_ref))):
        step_x = 1 - 2 * odd if which == 0 else 2 * odd - 1
        for source, ref in enumerate(refs):
            step_z = 0 if source == 0 else 1 - 2 * split
            valid, y = placed(step_x, step_z)
            z = pl.multiple_of(8 + 8 * step_z, 8)
            x_masked = jnp.where(step_x > 0, 10, 0)
            x_grad = jnp.where(step_x > 0, 9, 0)

            @pl.when(valid)
            def _():
                block = ref[...].astype(F32)
                masked_w[pl.ds(x_masked, 2), pl.ds(y, 8), pl.ds(z, 8), :] = block[:, :LANES].reshape(2, 8, 8, LANES)
                near = jnp.concatenate([block[:64, LANES:], block[64:, LANES:]], 1)
                grad_w[pl.ds(x_grad, 1), pl.ds(y, 8), pl.ds(z, 8), :] = near.reshape(1, 8, 8, wide)

    def stage(target, source, first_x, first_y, first_z):
        count_x, rows = target.shape[2:4]
        lanes = target.shape[4]
        for dz in range(3):
            block = source[
                first_x : first_x + count_x, first_y : first_y + rows // 8, first_z + dz : first_z + dz + 8, :
            ]
            target[dz, 0] = block.reshape(count_x, rows, lanes).astype(BF16)
            target[dz, 1, :, : rows - 16] = block[:, 1 : rows // 8 - 1].reshape(count_x, rows - 16, lanes).astype(BF16)

    beside = 16 - 9 * split
    stage(masked_s, masked_w, 0, 6, 7)
    for dz in range(3):
        plane = masked_w[:, 6:24, pl.ds(beside - 1 + dz, 1), :].reshape(12, 18, LANES)
        for dy in range(3):
            plane_s[dz, dy] = plane[:, dy : dy + 16, :].astype(BF16)
        if dz == 1:
            plane_flag = plane[1:11, 1:17, channels : channels + 1].reshape(160, 1) > 0

    def plane_rows(tap):
        code, dx = divmod(tap, 3)
        dy, dz = divmod(code, 3)
        return plane_s[dz, dy, dx : dx + 10].reshape(160, LANES)

    hidden_pre = None
    for chunk in CHUNKS:
        rows = jnp.concatenate(
            [jnp.concatenate([staged(masked_s, tap, 10), plane_rows(tap)], 0) for tap in chunk], 1
        )
        kernel = jnp.concatenate([one_ref[offset_of(tap)] for tap in chunk], 0)
        term = jnp.dot(rows, kernel, preferred_element_type=F32)
        hidden_pre = term if hidden_pre is None else hidden_pre + term
    flags = masked_w[1:11, 7:17, 8:16, channels : channels + 1].reshape(800, 1) > 0
    hidden_pre = jnp.where(jnp.concatenate([flags, plane_flag], 0), hidden_pre, 0.0)
    hidden = hidden_pre * jax.nn.sigmoid(hidden_pre)
    hidden = jnp.concatenate([hidden, jnp.zeros((960, LANES - channels), F32)], 1)
    hidden_w[:, :, 8:16, :] = hidden[:800].reshape(10, 10, 8, LANES)
    hidden_w[:, :, 0:8, :] = jnp.zeros((10, 10, 8, LANES), F32)
    hidden_w[:, :, 16:24, :] = jnp.zeros((10, 10, 8, LANES), F32)
    hidden_w[:, :, pl.ds(beside, 1), :] = hidden[800:].reshape(10, 16, LANES)[:, :10].reshape(10, 10, 1, LANES)
    own_pre = hidden_pre[:800].reshape(10, 10, 8, channels)[1:9, 1:9].reshape(512, channels)
    own_flag = masked_w[2:10, 8:16, 8:16, channels : channels + 1].reshape(512, 1) > 0

    first_one = 3 * (-(-27 // 4)) * outs
    turned_out = stack_ref[LANES : LANES + outs, :]
    stage(hidden_s, hidden_w, 0, 0, 7)
    for chunk in CHUNKS:
        rows = jnp.concatenate([staged(hidden_s, tap, 8) for tap in chunk], 1)
        product = jnp.dot(turned_out, rows, preferred_element_type=F32)
        for place, tap in enumerate(chunk):
            store_turned(total, product[:, place * LANES : (place + 1) * LANES], offset_of(tap), 0, channels)

    stage(grad_s, grad_w, 0, 7, 7)
    back = None
    for chunk in CHUNKS:
        rows = jnp.concatenate([staged(grad_s, tap, 8) for tap in chunk], 1)
        kernel = jnp.concatenate([two_ref[26 - offset_of(tap)] for tap in chunk], 1)
        term = lax.dot_general(rows, kernel, (((1,), (1,)), ((), ())), preferred_element_type=F32)
        back = term if back is None else back + term
    back = back[:, :channels]
    gate = jax.nn.sigmoid(own_pre)
    grad_pre = jnp.where(own_flag, back * gate * (1.0 + own_pre * (1.0 - gate)), 0.0)
    turned_pre = grad_pre.T.astype(BF16)

    for chunk in CHUNKS:
        rows = jnp.concatenate([staged(masked_s, tap, 8, 1) for tap in chunk], 1)
        product = jnp.dot(turned_pre, rows, preferred_element_type=F32)
        for place, tap in enumerate(chunk):
            store_turned(
                total, product[:, place * LANES : (place + 1) * LANES], offset_of(tap), first_one, channels
            )

    half = kept_p_ref.shape[0]
    for start, kept_ref, sent_ref in ((0, kept_p_ref, sent_p_ref), (2 * half, kept_q_ref, sent_q_ref)):
        kept_ref[...] = total[pl.ds(pl.multiple_of(start + split * half, 16), half), :]
        sent_ref[...] = total[pl.ds(pl.multiple_of(start + (1 - split) * half, 16), half), :].astype(BF16)


def unpack_kernel(own_p_ref, other_p_ref, own_q_ref, other_q_ref, one_hbm, two_hbm, sums, one_ref, two_ref, sems):
    split = lax.axis_index("split")
    offsets, channels, outs = two_ref.shape
    half = own_p_ref.shape[0]
    for start, own_ref, other_ref in ((0, own_p_ref, other_p_ref), (2 * half, own_q_ref, other_q_ref)):
        sums[pl.ds(pl.multiple_of(start + split * half, 16), half), :] = own_ref[...]
        sums[pl.ds(pl.multiple_of(start + (1 - split) * half, 16), half), :] = other_ref[...]
    row = lax.broadcasted_iota(jnp.int32, (LANES, LANES), 0)
    unit = jnp.where(row == lax.broadcasted_iota(jnp.int32, (LANES, LANES), 1), 1.0, 0.0).astype(BF16)
    spare = LANES - channels
    fours = -(-offsets // 4)
    copies = []
    for ref, target, first, rows in ((two_ref, two_hbm, 0, outs), (one_ref, one_hbm, 3 * fours * outs, channels)):
        for group in range(fours):
            for place in range(3):
                part = sums[pl.ds(first + (3 * group + place) * rows, rows), :]
                part = lax.dot_general(unit, part, (((1,), (1,)), ((), ())), preferred_element_type=F32)
                ref[4 * group + place] = part[:channels]
                if 4 * group + 3 < offsets:
                    ref[4 * group + 3, place * spare : (place + 1) * spare, :] = part[channels:]
            done = pl.ds(4 * group, min(4, offsets - 4 * group))
            copies.append(pltpu.make_async_copy(ref.at[done], target.at[done], sems.at[len(copies)]))
            copies[-1].start()
    for copy in copies:
        copy.wait()


def call(kernel, out_shape, args, scalars=0, scratch=(), cost=None, into=pltpu.VMEM):
    spaces = [pltpu.SMEM] * scalars + [pltpu.VMEM] * (len(args) - scalars)
    return pl.pallas_call(
        kernel,
        out_shape=out_shape,
        in_specs=[pl.BlockSpec(memory_space=space) for space in spaces],
        out_specs=jax.tree.map(lambda _: pl.BlockSpec(memory_space=into), out_shape),
        scratch_shapes=list(scratch),
        compiler_params=pltpu.CompilerParams(vmem_limit_bytes=VMEM_BYTES),
        cost_estimate=cost,
    )(*args)


def exchanged(value, axis, mask):
    return lax.ppermute(value, axis, [(i, i ^ mask) for i in range(lax.axis_size(axis))])


def halves(value, bit):
    half = value.shape[0] // 2
    return (
        lax.dynamic_slice_in_dim(value, bit * half, half, 0),
        lax.dynamic_slice_in_dim(value, (1 - bit) * half, half, 0),
    )


def shards(features, kernel_one, kernel_two, occupancy, neighbors, cotangent):
    channels, voxels = features.shape
    offsets, _, outs = kernel_two.shape
    regions = lax.axis_size("region")
    region = lax.axis_index("region").astype(jnp.int32)
    split = lax.axis_index("split").astype(jnp.int32)
    wide = up_to(outs, LANES)
    struct = jax.ShapeDtypeStruct

    stack = jnp.concatenate(
        [
            features,
            jnp.ones((LANES - channels, voxels), BF16),
            cotangent,
            jnp.zeros((wide - outs, voxels), BF16),
        ],
        0,
    )
    stack = jnp.where(occupancy > 0, stack, jnp.zeros((), BF16))
    planes = struct((128, 2 * LANES), BF16)
    packed, first, second = call(pack_kernel, (struct((voxels, LANES + wide), BF16), planes, planes), (stack,))
    pairs = [(i, i + 1) for i in range(1, regions - 1, 2)]
    second = lax.ppermute(second, "region", pairs + [(b, a) for a, b in pairs])
    first = lax.ppermute(first, "region", [(i, i ^ 1) for i in range(regions)])
    partner = exchanged(packed, "split", 1)
    one = jnp.pad(kernel_one, ((0, 0), (0, LANES - channels), (0, 0)))
    two = jnp.pad(kernel_two, ((0, 0), (0, LANES - channels), (0, wide - outs)))
    first, second, one, two = lax.optimization_barrier((first, second, one, two))
    first_far, second_far = exchanged(first, "split", 1), exchanged(second, "split", 1)

    tile_rows = 3 * -(-offsets // 4) * (outs + channels)
    half = up_to(tile_rows, 4 * regions * 8) // 4
    kept, sent = struct((half, LANES), F32), struct((half, LANES), BF16)
    *sums, hidden = call(
        functools.partial(main_kernel, outs),
        (kept, kept, sent, sent, struct((3, 2, 10, 80, LANES), BF16)),
        (neighbors, packed, partner, first, second, first_far, second_far, stack, one, two),
        scalars=1,
        scratch=(
            pltpu.VMEM((12, 24, 24, LANES), F32),
            pltpu.VMEM((10, 24, 24, wide), F32),
            pltpu.VMEM((10, 10, 24, LANES), F32),
            pltpu.VMEM((4 * half, LANES), F32),
            pltpu.VMEM((3, 2, 12, 96, LANES), BF16),
            pltpu.VMEM((3, 3, 12, 16, LANES), BF16),
            pltpu.VMEM((3, 2, 10, 80, wide), BF16),
        ),
    )
    sums = [sums[part] + exchanged(sums[2 + part], "split", 1).astype(F32) for part in range(2)]
    sums[0], hidden = lax.optimization_barrier((sums[0], hidden))
    output = call(
        second_layer_kernel,
        struct((outs, voxels), BF16),
        (occupancy, hidden, two),
        cost=pl.CostEstimate(flops=2 * voxels * offsets * channels * outs, bytes_accessed=4 * 2**20, transcendentals=0),
    )
    bits = list(range((regions - 1).bit_length()))
    orders = [bits, bits[1::-1] + bits[2:]]

    for step in range(len(bits) - 1):
        pieces = []
        for part, order in enumerate(orders):
            mask = 1 << order[step]
            keep, give = halves(sums[part], (region // mask) % 2)
            pieces.append((keep, exchanged(give.astype(BF16), "region", mask)))
        if step == 0:
            pieces[0], output = lax.optimization_barrier((pieces[0], output))
        sums = [keep + came.astype(F32) for keep, came in pieces]
    for part, order in enumerate(orders):
        own = sums[part].astype(BF16)
        sums[part] = (own.astype(F32) + exchanged(own, "region", 1 << order[-1]).astype(F32)).astype(BF16)

    def joined(own, other, bit):
        return jnp.where(bit == 0, jnp.concatenate([own, other], 0), jnp.concatenate([other, own], 0))

    for step in reversed(range(len(bits) - 1)):
        for part, order in enumerate(orders):
            mask = 1 << order[step]
            sums[part] = joined(sums[part], exchanged(sums[part], "region", mask), (region // mask) % 2)
    ends = [value for own in sums for value in (own, exchanged(own, "split", 1))]
    grad_one, grad_two = call(
        unpack_kernel,
        (struct((offsets, channels, channels), F32), struct((offsets, channels, outs), F32)),
        ends,
        scratch=(
            pltpu.VMEM((4 * half, LANES), BF16),
            pltpu.VMEM((offsets, channels, channels), F32),
            pltpu.VMEM((offsets, channels, outs), F32),
            pltpu.SemaphoreType.DMA((2 * -(-offsets // 4),)),
        ),
        into=pltpu.HBM,
    )
    return output, grad_one, grad_two


def solution(mesh):
    rows = P(("region", "split"), None)
    columns = P(None, ("region", "split"))
    return jax.shard_map(
        shards,
        mesh=mesh,
        in_specs=(columns, P(), P(), rows, rows, columns),
        out_specs=(columns, P(), P()),
        check_vma=False,
    )
```

time: 72.2 us -> 75.8 us (1.050)
  other arithmetic: 1.33 us -> 3.92 us
  starting transfers between devices: 27.7 us -> 30 us
  waiting for transfers between devices: 23.5 us -> 21.9 us
    ppermute x21, waiting for transfers between devices: 23.5 us -> 20.4 us  [exchanged(): lax.ppermute(value, axis, [(i, i ^ mask) for i in range(lax.axis_size(axi...]
    ppermute x21, starting transfers between devices: 24.4 us -> 26.8 us  [exchanged(): lax.ppermute(value, axis, [(i, i ^ mask) for i in range(lax.axis_size(axi...]
    ppermute x1, waiting for transfers between devices: 0.01 us -> 1.47 us  [shards(): first = lax.ppermute(first, 'region', [(i, i ^ 1) for i in range(regions)])]
    add x2, other arithmetic: 0.13 us -> 1.36 us  [shards(): sums[part] + exchanged(sums[2 + part], 'split', 1).astype(F32)]
    select_n x0 -> x1, other arithmetic: none -> 1.16 us  [shards(): stack = jnp.where(occupancy > 0, stack, jnp.zeros((), BF16))]
    gt x0 -> x1, other arithmetic: none -> 0.84 us  [shards(): stack = jnp.where(occupancy > 0, stack, jnp.zeros((), BF16))]
    unnamed x12 -> x14, local copies, waits for them, and re-layouts: 2.42 us -> 1.78 us
  transfers between devices with their start and end apart: 23 -> 23, of which waited for: 15 -> 15; matrix products, arithmetic and copies ran while one was open for 1% -> 3% of each run, Pallas kernels for 1% -> 2%
where the time goes in v5:
time: 75.8 us; the launch traced here: 75.6 us
  starting transfers between devices  30 us (40%)
  waiting for transfers between devices  21.9 us (29%)
  Pallas kernels  16.3 us (22%)
  other arithmetic  3.92 us (5%)
  local copies, waits for them, and re-layouts  2.61 us (3%)
  between operations  0.88 us (1%)
    ppermute x21, starting transfers between devices, exchanged(): lax.ppermute(value, axis, [(i, i ^ mask) for i in range(lax.axis_size(axi...  26.8 us
    ppermute x21, waiting for transfers between devices, exchanged(): lax.ppermute(value, axis, [(i, i ^ mask) for i in range(lax.axis_size(axi...  20.4 us
    pallas_call x4, Pallas kernels, call(): pl.pallas_call(kernel, out_shape=out_shape, in_specs=[pl.BlockSpec(memory...  16.3 us
    ppermute x1, starting transfers between devices, shards(): first = lax.ppermute(first, 'region', [(i, i ^ 1) for i in range(regions)])  2.56 us
    unnamed x14, local copies, waits for them, and re-layouts  1.78 us
  transfers between devices with their start and end apart: 23, of which 15 were waited for; matrix products, arithmetic and copies ran while one was open for 3% of the time, Pallas kernels for 2%

profile of v5, /device:TPU:0, one launch (start us, length us, event | category | flops | bytes accessed | tf_op | source)
XLA Modules:
  0.0 75.6 jit_solution(12393815233712898996)
XLA Ops:
  0.7 0.8 %compare_reduce_fusion = pred[512]{0:T(512)(128)(4,1)S(1)} fusion(s32[1,512]{1,0:T(1,128)} %occupancy_ref.1), kind=kLoop, calls=%fused_computation.23 | loop fusion | flops 512 | bytes 2560 | tf_op jit(solution)/shard_map/gt | solution.py:270
  1.7 1.2 %maximum_select_fusion.stack_ref = bf16[384,512]{1,0:T(8,128)(2,1)S(1)} fusion(bf16[192,512]{1,0:T(8,128)(2,1)} %param.11, bf16[96,512]{1,0:T(8,128)(2,1)} %param.6, pred[512]{0:T(512)(128)(4,1)S(1)} %compare_reduce_fusion, bf16[384]{0:T(512)(128)(2,1)S(1)} %pad.37.clone, bf16[384]{0:T(512)(128)(2,1)S(1)} %pad.35.clone), kind=kLoop, calls=%fused_computation.2 | loop fusion | flops 1769472 | bytes 690176 | tf_op jit(solution)/shard_map/jit(_where)/select_n | solution.py:270
  3.6 2.6 %collective-permute-start.1 = (bf16[128,256]{1,0:T(8,128)(2,1)S(1)}, bf16[128,256]{1,0:T(8,128)(2,1)S(1)}, u32[]{:S(2)}, u32[]{:S(2)}) collective-permute-start(bf16[128,256]{1,0:T(8,128)(2,1)S(1)} %get-tuple-element.23), channel_id=1, source_target_pairs={{0,2},{2,0},{4,6},{6,4},{8,10},{10,8},{12,14},{14,12},{16,18},{18,... | collective-permute-start | bytes 196616 | tf_op jit(solution)/shard_map/ppermute | solution.py:275
  7.3 1.5 %collective-permute-done.1.first_ref = bf16[128,256]{1,0:T(8,128)(2,1)S(1)} collective-permute-done((bf16[128,256]{1,0:T(8,128)(2,1)S(1)}, bf16[128,256]{1,0:T(8,128)(2,1)S(1)}, u32[]{:S(2)}, u32[]{:S(2)}) %collective-permute-start.1) | collective-permute-done | bytes 65568 | tf_op jit(solution)/shard_map/ppermute | solution.py:275
  9.3 0.7 collective-permute-done.3.first_far_ref
  10.2 11.8 %shard_map.86 = (f32[1536,128]{1,0:T(8,128)S(1)}, f32[1536,128]{1,0:T(8,128)S(1)}, bf16[1536,128]{1,0:T(8,128)(2,1)}, bf16[1536,128]{1,0:T(8,128)(2,1)S(1)}, bf16[3,2,10,80,128]{4,3,2,1,0:T(8,128)(2,1)S(1)}) custom-call(s32[1,27]{1,0:T(1,128)S(1)} %copy-done.4, bf16[512,384]{1,0:T(8,128)(2,1)S(1)} %get-tuple-element.22.own_ref, ...), custom_call_target="tpu_custom_call" | custom-call | tf_op jit(solution)/shard_map/pallas_call | solution.py:229
  22.0 0.9 %copy-done = f32[1536,128]{1,0:T(8,128)} copy-done((f32[1536,128]{1,0:T(8,128)}, f32[1536,128]{1,0:T(8,128)S(1)}, u32[]{:S(2)}) %copy-start) | copy-done | bytes 786456
  22.9 0.9 %copy-done.2 = f32[1536,128]{1,0:T(8,128)} copy-done((f32[1536,128]{1,0:T(8,128)}, f32[1536,128]{1,0:T(8,128)S(1)}, u32[]{:S(2)}) %copy-start.2) | copy-done | bytes 786456
  24.3 1.6 %collective-permute-done.5 = bf16[1536,128]{1,0:T(8,128)(2,1)} collective-permute-done((bf16[1536,128]{1,0:T(8,128)(2,1)}, bf16[1536,128]{1,0:T(8,128)(2,1)}, u32[]{:S(2)}, u32[]{:S(2)}) %collective-permute-start.5) | collective-permute-done | bytes 393248 | tf_op jit(solution)/shard_map/ppermute | solution.py:241
  25.9 1.3 %convert_add_fusion.1 = f32[1536,128]{1,0:T(8,128)S(1)} fusion(f32[1536,128]{1,0:T(8,128)} %copy-done.2, bf16[1536,128]{1,0:T(8,128)(2,1)} %collective-permute-done.5), kind=kLoop, calls=%fused_computation.1 | loop fusion | flops 393216 | bytes 1966080 | tf_op jit(solution)/shard_map/add | solution.py:300
  27.2 4.7 %collective-permute-start.6 = (bf16[768,128]{1,0:T(8,128)(2,1)S(1)}, bf16[768,128]{1,0:T(8,128)(2,1)S(1)}, u32[]{:S(2)}, u32[]{:S(2)}) collective-permute-start(bf16[768,128]{1,0:T(8,128)(2,1)S(1)} %dynamic-slice_convert_fusion.1), channel_id=1, source_target_pairs={{0,2},{2,0},{4,6},{6,4},{8,10},{10,8},{12,14},{14,12},{16,18},{18,... | collective-permute-start | bytes 589832 | tf_op jit(solution)/shard_map/ppermute | solution.py:241
  32.0 2.8 %collective-permute-start.15 = (bf16[768,128]{1,0:T(8,128)(2,1)S(1)}, bf16[768,128]{1,0:T(8,128)(2,1)S(1)}, u32[]{:S(2)}, u32[]{:S(2)}) collective-permute-start(bf16[768,128]{1,0:T(8,128)(2,1)S(1)} %dynamic-slice_convert_fusion), channel_id=1, source_target_pairs={{0,4},{2,6},{4,0},{6,2},{8,12},{10,14},{12,8},{14,10},{16,20},{18,... | collective-permute-start | bytes 589832 | tf_op jit(solution)/shard_map/ppermute | solution.py:241
  34.8 1.9 %shard_map.87 = bf16[192,512]{1,0:T(8,128)(2,1)} custom-call(s32[1,512]{1,0:T(1,128)S(1)} %copy-done.3, bf16[3,2,10,80,128]{4,3,2,1,0:T(8,128)(2,1)S(1)} %get-tuple-element.33.hidden_s, bf16[27,128,256]{2,1,0:T(8,128)(2,1)S(1)} %pad.9.two_ref), custom_call_target="tpu_custom_call" | custom-call | flops 509607936 | bytes 4194304 | tf_op jit(solution)/shard_map/pallas_call | solution.py:229
  37.4 3.1 %collective-permute-start.7 = (bf16[384,128]{1,0:T(8,128)(2,1)S(1)}, bf16[384,128]{1,0:T(8,128)(2,1)S(1)}, u32[]{:S(2)}, u32[]{:S(2)}) collective-permute-start(bf16[384,128]{1,0:T(8,128)(2,1)S(1)} %dynamic-slice_convert_fusion.3), channel_id=1, source_target_pairs={{0,4},{2,6},{4,0},{6,2},{8,12},{10,14},{12,8},{14,10},{16,20},{18,... | collective-permute-start | bytes 294920 | tf_op jit(solution)/shard_map/ppermute | solution.py:241
  40.5 1.5 %collective-permute-start.16 = (bf16[384,128]{1,0:T(8,128)(2,1)S(1)}, bf16[384,128]{1,0:T(8,128)(2,1)S(1)}, u32[]{:S(2)}, u32[]{:S(2)}) collective-permute-start(bf16[384,128]{1,0:T(8,128)(2,1)S(1)} %dynamic-slice_convert_fusion.2), channel_id=1, source_target_pairs={{0,2},{2,0},{4,6},{6,4},{8,10},{10,8},{12,14},{14,12},{16,18},{18,... | collective-permute-start | bytes 294920 | tf_op jit(solution)/shard_map/ppermute | solution.py:241
  42.0 1.0 %collective-permute-done.7 = bf16[384,128]{1,0:T(8,128)(2,1)S(1)} collective-permute-done((bf16[384,128]{1,0:T(8,128)(2,1)S(1)}, bf16[384,128]{1,0:T(8,128)(2,1)S(1)}, u32[]{:S(2)}, u32[]{:S(2)}) %collective-permute-start.7) | collective-permute-done | bytes 98336 | tf_op jit(solution)/shard_map/ppermute | solution.py:241
  43.1 3.0 %collective-permute-start.8 = (bf16[192,128]{1,0:T(8,128)(2,1)S(1)}, bf16[192,128]{1,0:T(8,128)(2,1)S(1)}, u32[]{:S(2)}, u32[]{:S(2)}) collective-permute-start(bf16[192,128]{1,0:T(8,128)(2,1)S(1)} %dynamic-slice_convert_fusion.5), channel_id=1, source_target_pairs={{0,8},{2,10},{4,12},{6,14},{8,0},{10,2},{12,4},{14,6},{16,24},{18,... | collective-permute-start | bytes 147464 | tf_op jit(solution)/shard_map/ppermute | solution.py:241
  46.9 1.3 %collective-permute-done.8 = bf16[192,128]{1,0:T(8,128)(2,1)S(1)} collective-permute-done((bf16[192,128]{1,0:T(8,128)(2,1)S(1)}, bf16[192,128]{1,0:T(8,128)(2,1)S(1)}, u32[]{:S(2)}, u32[]{:S(2)}) %collective-permute-start.8) | collective-permute-done | bytes 49184 | tf_op jit(solution)/shard_map/ppermute | solution.py:241
  48.2 3.3 %collective-permute-start.9 = (bf16[192,128]{1,0:T(8,128)(2,1)S(1)}, bf16[192,128]{1,0:T(8,128)(2,1)S(1)}, u32[]{:S(2)}, u32[]{:S(2)}) collective-permute-start(bf16[192,128]{1,0:T(8,128)(2,1)S(1)} %add_convert_fusion.3), channel_id=1, source_target_pairs={{0,16},{2,18},{4,20},{6,22},{8,24},{10,26},{12,28},{14,30},{16,0},... | collective-permute-start | bytes 147464 | tf_op jit(solution)/shard_map/ppermute | solution.py:241
  51.6 1.5 %collective-permute-start.18 = (bf16[192,128]{1,0:T(8,128)(2,1)S(1)}, bf16[192,128]{1,0:T(8,128)(2,1)S(1)}, u32[]{:S(2)}, u32[]{:S(2)}) collective-permute-start(bf16[192,128]{1,0:T(8,128)(2,1)S(1)} %add_convert_fusion.1), channel_id=1, source_target_pairs={{0,16},{2,18},{4,20},{6,22},{8,24},{10,26},{12,28},{14,30},{16,0},... | collective-permute-start | bytes 147464 | tf_op jit(solution)/shard_map/ppermute | solution.py:241
  53.0 0.9 %collective-permute-done.9 = bf16[192,128]{1,0:T(8,128)(2,1)S(1)} collective-permute-done((bf16[192,128]{1,0:T(8,128)(2,1)S(1)}, bf16[192,128]{1,0:T(8,128)(2,1)S(1)}, u32[]{:S(2)}, u32[]{:S(2)}) %collective-permute-start.9) | collective-permute-done | bytes 49184 | tf_op jit(solution)/shard_map/ppermute | solution.py:241
  53.9 1.5 %collective-permute-start.10 = (bf16[192,128]{1,0:T(8,128)(2,1)S(1)}, bf16[192,128]{1,0:T(8,128)(2,1)S(1)}, u32[]{:S(2)}, u32[]{:S(2)}) collective-permute-start(bf16[192,128]{1,0:T(8,128)(2,1)S(1)} %add_convert_fusion.2), channel_id=1, source_target_pairs={{0,8},{2,10},{4,12},{6,14},{8,0},{10,2},{12,4},{14,6},{16,24},{18,... | collective-permute-start | bytes 147464 | tf_op jit(solution)/shard_map/ppermute | solution.py:241
  55.4 1.2 %collective-permute-done.18 = bf16[192,128]{1,0:T(8,128)(2,1)S(1)} collective-permute-done((bf16[192,128]{1,0:T(8,128)(2,1)S(1)}, bf16[192,128]{1,0:T(8,128)(2,1)S(1)}, u32[]{:S(2)}, u32[]{:S(2)}) %collective-permute-start.18) | collective-permute-done | bytes 49184 | tf_op jit(solution)/shard_map/ppermute | solution.py:241
  56.6 1.4 %collective-permute-start.19 = (bf16[192,128]{1,0:T(8,128)(2,1)S(1)}, bf16[192,128]{1,0:T(8,128)(2,1)S(1)}, u32[]{:S(2)}, u32[]{:S(2)}) collective-permute-start(bf16[192,128]{1,0:T(8,128)(2,1)S(1)} %add_convert_fusion), channel_id=1, source_target_pairs={{0,8},{2,10},{4,12},{6,14},{8,0},{10,2},{12,4},{14,6},{16,24},{18,... | collective-permute-start | bytes 147464 | tf_op jit(solution)/shard_map/ppermute | solution.py:241
  58.1 0.9 %collective-permute-start.11 = (bf16[384,128]{1,0:T(8,128)(2,1)S(1)}, bf16[384,128]{1,0:T(8,128)(2,1)S(1)}, u32[]{:S(2)}, u32[]{:S(2)}) collective-permute-start(bf16[384,128]{1,0:T(8,128)(2,1)S(1)} %maximum_select_fusion.5), channel_id=1, source_target_pairs={{0,4},{2,6},{4,0},{6,2},{8,12},{10,14},{12,8},{14,10},{16,20},{18,... | collective-permute-start | bytes 294920 | tf_op jit(solution)/shard_map/ppermute | solution.py:241
  59.0 1.8 %collective-permute-done.19 = bf16[192,128]{1,0:T(8,128)(2,1)S(1)} collective-permute-done((bf16[192,128]{1,0:T(8,128)(2,1)S(1)}, bf16[192,128]{1,0:T(8,128)(2,1)S(1)}, u32[]{:S(2)}, u32[]{:S(2)}) %collective-permute-start.19) | collective-permute-done | bytes 49184 | tf_op jit(solution)/shard_map/ppermute | solution.py:241
  61.1 2.8 %collective-permute-done.11 = bf16[384,128]{1,0:T(8,128)(2,1)S(1)} collective-permute-done((bf16[384,128]{1,0:T(8,128)(2,1)S(1)}, bf16[384,128]{1,0:T(8,128)(2,1)S(1)}, u32[]{:S(2)}, u32[]{:S(2)}) %collective-permute-start.11) | collective-permute-done | bytes 98336 | tf_op jit(solution)/shard_map/ppermute | solution.py:241
  64.0 1.5 %collective-permute-done.20 = bf16[384,128]{1,0:T(8,128)(2,1)S(1)} collective-permute-done((bf16[384,128]{1,0:T(8,128)(2,1)S(1)}, bf16[384,128]{1,0:T(8,128)(2,1)S(1)}, u32[]{:S(2)}, u32[]{:S(2)}) %collective-permute-start.20) | collective-permute-done | bytes 98336 | tf_op jit(solution)/shard_map/ppermute | solution.py:241
  66.0 3.6 %collective-permute-done.12 = bf16[768,128]{1,0:T(8,128)(2,1)S(1)} collective-permute-done((bf16[768,128]{1,0:T(8,128)(2,1)S(1)}, bf16[768,128]{1,0:T(8,128)(2,1)S(1)}, u32[]{:S(2)}, u32[]{:S(2)}) %collective-permute-start.12) | collective-permute-done | bytes 196640 | tf_op jit(solution)/shard_map/ppermute | solution.py:241
  69.8 1.5 %collective-permute-done.21 = bf16[768,128]{1,0:T(8,128)(2,1)S(1)} collective-permute-done((bf16[768,128]{1,0:T(8,128)(2,1)S(1)}, bf16[768,128]{1,0:T(8,128)(2,1)S(1)}, u32[]{:S(2)}, u32[]{:S(2)}) %collective-permute-start.21) | collective-permute-done | bytes 196640 | tf_op jit(solution)/shard_map/ppermute | solution.py:241
  71.5 1.7 %collective-permute-done.22.other_q_ref = bf16[1536,128]{1,0:T(8,128)(2,1)S(1)} collective-permute-done((bf16[1536,128]{1,0:T(8,128)(2,1)S(1)}, bf16[1536,128]{1,0:T(8,128)(2,1)S(1)}, u32[]{:S(2)}, u32[]{:S(2)}) %collective-permute-start.22) | collective-permute-done | bytes 393248 | tf_op jit(solution)/shard_map/ppermute | solution.py:241
  73.2 2.4 %shard_map.88 = (f32[27,96,96]{2,1,0:T(8,128)}, f32[27,96,192]{2,1,0:T(8,128)}) custom-call(bf16[1536,128]{1,0:T(8,128)(2,1)S(1)} %maximum_select_fusion.1.own_p_ref, bf16[1536,128]{1,0:T(8,128)(2,1)S(1)} %collective-permute-done.13.other_p_ref, bf16[1536,128]{1,0:T(8,128)(2,1)S(1)} %maximum_select_fusion.2.own_q_ref, ...), custom_call_target="tpu_custom_call" | custom-call | tf_op jit(solution)/shard_map/pallas_call | solution.py:229
  (63 shorter events, 6.4 us)
Async XLA Ops:
  0.6 6.2 %copy-start.6 = (bf16[27,96,96]{2,1,0:T(8,128)(2,1)S(1)}, bf16[27,96,96]{2,1,0:T(8,128)(2,1)}, u32[]{:S(2)}) copy-start(bf16[27,96,96]{2,1,0:T(8,128)(2,1)} %param.7) | copy-start | bytes 1492996
  0.6 6.4 %copy-start.5 = (bf16[27,96,192]{2,1,0:T(8,128)(2,1)S(1)}, bf16[27,96,192]{2,1,0:T(8,128)(2,1)}, u32[]{:S(2)}) copy-start(bf16[27,96,192]{2,1,0:T(8,128)(2,1)} %param.8) | copy-start | bytes 2985988
  3.0 7.2 %collective-permute-start = (bf16[512,384]{1,0:T(8,128)(2,1)S(1)}, bf16[512,384]{1,0:T(8,128)(2,1)S(1)}, u32[]{:S(2)}, u32[]{:S(2)}) collective-permute-start(bf16[512,384]{1,0:T(8,128)(2,1)S(1)} %get-tuple-element.22.own_ref), channel_id=1, source_target_pairs={{0,1},{1,0},{2,3},{3,2},{4,5},{5,4},{6,7},{7,6},{8,9},{9,8},{10,11... | collective-permute-start | bytes 1179656 | tf_op jit(solution)/shard_map/ppermute | solution.py:241
  3.6 5.2 %collective-permute-start.1 = (bf16[128,256]{1,0:T(8,128)(2,1)S(1)}, bf16[128,256]{1,0:T(8,128)(2,1)S(1)}, u32[]{:S(2)}, u32[]{:S(2)}) collective-permute-start(bf16[128,256]{1,0:T(8,128)(2,1)S(1)} %get-tuple-element.23), channel_id=1, source_target_pairs={{0,2},{2,0},{4,6},{6,4},{8,10},{10,8},{12,14},{14,12},{16,18},{18,... | collective-permute-start | bytes 196616 | tf_op jit(solution)/shard_map/ppermute | solution.py:275
  6.1 2.7 %collective-permute-start.2 = (bf16[128,256]{1,0:T(8,128)(2,1)S(1)}, bf16[128,256]{1,0:T(8,128)(2,1)S(1)}, u32[]{:S(2)}, u32[]{:S(2)}) collective-permute-start(bf16[128,256]{1,0:T(8,128)(2,1)S(1)} %get-tuple-element.24), channel_id=1, source_target_pairs={{2,4},{6,8},{10,12},{14,16},{18,20},{22,24},{26,28},{4,2},{8,6},{1... | collective-permute-start | bytes 196616 | tf_op jit(solution)/shard_map/ppermute | solution.py:274
  7.0 3.2 %copy-start.4 = (s32[1,27]{1,0:T(1,128)S(1)}, s32[1,27]{1,0:T(1,128)}, u32[]{:S(2)}) copy-start(s32[1,27]{1,0:T(1,128)} %neighbors_ref.1) | copy-start | bytes 328
  8.8 1.3 %collective-permute-start.3 = (bf16[128,256]{1,0:T(8,128)(2,1)S(1)}, bf16[128,256]{1,0:T(8,128)(2,1)S(1)}, u32[]{:S(2)}, u32[]{:S(2)}) collective-permute-start(bf16[128,256]{1,0:T(8,128)(2,1)S(1)} %collective-permute-done.1.first_ref), channel_id=1, source_target_pairs={{0,1},{1,0},{2,3},{3,2},{4,5},{5,4},{6,7},{7,6},{8,9},{9,8},{10,11... | collective-permute-start | bytes 196616 | tf_op jit(solution)/shard_map/ppermute | solution.py:241
  8.8 1.4 %collective-permute-start.4 = (bf16[128,256]{1,0:T(8,128)(2,1)S(1)}, bf16[128,256]{1,0:T(8,128)(2,1)S(1)}, u32[]{:S(2)}, u32[]{:S(2)}) collective-permute-start(bf16[128,256]{1,0:T(8,128)(2,1)S(1)} %collective-permute-done.2.second_ref), channel_id=1, source_target_pairs={{0,1},{1,0},{2,3},{3,2},{4,5},{5,4},{6,7},{7,6},{8,9},{9,8},{10,11... | collective-permute-start | bytes 196616 | tf_op jit(solution)/shard_map/ppermute | solution.py:241
  22.0 0.9 %copy-start = (f32[1536,128]{1,0:T(8,128)}, f32[1536,128]{1,0:T(8,128)S(1)}, u32[]{:S(2)}) copy-start(f32[1536,128]{1,0:T(8,128)S(1)} %get-tuple-element.37) | copy-start | bytes 2359300
  22.9 0.9 %copy-start.2 = (f32[1536,128]{1,0:T(8,128)}, f32[1536,128]{1,0:T(8,128)S(1)}, u32[]{:S(2)}) copy-start(f32[1536,128]{1,0:T(8,128)S(1)} %get-tuple-element.29) | copy-start | bytes 2359300
  23.8 2.1 %collective-permute-start.5 = (bf16[1536,128]{1,0:T(8,128)(2,1)}, bf16[1536,128]{1,0:T(8,128)(2,1)}, u32[]{:S(2)}, u32[]{:S(2)}) collective-permute-start(bf16[1536,128]{1,0:T(8,128)(2,1)} %get-tuple-element.30), channel_id=1, source_target_pairs={{0,1},{1,0},{2,3},{3,2},{4,5},{5,4},{6,7},{7,6},{8,9},{9,8},{10,11... | collective-permute-start | bytes 1179656 | tf_op jit(solution)/shard_map/ppermute | solution.py:241
  24.1 7.8 %copy-start.1 = (f32[1536,128]{1,0:T(8,128)S(1)}, f32[1536,128]{1,0:T(8,128)}, u32[]{:S(2)}) copy-start(f32[1536,128]{1,0:T(8,128)} %copy-done) | copy-start | bytes 2359300
  24.1 7.8 %collective-permute-start.14 = (bf16[1536,128]{1,0:T(8,128)(2,1)S(1)}, bf16[1536,128]{1,0:T(8,128)(2,1)S(1)}, u32[]{:S(2)}, u32[]{:S(2)}) collective-permute-start(bf16[1536,128]{1,0:T(8,128)(2,1)S(1)} %get-tuple-element.38), channel_id=1, source_target_pairs={{0,1},{1,0},{2,3},{3,2},{4,5},{5,4},{6,7},{7,6},{8,9},{9,8},{10,11... | collective-permute-start | bytes 1179656 | tf_op jit(solution)/shard_map/ppermute | solution.py:241
  27.2 7.6 %copy-start.3 = (s32[1,512]{1,0:T(1,128)S(1)}, s32[1,512]{1,0:T(1,128)}, u32[]{:S(2)}) copy-start(s32[1,512]{1,0:T(1,128)} %occupancy_ref.1) | copy-start | bytes 6148
  27.2 10.1 %collective-permute-start.6 = (bf16[768,128]{1,0:T(8,128)(2,1)S(1)}, bf16[768,128]{1,0:T(8,128)(2,1)S(1)}, u32[]{:S(2)}, u32[]{:S(2)}) collective-permute-start(bf16[768,128]{1,0:T(8,128)(2,1)S(1)} %dynamic-slice_convert_fusion.1), channel_id=1, source_target_pairs={{0,2},{2,0},{4,6},{6,4},{8,10},{10,8},{12,14},{14,12},{16,18},{18,... | collective-permute-start | bytes 589832 | tf_op jit(solution)/shard_map/ppermute | solution.py:241
  32.0 8.4 %collective-permute-start.15 = (bf16[768,128]{1,0:T(8,128)(2,1)S(1)}, bf16[768,128]{1,0:T(8,128)(2,1)S(1)}, u32[]{:S(2)}, u32[]{:S(2)}) collective-permute-start(bf16[768,128]{1,0:T(8,128)(2,1)S(1)} %dynamic-slice_convert_fusion), channel_id=1, source_target_pairs={{0,4},{2,6},{4,0},{6,2},{8,12},{10,14},{12,8},{14,10},{16,20},{18,... | collective-permute-start | bytes 589832 | tf_op jit(solution)/shard_map/ppermute | solution.py:241
  37.4 5.7 %collective-permute-start.7 = (bf16[384,128]{1,0:T(8,128)(2,1)S(1)}, bf16[384,128]{1,0:T(8,128)(2,1)S(1)}, u32[]{:S(2)}, u32[]{:S(2)}) collective-permute-start(bf16[384,128]{1,0:T(8,128)(2,1)S(1)} %dynamic-slice_convert_fusion.3), channel_id=1, source_target_pairs={{0,4},{2,6},{4,0},{6,2},{8,12},{10,14},{12,8},{14,10},{16,20},{18,... | collective-permute-start | bytes 294920 | tf_op jit(solution)/shard_map/ppermute | solution.py:241
  40.5 5.6 %collective-permute-start.16 = (bf16[384,128]{1,0:T(8,128)(2,1)S(1)}, bf16[384,128]{1,0:T(8,128)(2,1)S(1)}, u32[]{:S(2)}, u32[]{:S(2)}) collective-permute-start(bf16[384,128]{1,0:T(8,128)(2,1)S(1)} %dynamic-slice_convert_fusion.2), channel_id=1, source_target_pairs={{0,2},{2,0},{4,6},{6,4},{8,10},{10,8},{12,14},{14,12},{16,18},{18,... | collective-permute-start | bytes 294920 | tf_op jit(solution)/shard_map/ppermute | solution.py:241
  43.1 5.1 %collective-permute-start.8 = (bf16[192,128]{1,0:T(8,128)(2,1)S(1)}, bf16[192,128]{1,0:T(8,128)(2,1)S(1)}, u32[]{:S(2)}, u32[]{:S(2)}) collective-permute-start(bf16[192,128]{1,0:T(8,128)(2,1)S(1)} %dynamic-slice_convert_fusion.5), channel_id=1, source_target_pairs={{0,8},{2,10},{4,12},{6,14},{8,0},{10,2},{12,4},{14,6},{16,24},{18,... | collective-permute-start | bytes 147464 | tf_op jit(solution)/shard_map/ppermute | solution.py:241
  46.2 5.4 %collective-permute-start.17 = (bf16[192,128]{1,0:T(8,128)(2,1)S(1)}, bf16[192,128]{1,0:T(8,128)(2,1)S(1)}, u32[]{:S(2)}, u32[]{:S(2)}) collective-permute-start(bf16[192,128]{1,0:T(8,128)(2,1)S(1)} %dynamic-slice_convert_fusion.4), channel_id=1, source_target_pairs={{0,8},{2,10},{4,12},{6,14},{8,0},{10,2},{12,4},{14,6},{16,24},{18,... | collective-permute-start | bytes 147464 | tf_op jit(solution)/shard_map/ppermute | solution.py:241
  48.2 5.7 %collective-permute-start.9 = (bf16[192,128]{1,0:T(8,128)(2,1)S(1)}, bf16[192,128]{1,0:T(8,128)(2,1)S(1)}, u32[]{:S(2)}, u32[]{:S(2)}) collective-permute-start(bf16[192,128]{1,0:T(8,128)(2,1)S(1)} %add_convert_fusion.3), channel_id=1, source_target_pairs={{0,16},{2,18},{4,20},{6,22},{8,24},{10,26},{12,28},{14,30},{16,0},... | collective-permute-start | bytes 147464 | tf_op jit(solution)/shard_map/ppermute | solution.py:241
  51.6 5.1 %collective-permute-start.18 = (bf16[192,128]{1,0:T(8,128)(2,1)S(1)}, bf16[192,128]{1,0:T(8,128)(2,1)S(1)}, u32[]{:S(2)}, u32[]{:S(2)}) collective-permute-start(bf16[192,128]{1,0:T(8,128)(2,1)S(1)} %add_convert_fusion.1), channel_id=1, source_target_pairs={{0,16},{2,18},{4,20},{6,22},{8,24},{10,26},{12,28},{14,30},{16,0},... | collective-permute-start | bytes 147464 | tf_op jit(solution)/shard_map/ppermute | solution.py:241
  53.9 4.2 %collective-permute-start.10 = (bf16[192,128]{1,0:T(8,128)(2,1)S(1)}, bf16[192,128]{1,0:T(8,128)(2,1)S(1)}, u32[]{:S(2)}, u32[]{:S(2)}) collective-permute-start(bf16[192,128]{1,0:T(8,128)(2,1)S(1)} %add_convert_fusion.2), channel_id=1, source_target_pairs={{0,8},{2,10},{4,12},{6,14},{8,0},{10,2},{12,4},{14,6},{16,24},{18,... | collective-permute-start | bytes 147464 | tf_op jit(solution)/shard_map/ppermute | solution.py:241
  56.6 4.2 %collective-permute-start.19 = (bf16[192,128]{1,0:T(8,128)(2,1)S(1)}, bf16[192,128]{1,0:T(8,128)(2,1)S(1)}, u32[]{:S(2)}, u32[]{:S(2)}) collective-permute-start(bf16[192,128]{1,0:T(8,128)(2,1)S(1)} %add_convert_fusion), channel_id=1, source_target_pairs={{0,8},{2,10},{4,12},{6,14},{8,0},{10,2},{12,4},{14,6},{16,24},{18,... | collective-permute-start | bytes 147464 | tf_op jit(solution)/shard_map/ppermute | solution.py:241
  58.1 5.7 %collective-permute-start.11 = (bf16[384,128]{1,0:T(8,128)(2,1)S(1)}, bf16[384,128]{1,0:T(8,128)(2,1)S(1)}, u32[]{:S(2)}, u32[]{:S(2)}) collective-permute-start(bf16[384,128]{1,0:T(8,128)(2,1)S(1)} %maximum_select_fusion.5), channel_id=1, source_target_pairs={{0,4},{2,6},{4,0},{6,2},{8,12},{10,14},{12,8},{14,10},{16,20},{18,... | collective-permute-start | bytes 294920 | tf_op jit(solution)/shard_map/ppermute | solution.py:241
  60.8 4.7 %collective-permute-start.20 = (bf16[384,128]{1,0:T(8,128)(2,1)S(1)}, bf16[384,128]{1,0:T(8,128)(2,1)S(1)}, u32[]{:S(2)}, u32[]{:S(2)}) collective-permute-start(bf16[384,128]{1,0:T(8,128)(2,1)S(1)} %maximum_select_fusion.6), channel_id=1, source_target_pairs={{0,2},{2,0},{4,6},{6,4},{8,10},{10,8},{12,14},{14,12},{16,18},{18,... | collective-permute-start | bytes 294920 | tf_op jit(solution)/shard_map/ppermute | solution.py:241
  63.9 5.7 %collective-permute-start.12 = (bf16[768,128]{1,0:T(8,128)(2,1)S(1)}, bf16[768,128]{1,0:T(8,128)(2,1)S(1)}, u32[]{:S(2)}, u32[]{:S(2)}) collective-permute-start(bf16[768,128]{1,0:T(8,128)(2,1)S(1)} %maximum_select_fusion.3), channel_id=1, source_target_pairs={{0,2},{2,0},{4,6},{6,4},{8,10},{10,8},{12,14},{14,12},{16,18},{18,... | collective-permute-start | bytes 589832 | tf_op jit(solution)/shard_map/ppermute | solution.py:241
  65.6 5.7 %collective-permute-start.21 = (bf16[768,128]{1,0:T(8,128)(2,1)S(1)}, bf16[768,128]{1,0:T(8,128)(2,1)S(1)}, u32[]{:S(2)}, u32[]{:S(2)}) collective-permute-start(bf16[768,128]{1,0:T(8,128)(2,1)S(1)} %maximum_select_fusion.4), channel_id=1, source_target_pairs={{0,4},{2,6},{4,0},{6,2},{8,12},{10,14},{12,8},{14,10},{16,20},{18,... | collective-permute-start | bytes 589832 | tf_op jit(solution)/shard_map/ppermute | solution.py:241
  69.8 1.8 %collective-permute-start.13 = (bf16[1536,128]{1,0:T(8,128)(2,1)S(1)}, bf16[1536,128]{1,0:T(8,128)(2,1)S(1)}, u32[]{:S(2)}, u32[]{:S(2)}) collective-permute-start(bf16[1536,128]{1,0:T(8,128)(2,1)S(1)} %maximum_select_fusion.1.own_p_ref), channel_id=1, source_target_pairs={{0,1},{1,0},{2,3},{3,2},{4,5},{5,4},{6,7},{7,6},{8,9},{9,8},{10,11... | collective-permute-start | bytes 1179656 | tf_op jit(solution)/shard_map/ppermute | solution.py:241
  71.4 1.8 %collective-permute-start.22 = (bf16[1536,128]{1,0:T(8,128)(2,1)S(1)}, bf16[1536,128]{1,0:T(8,128)(2,1)S(1)}, u32[]{:S(2)}, u32[]{:S(2)}) collective-permute-start(bf16[1536,128]{1,0:T(8,128)(2,1)S(1)} %maximum_select_fusion.2.own_q_ref), channel_id=1, source_target_pairs={{0,1},{1,0},{2,3},{3,2},{4,5},{5,4},{6,7},{7,6},{8,9},{9,8},{10,11... | collective-permute-start | bytes 1179656 | tf_op jit(solution)/shard_map/ppermute | solution.py:241

commit v6 on v5

--- a/solution.py
+++ b/solution.py
@@ -10,7 +10,6 @@
 F32 = jnp.float32
 BF16 = jnp.bfloat16
 LANES = 128
-VMEM_BYTES = 32 * 2**20
 
 
 def up_to(value, step):
@@ -25,8 +24,12 @@
     target_ref[64:, LANES:] = rows[pl.ds(near, 64), 2 * LANES :]
 
 
-def pack_kernel(stack_ref, packed_ref, first_ref, second_ref):
-    packed_ref[...] = stack_ref[...].astype(F32).T.astype(BF16)
+def pack_kernel(channels, stack_ref, occupancy_ref, packed_ref, first_ref, second_ref, turned_ref):
+    active = occupancy_ref[...] > 0
+    row = lax.broadcasted_iota(jnp.int32, stack_ref.shape, 0)
+    masked = jnp.where(active, jnp.where(row == channels, 1.0, stack_ref[...].astype(F32)), 0.0)
+    packed_ref[...] = masked.T.astype(BF16)
+    turned_ref[...] = masked[LANES : LANES + turned_ref.shape[0]].astype(BF16)
     odd = lax.axis_index("region") % 2
     store_planes(first_ref, packed_ref, 1 - odd)
     store_planes(second_ref, packed_ref, odd)
@@ -62,25 +65,15 @@
     return block.reshape(8 * count * count, target.shape[4])
 
 
-def second_layer_kernel(occupancy_ref, hidden_s, two_ref, output_ref):
-    outs = output_ref.shape[0]
-    output = None
-    for chunk in CHUNKS:
-        rows = jnp.concatenate([staged(hidden_s, tap, 8) for tap in chunk], 1)
-        kernel = jnp.concatenate([two_ref[offset_of(tap)] for tap in chunk], 0)[:, :outs]
-        term = jnp.dot(rows, kernel, preferred_element_type=F32)
-        output = term if output is None else output + term
-    output_ref[...] = jnp.where(occupancy_ref[...] > 0, output.T, 0.0).astype(BF16)
-
-
 def main_kernel(
-    outs, neighbors_ref, own_ref, partner_ref, first_ref, second_ref, first_far_ref, second_far_ref,
-    stack_ref, one_ref, two_ref, kept_p_ref, kept_q_ref, sent_p_ref, sent_q_ref, hidden_s,
-    masked_w, grad_w, hidden_w, total, masked_s, plane_s, grad_s,
+    neighbors_ref, own_ref, partner_ref, first_ref, second_ref, first_far_ref, second_far_ref,
+    turned_ref, one_ref, two_ref, output_ref, kept_p_ref, kept_q_ref, sent_p_ref, sent_q_ref,
+    masked_w, grad_w, hidden_w, total, masked_s, plane_s, hidden_s, grad_s,
 ):
     odd, split = lax.axis_index("region") % 2, lax.axis_index("split")
     channels = one_ref.shape[2]
     wide = grad_w.shape[3]
+    outs = turned_ref.shape[0]
     masked_w[:, 6:18] = jnp.zeros((12, 12, 24, LANES), F32)
     grad_w[:, 7:17] = jnp.zeros((10, 10, 24, wide), F32)
 
@@ -163,13 +156,19 @@
     own_flag = masked_w[2:10, 8:16, 8:16, channels : channels + 1].reshape(512, 1) > 0
 
     first_one = 3 * (-(-27 // 4)) * outs
-    turned_out = stack_ref[LANES : LANES + outs, :]
+    turned_out = turned_ref[...]
     stage(hidden_s, hidden_w, 0, 0, 7)
+    output = None
     for chunk in CHUNKS:
         rows = jnp.concatenate([staged(hidden_s, tap, 8) for tap in chunk], 1)
+        kernel = jnp.concatenate([two_ref[offset_of(tap)] for tap in chunk], 0)[:, :outs]
+        term = jnp.dot(rows, kernel, preferred_element_type=F32)
+        output = term if output is None else output + term
         product = jnp.dot(turned_out, rows, preferred_element_type=F32)
         for place, tap in enumerate(chunk):
             store_turned(total, product[:, place * LANES : (place + 1) * LANES], offset_of(tap), 0, channels)
+
+    output_ref[...] = jnp.where(own_flag, output, 0.0).T.astype(BF16)
 
     stage(grad_s, grad_w, 0, 7, 7)
     back = None
@@ -224,7 +223,7 @@
         copy.wait()
 
 
-def call(kernel, out_shape, args, scalars=0, scratch=(), cost=None, into=pltpu.VMEM):
+def call(kernel, out_shape, args, scalars=0, scratch=(), cost=None, into=pltpu.VMEM, mib=12):
     spaces = [pltpu.SMEM] * scalars + [pltpu.VMEM] * (len(args) - scalars)
     return pl.pallas_call(
         kernel,
@@ -232,7 +231,7 @@
         in_specs=[pl.BlockSpec(memory_space=space) for space in spaces],
         out_specs=jax.tree.map(lambda _: pl.BlockSpec(memory_space=into), out_shape),
         scratch_shapes=list(scratch),
-        compiler_params=pltpu.CompilerParams(vmem_limit_bytes=VMEM_BYTES),
+        compiler_params=pltpu.CompilerParams(vmem_limit_bytes=mib * 2**20),
         cost_estimate=cost,
     )(*args)
 
@@ -258,35 +257,33 @@
     wide = up_to(outs, LANES)
     struct = jax.ShapeDtypeStruct
 
-    stack = jnp.concatenate(
-        [
-            features,
-            jnp.ones((LANES - channels, voxels), BF16),
-            cotangent,
-            jnp.zeros((wide - outs, voxels), BF16),
-        ],
-        0,
-    )
-    stack = jnp.where(occupancy > 0, stack, jnp.zeros((), BF16))
+    spare = LANES - channels
+    stack = jnp.pad(features, ((0, spare + wide), (0, 0))) + jnp.pad(cotangent, ((LANES, wide - outs), (0, 0)))
     planes = struct((128, 2 * LANES), BF16)
-    packed, first, second = call(pack_kernel, (struct((voxels, LANES + wide), BF16), planes, planes), (stack,))
+    packed, first, second, turned = call(
+        functools.partial(pack_kernel, channels),
+        (struct((voxels, LANES + wide), BF16), planes, planes, struct((outs, voxels), BF16)),
+        (stack, occupancy),
+    )
     pairs = [(i, i + 1) for i in range(1, regions - 1, 2)]
     second = lax.ppermute(second, "region", pairs + [(b, a) for a, b in pairs])
     first = lax.ppermute(first, "region", [(i, i ^ 1) for i in range(regions)])
     partner = exchanged(packed, "split", 1)
     one = jnp.pad(kernel_one, ((0, 0), (0, LANES - channels), (0, 0)))
     two = jnp.pad(kernel_two, ((0, 0), (0, LANES - channels), (0, wide - outs)))
-    first, second, one, two = lax.optimization_barrier((first, second, one, two))
-    first_far, second_far = exchanged(first, "split", 1), exchanged(second, "split", 1)
+    second, one, two = lax.optimization_barrier((second, one, two))
+    second_far = exchanged(second, "split", 1)
+    first_far = exchanged(first, "split", 1)
 
     tile_rows = 3 * -(-offsets // 4) * (outs + channels)
     half = up_to(tile_rows, 4 * regions * 8) // 4
     kept, sent = struct((half, LANES), F32), struct((half, LANES), BF16)
-    *sums, hidden = call(
-        functools.partial(main_kernel, outs),
-        (kept, kept, sent, sent, struct((3, 2, 10, 80, LANES), BF16)),
-        (neighbors, packed, partner, first, second, first_far, second_far, stack, one, two),
+    output, *sums = call(
+        main_kernel,
+        (struct((outs, voxels), BF16), kept, kept, sent, sent),
+        (neighbors, packed, partner, first, second, first_far, second_far, turned, one, two),
         scalars=1,
+        mib=26,
         scratch=(
             pltpu.VMEM((12, 24, 24, LANES), F32),
             pltpu.VMEM((10, 24, 24, wide), F32),
@@ -294,17 +291,11 @@
             pltpu.VMEM((4 * half, LANES), F32),
             pltpu.VMEM((3, 2, 12, 96, LANES), BF16),
             pltpu.VMEM((3, 3, 12, 16, LANES), BF16),
+            pltpu.VMEM((3, 2, 10, 80, LANES), BF16),
             pltpu.VMEM((3, 2, 10, 80, wide), BF16),
         ),
     )
     sums = [sums[part] + exchanged(sums[2 + part], "split", 1).astype(F32) for part in range(2)]
-    sums[0], hidden = lax.optimization_barrier((sums[0], hidden))
-    output = call(
-        second_layer_kernel,
-        struct((outs, voxels), BF16),
-        (occupancy, hidden, two),
-        cost=pl.CostEstimate(flops=2 * voxels * offsets * channels * outs, bytes_accessed=4 * 2**20, transcendentals=0),
-    )
     bits = list(range((regions - 1).bit_length()))
     orders = [bits, bits[1::-1] + bits[2:]]
 
@@ -314,8 +305,6 @@
             mask = 1 << order[step]
             keep, give = halves(sums[part], (region // mask) % 2)
             pieces.append((keep, exchanged(give.astype(BF16), "region", mask)))
-        if step == 0:
-            pieces[0], output = lax.optimization_barrier((pieces[0], output))
         sums = [keep + came.astype(F32) for keep, came in pieces]
     for part, order in enumerate(orders):
         own = sums[part].astype(BF16)

time: 75.8 us -> 69 us (0.910)
  Pallas kernels: 16.3 us -> 12.1 us
  other arithmetic: 3.92 us -> 1.69 us
  starting transfers between devices: 30 us -> 29.1 us
  waiting for transfers between devices: 21.9 us -> 22.7 us
    pallas_call x4 -> x3, Pallas kernels: 16.3 us -> 12.1 us  [call(): pl.pallas_call(kernel, out_shape=out_shape, in_specs=[pl.BlockSpec(memory...]
    ppermute x21, starting transfers between devices: 26.8 us -> 23 us  [exchanged(): lax.ppermute(value, axis, [(i, i ^ mask) for i in range(lax.axis_size(axi...]
    ppermute x1, starting transfers between devices: 2.56 us -> 5.44 us  [shards(): first = lax.ppermute(first, 'region', [(i, i ^ 1) for i in range(regions)])]
    add x2, other arithmetic: 1.36 us -> 0.13 us  [shards(): sums[part] + exchanged(sums[2 + part], 'split', 1).astype(F32)]
    select_n x1 -> x0, other arithmetic: 1.16 us -> none  [shards(): stack = jnp.where(occupancy > 0, stack, jnp.zeros((), BF16))]
    unnamed x14 -> x6, local copies, waits for them, and re-layouts: 1.78 us -> 0.69 us
    pad x1, local copies, waits for them, and re-layouts: 0.22 us -> 1.3 us  [shards(): one = jnp.pad(kernel_one, ((0, 0), (0, LANES - channels), (0, 0)))]
    add x0 -> x1, other arithmetic: none -> 1.02 us  [shards(): jnp.pad(features, ((0, spare + wide), (0, 0)))]
  transfers between devices with their start and end apart: 23 -> 23, of which waited for: 15 -> 17; matrix products, arithmetic and copies ran while one was open for 3% -> 4% of each run, Pallas kernels for 2% -> 0%
where the time goes in v6:
time: 69 us; the launch traced here: 68.7 us
  starting transfers between devices  29.1 us (42%)
  waiting for transfers between devices  22.7 us (33%)
  Pallas kernels  12.1 us (18%)
  local copies, waits for them, and re-layouts  2.42 us (4%)
  other arithmetic  1.69 us (2%)
  between operations  0.84 us (1%)
    ppermute x21, starting transfers between devices, exchanged(): lax.ppermute(value, axis, [(i, i ^ mask) for i in range(lax.axis_size(axi...  23 us
    ppermute x21, waiting for transfers between devices, exchanged(): lax.ppermute(value, axis, [(i, i ^ mask) for i in range(lax.axis_size(axi...  20.7 us
    pallas_call x3, Pallas kernels, call(): pl.pallas_call(kernel, out_shape=out_shape, in_specs=[pl.BlockSpec(memory...  12.1 us
    ppermute x1, starting transfers between devices, shards(): first = lax.ppermute(first, 'region', [(i, i ^ 1) for i in range(regions)])  5.44 us
    ppermute x1, waiting for transfers between devices, shards(): first = lax.ppermute(first, 'region', [(i, i ^ 1) for i in range(regions)])  1.99 us
  transfers between devices with their start and end apart: 23, of which 17 were waited for; matrix products, arithmetic and copies ran while one was open for 4% of the time, Pallas kernels for 0%

profile of v6, /device:TPU:0, one launch (start us, length us, event | category | flops | bytes accessed | tf_op | source)
XLA Modules:
  0.0 68.7 jit_solution(6225858799650125256)
XLA Ops:
  0.6 1.0 %pad_add_fusion.stack_ref = bf16[384,512]{1,0:T(8,128)(2,1)S(1)} fusion(bf16[192,512]{1,0:T(8,128)(2,1)} %param.11, bf16[96,512]{1,0:T(8,128)(2,1)} %param.6), kind=kLoop, calls=%fused_computation.8 | loop fusion | flops 786432 | bytes 688128 | tf_op jit(solution)/shard_map/add | solution.py:261
  3.7 5.4 %collective-permute-start.1 = (bf16[128,256]{1,0:T(8,128)(2,1)S(1)}, bf16[128,256]{1,0:T(8,128)(2,1)S(1)}, u32[]{:S(2)}, u32[]{:S(2)}) collective-permute-start(bf16[128,256]{1,0:T(8,128)(2,1)S(1)} %get-tuple-element.18), channel_id=1, source_target_pairs={{0,2},{2,0},{4,6},{6,4},{8,10},{10,8},{12,14},{14,12},{16,18},{18,... | collective-permute-start | bytes 196616 | tf_op jit(solution)/shard_map/ppermute | solution.py:270
  9.2 1.3 %pad.18.one_ref = bf16[27,128,96]{2,1,0:T(8,128)(2,1)S(1)} pad(bf16[27,96,96]{2,1,0:T(8,128)(2,1)} %param.7, bf16[]{:T(256)} %constant.92.clone.1), padding=0_0x0_32x0_0 | pad | bytes 1161218 | tf_op jit(solution)/shard_map/jit(_pad)/pad | solution.py:272
  10.8 2.0 %collective-permute-done.1.first_ref = bf16[128,256]{1,0:T(8,128)(2,1)S(1)} collective-permute-done((bf16[128,256]{1,0:T(8,128)(2,1)S(1)}, bf16[128,256]{1,0:T(8,128)(2,1)S(1)}, u32[]{:S(2)}, u32[]{:S(2)}) %collective-permute-start.1) | collective-permute-done | bytes 65568 | tf_op jit(solution)/shard_map/ppermute | solution.py:270
  14.2 9.4 %shard_map.86 = (bf16[192,512]{1,0:T(8,128)(2,1)}, f32[1536,128]{1,0:T(8,128)S(1)}, f32[1536,128]{1,0:T(8,128)S(1)}, bf16[1536,128]{1,0:T(8,128)(2,1)S(1)}, bf16[1536,128]{1,0:T(8,128)(2,1)S(1)}) custom-call(s32[1,27]{1,0:T(1,128)S(1)} %copy-done.1, bf16[512,384]{1,0:T(8,128)(2,1)S(1)} %get-tuple-element.17.own_ref, ...), custom_call_target="tpu_custom_call" | custom-call | tf_op jit(solution)/shard_map/pallas_call | solution.py:228
  24.2 1.2 %collective-permute-done.5 = bf16[1536,128]{1,0:T(8,128)(2,1)S(1)} collective-permute-done((bf16[1536,128]{1,0:T(8,128)(2,1)S(1)}, bf16[1536,128]{1,0:T(8,128)(2,1)S(1)}, u32[]{:S(2)}, u32[]{:S(2)}) %collective-permute-start.5) | collective-permute-done | bytes 393248 | tf_op jit(solution)/shard_map/ppermute | solution.py:240
  25.5 1.9 %collective-permute-start.6 = (bf16[768,128]{1,0:T(8,128)(2,1)S(1)}, bf16[768,128]{1,0:T(8,128)(2,1)S(1)}, u32[]{:S(2)}, u32[]{:S(2)}) collective-permute-start(bf16[768,128]{1,0:T(8,128)(2,1)S(1)} %dynamic-slice_convert_fusion.1), channel_id=1, source_target_pairs={{0,2},{2,0},{4,6},{6,4},{8,10},{10,8},{12,14},{14,12},{16,18},{18,... | collective-permute-start | bytes 589832 | tf_op jit(solution)/shard_map/ppermute | solution.py:240
  27.5 0.8 %collective-permute-start.15 = (bf16[768,128]{1,0:T(8,128)(2,1)S(1)}, bf16[768,128]{1,0:T(8,128)(2,1)S(1)}, u32[]{:S(2)}, u32[]{:S(2)}) collective-permute-start(bf16[768,128]{1,0:T(8,128)(2,1)S(1)} %dynamic-slice_convert_fusion), channel_id=1, source_target_pairs={{0,4},{2,6},{4,0},{6,2},{8,12},{10,14},{12,8},{14,10},{16,20},{18,... | collective-permute-start | bytes 589832 | tf_op jit(solution)/shard_map/ppermute | solution.py:240
  28.3 4.5 %collective-permute-done.6 = bf16[768,128]{1,0:T(8,128)(2,1)S(1)} collective-permute-done((bf16[768,128]{1,0:T(8,128)(2,1)S(1)}, bf16[768,128]{1,0:T(8,128)(2,1)S(1)}, u32[]{:S(2)}, u32[]{:S(2)}) %collective-permute-start.6) | collective-permute-done | bytes 196640 | tf_op jit(solution)/shard_map/ppermute | solution.py:240
  32.9 0.8 %collective-permute-start.7 = (bf16[384,128]{1,0:T(8,128)(2,1)S(1)}, bf16[384,128]{1,0:T(8,128)(2,1)S(1)}, u32[]{:S(2)}, u32[]{:S(2)}) collective-permute-start(bf16[384,128]{1,0:T(8,128)(2,1)S(1)} %dynamic-slice_convert_fusion.3), channel_id=1, source_target_pairs={{0,4},{2,6},{4,0},{6,2},{8,12},{10,14},{12,8},{14,10},{16,20},{18,... | collective-permute-start | bytes 294920 | tf_op jit(solution)/shard_map/ppermute | solution.py:240
  33.7 0.8 %collective-permute-done.15 = bf16[768,128]{1,0:T(8,128)(2,1)S(1)} collective-permute-done((bf16[768,128]{1,0:T(8,128)(2,1)S(1)}, bf16[768,128]{1,0:T(8,128)(2,1)S(1)}, u32[]{:S(2)}, u32[]{:S(2)}) %collective-permute-start.15) | collective-permute-done | bytes 196640 | tf_op jit(solution)/shard_map/ppermute | solution.py:240
  34.5 1.0 %collective-permute-start.16 = (bf16[384,128]{1,0:T(8,128)(2,1)S(1)}, bf16[384,128]{1,0:T(8,128)(2,1)S(1)}, u32[]{:S(2)}, u32[]{:S(2)}) collective-permute-start(bf16[384,128]{1,0:T(8,128)(2,1)S(1)} %dynamic-slice_convert_fusion.2), channel_id=1, source_target_pairs={{0,2},{2,0},{4,6},{6,4},{8,10},{10,8},{12,14},{14,12},{16,18},{18,... | collective-permute-start | bytes 294920 | tf_op jit(solution)/shard_map/ppermute | solution.py:240
  35.6 2.0 %collective-permute-done.7 = bf16[384,128]{1,0:T(8,128)(2,1)S(1)} collective-permute-done((bf16[384,128]{1,0:T(8,128)(2,1)S(1)}, bf16[384,128]{1,0:T(8,128)(2,1)S(1)}, u32[]{:S(2)}, u32[]{:S(2)}) %collective-permute-start.7) | collective-permute-done | bytes 98336 | tf_op jit(solution)/shard_map/ppermute | solution.py:240
  37.6 1.6 %collective-permute-start.8 = (bf16[192,128]{1,0:T(8,128)(2,1)S(1)}, bf16[192,128]{1,0:T(8,128)(2,1)S(1)}, u32[]{:S(2)}, u32[]{:S(2)}) collective-permute-start(bf16[192,128]{1,0:T(8,128)(2,1)S(1)} %dynamic-slice_convert_fusion.5), channel_id=1, source_target_pairs={{0,8},{2,10},{4,12},{6,14},{8,0},{10,2},{12,4},{14,6},{16,24},{18,... | collective-permute-start | bytes 147464 | tf_op jit(solution)/shard_map/ppermute | solution.py:240
  39.3 1.6 %collective-permute-start.17 = (bf16[192,128]{1,0:T(8,128)(2,1)S(1)}, bf16[192,128]{1,0:T(8,128)(2,1)S(1)}, u32[]{:S(2)}, u32[]{:S(2)}) collective-permute-start(bf16[192,128]{1,0:T(8,128)(2,1)S(1)} %dynamic-slice_convert_fusion.4), channel_id=1, source_target_pairs={{0,8},{2,10},{4,12},{6,14},{8,0},{10,2},{12,4},{14,6},{16,24},{18,... | collective-permute-start | bytes 147464 | tf_op jit(solution)/shard_map/ppermute | solution.py:240
  40.9 0.9 %collective-permute-done.8 = bf16[192,128]{1,0:T(8,128)(2,1)S(1)} collective-permute-done((bf16[192,128]{1,0:T(8,128)(2,1)S(1)}, bf16[192,128]{1,0:T(8,128)(2,1)S(1)}, u32[]{:S(2)}, u32[]{:S(2)}) %collective-permute-start.8) | collective-permute-done | bytes 49184 | tf_op jit(solution)/shard_map/ppermute | solution.py:240
  41.8 2.6 %collective-permute-start.9 = (bf16[192,128]{1,0:T(8,128)(2,1)S(1)}, bf16[192,128]{1,0:T(8,128)(2,1)S(1)}, u32[]{:S(2)}, u32[]{:S(2)}) collective-permute-start(bf16[192,128]{1,0:T(8,128)(2,1)S(1)} %add_convert_fusion.3), channel_id=1, source_target_pairs={{0,16},{2,18},{4,20},{6,22},{8,24},{10,26},{12,28},{14,30},{16,0},... | collective-permute-start | bytes 147464 | tf_op jit(solution)/shard_map/ppermute | solution.py:240
  44.5 1.6 %collective-permute-start.18 = (bf16[192,128]{1,0:T(8,128)(2,1)S(1)}, bf16[192,128]{1,0:T(8,128)(2,1)S(1)}, u32[]{:S(2)}, u32[]{:S(2)}) collective-permute-start(bf16[192,128]{1,0:T(8,128)(2,1)S(1)} %add_convert_fusion.1), channel_id=1, source_target_pairs={{0,16},{2,18},{4,20},{6,22},{8,24},{10,26},{12,28},{14,30},{16,0},... | collective-permute-start | bytes 147464 | tf_op jit(solution)/shard_map/ppermute | solution.py:240
  46.1 1.1 %collective-permute-done.9 = bf16[192,128]{1,0:T(8,128)(2,1)S(1)} collective-permute-done((bf16[192,128]{1,0:T(8,128)(2,1)S(1)}, bf16[192,128]{1,0:T(8,128)(2,1)S(1)}, u32[]{:S(2)}, u32[]{:S(2)}) %collective-permute-start.9) | collective-permute-done | bytes 49184 | tf_op jit(solution)/shard_map/ppermute | solution.py:240
  47.2 1.3 %collective-permute-start.10 = (bf16[192,128]{1,0:T(8,128)(2,1)S(1)}, bf16[192,128]{1,0:T(8,128)(2,1)S(1)}, u32[]{:S(2)}, u32[]{:S(2)}) collective-permute-start(bf16[192,128]{1,0:T(8,128)(2,1)S(1)} %add_convert_fusion.2), channel_id=1, source_target_pairs={{0,8},{2,10},{4,12},{6,14},{8,0},{10,2},{12,4},{14,6},{16,24},{18,... | collective-permute-start | bytes 147464 | tf_op jit(solution)/shard_map/ppermute | solution.py:240
  48.5 1.0 %collective-permute-done.18 = bf16[192,128]{1,0:T(8,128)(2,1)S(1)} collective-permute-done((bf16[192,128]{1,0:T(8,128)(2,1)S(1)}, bf16[192,128]{1,0:T(8,128)(2,1)S(1)}, u32[]{:S(2)}, u32[]{:S(2)}) %collective-permute-start.18) | collective-permute-done | bytes 49184 | tf_op jit(solution)/shard_map/ppermute | solution.py:240
  49.5 1.7 %collective-permute-start.19 = (bf16[192,128]{1,0:T(8,128)(2,1)S(1)}, bf16[192,128]{1,0:T(8,128)(2,1)S(1)}, u32[]{:S(2)}, u32[]{:S(2)}) collective-permute-start(bf16[192,128]{1,0:T(8,128)(2,1)S(1)} %add_convert_fusion), channel_id=1, source_target_pairs={{0,8},{2,10},{4,12},{6,14},{8,0},{10,2},{12,4},{14,6},{16,24},{18,... | collective-permute-start | bytes 147464 | tf_op jit(solution)/shard_map/ppermute | solution.py:240
  51.4 1.2 %collective-permute-start.11 = (bf16[384,128]{1,0:T(8,128)(2,1)S(1)}, bf16[384,128]{1,0:T(8,128)(2,1)S(1)}, u32[]{:S(2)}, u32[]{:S(2)}) collective-permute-start(bf16[384,128]{1,0:T(8,128)(2,1)S(1)} %maximum_select_fusion.4), channel_id=1, source_target_pairs={{0,4},{2,6},{4,0},{6,2},{8,12},{10,14},{12,8},{14,10},{16,20},{18,... | collective-permute-start | bytes 294920 | tf_op jit(solution)/shard_map/ppermute | solution.py:240
  52.6 1.1 %collective-permute-done.19 = bf16[192,128]{1,0:T(8,128)(2,1)S(1)} collective-permute-done((bf16[192,128]{1,0:T(8,128)(2,1)S(1)}, bf16[192,128]{1,0:T(8,128)(2,1)S(1)}, u32[]{:S(2)}, u32[]{:S(2)}) %collective-permute-start.19) | collective-permute-done | bytes 49184 | tf_op jit(solution)/shard_map/ppermute | solution.py:240
  53.7 2.3 %collective-permute-start.20 = (bf16[384,128]{1,0:T(8,128)(2,1)S(1)}, bf16[384,128]{1,0:T(8,128)(2,1)S(1)}, u32[]{:S(2)}, u32[]{:S(2)}) collective-permute-start(bf16[384,128]{1,0:T(8,128)(2,1)S(1)} %maximum_select_fusion.5), channel_id=1, source_target_pairs={{0,2},{2,0},{4,6},{6,4},{8,10},{10,8},{12,14},{14,12},{16,18},{18,... | collective-permute-start | bytes 294920 | tf_op jit(solution)/shard_map/ppermute | solution.py:240
  56.1 0.9 %collective-permute-done.11 = bf16[384,128]{1,0:T(8,128)(2,1)S(1)} collective-permute-done((bf16[384,128]{1,0:T(8,128)(2,1)S(1)}, bf16[384,128]{1,0:T(8,128)(2,1)S(1)}, u32[]{:S(2)}, u32[]{:S(2)}) %collective-permute-start.11) | collective-permute-done | bytes 98336 | tf_op jit(solution)/shard_map/ppermute | solution.py:240
  57.0 1.3 %collective-permute-start.12 = (bf16[768,128]{1,0:T(8,128)(2,1)S(1)}, bf16[768,128]{1,0:T(8,128)(2,1)S(1)}, u32[]{:S(2)}, u32[]{:S(2)}) collective-permute-start(bf16[768,128]{1,0:T(8,128)(2,1)S(1)} %maximum_select_fusion.2), channel_id=1, source_target_pairs={{0,2},{2,0},{4,6},{6,4},{8,10},{10,8},{12,14},{14,12},{16,18},{18,... | collective-permute-start | bytes 589832 | tf_op jit(solution)/shard_map/ppermute | solution.py:240
  58.7 1.3 %collective-permute-start.21 = (bf16[768,128]{1,0:T(8,128)(2,1)S(1)}, bf16[768,128]{1,0:T(8,128)(2,1)S(1)}, u32[]{:S(2)}, u32[]{:S(2)}) collective-permute-start(bf16[768,128]{1,0:T(8,128)(2,1)S(1)} %maximum_select_fusion.3), channel_id=1, source_target_pairs={{0,4},{2,6},{4,0},{6,2},{8,12},{10,14},{12,8},{14,10},{16,20},{18,... | collective-permute-start | bytes 589832 | tf_op jit(solution)/shard_map/ppermute | solution.py:240
  60.0 2.7 %collective-permute-done.12 = bf16[768,128]{1,0:T(8,128)(2,1)S(1)} collective-permute-done((bf16[768,128]{1,0:T(8,128)(2,1)S(1)}, bf16[768,128]{1,0:T(8,128)(2,1)S(1)}, u32[]{:S(2)}, u32[]{:S(2)}) %collective-permute-start.12) | collective-permute-done | bytes 196640 | tf_op jit(solution)/shard_map/ppermute | solution.py:240
  63.0 1.5 %collective-permute-done.21 = bf16[768,128]{1,0:T(8,128)(2,1)S(1)} collective-permute-done((bf16[768,128]{1,0:T(8,128)(2,1)S(1)}, bf16[768,128]{1,0:T(8,128)(2,1)S(1)}, u32[]{:S(2)}, u32[]{:S(2)}) %collective-permute-start.21) | collective-permute-done | bytes 196640 | tf_op jit(solution)/shard_map/ppermute | solution.py:240
  64.7 1.7 %collective-permute-done.22.other_q_ref = bf16[1536,128]{1,0:T(8,128)(2,1)S(1)} collective-permute-done((bf16[1536,128]{1,0:T(8,128)(2,1)S(1)}, bf16[1536,128]{1,0:T(8,128)(2,1)S(1)}, u32[]{:S(2)}, u32[]{:S(2)}) %collective-permute-start.22) | collective-permute-done | bytes 393248 | tf_op jit(solution)/shard_map/ppermute | solution.py:240
  66.4 2.4 %shard_map.87 = (f32[27,96,96]{2,1,0:T(8,128)}, f32[27,96,192]{2,1,0:T(8,128)}) custom-call(bf16[1536,128]{1,0:T(8,128)(2,1)S(1)} %maximum_select_fusion.own_p_ref, bf16[1536,128]{1,0:T(8,128)(2,1)S(1)} %collective-permute-done.13.other_p_ref, bf16[1536,128]{1,0:T(8,128)(2,1)S(1)} %maximum_select_fusion.1.own_q_ref, ...), custom_call_target="tpu_custom_call" | custom-call | tf_op jit(solution)/shard_map/pallas_call | solution.py:228
  (48 shorter events, 5.7 us)
Async XLA Ops:
  1.7 0.7 copy-start
  2.3 8.2 %copy-start.2 = (bf16[27,96,192]{2,1,0:T(8,128)(2,1)S(1)}, bf16[27,96,192]{2,1,0:T(8,128)(2,1)}, u32[]{:S(2)}) copy-start(bf16[27,96,192]{2,1,0:T(8,128)(2,1)} %param.8) | copy-start | bytes 2985988
  2.6 11.7 %collective-permute-start = (bf16[512,384]{1,0:T(8,128)(2,1)S(1)}, bf16[512,384]{1,0:T(8,128)(2,1)S(1)}, u32[]{:S(2)}, u32[]{:S(2)}) collective-permute-start(bf16[512,384]{1,0:T(8,128)(2,1)S(1)} %get-tuple-element.17.own_ref), channel_id=1, source_target_pairs={{0,1},{1,0},{2,3},{3,2},{4,5},{5,4},{6,7},{7,6},{8,9},{9,8},{10,11... | collective-permute-start | bytes 1179656 | tf_op jit(solution)/shard_map/ppermute | solution.py:240
  3.1 7.7 %collective-permute-start.2 = (bf16[128,256]{1,0:T(8,128)(2,1)S(1)}, bf16[128,256]{1,0:T(8,128)(2,1)S(1)}, u32[]{:S(2)}, u32[]{:S(2)}) collective-permute-start(bf16[128,256]{1,0:T(8,128)(2,1)S(1)} %get-tuple-element.19), channel_id=1, source_target_pairs={{2,4},{6,8},{10,12},{14,16},{18,20},{22,24},{26,28},{4,2},{8,6},{1... | collective-permute-start | bytes 196616 | tf_op jit(solution)/shard_map/ppermute | solution.py:269
  3.7 9.1 %collective-permute-start.1 = (bf16[128,256]{1,0:T(8,128)(2,1)S(1)}, bf16[128,256]{1,0:T(8,128)(2,1)S(1)}, u32[]{:S(2)}, u32[]{:S(2)}) collective-permute-start(bf16[128,256]{1,0:T(8,128)(2,1)S(1)} %get-tuple-element.18), channel_id=1, source_target_pairs={{0,2},{2,0},{4,6},{6,4},{8,10},{10,8},{12,14},{14,12},{16,18},{18,... | collective-permute-start | bytes 196616 | tf_op jit(solution)/shard_map/ppermute | solution.py:270
  10.5 3.7 %copy-start.1 = (s32[1,27]{1,0:T(1,128)S(1)}, s32[1,27]{1,0:T(1,128)}, u32[]{:S(2)}) copy-start(s32[1,27]{1,0:T(1,128)} %neighbors_ref.1) | copy-start | bytes 328
  12.8 1.3 %collective-permute-start.3 = (bf16[128,256]{1,0:T(8,128)(2,1)S(1)}, bf16[128,256]{1,0:T(8,128)(2,1)S(1)}, u32[]{:S(2)}, u32[]{:S(2)}) collective-permute-start(bf16[128,256]{1,0:T(8,128)(2,1)S(1)} %collective-permute-done.1.first_ref), channel_id=1, source_target_pairs={{0,1},{1,0},{2,3},{3,2},{4,5},{5,4},{6,7},{7,6},{8,9},{9,8},{10,11... | collective-permute-start | bytes 196616 | tf_op jit(solution)/shard_map/ppermute | solution.py:240
  12.8 1.4 %collective-permute-start.4 = (bf16[128,256]{1,0:T(8,128)(2,1)S(1)}, bf16[128,256]{1,0:T(8,128)(2,1)S(1)}, u32[]{:S(2)}, u32[]{:S(2)}) collective-permute-start(bf16[128,256]{1,0:T(8,128)(2,1)S(1)} %collective-permute-done.2.second_ref), channel_id=1, source_target_pairs={{0,1},{1,0},{2,3},{3,2},{4,5},{5,4},{6,7},{7,6},{8,9},{9,8},{10,11... | collective-permute-start | bytes 196616 | tf_op jit(solution)/shard_map/ppermute | solution.py:240
  23.7 1.7 %collective-permute-start.5 = (bf16[1536,128]{1,0:T(8,128)(2,1)S(1)}, bf16[1536,128]{1,0:T(8,128)(2,1)S(1)}, u32[]{:S(2)}, u32[]{:S(2)}) collective-permute-start(bf16[1536,128]{1,0:T(8,128)(2,1)S(1)} %get-tuple-element.26), channel_id=1, source_target_pairs={{0,1},{1,0},{2,3},{3,2},{4,5},{5,4},{6,7},{7,6},{8,9},{9,8},{10,11... | collective-permute-start | bytes 1179656 | tf_op jit(solution)/shard_map/ppermute | solution.py:240
  24.0 3.4 %collective-permute-start.14 = (bf16[1536,128]{1,0:T(8,128)(2,1)S(1)}, bf16[1536,128]{1,0:T(8,128)(2,1)S(1)}, u32[]{:S(2)}, u32[]{:S(2)}) collective-permute-start(bf16[1536,128]{1,0:T(8,128)(2,1)S(1)} %get-tuple-element.28), channel_id=1, source_target_pairs={{0,1},{1,0},{2,3},{3,2},{4,5},{5,4},{6,7},{7,6},{8,9},{9,8},{10,11... | collective-permute-start | bytes 1179656 | tf_op jit(solution)/shard_map/ppermute | solution.py:240
  25.5 7.3 %collective-permute-start.6 = (bf16[768,128]{1,0:T(8,128)(2,1)S(1)}, bf16[768,128]{1,0:T(8,128)(2,1)S(1)}, u32[]{:S(2)}, u32[]{:S(2)}) collective-permute-start(bf16[768,128]{1,0:T(8,128)(2,1)S(1)} %dynamic-slice_convert_fusion.1), channel_id=1, source_target_pairs={{0,2},{2,0},{4,6},{6,4},{8,10},{10,8},{12,14},{14,12},{16,18},{18,... | collective-permute-start | bytes 589832 | tf_op jit(solution)/shard_map/ppermute | solution.py:240
  27.5 6.9 %collective-permute-start.15 = (bf16[768,128]{1,0:T(8,128)(2,1)S(1)}, bf16[768,128]{1,0:T(8,128)(2,1)S(1)}, u32[]{:S(2)}, u32[]{:S(2)}) collective-permute-start(bf16[768,128]{1,0:T(8,128)(2,1)S(1)} %dynamic-slice_convert_fusion), channel_id=1, source_target_pairs={{0,4},{2,6},{4,0},{6,2},{8,12},{10,14},{12,8},{14,10},{16,20},{18,... | collective-permute-start | bytes 589832 | tf_op jit(solution)/shard_map/ppermute | solution.py:240
  32.9 4.7 %collective-permute-start.7 = (bf16[384,128]{1,0:T(8,128)(2,1)S(1)}, bf16[384,128]{1,0:T(8,128)(2,1)S(1)}, u32[]{:S(2)}, u32[]{:S(2)}) collective-permute-start(bf16[384,128]{1,0:T(8,128)(2,1)S(1)} %dynamic-slice_convert_fusion.3), channel_id=1, source_target_pairs={{0,4},{2,6},{4,0},{6,2},{8,12},{10,14},{12,8},{14,10},{16,20},{18,... | collective-permute-start | bytes 294920 | tf_op jit(solution)/shard_map/ppermute | solution.py:240
  34.5 4.7 %collective-permute-start.16 = (bf16[384,128]{1,0:T(8,128)(2,1)S(1)}, bf16[384,128]{1,0:T(8,128)(2,1)S(1)}, u32[]{:S(2)}, u32[]{:S(2)}) collective-permute-start(bf16[384,128]{1,0:T(8,128)(2,1)S(1)} %dynamic-slice_convert_fusion.2), channel_id=1, source_target_pairs={{0,2},{2,0},{4,6},{6,4},{8,10},{10,8},{12,14},{14,12},{16,18},{18,... | collective-permute-start | bytes 294920 | tf_op jit(solution)/shard_map/ppermute | solution.py:240
  37.6 4.2 %collective-permute-start.8 = (bf16[192,128]{1,0:T(8,128)(2,1)S(1)}, bf16[192,128]{1,0:T(8,128)(2,1)S(1)}, u32[]{:S(2)}, u32[]{:S(2)}) collective-permute-start(bf16[192,128]{1,0:T(8,128)(2,1)S(1)} %dynamic-slice_convert_fusion.5), channel_id=1, source_target_pairs={{0,8},{2,10},{4,12},{6,14},{8,0},{10,2},{12,4},{14,6},{16,24},{18,... | collective-permute-start | bytes 147464 | tf_op jit(solution)/shard_map/ppermute | solution.py:240
  39.3 5.1 %collective-permute-start.17 = (bf16[192,128]{1,0:T(8,128)(2,1)S(1)}, bf16[192,128]{1,0:T(8,128)(2,1)S(1)}, u32[]{:S(2)}, u32[]{:S(2)}) collective-permute-start(bf16[192,128]{1,0:T(8,128)(2,1)S(1)} %dynamic-slice_convert_fusion.4), channel_id=1, source_target_pairs={{0,8},{2,10},{4,12},{6,14},{8,0},{10,2},{12,4},{14,6},{16,24},{18,... | collective-permute-start | bytes 147464 | tf_op jit(solution)/shard_map/ppermute | solution.py:240
  41.8 5.4 %collective-permute-start.9 = (bf16[192,128]{1,0:T(8,128)(2,1)S(1)}, bf16[192,128]{1,0:T(8,128)(2,1)S(1)}, u32[]{:S(2)}, u32[]{:S(2)}) collective-permute-start(bf16[192,128]{1,0:T(8,128)(2,1)S(1)} %add_convert_fusion.3), channel_id=1, source_target_pairs={{0,16},{2,18},{4,20},{6,22},{8,24},{10,26},{12,28},{14,30},{16,0},... | collective-permute-start | bytes 147464 | tf_op jit(solution)/shard_map/ppermute | solution.py:240
  44.5 5.1 %collective-permute-start.18 = (bf16[192,128]{1,0:T(8,128)(2,1)S(1)}, bf16[192,128]{1,0:T(8,128)(2,1)S(1)}, u32[]{:S(2)}, u32[]{:S(2)}) collective-permute-start(bf16[192,128]{1,0:T(8,128)(2,1)S(1)} %add_convert_fusion.1), channel_id=1, source_target_pairs={{0,16},{2,18},{4,20},{6,22},{8,24},{10,26},{12,28},{14,30},{16,0},... | collective-permute-start | bytes 147464 | tf_op jit(solution)/shard_map/ppermute | solution.py:240
  47.2 4.2 %collective-permute-start.10 = (bf16[192,128]{1,0:T(8,128)(2,1)S(1)}, bf16[192,128]{1,0:T(8,128)(2,1)S(1)}, u32[]{:S(2)}, u32[]{:S(2)}) collective-permute-start(bf16[192,128]{1,0:T(8,128)(2,1)S(1)} %add_convert_fusion.2), channel_id=1, source_target_pairs={{0,8},{2,10},{4,12},{6,14},{8,0},{10,2},{12,4},{14,6},{16,24},{18,... | collective-permute-start | bytes 147464 | tf_op jit(solution)/shard_map/ppermute | solution.py:240
  49.5 4.2 %collective-permute-start.19 = (bf16[192,128]{1,0:T(8,128)(2,1)S(1)}, bf16[192,128]{1,0:T(8,128)(2,1)S(1)}, u32[]{:S(2)}, u32[]{:S(2)}) collective-permute-start(bf16[192,128]{1,0:T(8,128)(2,1)S(1)} %add_convert_fusion), channel_id=1, source_target_pairs={{0,8},{2,10},{4,12},{6,14},{8,0},{10,2},{12,4},{14,6},{16,24},{18,... | collective-permute-start | bytes 147464 | tf_op jit(solution)/shard_map/ppermute | solution.py:240
  51.4 5.6 %collective-permute-start.11 = (bf16[384,128]{1,0:T(8,128)(2,1)S(1)}, bf16[384,128]{1,0:T(8,128)(2,1)S(1)}, u32[]{:S(2)}, u32[]{:S(2)}) collective-permute-start(bf16[384,128]{1,0:T(8,128)(2,1)S(1)} %maximum_select_fusion.4), channel_id=1, source_target_pairs={{0,4},{2,6},{4,0},{6,2},{8,12},{10,14},{12,8},{14,10},{16,20},{18,... | collective-permute-start | bytes 294920 | tf_op jit(solution)/shard_map/ppermute | solution.py:240
  53.7 4.9 %collective-permute-start.20 = (bf16[384,128]{1,0:T(8,128)(2,1)S(1)}, bf16[384,128]{1,0:T(8,128)(2,1)S(1)}, u32[]{:S(2)}, u32[]{:S(2)}) collective-permute-start(bf16[384,128]{1,0:T(8,128)(2,1)S(1)} %maximum_select_fusion.5), channel_id=1, source_target_pairs={{0,2},{2,0},{4,6},{6,4},{8,10},{10,8},{12,14},{14,12},{16,18},{18,... | collective-permute-start | bytes 294920 | tf_op jit(solution)/shard_map/ppermute | solution.py:240
  57.0 5.7 %collective-permute-start.12 = (bf16[768,128]{1,0:T(8,128)(2,1)S(1)}, bf16[768,128]{1,0:T(8,128)(2,1)S(1)}, u32[]{:S(2)}, u32[]{:S(2)}) collective-permute-start(bf16[768,128]{1,0:T(8,128)(2,1)S(1)} %maximum_select_fusion.2), channel_id=1, source_target_pairs={{0,2},{2,0},{4,6},{6,4},{8,10},{10,8},{12,14},{14,12},{16,18},{18,... | collective-permute-start | bytes 589832 | tf_op jit(solution)/shard_map/ppermute | solution.py:240
  58.7 5.7 %collective-permute-start.21 = (bf16[768,128]{1,0:T(8,128)(2,1)S(1)}, bf16[768,128]{1,0:T(8,128)(2,1)S(1)}, u32[]{:S(2)}, u32[]{:S(2)}) collective-permute-start(bf16[768,128]{1,0:T(8,128)(2,1)S(1)} %maximum_select_fusion.3), channel_id=1, source_target_pairs={{0,4},{2,6},{4,0},{6,2},{8,12},{10,14},{12,8},{14,10},{16,20},{18,... | collective-permute-start | bytes 589832 | tf_op jit(solution)/shard_map/ppermute | solution.py:240
  62.9 1.8 %collective-permute-start.13 = (bf16[1536,128]{1,0:T(8,128)(2,1)S(1)}, bf16[1536,128]{1,0:T(8,128)(2,1)S(1)}, u32[]{:S(2)}, u32[]{:S(2)}) collective-permute-start(bf16[1536,128]{1,0:T(8,128)(2,1)S(1)} %maximum_select_fusion.own_p_ref), channel_id=1, source_target_pairs={{0,1},{1,0},{2,3},{3,2},{4,5},{5,4},{6,7},{7,6},{8,9},{9,8},{10,11... | collective-permute-start | bytes 1179656 | tf_op jit(solution)/shard_map/ppermute | solution.py:240
  64.6 1.8 %collective-permute-start.22 = (bf16[1536,128]{1,0:T(8,128)(2,1)S(1)}, bf16[1536,128]{1,0:T(8,128)(2,1)S(1)}, u32[]{:S(2)}, u32[]{:S(2)}) collective-permute-start(bf16[1536,128]{1,0:T(8,128)(2,1)S(1)} %maximum_select_fusion.1.own_q_ref), channel_id=1, source_target_pairs={{0,1},{1,0},{2,3},{3,2},{4,5},{5,4},{6,7},{7,6},{8,9},{9,8},{10,11... | collective-permute-start | bytes 1179656 | tf_op jit(solution)/shard_map/ppermute | solution.py:240

commit v7 on v6

--- a/solution.py
+++ b/solution.py
@@ -196,35 +196,55 @@
         sent_ref[...] = total[pl.ds(pl.multiple_of(start + (1 - split) * half, 16), half), :].astype(BF16)
 
 
-def unpack_kernel(own_p_ref, other_p_ref, own_q_ref, other_q_ref, one_hbm, two_hbm, sums, one_ref, two_ref, sems):
+def assemble(sums, start, own_ref, other_ref):
     split = lax.axis_index("split")
-    offsets, channels, outs = two_ref.shape
-    half = own_p_ref.shape[0]
-    for start, own_ref, other_ref in ((0, own_p_ref, other_p_ref), (2 * half, own_q_ref, other_q_ref)):
-        sums[pl.ds(pl.multiple_of(start + split * half, 16), half), :] = own_ref[...]
-        sums[pl.ds(pl.multiple_of(start + (1 - split) * half, 16), half), :] = other_ref[...]
+    half = own_ref.shape[0]
+    sums[pl.ds(pl.multiple_of(start + split * half, 16), half), :] = own_ref[...]
+    sums[pl.ds(pl.multiple_of(start + (1 - split) * half, 16), half), :] = other_ref[...]
+
+
+def unpack(sums, first, groups, ref, target, sems):
+    offsets, channels, outs = ref.shape
     row = lax.broadcasted_iota(jnp.int32, (LANES, LANES), 0)
     unit = jnp.where(row == lax.broadcasted_iota(jnp.int32, (LANES, LANES), 1), 1.0, 0.0).astype(BF16)
     spare = LANES - channels
+    copies = []
+    for group in groups:
+        for place in range(3):
+            part = sums[pl.ds(first + (3 * group + place) * outs, outs), :]
+            part = lax.dot_general(unit, part, (((1,), (1,)), ((), ())), preferred_element_type=F32)
+            ref[4 * group + place] = part[:channels]
+            if 4 * group + 3 < offsets:
+                ref[4 * group + 3, place * spare : (place + 1) * spare, :] = part[channels:]
+        done = pl.ds(4 * group, min(4, offsets - 4 * group))
+        copies.append(pltpu.make_async_copy(ref.at[done], target.at[done], sems.at[len(copies)]))
+        copies[-1].start()
+    return copies
+
+
+def first_unpack_kernel(groups, own_ref, other_ref, two_hbm, sums, two_ref, sems):
+    assemble(sums, 0, own_ref, other_ref)
+    for copy in unpack(sums, 0, groups, two_ref, two_hbm, sems):
+        copy.wait()
+
+
+def second_unpack_kernel(
+    groups, own_p_ref, other_p_ref, own_q_ref, other_q_ref, _, one_hbm, two_hbm, sums, one_ref, two_ref, one_sems, two_sems
+):
+    offsets, _, outs = two_ref.shape
+    assemble(sums, 0, own_p_ref, other_p_ref)
+    assemble(sums, 2 * own_p_ref.shape[0], own_q_ref, other_q_ref)
     fours = -(-offsets // 4)
-    copies = []
-    for ref, target, first, rows in ((two_ref, two_hbm, 0, outs), (one_ref, one_hbm, 3 * fours * outs, channels)):
-        for group in range(fours):
-            for place in range(3):
-                part = sums[pl.ds(first + (3 * group + place) * rows, rows), :]
-                part = lax.dot_general(unit, part, (((1,), (1,)), ((), ())), preferred_element_type=F32)
-                ref[4 * group + place] = part[:channels]
-                if 4 * group + 3 < offsets:
-                    ref[4 * group + 3, place * spare : (place + 1) * spare, :] = part[channels:]
-            done = pl.ds(4 * group, min(4, offsets - 4 * group))
-            copies.append(pltpu.make_async_copy(ref.at[done], target.at[done], sems.at[len(copies)]))
-            copies[-1].start()
+    copies = unpack(sums, 0, groups, two_ref, two_hbm, two_sems)
+    copies += unpack(sums, 3 * fours * outs, range(fours), one_ref, one_hbm, one_sems)
     for copy in copies:
         copy.wait()
 
 
-def call(kernel, out_shape, args, scalars=0, scratch=(), cost=None, into=pltpu.VMEM, mib=12):
+def call(kernel, out_shape, args, scalars=0, scratch=(), cost=None, into=pltpu.VMEM, mib=12, filled=False):
     spaces = [pltpu.SMEM] * scalars + [pltpu.VMEM] * (len(args) - scalars)
+    if filled:
+        spaces[-1] = into
     return pl.pallas_call(
         kernel,
         out_shape=out_shape,
@@ -233,6 +253,7 @@
         scratch_shapes=list(scratch),
         compiler_params=pltpu.CompilerParams(vmem_limit_bytes=mib * 2**20),
         cost_estimate=cost,
+        input_output_aliases={len(args) - 1: len(out_shape) - 1} if filled else {},
     )(*args)
 
 
@@ -297,38 +318,56 @@
     )
     sums = [sums[part] + exchanged(sums[2 + part], "split", 1).astype(F32) for part in range(2)]
     bits = list(range((regions - 1).bit_length()))
-    orders = [bits, bits[1::-1] + bits[2:]]
-
-    for step in range(len(bits) - 1):
-        pieces = []
+    orders = [bits[:-2] + bits[:-3:-1], bits[1::-1] + bits[2:]]
+    whole_steps = 2
+
+    for step in range(len(bits) - whole_steps):
         for part, order in enumerate(orders):
             mask = 1 << order[step]
             keep, give = halves(sums[part], (region // mask) % 2)
-            pieces.append((keep, exchanged(give.astype(BF16), "region", mask)))
-        sums = [keep + came.astype(F32) for keep, came in pieces]
-    for part, order in enumerate(orders):
-        own = sums[part].astype(BF16)
-        sums[part] = (own.astype(F32) + exchanged(own, "region", 1 << order[-1]).astype(F32)).astype(BF16)
+            sums[part] = keep + exchanged(give.astype(BF16), "region", mask).astype(F32)
+    for step in range(len(bits) - whole_steps, len(bits)):
+        for part, order in enumerate(orders):
+            own = sums[part].astype(BF16)
+            sums[part] = own.astype(F32) + exchanged(own, "region", 1 << order[step]).astype(F32)
+    sums = [value.astype(BF16) for value in sums]
 
     def joined(own, other, bit):
         return jnp.where(bit == 0, jnp.concatenate([own, other], 0), jnp.concatenate([other, own], 0))
 
-    for step in reversed(range(len(bits) - 1)):
+    for step in reversed(range(len(bits) - whole_steps)):
         for part, order in enumerate(orders):
             mask = 1 << order[step]
             sums[part] = joined(sums[part], exchanged(sums[part], "region", mask), (region // mask) % 2)
-    ends = [value for own in sums for value in (own, exchanged(own, "split", 1))]
+    ends = [(own, exchanged(own, "split", 1)) for own in sums]
+    fours = -(-offsets // 4)
+    early = min(fours, 2 * half // (3 * outs))
+    one_shape, two_shape = struct((offsets, channels, channels), F32), struct((offsets, channels, outs), F32)
+    grad_two = call(
+        functools.partial(first_unpack_kernel, range(early)),
+        two_shape,
+        ends[0],
+        scratch=(
+            pltpu.VMEM((2 * half, LANES), BF16),
+            pltpu.VMEM(two_shape.shape, F32),
+            pltpu.SemaphoreType.DMA((fours,)),
+        ),
+        cost=pl.CostEstimate(flops=10**8, bytes_accessed=4 * 2**20, transcendentals=0),
+        into=pltpu.HBM,
+    )
     grad_one, grad_two = call(
-        unpack_kernel,
-        (struct((offsets, channels, channels), F32), struct((offsets, channels, outs), F32)),
-        ends,
+        functools.partial(second_unpack_kernel, range(early, fours)),
+        (one_shape, two_shape),
+        (*ends[0], *ends[1], grad_two),
         scratch=(
             pltpu.VMEM((4 * half, LANES), BF16),
-            pltpu.VMEM((offsets, channels, channels), F32),
-            pltpu.VMEM((offsets, channels, outs), F32),
-            pltpu.SemaphoreType.DMA((2 * -(-offsets // 4),)),
+            pltpu.VMEM(one_shape.shape, F32),
+            pltpu.VMEM(two_shape.shape, F32),
+            pltpu.SemaphoreType.DMA((fours,)),
+            pltpu.SemaphoreType.DMA((fours,)),
         ),
         into=pltpu.HBM,
+        filled=True,
     )
     return output, grad_one, grad_two
 

time: 69 us -> 65.6 us (0.951)
  starting transfers between devices: 29.1 us -> 26.7 us
  waiting for transfers between devices: 22.7 us -> 20.7 us
  Pallas kernels: 12.1 us -> 13.2 us
    ppermute x21 -> x19, starting transfers between devices: 23 us -> 20.6 us  [exchanged(): lax.ppermute(value, axis, [(i, i ^ mask) for i in range(lax.axis_size(axi...]
    ppermute x21 -> x19, waiting for transfers between devices: 20.7 us -> 18.7 us  [exchanged(): lax.ppermute(value, axis, [(i, i ^ mask) for i in range(lax.axis_size(axi...]
    pallas_call x3 -> x4, Pallas kernels: 12.1 us -> 13.2 us  [call(): pl.pallas_call(kernel, out_shape=out_shape, in_specs=[pl.BlockSpec(memory...]
  transfers between devices with their start and end apart: 23 -> 21, of which waited for: 17 -> 14; matrix products, arithmetic and copies ran while one was open for 4% -> 4% of each run, Pallas kernels for 0% -> 3%
where the time goes in v7:
time: 65.6 us; the launch traced here: 65.4 us
  starting transfers between devices  26.7 us (41%)
  waiting for transfers between devices  20.7 us (32%)
  Pallas kernels  13.2 us (20%)
  local copies, waits for them, and re-layouts  2.39 us (4%)
  other arithmetic  1.71 us (3%)
  between operations  0.83 us (1%)
    ppermute x19, starting transfers between devices, exchanged(): lax.ppermute(value, axis, [(i, i ^ mask) for i in range(lax.axis_size(axi...  20.6 us
    ppermute x19, waiting for transfers between devices, exchanged(): lax.ppermute(value, axis, [(i, i ^ mask) for i in range(lax.axis_size(axi...  18.7 us
    pallas_call x4, Pallas kernels, call(): pl.pallas_call(kernel, out_shape=out_shape, in_specs=[pl.BlockSpec(memory...  13.2 us
    ppermute x1, starting transfers between devices, shards(): first = lax.ppermute(first, 'region', [(i, i ^ 1) for i in range(regions)])  5.44 us
    ppermute x1, waiting for transfers between devices, shards(): first = lax.ppermute(first, 'region', [(i, i ^ 1) for i in range(regions)])  1.99 us
  transfers between devices with their start and end apart: 21, of which 14 were waited for; matrix products, arithmetic and copies ran while one was open for 4% of the time, Pallas kernels for 3%

profile of v7, /device:TPU:0, one launch (start us, length us, event | category | flops | bytes accessed | tf_op | source)
XLA Modules:
  0.0 65.4 jit_solution(1359237349499359049)
XLA Ops:
  0.6 1.0 %pad_add_fusion.stack_ref = bf16[384,512]{1,0:T(8,128)(2,1)S(1)} fusion(bf16[192,512]{1,0:T(8,128)(2,1)} %param.11, bf16[96,512]{1,0:T(8,128)(2,1)} %param.6), kind=kLoop, calls=%fused_computation.8 | loop fusion | flops 786432 | bytes 688128 | tf_op jit(solution)/shard_map/add | solution.py:282
  1.7 0.7 %copy-done = s32[1,512]{1,0:T(1,128)S(1)} copy-done((s32[1,512]{1,0:T(1,128)S(1)}, s32[1,512]{1,0:T(1,128)}, u32[]{:S(2)}) %copy-start) | copy-done | bytes 2072
  3.1 0.7 collective-permute-start.2
  3.7 5.4 %collective-permute-start.1 = (bf16[128,256]{1,0:T(8,128)(2,1)S(1)}, bf16[128,256]{1,0:T(8,128)(2,1)S(1)}, u32[]{:S(2)}, u32[]{:S(2)}) collective-permute-start(bf16[128,256]{1,0:T(8,128)(2,1)S(1)} %get-tuple-element.18), channel_id=1, source_target_pairs={{0,2},{2,0},{4,6},{6,4},{8,10},{10,8},{12,14},{14,12},{16,18},{18,... | collective-permute-start | bytes 196616 | tf_op jit(solution)/shard_map/ppermute | solution.py:291
  9.2 1.3 %pad.18.one_ref = bf16[27,128,96]{2,1,0:T(8,128)(2,1)S(1)} pad(bf16[27,96,96]{2,1,0:T(8,128)(2,1)} %param.7, bf16[]{:T(256)} %constant.66.clone.1), padding=0_0x0_32x0_0 | pad | bytes 1161218 | tf_op jit(solution)/shard_map/jit(_pad)/pad | solution.py:293
  10.8 2.0 %collective-permute-done.1.first_ref = bf16[128,256]{1,0:T(8,128)(2,1)S(1)} collective-permute-done((bf16[128,256]{1,0:T(8,128)(2,1)S(1)}, bf16[128,256]{1,0:T(8,128)(2,1)S(1)}, u32[]{:S(2)}, u32[]{:S(2)}) %collective-permute-start.1) | collective-permute-done | bytes 65568 | tf_op jit(solution)/shard_map/ppermute | solution.py:291
  13.3 0.7 %collective-permute-done.3.first_far_ref = bf16[128,256]{1,0:T(8,128)(2,1)S(1)} collective-permute-done((bf16[128,256]{1,0:T(8,128)(2,1)S(1)}, bf16[128,256]{1,0:T(8,128)(2,1)S(1)}, u32[]{:S(2)}, u32[]{:S(2)}) %collective-permute-start.3) | collective-permute-done | bytes 65568 | tf_op jit(solution)/shard_map/ppermute | solution.py:261
  14.2 9.4 %shard_map.86 = (bf16[192,512]{1,0:T(8,128)(2,1)}, f32[1536,128]{1,0:T(8,128)S(1)}, f32[1536,128]{1,0:T(8,128)S(1)}, bf16[1536,128]{1,0:T(8,128)(2,1)S(1)}, bf16[1536,128]{1,0:T(8,128)(2,1)S(1)}) custom-call(s32[1,27]{1,0:T(1,128)S(1)} %copy-done.1, bf16[512,384]{1,0:T(8,128)(2,1)S(1)} %get-tuple-element.17.own_ref, ...), custom_call_target="tpu_custom_call" | custom-call | tf_op jit(solution)/shard_map/pallas_call | solution.py:248
  24.2 1.2 %collective-permute-done.5 = bf16[1536,128]{1,0:T(8,128)(2,1)S(1)} collective-permute-done((bf16[1536,128]{1,0:T(8,128)(2,1)S(1)}, bf16[1536,128]{1,0:T(8,128)(2,1)S(1)}, u32[]{:S(2)}, u32[]{:S(2)}) %collective-permute-start.5) | collective-permute-done | bytes 393248 | tf_op jit(solution)/shard_map/ppermute | solution.py:261
  25.5 1.9 %collective-permute-start.6 = (bf16[768,128]{1,0:T(8,128)(2,1)S(1)}, bf16[768,128]{1,0:T(8,128)(2,1)S(1)}, u32[]{:S(2)}, u32[]{:S(2)}) collective-permute-start(bf16[768,128]{1,0:T(8,128)(2,1)S(1)} %dynamic-slice_convert_fusion.1), channel_id=1, source_target_pairs={{0,2},{2,0},{4,6},{6,4},{8,10},{10,8},{12,14},{14,12},{16,18},{18,... | collective-permute-start | bytes 589832 | tf_op jit(solution)/shard_map/ppermute | solution.py:261
  27.5 0.8 %collective-permute-start.14 = (bf16[768,128]{1,0:T(8,128)(2,1)S(1)}, bf16[768,128]{1,0:T(8,128)(2,1)S(1)}, u32[]{:S(2)}, u32[]{:S(2)}) collective-permute-start(bf16[768,128]{1,0:T(8,128)(2,1)S(1)} %dynamic-slice_convert_fusion), channel_id=1, source_target_pairs={{0,4},{2,6},{4,0},{6,2},{8,12},{10,14},{12,8},{14,10},{16,20},{18,... | collective-permute-start | bytes 589832 | tf_op jit(solution)/shard_map/ppermute | solution.py:261
  28.3 4.5 %collective-permute-done.6 = bf16[768,128]{1,0:T(8,128)(2,1)S(1)} collective-permute-done((bf16[768,128]{1,0:T(8,128)(2,1)S(1)}, bf16[768,128]{1,0:T(8,128)(2,1)S(1)}, u32[]{:S(2)}, u32[]{:S(2)}) %collective-permute-start.6) | collective-permute-done | bytes 196640 | tf_op jit(solution)/shard_map/ppermute | solution.py:261
  32.9 0.8 %collective-permute-start.7 = (bf16[384,128]{1,0:T(8,128)(2,1)S(1)}, bf16[384,128]{1,0:T(8,128)(2,1)S(1)}, u32[]{:S(2)}, u32[]{:S(2)}) collective-permute-start(bf16[384,128]{1,0:T(8,128)(2,1)S(1)} %dynamic-slice_convert_fusion.3), channel_id=1, source_target_pairs={{0,4},{2,6},{4,0},{6,2},{8,12},{10,14},{12,8},{14,10},{16,20},{18,... | collective-permute-start | bytes 294920 | tf_op jit(solution)/shard_map/ppermute | solution.py:261
  33.7 0.8 %collective-permute-done.14 = bf16[768,128]{1,0:T(8,128)(2,1)S(1)} collective-permute-done((bf16[768,128]{1,0:T(8,128)(2,1)S(1)}, bf16[768,128]{1,0:T(8,128)(2,1)S(1)}, u32[]{:S(2)}, u32[]{:S(2)}) %collective-permute-start.14) | collective-permute-done | bytes 196640 | tf_op jit(solution)/shard_map/ppermute | solution.py:261
  34.5 1.0 %collective-permute-start.15 = (bf16[384,128]{1,0:T(8,128)(2,1)S(1)}, bf16[384,128]{1,0:T(8,128)(2,1)S(1)}, u32[]{:S(2)}, u32[]{:S(2)}) collective-permute-start(bf16[384,128]{1,0:T(8,128)(2,1)S(1)} %dynamic-slice_convert_fusion.2), channel_id=1, source_target_pairs={{0,2},{2,0},{4,6},{6,4},{8,10},{10,8},{12,14},{14,12},{16,18},{18,... | collective-permute-start | bytes 294920 | tf_op jit(solution)/shard_map/ppermute | solution.py:261
  35.6 2.0 %collective-permute-done.7 = bf16[384,128]{1,0:T(8,128)(2,1)S(1)} collective-permute-done((bf16[384,128]{1,0:T(8,128)(2,1)S(1)}, bf16[384,128]{1,0:T(8,128)(2,1)S(1)}, u32[]{:S(2)}, u32[]{:S(2)}) %collective-permute-start.7) | collective-permute-done | bytes 98336 | tf_op jit(solution)/shard_map/ppermute | solution.py:261
  37.6 2.6 %collective-permute-start.8 = (bf16[384,128]{1,0:T(8,128)(2,1)S(1)}, bf16[384,128]{1,0:T(8,128)(2,1)S(1)}, u32[]{:S(2)}, u32[]{:S(2)}) collective-permute-start(bf16[384,128]{1,0:T(8,128)(2,1)S(1)} %add_convert_fusion.5), channel_id=1, source_target_pairs={{0,16},{2,18},{4,20},{6,22},{8,24},{10,26},{12,28},{14,30},{16,0},... | collective-permute-start | bytes 294920 | tf_op jit(solution)/shard_map/ppermute | solution.py:261
  40.3 1.6 %collective-permute-start.16 = (bf16[384,128]{1,0:T(8,128)(2,1)S(1)}, bf16[384,128]{1,0:T(8,128)(2,1)S(1)}, u32[]{:S(2)}, u32[]{:S(2)}) collective-permute-start(bf16[384,128]{1,0:T(8,128)(2,1)S(1)} %add_convert_fusion.2), channel_id=1, source_target_pairs={{0,8},{2,10},{4,12},{6,14},{8,0},{10,2},{12,4},{14,6},{16,24},{18,... | collective-permute-start | bytes 294920 | tf_op jit(solution)/shard_map/ppermute | solution.py:261
  41.8 1.4 %collective-permute-done.8 = bf16[384,128]{1,0:T(8,128)(2,1)S(1)} collective-permute-done((bf16[384,128]{1,0:T(8,128)(2,1)S(1)}, bf16[384,128]{1,0:T(8,128)(2,1)S(1)}, u32[]{:S(2)}, u32[]{:S(2)}) %collective-permute-start.8) | collective-permute-done | bytes 98336 | tf_op jit(solution)/shard_map/ppermute | solution.py:261
  43.3 1.8 %collective-permute-start.9 = (bf16[384,128]{1,0:T(8,128)(2,1)S(1)}, bf16[384,128]{1,0:T(8,128)(2,1)S(1)}, u32[]{:S(2)}, u32[]{:S(2)}) collective-permute-start(bf16[384,128]{1,0:T(8,128)(2,1)S(1)} %add_convert_fusion.4), channel_id=1, source_target_pairs={{0,8},{2,10},{4,12},{6,14},{8,0},{10,2},{12,4},{14,6},{16,24},{18,... | collective-permute-start | bytes 294920 | tf_op jit(solution)/shard_map/ppermute | solution.py:261
  45.5 3.1 %collective-permute-start.17 = (bf16[384,128]{1,0:T(8,128)(2,1)S(1)}, bf16[384,128]{1,0:T(8,128)(2,1)S(1)}, u32[]{:S(2)}, u32[]{:S(2)}) collective-permute-start(bf16[384,128]{1,0:T(8,128)(2,1)S(1)} %add_convert_fusion.1), channel_id=1, source_target_pairs={{0,16},{2,18},{4,20},{6,22},{8,24},{10,26},{12,28},{14,30},{16,0},... | collective-permute-start | bytes 294920 | tf_op jit(solution)/shard_map/ppermute | solution.py:261
  48.6 1.3 %collective-permute-start.10 = (bf16[384,128]{1,0:T(8,128)(2,1)S(1)}, bf16[384,128]{1,0:T(8,128)(2,1)S(1)}, u32[]{:S(2)}, u32[]{:S(2)}) collective-permute-start(bf16[384,128]{1,0:T(8,128)(2,1)S(1)} %add_convert_fusion.3), channel_id=1, source_target_pairs={{0,4},{2,6},{4,0},{6,2},{8,12},{10,14},{12,8},{14,10},{16,20},{18,... | collective-permute-start | bytes 294920 | tf_op jit(solution)/shard_map/ppermute | solution.py:261
  49.9 1.3 %collective-permute-done.17 = bf16[384,128]{1,0:T(8,128)(2,1)S(1)} collective-permute-done((bf16[384,128]{1,0:T(8,128)(2,1)S(1)}, bf16[384,128]{1,0:T(8,128)(2,1)S(1)}, u32[]{:S(2)}, u32[]{:S(2)}) %collective-permute-start.17) | collective-permute-done | bytes 98336 | tf_op jit(solution)/shard_map/ppermute | solution.py:261
  51.2 1.5 %collective-permute-start.18 = (bf16[384,128]{1,0:T(8,128)(2,1)S(1)}, bf16[384,128]{1,0:T(8,128)(2,1)S(1)}, u32[]{:S(2)}, u32[]{:S(2)}) collective-permute-start(bf16[384,128]{1,0:T(8,128)(2,1)S(1)} %add_convert_fusion), channel_id=1, source_target_pairs={{0,2},{2,0},{4,6},{6,4},{8,10},{10,8},{12,14},{14,12},{16,18},{18,... | collective-permute-start | bytes 294920 | tf_op jit(solution)/shard_map/ppermute | solution.py:261
  52.7 0.6 collective-permute-done.10
  53.4 1.3 %collective-permute-start.11 = (bf16[768,128]{1,0:T(8,128)(2,1)S(1)}, bf16[768,128]{1,0:T(8,128)(2,1)S(1)}, u32[]{:S(2)}, u32[]{:S(2)}) collective-permute-start(bf16[768,128]{1,0:T(8,128)(2,1)S(1)} %maximum_select_fusion.2), channel_id=1, source_target_pairs={{0,2},{2,0},{4,6},{6,4},{8,10},{10,8},{12,14},{14,12},{16,18},{18,... | collective-permute-start | bytes 589832 | tf_op jit(solution)/shard_map/ppermute | solution.py:261
  54.6 1.3 %collective-permute-done.18 = bf16[384,128]{1,0:T(8,128)(2,1)S(1)} collective-permute-done((bf16[384,128]{1,0:T(8,128)(2,1)S(1)}, bf16[384,128]{1,0:T(8,128)(2,1)S(1)}, u32[]{:S(2)}, u32[]{:S(2)}) %collective-permute-start.18) | collective-permute-done | bytes 98336 | tf_op jit(solution)/shard_map/ppermute | solution.py:261
  56.0 1.3 %collective-permute-start.19 = (bf16[768,128]{1,0:T(8,128)(2,1)S(1)}, bf16[768,128]{1,0:T(8,128)(2,1)S(1)}, u32[]{:S(2)}, u32[]{:S(2)}) collective-permute-start(bf16[768,128]{1,0:T(8,128)(2,1)S(1)} %maximum_select_fusion.3), channel_id=1, source_target_pairs={{0,4},{2,6},{4,0},{6,2},{8,12},{10,14},{12,8},{14,10},{16,20},{18,... | collective-permute-start | bytes 589832 | tf_op jit(solution)/shard_map/ppermute | solution.py:261
  57.2 1.9 %collective-permute-done.11 = bf16[768,128]{1,0:T(8,128)(2,1)S(1)} collective-permute-done((bf16[768,128]{1,0:T(8,128)(2,1)S(1)}, bf16[768,128]{1,0:T(8,128)(2,1)S(1)}, u32[]{:S(2)}, u32[]{:S(2)}) %collective-permute-start.11) | collective-permute-done | bytes 196640 | tf_op jit(solution)/shard_map/ppermute | solution.py:261
  59.3 2.4 %collective-permute-done.19 = bf16[768,128]{1,0:T(8,128)(2,1)S(1)} collective-permute-done((bf16[768,128]{1,0:T(8,128)(2,1)S(1)}, bf16[768,128]{1,0:T(8,128)(2,1)S(1)}, u32[]{:S(2)}, u32[]{:S(2)}) %collective-permute-start.19) | collective-permute-done | bytes 196640 | tf_op jit(solution)/shard_map/ppermute | solution.py:261
  61.9 1.7 %shard_map.87._ = f32[27,96,192]{2,1,0:T(8,128)} custom-call(bf16[1536,128]{1,0:T(8,128)(2,1)S(1)} %maximum_select_fusion.own_ref.own_p_ref, bf16[1536,128]{1,0:T(8,128)(2,1)S(1)} %collective-permute-done.12.other_ref.other_p_ref), custom_call_target="tpu_custom_call" | custom-call | flops 100000000 | bytes 4194304 | tf_op jit(solution)/shard_map/pallas_call | solution.py:248
  63.6 1.8 %shard_map.88 = (f32[27,96,96]{2,1,0:T(8,128)}, f32[27,96,192]{2,1,0:T(8,128)}) custom-call(bf16[1536,128]{1,0:T(8,128)(2,1)S(1)} %maximum_select_fusion.own_ref.own_p_ref, bf16[1536,128]{1,0:T(8,128)(2,1)S(1)} %collective-permute-done.12.other_ref.other_p_ref, ...), custom_call_target="tpu_custom_call", output_to_operand_aliasing={{1}: (4, {})} | custom-call | tf_op jit(solution)/shard_map/pallas_call | solution.py:248
  (41 shorter events, 3.7 us)
Async XLA Ops:
  1.7 0.7 %copy-start = (s32[1,512]{1,0:T(1,128)S(1)}, s32[1,512]{1,0:T(1,128)}, u32[]{:S(2)}) copy-start(s32[1,512]{1,0:T(1,128)} %occupancy_ref.1) | copy-start | bytes 6148
  2.3 8.2 %copy-start.2 = (bf16[27,96,192]{2,1,0:T(8,128)(2,1)S(1)}, bf16[27,96,192]{2,1,0:T(8,128)(2,1)}, u32[]{:S(2)}) copy-start(bf16[27,96,192]{2,1,0:T(8,128)(2,1)} %param.8) | copy-start | bytes 2985988
  2.6 11.7 %collective-permute-start = (bf16[512,384]{1,0:T(8,128)(2,1)S(1)}, bf16[512,384]{1,0:T(8,128)(2,1)S(1)}, u32[]{:S(2)}, u32[]{:S(2)}) collective-permute-start(bf16[512,384]{1,0:T(8,128)(2,1)S(1)} %get-tuple-element.17.own_ref), channel_id=1, source_target_pairs={{0,1},{1,0},{2,3},{3,2},{4,5},{5,4},{6,7},{7,6},{8,9},{9,8},{10,11... | collective-permute-start | bytes 1179656 | tf_op jit(solution)/shard_map/ppermute | solution.py:261
  3.1 7.7 %collective-permute-start.2 = (bf16[128,256]{1,0:T(8,128)(2,1)S(1)}, bf16[128,256]{1,0:T(8,128)(2,1)S(1)}, u32[]{:S(2)}, u32[]{:S(2)}) collective-permute-start(bf16[128,256]{1,0:T(8,128)(2,1)S(1)} %get-tuple-element.19), channel_id=1, source_target_pairs={{2,4},{6,8},{10,12},{14,16},{18,20},{22,24},{26,28},{4,2},{8,6},{1... | collective-permute-start | bytes 196616 | tf_op jit(solution)/shard_map/ppermute | solution.py:290
  3.7 9.1 %collective-permute-start.1 = (bf16[128,256]{1,0:T(8,128)(2,1)S(1)}, bf16[128,256]{1,0:T(8,128)(2,1)S(1)}, u32[]{:S(2)}, u32[]{:S(2)}) collective-permute-start(bf16[128,256]{1,0:T(8,128)(2,1)S(1)} %get-tuple-element.18), channel_id=1, source_target_pairs={{0,2},{2,0},{4,6},{6,4},{8,10},{10,8},{12,14},{14,12},{16,18},{18,... | collective-permute-start | bytes 196616 | tf_op jit(solution)/shard_map/ppermute | solution.py:291
  10.5 3.7 %copy-start.1 = (s32[1,27]{1,0:T(1,128)S(1)}, s32[1,27]{1,0:T(1,128)}, u32[]{:S(2)}) copy-start(s32[1,27]{1,0:T(1,128)} %neighbors_ref.1) | copy-start | bytes 328
  12.8 1.3 %collective-permute-start.3 = (bf16[128,256]{1,0:T(8,128)(2,1)S(1)}, bf16[128,256]{1,0:T(8,128)(2,1)S(1)}, u32[]{:S(2)}, u32[]{:S(2)}) collective-permute-start(bf16[128,256]{1,0:T(8,128)(2,1)S(1)} %collective-permute-done.1.first_ref), channel_id=1, source_target_pairs={{0,1},{1,0},{2,3},{3,2},{4,5},{5,4},{6,7},{7,6},{8,9},{9,8},{10,11... | collective-permute-start | bytes 196616 | tf_op jit(solution)/shard_map/ppermute | solution.py:261
  12.8 1.4 %collective-permute-start.4 = (bf16[128,256]{1,0:T(8,128)(2,1)S(1)}, bf16[128,256]{1,0:T(8,128)(2,1)S(1)}, u32[]{:S(2)}, u32[]{:S(2)}) collective-permute-start(bf16[128,256]{1,0:T(8,128)(2,1)S(1)} %collective-permute-done.2.second_ref), channel_id=1, source_target_pairs={{0,1},{1,0},{2,3},{3,2},{4,5},{5,4},{6,7},{7,6},{8,9},{9,8},{10,11... | collective-permute-start | bytes 196616 | tf_op jit(solution)/shard_map/ppermute | solution.py:261
  23.7 1.7 %collective-permute-start.5 = (bf16[1536,128]{1,0:T(8,128)(2,1)S(1)}, bf16[1536,128]{1,0:T(8,128)(2,1)S(1)}, u32[]{:S(2)}, u32[]{:S(2)}) collective-permute-start(bf16[1536,128]{1,0:T(8,128)(2,1)S(1)} %get-tuple-element.26), channel_id=1, source_target_pairs={{0,1},{1,0},{2,3},{3,2},{4,5},{5,4},{6,7},{7,6},{8,9},{9,8},{10,11... | collective-permute-start | bytes 1179656 | tf_op jit(solution)/shard_map/ppermute | solution.py:261
  24.0 3.4 %collective-permute-start.13 = (bf16[1536,128]{1,0:T(8,128)(2,1)S(1)}, bf16[1536,128]{1,0:T(8,128)(2,1)S(1)}, u32[]{:S(2)}, u32[]{:S(2)}) collective-permute-start(bf16[1536,128]{1,0:T(8,128)(2,1)S(1)} %get-tuple-element.28), channel_id=1, source_target_pairs={{0,1},{1,0},{2,3},{3,2},{4,5},{5,4},{6,7},{7,6},{8,9},{9,8},{10,11... | collective-permute-start | bytes 1179656 | tf_op jit(solution)/shard_map/ppermute | solution.py:261
  25.5 7.3 %collective-permute-start.6 = (bf16[768,128]{1,0:T(8,128)(2,1)S(1)}, bf16[768,128]{1,0:T(8,128)(2,1)S(1)}, u32[]{:S(2)}, u32[]{:S(2)}) collective-permute-start(bf16[768,128]{1,0:T(8,128)(2,1)S(1)} %dynamic-slice_convert_fusion.1), channel_id=1, source_target_pairs={{0,2},{2,0},{4,6},{6,4},{8,10},{10,8},{12,14},{14,12},{16,18},{18,... | collective-permute-start | bytes 589832 | tf_op jit(solution)/shard_map/ppermute | solution.py:261
  27.5 6.9 %collective-permute-start.14 = (bf16[768,128]{1,0:T(8,128)(2,1)S(1)}, bf16[768,128]{1,0:T(8,128)(2,1)S(1)}, u32[]{:S(2)}, u32[]{:S(2)}) collective-permute-start(bf16[768,128]{1,0:T(8,128)(2,1)S(1)} %dynamic-slice_convert_fusion), channel_id=1, source_target_pairs={{0,4},{2,6},{4,0},{6,2},{8,12},{10,14},{12,8},{14,10},{16,20},{18,... | collective-permute-start | bytes 589832 | tf_op jit(solution)/shard_map/ppermute | solution.py:261
  32.9 4.7 %collective-permute-start.7 = (bf16[384,128]{1,0:T(8,128)(2,1)S(1)}, bf16[384,128]{1,0:T(8,128)(2,1)S(1)}, u32[]{:S(2)}, u32[]{:S(2)}) collective-permute-start(bf16[384,128]{1,0:T(8,128)(2,1)S(1)} %dynamic-slice_convert_fusion.3), channel_id=1, source_target_pairs={{0,4},{2,6},{4,0},{6,2},{8,12},{10,14},{12,8},{14,10},{16,20},{18,... | collective-permute-start | bytes 294920 | tf_op jit(solution)/shard_map/ppermute | solution.py:261
  34.5 5.7 %collective-permute-start.15 = (bf16[384,128]{1,0:T(8,128)(2,1)S(1)}, bf16[384,128]{1,0:T(8,128)(2,1)S(1)}, u32[]{:S(2)}, u32[]{:S(2)}) collective-permute-start(bf16[384,128]{1,0:T(8,128)(2,1)S(1)} %dynamic-slice_convert_fusion.2), channel_id=1, source_target_pairs={{0,2},{2,0},{4,6},{6,4},{8,10},{10,8},{12,14},{14,12},{16,18},{18,... | collective-permute-start | bytes 294920 | tf_op jit(solution)/shard_map/ppermute | solution.py:261
  37.6 5.6 %collective-permute-start.8 = (bf16[384,128]{1,0:T(8,128)(2,1)S(1)}, bf16[384,128]{1,0:T(8,128)(2,1)S(1)}, u32[]{:S(2)}, u32[]{:S(2)}) collective-permute-start(bf16[384,128]{1,0:T(8,128)(2,1)S(1)} %add_convert_fusion.5), channel_id=1, source_target_pairs={{0,16},{2,18},{4,20},{6,22},{8,24},{10,26},{12,28},{14,30},{16,0},... | collective-permute-start | bytes 294920 | tf_op jit(solution)/shard_map/ppermute | solution.py:261
  40.3 5.2 %collective-permute-start.16 = (bf16[384,128]{1,0:T(8,128)(2,1)S(1)}, bf16[384,128]{1,0:T(8,128)(2,1)S(1)}, u32[]{:S(2)}, u32[]{:S(2)}) collective-permute-start(bf16[384,128]{1,0:T(8,128)(2,1)S(1)} %add_convert_fusion.2), channel_id=1, source_target_pairs={{0,8},{2,10},{4,12},{6,14},{8,0},{10,2},{12,4},{14,6},{16,24},{18,... | collective-permute-start | bytes 294920 | tf_op jit(solution)/shard_map/ppermute | solution.py:261
  43.3 5.3 %collective-permute-start.9 = (bf16[384,128]{1,0:T(8,128)(2,1)S(1)}, bf16[384,128]{1,0:T(8,128)(2,1)S(1)}, u32[]{:S(2)}, u32[]{:S(2)}) collective-permute-start(bf16[384,128]{1,0:T(8,128)(2,1)S(1)} %add_convert_fusion.4), channel_id=1, source_target_pairs={{0,8},{2,10},{4,12},{6,14},{8,0},{10,2},{12,4},{14,6},{16,24},{18,... | collective-permute-start | bytes 294920 | tf_op jit(solution)/shard_map/ppermute | solution.py:261
  45.5 5.7 %collective-permute-start.17 = (bf16[384,128]{1,0:T(8,128)(2,1)S(1)}, bf16[384,128]{1,0:T(8,128)(2,1)S(1)}, u32[]{:S(2)}, u32[]{:S(2)}) collective-permute-start(bf16[384,128]{1,0:T(8,128)(2,1)S(1)} %add_convert_fusion.1), channel_id=1, source_target_pairs={{0,16},{2,18},{4,20},{6,22},{8,24},{10,26},{12,28},{14,30},{16,0},... | collective-permute-start | bytes 294920 | tf_op jit(solution)/shard_map/ppermute | solution.py:261
  48.6 4.7 %collective-permute-start.10 = (bf16[384,128]{1,0:T(8,128)(2,1)S(1)}, bf16[384,128]{1,0:T(8,128)(2,1)S(1)}, u32[]{:S(2)}, u32[]{:S(2)}) collective-permute-start(bf16[384,128]{1,0:T(8,128)(2,1)S(1)} %add_convert_fusion.3), channel_id=1, source_target_pairs={{0,4},{2,6},{4,0},{6,2},{8,12},{10,14},{12,8},{14,10},{16,20},{18,... | collective-permute-start | bytes 294920 | tf_op jit(solution)/shard_map/ppermute | solution.py:261
  51.2 4.7 %collective-permute-start.18 = (bf16[384,128]{1,0:T(8,128)(2,1)S(1)}, bf16[384,128]{1,0:T(8,128)(2,1)S(1)}, u32[]{:S(2)}, u32[]{:S(2)}) collective-permute-start(bf16[384,128]{1,0:T(8,128)(2,1)S(1)} %add_convert_fusion), channel_id=1, source_target_pairs={{0,2},{2,0},{4,6},{6,4},{8,10},{10,8},{12,14},{14,12},{16,18},{18,... | collective-permute-start | bytes 294920 | tf_op jit(solution)/shard_map/ppermute | solution.py:261
  53.4 5.7 %collective-permute-start.11 = (bf16[768,128]{1,0:T(8,128)(2,1)S(1)}, bf16[768,128]{1,0:T(8,128)(2,1)S(1)}, u32[]{:S(2)}, u32[]{:S(2)}) collective-permute-start(bf16[768,128]{1,0:T(8,128)(2,1)S(1)} %maximum_select_fusion.2), channel_id=1, source_target_pairs={{0,2},{2,0},{4,6},{6,4},{8,10},{10,8},{12,14},{14,12},{16,18},{18,... | collective-permute-start | bytes 589832 | tf_op jit(solution)/shard_map/ppermute | solution.py:261
  56.0 5.7 %collective-permute-start.19 = (bf16[768,128]{1,0:T(8,128)(2,1)S(1)}, bf16[768,128]{1,0:T(8,128)(2,1)S(1)}, u32[]{:S(2)}, u32[]{:S(2)}) collective-permute-start(bf16[768,128]{1,0:T(8,128)(2,1)S(1)} %maximum_select_fusion.3), channel_id=1, source_target_pairs={{0,4},{2,6},{4,0},{6,2},{8,12},{10,14},{12,8},{14,10},{16,20},{18,... | collective-permute-start | bytes 589832 | tf_op jit(solution)/shard_map/ppermute | solution.py:261
  59.2 2.7 %collective-permute-start.12 = (bf16[1536,128]{1,0:T(8,128)(2,1)S(1)}, bf16[1536,128]{1,0:T(8,128)(2,1)S(1)}, u32[]{:S(2)}, u32[]{:S(2)}) collective-permute-start(bf16[1536,128]{1,0:T(8,128)(2,1)S(1)} %maximum_select_fusion.own_ref.own_p_ref), channel_id=1, source_target_pairs={{0,1},{1,0},{2,3},{3,2},{4,5},{5,4},{6,7},{7,6},{8,9},{9,8},{10,11... | collective-permute-start | bytes 1179656 | tf_op jit(solution)/shard_map/ppermute | solution.py:261
  61.8 1.8 %collective-permute-start.20 = (bf16[1536,128]{1,0:T(8,128)(2,1)S(1)}, bf16[1536,128]{1,0:T(8,128)(2,1)S(1)}, u32[]{:S(2)}, u32[]{:S(2)}) collective-permute-start(bf16[1536,128]{1,0:T(8,128)(2,1)S(1)} %maximum_select_fusion.1.own_q_ref), channel_id=1, source_target_pairs={{0,1},{1,0},{2,3},{3,2},{4,5},{5,4},{6,7},{7,6},{8,9},{9,8},{10,11... | collective-permute-start | bytes 1179656 | tf_op jit(solution)/shard_map/ppermute | solution.py:261

commit v8 on v7

--- a/solution.py
+++ b/solution.py
@@ -157,6 +157,11 @@
 
     first_one = 3 * (-(-27 // 4)) * outs
     turned_out = turned_ref[...]
+    spare_rows = 3 * (-(-27 // 4) - 1)
+    total[spare_rows * outs : first_one, channels:] = jnp.zeros((3 * outs, LANES - channels), F32)
+    total[first_one + spare_rows * channels : first_one + (spare_rows + 3) * channels, channels:] = jnp.zeros(
+        (3 * channels, LANES - channels), F32
+    )
     stage(hidden_s, hidden_w, 0, 0, 7)
     output = None
     for chunk in CHUNKS:

time: 65.6 us -> 65.7 us (level)
  no operation moved by 1% of the time
where the time goes in v8:
time: 65.7 us; the launch traced here: 65.4 us
  starting transfers between devices  26.7 us (41%)
  waiting for transfers between devices  20.7 us (32%)
  Pallas kernels  13.2 us (20%)
  local copies, waits for them, and re-layouts  2.39 us (4%)
  other arithmetic  1.71 us (3%)
  between operations  0.83 us (1%)
    ppermute x19, starting transfers between devices, exchanged(): lax.ppermute(value, axis, [(i, i ^ mask) for i in range(lax.axis_size(axi...  20.6 us
    ppermute x19, waiting for transfers between devices, exchanged(): lax.ppermute(value, axis, [(i, i ^ mask) for i in range(lax.axis_size(axi...  18.7 us
    pallas_call x4, Pallas kernels, call(): pl.pallas_call(kernel, out_shape=out_shape, in_specs=[pl.BlockSpec(memory...  13.2 us
    ppermute x1, starting transfers between devices, shards(): first = lax.ppermute(first, 'region', [(i, i ^ 1) for i in range(regions)])  5.44 us
    ppermute x1, waiting for transfers between devices, shards(): first = lax.ppermute(first, 'region', [(i, i ^ 1) for i in range(regions)])  1.99 us
  transfers between devices with their start and end apart: 21, of which 14 were waited for; matrix products, arithmetic and copies ran while one was open for 4% of the time, Pallas kernels for 3%

profile of v8, /device:TPU:0, one launch (start us, length us, event | category | flops | bytes accessed | tf_op | source)
XLA Modules:
  0.0 65.4 jit_solution(411328429025929253)
XLA Ops:
  0.6 1.0 %pad_add_fusion.stack_ref = bf16[384,512]{1,0:T(8,128)(2,1)S(1)} fusion(bf16[192,512]{1,0:T(8,128)(2,1)} %param.11, bf16[96,512]{1,0:T(8,128)(2,1)} %param.6), kind=kLoop, calls=%fused_computation.8 | loop fusion | flops 786432 | bytes 688128 | tf_op jit(solution)/shard_map/add | solution.py:287
  1.7 0.7 %copy-done = s32[1,512]{1,0:T(1,128)S(1)} copy-done((s32[1,512]{1,0:T(1,128)S(1)}, s32[1,512]{1,0:T(1,128)}, u32[]{:S(2)}) %copy-start) | copy-done | bytes 2072
  3.1 0.7 collective-permute-start.2
  3.7 5.4 %collective-permute-start.1 = (bf16[128,256]{1,0:T(8,128)(2,1)S(1)}, bf16[128,256]{1,0:T(8,128)(2,1)S(1)}, u32[]{:S(2)}, u32[]{:S(2)}) collective-permute-start(bf16[128,256]{1,0:T(8,128)(2,1)S(1)} %get-tuple-element.18), channel_id=1, source_target_pairs={{0,2},{2,0},{4,6},{6,4},{8,10},{10,8},{12,14},{14,12},{16,18},{18,... | collective-permute-start | bytes 196616 | tf_op jit(solution)/shard_map/ppermute | solution.py:296
  9.2 1.3 %pad.18.one_ref = bf16[27,128,96]{2,1,0:T(8,128)(2,1)S(1)} pad(bf16[27,96,96]{2,1,0:T(8,128)(2,1)} %param.7, bf16[]{:T(256)} %constant.66.clone.1), padding=0_0x0_32x0_0 | pad | bytes 1161218 | tf_op jit(solution)/shard_map/jit(_pad)/pad | solution.py:298
  10.8 2.0 %collective-permute-done.1.first_ref = bf16[128,256]{1,0:T(8,128)(2,1)S(1)} collective-permute-done((bf16[128,256]{1,0:T(8,128)(2,1)S(1)}, bf16[128,256]{1,0:T(8,128)(2,1)S(1)}, u32[]{:S(2)}, u32[]{:S(2)}) %collective-permute-start.1) | collective-permute-done | bytes 65568 | tf_op jit(solution)/shard_map/ppermute | solution.py:296
  13.3 0.7 %collective-permute-done.3.first_far_ref = bf16[128,256]{1,0:T(8,128)(2,1)S(1)} collective-permute-done((bf16[128,256]{1,0:T(8,128)(2,1)S(1)}, bf16[128,256]{1,0:T(8,128)(2,1)S(1)}, u32[]{:S(2)}, u32[]{:S(2)}) %collective-permute-start.3) | collective-permute-done | bytes 65568 | tf_op jit(solution)/shard_map/ppermute | solution.py:266
  14.2 9.5 %shard_map.86 = (bf16[192,512]{1,0:T(8,128)(2,1)}, f32[1536,128]{1,0:T(8,128)S(1)}, f32[1536,128]{1,0:T(8,128)S(1)}, bf16[1536,128]{1,0:T(8,128)(2,1)S(1)}, bf16[1536,128]{1,0:T(8,128)(2,1)S(1)}) custom-call(s32[1,27]{1,0:T(1,128)S(1)} %copy-done.1, bf16[512,384]{1,0:T(8,128)(2,1)S(1)} %get-tuple-element.17.own_ref, ...), custom_call_target="tpu_custom_call" | custom-call | tf_op jit(solution)/shard_map/pallas_call | solution.py:253
  24.2 1.2 %collective-permute-done.5 = bf16[1536,128]{1,0:T(8,128)(2,1)S(1)} collective-permute-done((bf16[1536,128]{1,0:T(8,128)(2,1)S(1)}, bf16[1536,128]{1,0:T(8,128)(2,1)S(1)}, u32[]{:S(2)}, u32[]{:S(2)}) %collective-permute-start.5) | collective-permute-done | bytes 393248 | tf_op jit(solution)/shard_map/ppermute | solution.py:266
  25.5 1.9 %collective-permute-start.6 = (bf16[768,128]{1,0:T(8,128)(2,1)S(1)}, bf16[768,128]{1,0:T(8,128)(2,1)S(1)}, u32[]{:S(2)}, u32[]{:S(2)}) collective-permute-start(bf16[768,128]{1,0:T(8,128)(2,1)S(1)} %dynamic-slice_convert_fusion.1), channel_id=1, source_target_pairs={{0,2},{2,0},{4,6},{6,4},{8,10},{10,8},{12,14},{14,12},{16,18},{18,... | collective-permute-start | bytes 589832 | tf_op jit(solution)/shard_map/ppermute | solution.py:266
  27.6 0.8 %collective-permute-start.14 = (bf16[768,128]{1,0:T(8,128)(2,1)S(1)}, bf16[768,128]{1,0:T(8,128)(2,1)S(1)}, u32[]{:S(2)}, u32[]{:S(2)}) collective-permute-start(bf16[768,128]{1,0:T(8,128)(2,1)S(1)} %dynamic-slice_convert_fusion), channel_id=1, source_target_pairs={{0,4},{2,6},{4,0},{6,2},{8,12},{10,14},{12,8},{14,10},{16,20},{18,... | collective-permute-start | bytes 589832 | tf_op jit(solution)/shard_map/ppermute | solution.py:266
  28.4 4.5 %collective-permute-done.6 = bf16[768,128]{1,0:T(8,128)(2,1)S(1)} collective-permute-done((bf16[768,128]{1,0:T(8,128)(2,1)S(1)}, bf16[768,128]{1,0:T(8,128)(2,1)S(1)}, u32[]{:S(2)}, u32[]{:S(2)}) %collective-permute-start.6) | collective-permute-done | bytes 196640 | tf_op jit(solution)/shard_map/ppermute | solution.py:266
  32.9 0.8 %collective-permute-start.7 = (bf16[384,128]{1,0:T(8,128)(2,1)S(1)}, bf16[384,128]{1,0:T(8,128)(2,1)S(1)}, u32[]{:S(2)}, u32[]{:S(2)}) collective-permute-start(bf16[384,128]{1,0:T(8,128)(2,1)S(1)} %dynamic-slice_convert_fusion.3), channel_id=1, source_target_pairs={{0,4},{2,6},{4,0},{6,2},{8,12},{10,14},{12,8},{14,10},{16,20},{18,... | collective-permute-start | bytes 294920 | tf_op jit(solution)/shard_map/ppermute | solution.py:266
  33.7 0.8 %collective-permute-done.14 = bf16[768,128]{1,0:T(8,128)(2,1)S(1)} collective-permute-done((bf16[768,128]{1,0:T(8,128)(2,1)S(1)}, bf16[768,128]{1,0:T(8,128)(2,1)S(1)}, u32[]{:S(2)}, u32[]{:S(2)}) %collective-permute-start.14) | collective-permute-done | bytes 196640 | tf_op jit(solution)/shard_map/ppermute | solution.py:266
  34.5 1.0 %collective-permute-start.15 = (bf16[384,128]{1,0:T(8,128)(2,1)S(1)}, bf16[384,128]{1,0:T(8,128)(2,1)S(1)}, u32[]{:S(2)}, u32[]{:S(2)}) collective-permute-start(bf16[384,128]{1,0:T(8,128)(2,1)S(1)} %dynamic-slice_convert_fusion.2), channel_id=1, source_target_pairs={{0,2},{2,0},{4,6},{6,4},{8,10},{10,8},{12,14},{14,12},{16,18},{18,... | collective-permute-start | bytes 294920 | tf_op jit(solution)/shard_map/ppermute | solution.py:266
  35.6 2.0 %collective-permute-done.7 = bf16[384,128]{1,0:T(8,128)(2,1)S(1)} collective-permute-done((bf16[384,128]{1,0:T(8,128)(2,1)S(1)}, bf16[384,128]{1,0:T(8,128)(2,1)S(1)}, u32[]{:S(2)}, u32[]{:S(2)}) %collective-permute-start.7) | collective-permute-done | bytes 98336 | tf_op jit(solution)/shard_map/ppermute | solution.py:266
  37.6 2.7 %collective-permute-start.8 = (bf16[384,128]{1,0:T(8,128)(2,1)S(1)}, bf16[384,128]{1,0:T(8,128)(2,1)S(1)}, u32[]{:S(2)}, u32[]{:S(2)}) collective-permute-start(bf16[384,128]{1,0:T(8,128)(2,1)S(1)} %add_convert_fusion.5), channel_id=1, source_target_pairs={{0,16},{2,18},{4,20},{6,22},{8,24},{10,26},{12,28},{14,30},{16,0},... | collective-permute-start | bytes 294920 | tf_op jit(solution)/shard_map/ppermute | solution.py:266
  40.3 1.5 %collective-permute-start.16 = (bf16[384,128]{1,0:T(8,128)(2,1)S(1)}, bf16[384,128]{1,0:T(8,128)(2,1)S(1)}, u32[]{:S(2)}, u32[]{:S(2)}) collective-permute-start(bf16[384,128]{1,0:T(8,128)(2,1)S(1)} %add_convert_fusion.2), channel_id=1, source_target_pairs={{0,8},{2,10},{4,12},{6,14},{8,0},{10,2},{12,4},{14,6},{16,24},{18,... | collective-permute-start | bytes 294920 | tf_op jit(solution)/shard_map/ppermute | solution.py:266
  41.8 1.4 %collective-permute-done.8 = bf16[384,128]{1,0:T(8,128)(2,1)S(1)} collective-permute-done((bf16[384,128]{1,0:T(8,128)(2,1)S(1)}, bf16[384,128]{1,0:T(8,128)(2,1)S(1)}, u32[]{:S(2)}, u32[]{:S(2)}) %collective-permute-start.8) | collective-permute-done | bytes 98336 | tf_op jit(solution)/shard_map/ppermute | solution.py:266
  43.3 1.8 %collective-permute-start.9 = (bf16[384,128]{1,0:T(8,128)(2,1)S(1)}, bf16[384,128]{1,0:T(8,128)(2,1)S(1)}, u32[]{:S(2)}, u32[]{:S(2)}) collective-permute-start(bf16[384,128]{1,0:T(8,128)(2,1)S(1)} %add_convert_fusion.4), channel_id=1, source_target_pairs={{0,8},{2,10},{4,12},{6,14},{8,0},{10,2},{12,4},{14,6},{16,24},{18,... | collective-permute-start | bytes 294920 | tf_op jit(solution)/shard_map/ppermute | solution.py:266
  45.5 3.1 %collective-permute-start.17 = (bf16[384,128]{1,0:T(8,128)(2,1)S(1)}, bf16[384,128]{1,0:T(8,128)(2,1)S(1)}, u32[]{:S(2)}, u32[]{:S(2)}) collective-permute-start(bf16[384,128]{1,0:T(8,128)(2,1)S(1)} %add_convert_fusion.1), channel_id=1, source_target_pairs={{0,16},{2,18},{4,20},{6,22},{8,24},{10,26},{12,28},{14,30},{16,0},... | collective-permute-start | bytes 294920 | tf_op jit(solution)/shard_map/ppermute | solution.py:266
  48.6 1.3 %collective-permute-start.10 = (bf16[384,128]{1,0:T(8,128)(2,1)S(1)}, bf16[384,128]{1,0:T(8,128)(2,1)S(1)}, u32[]{:S(2)}, u32[]{:S(2)}) collective-permute-start(bf16[384,128]{1,0:T(8,128)(2,1)S(1)} %add_convert_fusion.3), channel_id=1, source_target_pairs={{0,4},{2,6},{4,0},{6,2},{8,12},{10,14},{12,8},{14,10},{16,20},{18,... | collective-permute-start | bytes 294920 | tf_op jit(solution)/shard_map/ppermute | solution.py:266
  49.9 1.3 %collective-permute-done.17 = bf16[384,128]{1,0:T(8,128)(2,1)S(1)} collective-permute-done((bf16[384,128]{1,0:T(8,128)(2,1)S(1)}, bf16[384,128]{1,0:T(8,128)(2,1)S(1)}, u32[]{:S(2)}, u32[]{:S(2)}) %collective-permute-start.17) | collective-permute-done | bytes 98336 | tf_op jit(solution)/shard_map/ppermute | solution.py:266
  51.2 1.5 %collective-permute-start.18 = (bf16[384,128]{1,0:T(8,128)(2,1)S(1)}, bf16[384,128]{1,0:T(8,128)(2,1)S(1)}, u32[]{:S(2)}, u32[]{:S(2)}) collective-permute-start(bf16[384,128]{1,0:T(8,128)(2,1)S(1)} %add_convert_fusion), channel_id=1, source_target_pairs={{0,2},{2,0},{4,6},{6,4},{8,10},{10,8},{12,14},{14,12},{16,18},{18,... | collective-permute-start | bytes 294920 | tf_op jit(solution)/shard_map/ppermute | solution.py:266
  52.7 0.6 collective-permute-done.10
  53.4 1.3 %collective-permute-start.11 = (bf16[768,128]{1,0:T(8,128)(2,1)S(1)}, bf16[768,128]{1,0:T(8,128)(2,1)S(1)}, u32[]{:S(2)}, u32[]{:S(2)}) collective-permute-start(bf16[768,128]{1,0:T(8,128)(2,1)S(1)} %maximum_select_fusion.2), channel_id=1, source_target_pairs={{0,2},{2,0},{4,6},{6,4},{8,10},{10,8},{12,14},{14,12},{16,18},{18,... | collective-permute-start | bytes 589832 | tf_op jit(solution)/shard_map/ppermute | solution.py:266
  54.6 1.3 %collective-permute-done.18 = bf16[384,128]{1,0:T(8,128)(2,1)S(1)} collective-permute-done((bf16[384,128]{1,0:T(8,128)(2,1)S(1)}, bf16[384,128]{1,0:T(8,128)(2,1)S(1)}, u32[]{:S(2)}, u32[]{:S(2)}) %collective-permute-start.18) | collective-permute-done | bytes 98336 | tf_op jit(solution)/shard_map/ppermute | solution.py:266
  56.0 1.3 %collective-permute-start.19 = (bf16[768,128]{1,0:T(8,128)(2,1)S(1)}, bf16[768,128]{1,0:T(8,128)(2,1)S(1)}, u32[]{:S(2)}, u32[]{:S(2)}) collective-permute-start(bf16[768,128]{1,0:T(8,128)(2,1)S(1)} %maximum_select_fusion.3), channel_id=1, source_target_pairs={{0,4},{2,6},{4,0},{6,2},{8,12},{10,14},{12,8},{14,10},{16,20},{18,... | collective-permute-start | bytes 589832 | tf_op jit(solution)/shard_map/ppermute | solution.py:266
  57.3 1.9 %collective-permute-done.11 = bf16[768,128]{1,0:T(8,128)(2,1)S(1)} collective-permute-done((bf16[768,128]{1,0:T(8,128)(2,1)S(1)}, bf16[768,128]{1,0:T(8,128)(2,1)S(1)}, u32[]{:S(2)}, u32[]{:S(2)}) %collective-permute-start.11) | collective-permute-done | bytes 196640 | tf_op jit(solution)/shard_map/ppermute | solution.py:266
  59.3 2.4 %collective-permute-done.19 = bf16[768,128]{1,0:T(8,128)(2,1)S(1)} collective-permute-done((bf16[768,128]{1,0:T(8,128)(2,1)S(1)}, bf16[768,128]{1,0:T(8,128)(2,1)S(1)}, u32[]{:S(2)}, u32[]{:S(2)}) %collective-permute-start.19) | collective-permute-done | bytes 196640 | tf_op jit(solution)/shard_map/ppermute | solution.py:266
  61.9 1.7 %shard_map.87._ = f32[27,96,192]{2,1,0:T(8,128)} custom-call(bf16[1536,128]{1,0:T(8,128)(2,1)S(1)} %maximum_select_fusion.own_ref.own_p_ref, bf16[1536,128]{1,0:T(8,128)(2,1)S(1)} %collective-permute-done.12.other_ref.other_p_ref), custom_call_target="tpu_custom_call" | custom-call | flops 100000000 | bytes 4194304 | tf_op jit(solution)/shard_map/pallas_call | solution.py:253
  63.6 1.8 %shard_map.88 = (f32[27,96,96]{2,1,0:T(8,128)}, f32[27,96,192]{2,1,0:T(8,128)}) custom-call(bf16[1536,128]{1,0:T(8,128)(2,1)S(1)} %maximum_select_fusion.own_ref.own_p_ref, bf16[1536,128]{1,0:T(8,128)(2,1)S(1)} %collective-permute-done.12.other_ref.other_p_ref, ...), custom_call_target="tpu_custom_call", output_to_operand_aliasing={{1}: (4, {})} | custom-call | tf_op jit(solution)/shard_map/pallas_call | solution.py:253
  (41 shorter events, 3.6 us)
Async XLA Ops:
  1.7 0.7 %copy-start = (s32[1,512]{1,0:T(1,128)S(1)}, s32[1,512]{1,0:T(1,128)}, u32[]{:S(2)}) copy-start(s32[1,512]{1,0:T(1,128)} %occupancy_ref.1) | copy-start | bytes 6148
  2.3 8.2 %copy-start.2 = (bf16[27,96,192]{2,1,0:T(8,128)(2,1)S(1)}, bf16[27,96,192]{2,1,0:T(8,128)(2,1)}, u32[]{:S(2)}) copy-start(bf16[27,96,192]{2,1,0:T(8,128)(2,1)} %param.8) | copy-start | bytes 2985988
  2.6 11.7 %collective-permute-start = (bf16[512,384]{1,0:T(8,128)(2,1)S(1)}, bf16[512,384]{1,0:T(8,128)(2,1)S(1)}, u32[]{:S(2)}, u32[]{:S(2)}) collective-permute-start(bf16[512,384]{1,0:T(8,128)(2,1)S(1)} %get-tuple-element.17.own_ref), channel_id=1, source_target_pairs={{0,1},{1,0},{2,3},{3,2},{4,5},{5,4},{6,7},{7,6},{8,9},{9,8},{10,11... | collective-permute-start | bytes 1179656 | tf_op jit(solution)/shard_map/ppermute | solution.py:266
  3.1 7.7 %collective-permute-start.2 = (bf16[128,256]{1,0:T(8,128)(2,1)S(1)}, bf16[128,256]{1,0:T(8,128)(2,1)S(1)}, u32[]{:S(2)}, u32[]{:S(2)}) collective-permute-start(bf16[128,256]{1,0:T(8,128)(2,1)S(1)} %get-tuple-element.19), channel_id=1, source_target_pairs={{2,4},{6,8},{10,12},{14,16},{18,20},{22,24},{26,28},{4,2},{8,6},{1... | collective-permute-start | bytes 196616 | tf_op jit(solution)/shard_map/ppermute | solution.py:295
  3.7 9.1 %collective-permute-start.1 = (bf16[128,256]{1,0:T(8,128)(2,1)S(1)}, bf16[128,256]{1,0:T(8,128)(2,1)S(1)}, u32[]{:S(2)}, u32[]{:S(2)}) collective-permute-start(bf16[128,256]{1,0:T(8,128)(2,1)S(1)} %get-tuple-element.18), channel_id=1, source_target_pairs={{0,2},{2,0},{4,6},{6,4},{8,10},{10,8},{12,14},{14,12},{16,18},{18,... | collective-permute-start | bytes 196616 | tf_op jit(solution)/shard_map/ppermute | solution.py:296
  10.5 3.7 %copy-start.1 = (s32[1,27]{1,0:T(1,128)S(1)}, s32[1,27]{1,0:T(1,128)}, u32[]{:S(2)}) copy-start(s32[1,27]{1,0:T(1,128)} %neighbors_ref.1) | copy-start | bytes 328
  12.8 1.3 %collective-permute-start.3 = (bf16[128,256]{1,0:T(8,128)(2,1)S(1)}, bf16[128,256]{1,0:T(8,128)(2,1)S(1)}, u32[]{:S(2)}, u32[]{:S(2)}) collective-permute-start(bf16[128,256]{1,0:T(8,128)(2,1)S(1)} %collective-permute-done.1.first_ref), channel_id=1, source_target_pairs={{0,1},{1,0},{2,3},{3,2},{4,5},{5,4},{6,7},{7,6},{8,9},{9,8},{10,11... | collective-permute-start | bytes 196616 | tf_op jit(solution)/shard_map/ppermute | solution.py:266
  12.8 1.4 %collective-permute-start.4 = (bf16[128,256]{1,0:T(8,128)(2,1)S(1)}, bf16[128,256]{1,0:T(8,128)(2,1)S(1)}, u32[]{:S(2)}, u32[]{:S(2)}) collective-permute-start(bf16[128,256]{1,0:T(8,128)(2,1)S(1)} %collective-permute-done.2.second_ref), channel_id=1, source_target_pairs={{0,1},{1,0},{2,3},{3,2},{4,5},{5,4},{6,7},{7,6},{8,9},{9,8},{10,11... | collective-permute-start | bytes 196616 | tf_op jit(solution)/shard_map/ppermute | solution.py:266
  23.7 1.7 %collective-permute-start.5 = (bf16[1536,128]{1,0:T(8,128)(2,1)S(1)}, bf16[1536,128]{1,0:T(8,128)(2,1)S(1)}, u32[]{:S(2)}, u32[]{:S(2)}) collective-permute-start(bf16[1536,128]{1,0:T(8,128)(2,1)S(1)} %get-tuple-element.26), channel_id=1, source_target_pairs={{0,1},{1,0},{2,3},{3,2},{4,5},{5,4},{6,7},{7,6},{8,9},{9,8},{10,11... | collective-permute-start | bytes 1179656 | tf_op jit(solution)/shard_map/ppermute | solution.py:266
  24.0 3.4 %collective-permute-start.13 = (bf16[1536,128]{1,0:T(8,128)(2,1)S(1)}, bf16[1536,128]{1,0:T(8,128)(2,1)S(1)}, u32[]{:S(2)}, u32[]{:S(2)}) collective-permute-start(bf16[1536,128]{1,0:T(8,128)(2,1)S(1)} %get-tuple-element.28), channel_id=1, source_target_pairs={{0,1},{1,0},{2,3},{3,2},{4,5},{5,4},{6,7},{7,6},{8,9},{9,8},{10,11... | collective-permute-start | bytes 1179656 | tf_op jit(solution)/shard_map/ppermute | solution.py:266
  25.5 7.3 %collective-permute-start.6 = (bf16[768,128]{1,0:T(8,128)(2,1)S(1)}, bf16[768,128]{1,0:T(8,128)(2,1)S(1)}, u32[]{:S(2)}, u32[]{:S(2)}) collective-permute-start(bf16[768,128]{1,0:T(8,128)(2,1)S(1)} %dynamic-slice_convert_fusion.1), channel_id=1, source_target_pairs={{0,2},{2,0},{4,6},{6,4},{8,10},{10,8},{12,14},{14,12},{16,18},{18,... | collective-permute-start | bytes 589832 | tf_op jit(solution)/shard_map/ppermute | solution.py:266
  27.6 6.9 %collective-permute-start.14 = (bf16[768,128]{1,0:T(8,128)(2,1)S(1)}, bf16[768,128]{1,0:T(8,128)(2,1)S(1)}, u32[]{:S(2)}, u32[]{:S(2)}) collective-permute-start(bf16[768,128]{1,0:T(8,128)(2,1)S(1)} %dynamic-slice_convert_fusion), channel_id=1, source_target_pairs={{0,4},{2,6},{4,0},{6,2},{8,12},{10,14},{12,8},{14,10},{16,20},{18,... | collective-permute-start | bytes 589832 | tf_op jit(solution)/shard_map/ppermute | solution.py:266
  32.9 4.7 %collective-permute-start.7 = (bf16[384,128]{1,0:T(8,128)(2,1)S(1)}, bf16[384,128]{1,0:T(8,128)(2,1)S(1)}, u32[]{:S(2)}, u32[]{:S(2)}) collective-permute-start(bf16[384,128]{1,0:T(8,128)(2,1)S(1)} %dynamic-slice_convert_fusion.3), channel_id=1, source_target_pairs={{0,4},{2,6},{4,0},{6,2},{8,12},{10,14},{12,8},{14,10},{16,20},{18,... | collective-permute-start | bytes 294920 | tf_op jit(solution)/shard_map/ppermute | solution.py:266
  34.5 5.7 %collective-permute-start.15 = (bf16[384,128]{1,0:T(8,128)(2,1)S(1)}, bf16[384,128]{1,0:T(8,128)(2,1)S(1)}, u32[]{:S(2)}, u32[]{:S(2)}) collective-permute-start(bf16[384,128]{1,0:T(8,128)(2,1)S(1)} %dynamic-slice_convert_fusion.2), channel_id=1, source_target_pairs={{0,2},{2,0},{4,6},{6,4},{8,10},{10,8},{12,14},{14,12},{16,18},{18,... | collective-permute-start | bytes 294920 | tf_op jit(solution)/shard_map/ppermute | solution.py:266
  37.6 5.6 %collective-permute-start.8 = (bf16[384,128]{1,0:T(8,128)(2,1)S(1)}, bf16[384,128]{1,0:T(8,128)(2,1)S(1)}, u32[]{:S(2)}, u32[]{:S(2)}) collective-permute-start(bf16[384,128]{1,0:T(8,128)(2,1)S(1)} %add_convert_fusion.5), channel_id=1, source_target_pairs={{0,16},{2,18},{4,20},{6,22},{8,24},{10,26},{12,28},{14,30},{16,0},... | collective-permute-start | bytes 294920 | tf_op jit(solution)/shard_map/ppermute | solution.py:266
  40.3 5.2 %collective-permute-start.16 = (bf16[384,128]{1,0:T(8,128)(2,1)S(1)}, bf16[384,128]{1,0:T(8,128)(2,1)S(1)}, u32[]{:S(2)}, u32[]{:S(2)}) collective-permute-start(bf16[384,128]{1,0:T(8,128)(2,1)S(1)} %add_convert_fusion.2), channel_id=1, source_target_pairs={{0,8},{2,10},{4,12},{6,14},{8,0},{10,2},{12,4},{14,6},{16,24},{18,... | collective-permute-start | bytes 294920 | tf_op jit(solution)/shard_map/ppermute | solution.py:266
  43.3 5.3 %collective-permute-start.9 = (bf16[384,128]{1,0:T(8,128)(2,1)S(1)}, bf16[384,128]{1,0:T(8,128)(2,1)S(1)}, u32[]{:S(2)}, u32[]{:S(2)}) collective-permute-start(bf16[384,128]{1,0:T(8,128)(2,1)S(1)} %add_convert_fusion.4), channel_id=1, source_target_pairs={{0,8},{2,10},{4,12},{6,14},{8,0},{10,2},{12,4},{14,6},{16,24},{18,... | collective-permute-start | bytes 294920 | tf_op jit(solution)/shard_map/ppermute | solution.py:266
  45.5 5.7 %collective-permute-start.17 = (bf16[384,128]{1,0:T(8,128)(2,1)S(1)}, bf16[384,128]{1,0:T(8,128)(2,1)S(1)}, u32[]{:S(2)}, u32[]{:S(2)}) collective-permute-start(bf16[384,128]{1,0:T(8,128)(2,1)S(1)} %add_convert_fusion.1), channel_id=1, source_target_pairs={{0,16},{2,18},{4,20},{6,22},{8,24},{10,26},{12,28},{14,30},{16,0},... | collective-permute-start | bytes 294920 | tf_op jit(solution)/shard_map/ppermute | solution.py:266
  48.6 4.7 %collective-permute-start.10 = (bf16[384,128]{1,0:T(8,128)(2,1)S(1)}, bf16[384,128]{1,0:T(8,128)(2,1)S(1)}, u32[]{:S(2)}, u32[]{:S(2)}) collective-permute-start(bf16[384,128]{1,0:T(8,128)(2,1)S(1)} %add_convert_fusion.3), channel_id=1, source_target_pairs={{0,4},{2,6},{4,0},{6,2},{8,12},{10,14},{12,8},{14,10},{16,20},{18,... | collective-permute-start | bytes 294920 | tf_op jit(solution)/shard_map/ppermute | solution.py:266
  51.2 4.7 %collective-permute-start.18 = (bf16[384,128]{1,0:T(8,128)(2,1)S(1)}, bf16[384,128]{1,0:T(8,128)(2,1)S(1)}, u32[]{:S(2)}, u32[]{:S(2)}) collective-permute-start(bf16[384,128]{1,0:T(8,128)(2,1)S(1)} %add_convert_fusion), channel_id=1, source_target_pairs={{0,2},{2,0},{4,6},{6,4},{8,10},{10,8},{12,14},{14,12},{16,18},{18,... | collective-permute-start | bytes 294920 | tf_op jit(solution)/shard_map/ppermute | solution.py:266
  53.4 5.7 %collective-permute-start.11 = (bf16[768,128]{1,0:T(8,128)(2,1)S(1)}, bf16[768,128]{1,0:T(8,128)(2,1)S(1)}, u32[]{:S(2)}, u32[]{:S(2)}) collective-permute-start(bf16[768,128]{1,0:T(8,128)(2,1)S(1)} %maximum_select_fusion.2), channel_id=1, source_target_pairs={{0,2},{2,0},{4,6},{6,4},{8,10},{10,8},{12,14},{14,12},{16,18},{18,... | collective-permute-start | bytes 589832 | tf_op jit(solution)/shard_map/ppermute | solution.py:266
  56.0 5.7 %collective-permute-start.19 = (bf16[768,128]{1,0:T(8,128)(2,1)S(1)}, bf16[768,128]{1,0:T(8,128)(2,1)S(1)}, u32[]{:S(2)}, u32[]{:S(2)}) collective-permute-start(bf16[768,128]{1,0:T(8,128)(2,1)S(1)} %maximum_select_fusion.3), channel_id=1, source_target_pairs={{0,4},{2,6},{4,0},{6,2},{8,12},{10,14},{12,8},{14,10},{16,20},{18,... | collective-permute-start | bytes 589832 | tf_op jit(solution)/shard_map/ppermute | solution.py:266
  59.2 2.7 %collective-permute-start.12 = (bf16[1536,128]{1,0:T(8,128)(2,1)S(1)}, bf16[1536,128]{1,0:T(8,128)(2,1)S(1)}, u32[]{:S(2)}, u32[]{:S(2)}) collective-permute-start(bf16[1536,128]{1,0:T(8,128)(2,1)S(1)} %maximum_select_fusion.own_ref.own_p_ref), channel_id=1, source_target_pairs={{0,1},{1,0},{2,3},{3,2},{4,5},{5,4},{6,7},{7,6},{8,9},{9,8},{10,11... | collective-permute-start | bytes 1179656 | tf_op jit(solution)/shard_map/ppermute | solution.py:266
  61.8 1.8 %collective-permute-start.20 = (bf16[1536,128]{1,0:T(8,128)(2,1)S(1)}, bf16[1536,128]{1,0:T(8,128)(2,1)S(1)}, u32[]{:S(2)}, u32[]{:S(2)}) collective-permute-start(bf16[1536,128]{1,0:T(8,128)(2,1)S(1)} %maximum_select_fusion.1.own_q_ref), channel_id=1, source_target_pairs={{0,1},{1,0},{2,3},{3,2},{4,5},{5,4},{6,7},{7,6},{8,9},{9,8},{10,11... | collective-permute-start | bytes 1179656 | tf_op jit(solution)/shard_map/ppermute | solution.py:266

commit v9 on v8

--- a/solution.py
+++ b/solution.py
@@ -175,6 +175,13 @@
 
     output_ref[...] = jnp.where(own_flag, output, 0.0).T.astype(BF16)
 
+    def hand_over(start, kept_ref, sent_ref):
+        half = kept_ref.shape[0]
+        kept_ref[...] = total[pl.ds(pl.multiple_of(start + split * half, 16), half), :]
+        sent_ref[...] = total[pl.ds(pl.multiple_of(start + (1 - split) * half, 16), half), :].astype(BF16)
+
+    hand_over(0, kept_p_ref, sent_p_ref)
+
     stage(grad_s, grad_w, 0, 7, 7)
     back = None
     for chunk in CHUNKS:
@@ -195,10 +202,7 @@
                 total, product[:, place * LANES : (place + 1) * LANES], offset_of(tap), first_one, channels
             )
 
-    half = kept_p_ref.shape[0]
-    for start, kept_ref, sent_ref in ((0, kept_p_ref, sent_p_ref), (2 * half, kept_q_ref, sent_q_ref)):
-        kept_ref[...] = total[pl.ds(pl.multiple_of(start + split * half, 16), half), :]
-        sent_ref[...] = total[pl.ds(pl.multiple_of(start + (1 - split) * half, 16), half), :].astype(BF16)
+    hand_over(2 * kept_p_ref.shape[0], kept_q_ref, sent_q_ref)
 
 
 def assemble(sums, start, own_ref, other_ref):

time: 65.7 us -> 65.3 us (level)
  no operation moved by 1% of the time
where the time goes in v9:
time: 65.3 us; the launch traced here: 65 us
  starting transfers between devices  26.9 us (41%)
  waiting for transfers between devices  20.5 us (31%)
  Pallas kernels  12.8 us (20%)
  local copies, waits for them, and re-layouts  2.39 us (4%)
  other arithmetic  1.71 us (3%)
  between operations  0.83 us (1%)
    ppermute x19, starting transfers between devices, exchanged(): lax.ppermute(value, axis, [(i, i ^ mask) for i in range(lax.axis_size(axi...  20.8 us
    ppermute x19, waiting for transfers between devices, exchanged(): lax.ppermute(value, axis, [(i, i ^ mask) for i in range(lax.axis_size(axi...  18.5 us
    pallas_call x4, Pallas kernels, call(): pl.pallas_call(kernel, out_shape=out_shape, in_specs=[pl.BlockSpec(memory...  12.8 us
    ppermute x1, starting transfers between devices, shards(): first = lax.ppermute(first, 'region', [(i, i ^ 1) for i in range(regions)])  5.44 us
    ppermute x1, waiting for transfers between devices, shards(): first = lax.ppermute(first, 'region', [(i, i ^ 1) for i in range(regions)])  1.99 us
  transfers between devices with their start and end apart: 21, of which 14 were waited for; matrix products, arithmetic and copies ran while one was open for 4% of the time, Pallas kernels for 3%

profile of v9, /device:TPU:0, one launch (start us, length us, event | category | flops | bytes accessed | tf_op | source)
XLA Modules:
  0.0 65.0 jit_solution(12526181109510864708)
XLA Ops:
  0.6 1.0 %pad_add_fusion.stack_ref = bf16[384,512]{1,0:T(8,128)(2,1)S(1)} fusion(bf16[192,512]{1,0:T(8,128)(2,1)} %param.11, bf16[96,512]{1,0:T(8,128)(2,1)} %param.6), kind=kLoop, calls=%fused_computation.8 | loop fusion | flops 786432 | bytes 688128 | tf_op jit(solution)/shard_map/add | solution.py:291
  1.7 0.7 %copy-done = s32[1,512]{1,0:T(1,128)S(1)} copy-done((s32[1,512]{1,0:T(1,128)S(1)}, s32[1,512]{1,0:T(1,128)}, u32[]{:S(2)}) %copy-start) | copy-done | bytes 2072
  3.1 0.7 %collective-permute-start.2 = (bf16[128,256]{1,0:T(8,128)(2,1)S(1)}, bf16[128,256]{1,0:T(8,128)(2,1)S(1)}, u32[]{:S(2)}, u32[]{:S(2)}) collective-permute-start(bf16[128,256]{1,0:T(8,128)(2,1)S(1)} %get-tuple-element.19), channel_id=1, source_target_pairs={{2,4},{6,8},{10,12},{14,16},{18,20},{22,24},{26,28},{4,2},{8,6},{1... | collective-permute-start | bytes 196616 | tf_op jit(solution)/shard_map/ppermute | solution.py:299
  3.7 5.4 %collective-permute-start.1 = (bf16[128,256]{1,0:T(8,128)(2,1)S(1)}, bf16[128,256]{1,0:T(8,128)(2,1)S(1)}, u32[]{:S(2)}, u32[]{:S(2)}) collective-permute-start(bf16[128,256]{1,0:T(8,128)(2,1)S(1)} %get-tuple-element.18), channel_id=1, source_target_pairs={{0,2},{2,0},{4,6},{6,4},{8,10},{10,8},{12,14},{14,12},{16,18},{18,... | collective-permute-start | bytes 196616 | tf_op jit(solution)/shard_map/ppermute | solution.py:300
  9.2 1.3 %pad.18.one_ref = bf16[27,128,96]{2,1,0:T(8,128)(2,1)S(1)} pad(bf16[27,96,96]{2,1,0:T(8,128)(2,1)} %param.7, bf16[]{:T(256)} %constant.66.clone.1), padding=0_0x0_32x0_0 | pad | bytes 1161218 | tf_op jit(solution)/shard_map/jit(_pad)/pad | solution.py:302
  10.8 2.0 %collective-permute-done.1.first_ref = bf16[128,256]{1,0:T(8,128)(2,1)S(1)} collective-permute-done((bf16[128,256]{1,0:T(8,128)(2,1)S(1)}, bf16[128,256]{1,0:T(8,128)(2,1)S(1)}, u32[]{:S(2)}, u32[]{:S(2)}) %collective-permute-start.1) | collective-permute-done | bytes 65568 | tf_op jit(solution)/shard_map/ppermute | solution.py:300
  13.3 0.7 %collective-permute-done.3.first_far_ref = bf16[128,256]{1,0:T(8,128)(2,1)S(1)} collective-permute-done((bf16[128,256]{1,0:T(8,128)(2,1)S(1)}, bf16[128,256]{1,0:T(8,128)(2,1)S(1)}, u32[]{:S(2)}, u32[]{:S(2)}) %collective-permute-start.3) | collective-permute-done | bytes 65568 | tf_op jit(solution)/shard_map/ppermute | solution.py:270
  14.2 9.1 %shard_map.86 = (bf16[192,512]{1,0:T(8,128)(2,1)}, f32[1536,128]{1,0:T(8,128)S(1)}, f32[1536,128]{1,0:T(8,128)S(1)}, bf16[1536,128]{1,0:T(8,128)(2,1)S(1)}, bf16[1536,128]{1,0:T(8,128)(2,1)S(1)}) custom-call(s32[1,27]{1,0:T(1,128)S(1)} %copy-done.1, bf16[512,384]{1,0:T(8,128)(2,1)S(1)} %get-tuple-element.17.own_ref, ...), custom_call_target="tpu_custom_call" | custom-call | tf_op jit(solution)/shard_map/pallas_call | solution.py:257
  23.9 1.2 %collective-permute-done.5 = bf16[1536,128]{1,0:T(8,128)(2,1)S(1)} collective-permute-done((bf16[1536,128]{1,0:T(8,128)(2,1)S(1)}, bf16[1536,128]{1,0:T(8,128)(2,1)S(1)}, u32[]{:S(2)}, u32[]{:S(2)}) %collective-permute-start.5) | collective-permute-done | bytes 393248 | tf_op jit(solution)/shard_map/ppermute | solution.py:270
  25.2 1.9 %collective-permute-start.6 = (bf16[768,128]{1,0:T(8,128)(2,1)S(1)}, bf16[768,128]{1,0:T(8,128)(2,1)S(1)}, u32[]{:S(2)}, u32[]{:S(2)}) collective-permute-start(bf16[768,128]{1,0:T(8,128)(2,1)S(1)} %dynamic-slice_convert_fusion.1), channel_id=1, source_target_pairs={{0,2},{2,0},{4,6},{6,4},{8,10},{10,8},{12,14},{14,12},{16,18},{18,... | collective-permute-start | bytes 589832 | tf_op jit(solution)/shard_map/ppermute | solution.py:270
  27.2 0.8 %collective-permute-start.14 = (bf16[768,128]{1,0:T(8,128)(2,1)S(1)}, bf16[768,128]{1,0:T(8,128)(2,1)S(1)}, u32[]{:S(2)}, u32[]{:S(2)}) collective-permute-start(bf16[768,128]{1,0:T(8,128)(2,1)S(1)} %dynamic-slice_convert_fusion), channel_id=1, source_target_pairs={{0,4},{2,6},{4,0},{6,2},{8,12},{10,14},{12,8},{14,10},{16,20},{18,... | collective-permute-start | bytes 589832 | tf_op jit(solution)/shard_map/ppermute | solution.py:270
  28.0 4.5 %collective-permute-done.6 = bf16[768,128]{1,0:T(8,128)(2,1)S(1)} collective-permute-done((bf16[768,128]{1,0:T(8,128)(2,1)S(1)}, bf16[768,128]{1,0:T(8,128)(2,1)S(1)}, u32[]{:S(2)}, u32[]{:S(2)}) %collective-permute-start.6) | collective-permute-done | bytes 196640 | tf_op jit(solution)/shard_map/ppermute | solution.py:270
  32.6 0.8 %collective-permute-start.7 = (bf16[384,128]{1,0:T(8,128)(2,1)S(1)}, bf16[384,128]{1,0:T(8,128)(2,1)S(1)}, u32[]{:S(2)}, u32[]{:S(2)}) collective-permute-start(bf16[384,128]{1,0:T(8,128)(2,1)S(1)} %dynamic-slice_convert_fusion.3), channel_id=1, source_target_pairs={{0,4},{2,6},{4,0},{6,2},{8,12},{10,14},{12,8},{14,10},{16,20},{18,... | collective-permute-start | bytes 294920 | tf_op jit(solution)/shard_map/ppermute | solution.py:270
  33.4 0.8 %collective-permute-done.14 = bf16[768,128]{1,0:T(8,128)(2,1)S(1)} collective-permute-done((bf16[768,128]{1,0:T(8,128)(2,1)S(1)}, bf16[768,128]{1,0:T(8,128)(2,1)S(1)}, u32[]{:S(2)}, u32[]{:S(2)}) %collective-permute-start.14) | collective-permute-done | bytes 196640 | tf_op jit(solution)/shard_map/ppermute | solution.py:270
  34.2 1.0 %collective-permute-start.15 = (bf16[384,128]{1,0:T(8,128)(2,1)S(1)}, bf16[384,128]{1,0:T(8,128)(2,1)S(1)}, u32[]{:S(2)}, u32[]{:S(2)}) collective-permute-start(bf16[384,128]{1,0:T(8,128)(2,1)S(1)} %dynamic-slice_convert_fusion.2), channel_id=1, source_target_pairs={{0,2},{2,0},{4,6},{6,4},{8,10},{10,8},{12,14},{14,12},{16,18},{18,... | collective-permute-start | bytes 294920 | tf_op jit(solution)/shard_map/ppermute | solution.py:270
  35.2 2.0 %collective-permute-done.7 = bf16[384,128]{1,0:T(8,128)(2,1)S(1)} collective-permute-done((bf16[384,128]{1,0:T(8,128)(2,1)S(1)}, bf16[384,128]{1,0:T(8,128)(2,1)S(1)}, u32[]{:S(2)}, u32[]{:S(2)}) %collective-permute-start.7) | collective-permute-done | bytes 98336 | tf_op jit(solution)/shard_map/ppermute | solution.py:270
  37.3 2.7 %collective-permute-start.8 = (bf16[384,128]{1,0:T(8,128)(2,1)S(1)}, bf16[384,128]{1,0:T(8,128)(2,1)S(1)}, u32[]{:S(2)}, u32[]{:S(2)}) collective-permute-start(bf16[384,128]{1,0:T(8,128)(2,1)S(1)} %add_convert_fusion.5), channel_id=1, source_target_pairs={{0,16},{2,18},{4,20},{6,22},{8,24},{10,26},{12,28},{14,30},{16,0},... | collective-permute-start | bytes 294920 | tf_op jit(solution)/shard_map/ppermute | solution.py:270
  40.0 1.5 %collective-permute-start.16 = (bf16[384,128]{1,0:T(8,128)(2,1)S(1)}, bf16[384,128]{1,0:T(8,128)(2,1)S(1)}, u32[]{:S(2)}, u32[]{:S(2)}) collective-permute-start(bf16[384,128]{1,0:T(8,128)(2,1)S(1)} %add_convert_fusion.2), channel_id=1, source_target_pairs={{0,8},{2,10},{4,12},{6,14},{8,0},{10,2},{12,4},{14,6},{16,24},{18,... | collective-permute-start | bytes 294920 | tf_op jit(solution)/shard_map/ppermute | solution.py:270
  41.5 1.4 %collective-permute-done.8 = bf16[384,128]{1,0:T(8,128)(2,1)S(1)} collective-permute-done((bf16[384,128]{1,0:T(8,128)(2,1)S(1)}, bf16[384,128]{1,0:T(8,128)(2,1)S(1)}, u32[]{:S(2)}, u32[]{:S(2)}) %collective-permute-start.8) | collective-permute-done | bytes 98336 | tf_op jit(solution)/shard_map/ppermute | solution.py:270
  43.0 1.8 %collective-permute-start.9 = (bf16[384,128]{1,0:T(8,128)(2,1)S(1)}, bf16[384,128]{1,0:T(8,128)(2,1)S(1)}, u32[]{:S(2)}, u32[]{:S(2)}) collective-permute-start(bf16[384,128]{1,0:T(8,128)(2,1)S(1)} %add_convert_fusion.4), channel_id=1, source_target_pairs={{0,8},{2,10},{4,12},{6,14},{8,0},{10,2},{12,4},{14,6},{16,24},{18,... | collective-permute-start | bytes 294920 | tf_op jit(solution)/shard_map/ppermute | solution.py:270
  45.2 3.0 %collective-permute-start.17 = (bf16[384,128]{1,0:T(8,128)(2,1)S(1)}, bf16[384,128]{1,0:T(8,128)(2,1)S(1)}, u32[]{:S(2)}, u32[]{:S(2)}) collective-permute-start(bf16[384,128]{1,0:T(8,128)(2,1)S(1)} %add_convert_fusion.1), channel_id=1, source_target_pairs={{0,16},{2,18},{4,20},{6,22},{8,24},{10,26},{12,28},{14,30},{16,0},... | collective-permute-start | bytes 294920 | tf_op jit(solution)/shard_map/ppermute | solution.py:270
  48.3 1.3 %collective-permute-start.10 = (bf16[384,128]{1,0:T(8,128)(2,1)S(1)}, bf16[384,128]{1,0:T(8,128)(2,1)S(1)}, u32[]{:S(2)}, u32[]{:S(2)}) collective-permute-start(bf16[384,128]{1,0:T(8,128)(2,1)S(1)} %add_convert_fusion.3), channel_id=1, source_target_pairs={{0,4},{2,6},{4,0},{6,2},{8,12},{10,14},{12,8},{14,10},{16,20},{18,... | collective-permute-start | bytes 294920 | tf_op jit(solution)/shard_map/ppermute | solution.py:270
  49.6 1.2 %collective-permute-done.17 = bf16[384,128]{1,0:T(8,128)(2,1)S(1)} collective-permute-done((bf16[384,128]{1,0:T(8,128)(2,1)S(1)}, bf16[384,128]{1,0:T(8,128)(2,1)S(1)}, u32[]{:S(2)}, u32[]{:S(2)}) %collective-permute-start.17) | collective-permute-done | bytes 98336 | tf_op jit(solution)/shard_map/ppermute | solution.py:270
  50.9 1.6 %collective-permute-start.18 = (bf16[384,128]{1,0:T(8,128)(2,1)S(1)}, bf16[384,128]{1,0:T(8,128)(2,1)S(1)}, u32[]{:S(2)}, u32[]{:S(2)}) collective-permute-start(bf16[384,128]{1,0:T(8,128)(2,1)S(1)} %add_convert_fusion), channel_id=1, source_target_pairs={{0,2},{2,0},{4,6},{6,4},{8,10},{10,8},{12,14},{14,12},{16,18},{18,... | collective-permute-start | bytes 294920 | tf_op jit(solution)/shard_map/ppermute | solution.py:270
  52.4 0.5 collective-permute-done.10
  53.0 1.3 %collective-permute-start.11 = (bf16[768,128]{1,0:T(8,128)(2,1)S(1)}, bf16[768,128]{1,0:T(8,128)(2,1)S(1)}, u32[]{:S(2)}, u32[]{:S(2)}) collective-permute-start(bf16[768,128]{1,0:T(8,128)(2,1)S(1)} %maximum_select_fusion.2), channel_id=1, source_target_pairs={{0,2},{2,0},{4,6},{6,4},{8,10},{10,8},{12,14},{14,12},{16,18},{18,... | collective-permute-start | bytes 589832 | tf_op jit(solution)/shard_map/ppermute | solution.py:270
  54.3 1.2 %collective-permute-done.18 = bf16[384,128]{1,0:T(8,128)(2,1)S(1)} collective-permute-done((bf16[384,128]{1,0:T(8,128)(2,1)S(1)}, bf16[384,128]{1,0:T(8,128)(2,1)S(1)}, u32[]{:S(2)}, u32[]{:S(2)}) %collective-permute-start.18) | collective-permute-done | bytes 98336 | tf_op jit(solution)/shard_map/ppermute | solution.py:270
  55.6 1.3 %collective-permute-start.19 = (bf16[768,128]{1,0:T(8,128)(2,1)S(1)}, bf16[768,128]{1,0:T(8,128)(2,1)S(1)}, u32[]{:S(2)}, u32[]{:S(2)}) collective-permute-start(bf16[768,128]{1,0:T(8,128)(2,1)S(1)} %maximum_select_fusion.3), channel_id=1, source_target_pairs={{0,4},{2,6},{4,0},{6,2},{8,12},{10,14},{12,8},{14,10},{16,20},{18,... | collective-permute-start | bytes 589832 | tf_op jit(solution)/shard_map/ppermute | solution.py:270
  56.9 1.8 %collective-permute-done.11 = bf16[768,128]{1,0:T(8,128)(2,1)S(1)} collective-permute-done((bf16[768,128]{1,0:T(8,128)(2,1)S(1)}, bf16[768,128]{1,0:T(8,128)(2,1)S(1)}, u32[]{:S(2)}, u32[]{:S(2)}) %collective-permute-start.11) | collective-permute-done | bytes 196640 | tf_op jit(solution)/shard_map/ppermute | solution.py:270
  58.9 2.4 %collective-permute-done.19 = bf16[768,128]{1,0:T(8,128)(2,1)S(1)} collective-permute-done((bf16[768,128]{1,0:T(8,128)(2,1)S(1)}, bf16[768,128]{1,0:T(8,128)(2,1)S(1)}, u32[]{:S(2)}, u32[]{:S(2)}) %collective-permute-start.19) | collective-permute-done | bytes 196640 | tf_op jit(solution)/shard_map/ppermute | solution.py:270
  61.5 1.7 %shard_map.87._ = f32[27,96,192]{2,1,0:T(8,128)} custom-call(bf16[1536,128]{1,0:T(8,128)(2,1)S(1)} %maximum_select_fusion.own_ref.own_p_ref, bf16[1536,128]{1,0:T(8,128)(2,1)S(1)} %collective-permute-done.12.other_ref.other_p_ref), custom_call_target="tpu_custom_call" | custom-call | flops 100000000 | bytes 4194304 | tf_op jit(solution)/shard_map/pallas_call | solution.py:257
  63.2 1.8 %shard_map.88 = (f32[27,96,96]{2,1,0:T(8,128)}, f32[27,96,192]{2,1,0:T(8,128)}) custom-call(bf16[1536,128]{1,0:T(8,128)(2,1)S(1)} %maximum_select_fusion.own_ref.own_p_ref, bf16[1536,128]{1,0:T(8,128)(2,1)S(1)} %collective-permute-done.12.other_ref.other_p_ref, ...), custom_call_target="tpu_custom_call", output_to_operand_aliasing={{1}: (4, {})} | custom-call | tf_op jit(solution)/shard_map/pallas_call | solution.py:257
  (41 shorter events, 3.7 us)
Async XLA Ops:
  1.7 0.7 %copy-start = (s32[1,512]{1,0:T(1,128)S(1)}, s32[1,512]{1,0:T(1,128)}, u32[]{:S(2)}) copy-start(s32[1,512]{1,0:T(1,128)} %occupancy_ref.1) | copy-start | bytes 6148
  2.3 8.2 %copy-start.2 = (bf16[27,96,192]{2,1,0:T(8,128)(2,1)S(1)}, bf16[27,96,192]{2,1,0:T(8,128)(2,1)}, u32[]{:S(2)}) copy-start(bf16[27,96,192]{2,1,0:T(8,128)(2,1)} %param.8) | copy-start | bytes 2985988
  2.6 11.7 %collective-permute-start = (bf16[512,384]{1,0:T(8,128)(2,1)S(1)}, bf16[512,384]{1,0:T(8,128)(2,1)S(1)}, u32[]{:S(2)}, u32[]{:S(2)}) collective-permute-start(bf16[512,384]{1,0:T(8,128)(2,1)S(1)} %get-tuple-element.17.own_ref), channel_id=1, source_target_pairs={{0,1},{1,0},{2,3},{3,2},{4,5},{5,4},{6,7},{7,6},{8,9},{9,8},{10,11... | collective-permute-start | bytes 1179656 | tf_op jit(solution)/shard_map/ppermute | solution.py:270
  3.1 7.7 %collective-permute-start.2 = (bf16[128,256]{1,0:T(8,128)(2,1)S(1)}, bf16[128,256]{1,0:T(8,128)(2,1)S(1)}, u32[]{:S(2)}, u32[]{:S(2)}) collective-permute-start(bf16[128,256]{1,0:T(8,128)(2,1)S(1)} %get-tuple-element.19), channel_id=1, source_target_pairs={{2,4},{6,8},{10,12},{14,16},{18,20},{22,24},{26,28},{4,2},{8,6},{1... | collective-permute-start | bytes 196616 | tf_op jit(solution)/shard_map/ppermute | solution.py:299
  3.7 9.1 %collective-permute-start.1 = (bf16[128,256]{1,0:T(8,128)(2,1)S(1)}, bf16[128,256]{1,0:T(8,128)(2,1)S(1)}, u32[]{:S(2)}, u32[]{:S(2)}) collective-permute-start(bf16[128,256]{1,0:T(8,128)(2,1)S(1)} %get-tuple-element.18), channel_id=1, source_target_pairs={{0,2},{2,0},{4,6},{6,4},{8,10},{10,8},{12,14},{14,12},{16,18},{18,... | collective-permute-start | bytes 196616 | tf_op jit(solution)/shard_map/ppermute | solution.py:300
  10.5 3.7 %copy-start.1 = (s32[1,27]{1,0:T(1,128)S(1)}, s32[1,27]{1,0:T(1,128)}, u32[]{:S(2)}) copy-start(s32[1,27]{1,0:T(1,128)} %neighbors_ref.1) | copy-start | bytes 328
  12.8 1.3 %collective-permute-start.3 = (bf16[128,256]{1,0:T(8,128)(2,1)S(1)}, bf16[128,256]{1,0:T(8,128)(2,1)S(1)}, u32[]{:S(2)}, u32[]{:S(2)}) collective-permute-start(bf16[128,256]{1,0:T(8,128)(2,1)S(1)} %collective-permute-done.1.first_ref), channel_id=1, source_target_pairs={{0,1},{1,0},{2,3},{3,2},{4,5},{5,4},{6,7},{7,6},{8,9},{9,8},{10,11... | collective-permute-start | bytes 196616 | tf_op jit(solution)/shard_map/ppermute | solution.py:270
  12.8 1.4 %collective-permute-start.4 = (bf16[128,256]{1,0:T(8,128)(2,1)S(1)}, bf16[128,256]{1,0:T(8,128)(2,1)S(1)}, u32[]{:S(2)}, u32[]{:S(2)}) collective-permute-start(bf16[128,256]{1,0:T(8,128)(2,1)S(1)} %collective-permute-done.2.second_ref), channel_id=1, source_target_pairs={{0,1},{1,0},{2,3},{3,2},{4,5},{5,4},{6,7},{7,6},{8,9},{9,8},{10,11... | collective-permute-start | bytes 196616 | tf_op jit(solution)/shard_map/ppermute | solution.py:270
  23.3 1.8 %collective-permute-start.5 = (bf16[1536,128]{1,0:T(8,128)(2,1)S(1)}, bf16[1536,128]{1,0:T(8,128)(2,1)S(1)}, u32[]{:S(2)}, u32[]{:S(2)}) collective-permute-start(bf16[1536,128]{1,0:T(8,128)(2,1)S(1)} %get-tuple-element.26), channel_id=1, source_target_pairs={{0,1},{1,0},{2,3},{3,2},{4,5},{5,4},{6,7},{7,6},{8,9},{9,8},{10,11... | collective-permute-start | bytes 1179656 | tf_op jit(solution)/shard_map/ppermute | solution.py:270
  23.7 3.4 %collective-permute-start.13 = (bf16[1536,128]{1,0:T(8,128)(2,1)S(1)}, bf16[1536,128]{1,0:T(8,128)(2,1)S(1)}, u32[]{:S(2)}, u32[]{:S(2)}) collective-permute-start(bf16[1536,128]{1,0:T(8,128)(2,1)S(1)} %get-tuple-element.28), channel_id=1, source_target_pairs={{0,1},{1,0},{2,3},{3,2},{4,5},{5,4},{6,7},{7,6},{8,9},{9,8},{10,11... | collective-permute-start | bytes 1179656 | tf_op jit(solution)/shard_map/ppermute | solution.py:270
  25.2 7.3 %collective-permute-start.6 = (bf16[768,128]{1,0:T(8,128)(2,1)S(1)}, bf16[768,128]{1,0:T(8,128)(2,1)S(1)}, u32[]{:S(2)}, u32[]{:S(2)}) collective-permute-start(bf16[768,128]{1,0:T(8,128)(2,1)S(1)} %dynamic-slice_convert_fusion.1), channel_id=1, source_target_pairs={{0,2},{2,0},{4,6},{6,4},{8,10},{10,8},{12,14},{14,12},{16,18},{18,... | collective-permute-start | bytes 589832 | tf_op jit(solution)/shard_map/ppermute | solution.py:270
  27.2 6.9 %collective-permute-start.14 = (bf16[768,128]{1,0:T(8,128)(2,1)S(1)}, bf16[768,128]{1,0:T(8,128)(2,1)S(1)}, u32[]{:S(2)}, u32[]{:S(2)}) collective-permute-start(bf16[768,128]{1,0:T(8,128)(2,1)S(1)} %dynamic-slice_convert_fusion), channel_id=1, source_target_pairs={{0,4},{2,6},{4,0},{6,2},{8,12},{10,14},{12,8},{14,10},{16,20},{18,... | collective-permute-start | bytes 589832 | tf_op jit(solution)/shard_map/ppermute | solution.py:270
  32.6 4.7 %collective-permute-start.7 = (bf16[384,128]{1,0:T(8,128)(2,1)S(1)}, bf16[384,128]{1,0:T(8,128)(2,1)S(1)}, u32[]{:S(2)}, u32[]{:S(2)}) collective-permute-start(bf16[384,128]{1,0:T(8,128)(2,1)S(1)} %dynamic-slice_convert_fusion.3), channel_id=1, source_target_pairs={{0,4},{2,6},{4,0},{6,2},{8,12},{10,14},{12,8},{14,10},{16,20},{18,... | collective-permute-start | bytes 294920 | tf_op jit(solution)/shard_map/ppermute | solution.py:270
  34.2 5.7 %collective-permute-start.15 = (bf16[384,128]{1,0:T(8,128)(2,1)S(1)}, bf16[384,128]{1,0:T(8,128)(2,1)S(1)}, u32[]{:S(2)}, u32[]{:S(2)}) collective-permute-start(bf16[384,128]{1,0:T(8,128)(2,1)S(1)} %dynamic-slice_convert_fusion.2), channel_id=1, source_target_pairs={{0,2},{2,0},{4,6},{6,4},{8,10},{10,8},{12,14},{14,12},{16,18},{18,... | collective-permute-start | bytes 294920 | tf_op jit(solution)/shard_map/ppermute | solution.py:270
  37.3 5.7 %collective-permute-start.8 = (bf16[384,128]{1,0:T(8,128)(2,1)S(1)}, bf16[384,128]{1,0:T(8,128)(2,1)S(1)}, u32[]{:S(2)}, u32[]{:S(2)}) collective-permute-start(bf16[384,128]{1,0:T(8,128)(2,1)S(1)} %add_convert_fusion.5), channel_id=1, source_target_pairs={{0,16},{2,18},{4,20},{6,22},{8,24},{10,26},{12,28},{14,30},{16,0},... | collective-permute-start | bytes 294920 | tf_op jit(solution)/shard_map/ppermute | solution.py:270
  40.0 5.2 %collective-permute-start.16 = (bf16[384,128]{1,0:T(8,128)(2,1)S(1)}, bf16[384,128]{1,0:T(8,128)(2,1)S(1)}, u32[]{:S(2)}, u32[]{:S(2)}) collective-permute-start(bf16[384,128]{1,0:T(8,128)(2,1)S(1)} %add_convert_fusion.2), channel_id=1, source_target_pairs={{0,8},{2,10},{4,12},{6,14},{8,0},{10,2},{12,4},{14,6},{16,24},{18,... | collective-permute-start | bytes 294920 | tf_op jit(solution)/shard_map/ppermute | solution.py:270
  43.0 5.3 %collective-permute-start.9 = (bf16[384,128]{1,0:T(8,128)(2,1)S(1)}, bf16[384,128]{1,0:T(8,128)(2,1)S(1)}, u32[]{:S(2)}, u32[]{:S(2)}) collective-permute-start(bf16[384,128]{1,0:T(8,128)(2,1)S(1)} %add_convert_fusion.4), channel_id=1, source_target_pairs={{0,8},{2,10},{4,12},{6,14},{8,0},{10,2},{12,4},{14,6},{16,24},{18,... | collective-permute-start | bytes 294920 | tf_op jit(solution)/shard_map/ppermute | solution.py:270
  45.2 5.6 %collective-permute-start.17 = (bf16[384,128]{1,0:T(8,128)(2,1)S(1)}, bf16[384,128]{1,0:T(8,128)(2,1)S(1)}, u32[]{:S(2)}, u32[]{:S(2)}) collective-permute-start(bf16[384,128]{1,0:T(8,128)(2,1)S(1)} %add_convert_fusion.1), channel_id=1, source_target_pairs={{0,16},{2,18},{4,20},{6,22},{8,24},{10,26},{12,28},{14,30},{16,0},... | collective-permute-start | bytes 294920 | tf_op jit(solution)/shard_map/ppermute | solution.py:270
  48.3 4.7 %collective-permute-start.10 = (bf16[384,128]{1,0:T(8,128)(2,1)S(1)}, bf16[384,128]{1,0:T(8,128)(2,1)S(1)}, u32[]{:S(2)}, u32[]{:S(2)}) collective-permute-start(bf16[384,128]{1,0:T(8,128)(2,1)S(1)} %add_convert_fusion.3), channel_id=1, source_target_pairs={{0,4},{2,6},{4,0},{6,2},{8,12},{10,14},{12,8},{14,10},{16,20},{18,... | collective-permute-start | bytes 294920 | tf_op jit(solution)/shard_map/ppermute | solution.py:270
  50.9 4.7 %collective-permute-start.18 = (bf16[384,128]{1,0:T(8,128)(2,1)S(1)}, bf16[384,128]{1,0:T(8,128)(2,1)S(1)}, u32[]{:S(2)}, u32[]{:S(2)}) collective-permute-start(bf16[384,128]{1,0:T(8,128)(2,1)S(1)} %add_convert_fusion), channel_id=1, source_target_pairs={{0,2},{2,0},{4,6},{6,4},{8,10},{10,8},{12,14},{14,12},{16,18},{18,... | collective-permute-start | bytes 294920 | tf_op jit(solution)/shard_map/ppermute | solution.py:270
  53.0 5.7 %collective-permute-start.11 = (bf16[768,128]{1,0:T(8,128)(2,1)S(1)}, bf16[768,128]{1,0:T(8,128)(2,1)S(1)}, u32[]{:S(2)}, u32[]{:S(2)}) collective-permute-start(bf16[768,128]{1,0:T(8,128)(2,1)S(1)} %maximum_select_fusion.2), channel_id=1, source_target_pairs={{0,2},{2,0},{4,6},{6,4},{8,10},{10,8},{12,14},{14,12},{16,18},{18,... | collective-permute-start | bytes 589832 | tf_op jit(solution)/shard_map/ppermute | solution.py:270
  55.6 5.7 %collective-permute-start.19 = (bf16[768,128]{1,0:T(8,128)(2,1)S(1)}, bf16[768,128]{1,0:T(8,128)(2,1)S(1)}, u32[]{:S(2)}, u32[]{:S(2)}) collective-permute-start(bf16[768,128]{1,0:T(8,128)(2,1)S(1)} %maximum_select_fusion.3), channel_id=1, source_target_pairs={{0,4},{2,6},{4,0},{6,2},{8,12},{10,14},{12,8},{14,10},{16,20},{18,... | collective-permute-start | bytes 589832 | tf_op jit(solution)/shard_map/ppermute | solution.py:270
  58.8 2.7 %collective-permute-start.12 = (bf16[1536,128]{1,0:T(8,128)(2,1)S(1)}, bf16[1536,128]{1,0:T(8,128)(2,1)S(1)}, u32[]{:S(2)}, u32[]{:S(2)}) collective-permute-start(bf16[1536,128]{1,0:T(8,128)(2,1)S(1)} %maximum_select_fusion.own_ref.own_p_ref), channel_id=1, source_target_pairs={{0,1},{1,0},{2,3},{3,2},{4,5},{5,4},{6,7},{7,6},{8,9},{9,8},{10,11... | collective-permute-start | bytes 1179656 | tf_op jit(solution)/shard_map/ppermute | solution.py:270
  61.4 1.8 %collective-permute-start.20 = (bf16[1536,128]{1,0:T(8,128)(2,1)S(1)}, bf16[1536,128]{1,0:T(8,128)(2,1)S(1)}, u32[]{:S(2)}, u32[]{:S(2)}) collective-permute-start(bf16[1536,128]{1,0:T(8,128)(2,1)S(1)} %maximum_select_fusion.1.own_q_ref), channel_id=1, source_target_pairs={{0,1},{1,0},{2,3},{3,2},{4,5},{5,4},{6,7},{7,6},{8,9},{9,8},{10,11... | collective-permute-start | bytes 1179656 | tf_op jit(solution)/shard_map/ppermute | solution.py:270

commit v10 on v9

--- a/solution.py
+++ b/solution.py
@@ -67,7 +67,7 @@
 
 def main_kernel(
     neighbors_ref, own_ref, partner_ref, first_ref, second_ref, first_far_ref, second_far_ref,
-    turned_ref, one_ref, two_ref, output_ref, kept_p_ref, kept_q_ref, sent_p_ref, sent_q_ref,
+    turned_ref, one_ref, two_ref, output_ref, kept_p_ref, kept_q_ref, kept_r_ref, sent_p_ref, sent_q_ref, sent_r_ref,
     masked_w, grad_w, hidden_w, total, masked_s, plane_s, hidden_s, grad_s,
 ):
     odd, split = lax.axis_index("region") % 2, lax.axis_index("split")
@@ -203,6 +203,7 @@
             )
 
     hand_over(2 * kept_p_ref.shape[0], kept_q_ref, sent_q_ref)
+    hand_over(4 * kept_p_ref.shape[0], kept_r_ref, sent_r_ref)
 
 
 def assemble(sums, start, own_ref, other_ref):
@@ -238,11 +239,12 @@
 
 
 def second_unpack_kernel(
-    groups, own_p_ref, other_p_ref, own_q_ref, other_q_ref, _, one_hbm, two_hbm, sums, one_ref, two_ref, one_sems, two_sems
+    groups, own_p_ref, other_p_ref, own_q_ref, other_q_ref, own_r_ref, other_r_ref, _, one_hbm, two_hbm, sums, one_ref, two_ref, one_sems, two_sems
 ):
     offsets, _, outs = two_ref.shape
     assemble(sums, 0, own_p_ref, other_p_ref)
     assemble(sums, 2 * own_p_ref.shape[0], own_q_ref, other_q_ref)
+    assemble(sums, 4 * own_p_ref.shape[0], own_r_ref, other_r_ref)
     fours = -(-offsets // 4)
     copies = unpack(sums, 0, groups, two_ref, two_hbm, two_sems)
     copies += unpack(sums, 3 * fours * outs, range(fours), one_ref, one_hbm, one_sems)
@@ -306,11 +308,11 @@
     first_far = exchanged(first, "split", 1)
 
     tile_rows = 3 * -(-offsets // 4) * (outs + channels)
-    half = up_to(tile_rows, 4 * regions * 8) // 4
+    half = up_to(tile_rows, 6 * regions * 8) // 6
     kept, sent = struct((half, LANES), F32), struct((half, LANES), BF16)
     output, *sums = call(
         main_kernel,
-        (struct((outs, voxels), BF16), kept, kept, sent, sent),
+        (struct((outs, voxels), BF16), *([kept] * 3), *([sent] * 3)),
         (neighbors, packed, partner, first, second, first_far, second_far, turned, one, two),
         scalars=1,
         mib=26,
@@ -318,16 +320,16 @@
             pltpu.VMEM((12, 24, 24, LANES), F32),
             pltpu.VMEM((10, 24, 24, wide), F32),
             pltpu.VMEM((10, 10, 24, LANES), F32),
-            pltpu.VMEM((4 * half, LANES), F32),
+            pltpu.VMEM((6 * half, LANES), F32),
             pltpu.VMEM((3, 2, 12, 96, LANES), BF16),
             pltpu.VMEM((3, 3, 12, 16, LANES), BF16),
             pltpu.VMEM((3, 2, 10, 80, LANES), BF16),
             pltpu.VMEM((3, 2, 10, 80, wide), BF16),
         ),
     )
-    sums = [sums[part] + exchanged(sums[2 + part], "split", 1).astype(F32) for part in range(2)]
+    sums = [sums[part] + exchanged(sums[3 + part], "split", 1).astype(F32) for part in range(3)]
     bits = list(range((regions - 1).bit_length()))
-    orders = [bits[:-2] + bits[:-3:-1], bits[1::-1] + bits[2:]]
+    orders = [bits[:-2] + bits[:-3:-1], bits[1::-1] + bits[2:], [2, 0] + bits[4:] + [3, 1]]
     whole_steps = 2
 
     for step in range(len(bits) - whole_steps):
@@ -367,9 +369,9 @@
     grad_one, grad_two = call(
         functools.partial(second_unpack_kernel, range(early, fours)),
         (one_shape, two_shape),
-        (*ends[0], *ends[1], grad_two),
+        (*ends[0], *ends[1], *ends[2], grad_two),
         scratch=(
-            pltpu.VMEM((4 * half, LANES), BF16),
+            pltpu.VMEM((6 * half, LANES), BF16),
             pltpu.VMEM(one_shape.shape, F32),
             pltpu.VMEM(two_shape.shape, F32),
             pltpu.SemaphoreType.DMA((fours,)),

time: 65.3 us -> 64.5 us (0.988)
  waiting for transfers between devices: 20.5 us -> 14.7 us
  starting transfers between devices: 26.9 us -> 31.7 us
    ppermute x19 -> x27, waiting for transfers between devices: 18.5 us -> 12.7 us  [exchanged(): lax.ppermute(value, axis, [(i, i ^ mask) for i in range(lax.axis_size(axi...]
    ppermute x19 -> x27, starting transfers between devices: 20.8 us -> 25.6 us  [exchanged(): lax.ppermute(value, axis, [(i, i ^ mask) for i in range(lax.axis_size(axi...]
  transfers between devices with their start and end apart: 21 -> 29, of which waited for: 14 -> 16; matrix products, arithmetic and copies ran while one was open for 4% -> 4% of each run, Pallas kernels for 3% -> 2%
where the time goes in v10:
time: 64.5 us; the launch traced here: 64.3 us
  starting transfers between devices  31.7 us (49%)
  waiting for transfers between devices  14.7 us (23%)
  Pallas kernels  12.8 us (20%)
  local copies, waits for them, and re-layouts  2.41 us (4%)
  other arithmetic  1.81 us (3%)
  between operations  0.89 us (1%)
    ppermute x27, starting transfers between devices, exchanged(): lax.ppermute(value, axis, [(i, i ^ mask) for i in range(lax.axis_size(axi...  25.6 us
    pallas_call x4, Pallas kernels, call(): pl.pallas_call(kernel, out_shape=out_shape, in_specs=[pl.BlockSpec(memory...  12.8 us
    ppermute x27, waiting for transfers between devices, exchanged(): lax.ppermute(value, axis, [(i, i ^ mask) for i in range(lax.axis_size(axi...  12.7 us
    ppermute x1, starting transfers between devices, shards(): first = lax.ppermute(first, 'region', [(i, i ^ 1) for i in range(regions)])  5.44 us
    ppermute x1, waiting for transfers between devices, shards(): first = lax.ppermute(first, 'region', [(i, i ^ 1) for i in range(regions)])  1.99 us
    pad x1, local copies, waits for them, and re-layouts, shards(): one = jnp.pad(kernel_one, ((0, 0), (0, LANES - channels), (0, 0)))  1.3 us
  transfers between devices with their start and end apart: 29, of which 16 were waited for; matrix products, arithmetic and copies ran while one was open for 4% of the time, Pallas kernels for 2%

profile of v10, /device:TPU:0, one launch (start us, length us, event | category | flops | bytes accessed | tf_op | source)
XLA Modules:
  0.0 64.3 jit_solution(8303964737504427135)
XLA Ops:
  0.6 1.0 %pad_add_fusion.stack_ref = bf16[384,512]{1,0:T(8,128)(2,1)S(1)} fusion(bf16[192,512]{1,0:T(8,128)(2,1)} %param.11, bf16[96,512]{1,0:T(8,128)(2,1)} %param.6), kind=kLoop, calls=%fused_computation.3 | loop fusion | flops 786432 | bytes 688128 | tf_op jit(solution)/shard_map/add | solution.py:293
  3.7 5.4 %collective-permute-start.1 = (bf16[128,256]{1,0:T(8,128)(2,1)S(1)}, bf16[128,256]{1,0:T(8,128)(2,1)S(1)}, u32[]{:S(2)}, u32[]{:S(2)}) collective-permute-start(bf16[128,256]{1,0:T(8,128)(2,1)S(1)} %get-tuple-element.20), channel_id=1, source_target_pairs={{0,2},{2,0},{4,6},{6,4},{8,10},{10,8},{12,14},{14,12},{16,18},{18,... | collective-permute-start | bytes 196616 | tf_op jit(solution)/shard_map/ppermute | solution.py:302
  9.2 1.3 %pad.18.one_ref = bf16[27,128,96]{2,1,0:T(8,128)(2,1)S(1)} pad(bf16[27,96,96]{2,1,0:T(8,128)(2,1)} %param.7, bf16[]{:T(256)} %constant.91.clone.1), padding=0_0x0_32x0_0 | pad | bytes 1161218 | tf_op jit(solution)/shard_map/jit(_pad)/pad | solution.py:304
  10.8 2.0 %collective-permute-done.1.first_ref = bf16[128,256]{1,0:T(8,128)(2,1)S(1)} collective-permute-done((bf16[128,256]{1,0:T(8,128)(2,1)S(1)}, bf16[128,256]{1,0:T(8,128)(2,1)S(1)}, u32[]{:S(2)}, u32[]{:S(2)}) %collective-permute-start.1) | collective-permute-done | bytes 65568 | tf_op jit(solution)/shard_map/ppermute | solution.py:302
  13.3 0.7 %collective-permute-done.3.first_far_ref = bf16[128,256]{1,0:T(8,128)(2,1)S(1)} collective-permute-done((bf16[128,256]{1,0:T(8,128)(2,1)S(1)}, bf16[128,256]{1,0:T(8,128)(2,1)S(1)}, u32[]{:S(2)}, u32[]{:S(2)}) %collective-permute-start.3) | collective-permute-done | bytes 65568 | tf_op jit(solution)/shard_map/ppermute | solution.py:272
  14.2 9.1 %shard_map.86 = (bf16[192,512]{1,0:T(8,128)(2,1)}, f32[1024,128]{1,0:T(8,128)S(1)}, f32[1024,128]{1,0:T(8,128)S(1)}, f32[1024,128]{1,0:T(8,128)S(1)}, bf16[1024,...) custom-call(s32[1,27]{1,0:T(1,128)S(1)} %copy-done.1, ...), custom_call_target="tpu_custom_call" | custom-call | tf_op jit(solution)/shard_map/pallas_call | solution.py:259
  25.0 1.9 %collective-permute-start.6 = (bf16[512,128]{1,0:T(8,128)(2,1)S(1)}, bf16[512,128]{1,0:T(8,128)(2,1)S(1)}, u32[]{:S(2)}, u32[]{:S(2)}) collective-permute-start(bf16[512,128]{1,0:T(8,128)(2,1)S(1)} %dynamic-slice_convert_fusion.2), channel_id=1, source_target_pairs={{0,2},{2,0},{4,6},{6,4},{8,10},{10,8},{12,14},{14,12},{16,18},{18,... | collective-permute-start | bytes 393224 | tf_op jit(solution)/shard_map/ppermute | solution.py:272
  27.0 0.8 %collective-permute-start.14 = (bf16[512,128]{1,0:T(8,128)(2,1)S(1)}, bf16[512,128]{1,0:T(8,128)(2,1)S(1)}, u32[]{:S(2)}, u32[]{:S(2)}) collective-permute-start(bf16[512,128]{1,0:T(8,128)(2,1)S(1)} %dynamic-slice_convert_fusion.1), channel_id=1, source_target_pairs={{0,4},{2,6},{4,0},{6,2},{8,12},{10,14},{12,8},{14,10},{16,20},{18,... | collective-permute-start | bytes 393224 | tf_op jit(solution)/shard_map/ppermute | solution.py:272
  27.9 1.6 %collective-permute-start.22 = (bf16[512,128]{1,0:T(8,128)(2,1)S(1)}, bf16[512,128]{1,0:T(8,128)(2,1)S(1)}, u32[]{:S(2)}, u32[]{:S(2)}) collective-permute-start(bf16[512,128]{1,0:T(8,128)(2,1)S(1)} %dynamic-slice_convert_fusion), channel_id=1, source_target_pairs={{0,8},{2,10},{4,12},{6,14},{8,0},{10,2},{12,4},{14,6},{16,24},{18,... | collective-permute-start | bytes 393224 | tf_op jit(solution)/shard_map/ppermute | solution.py:272
  29.5 1.3 %collective-permute-done.6 = bf16[512,128]{1,0:T(8,128)(2,1)S(1)} collective-permute-done((bf16[512,128]{1,0:T(8,128)(2,1)S(1)}, bf16[512,128]{1,0:T(8,128)(2,1)S(1)}, u32[]{:S(2)}, u32[]{:S(2)}) %collective-permute-start.6) | collective-permute-done | bytes 131104 | tf_op jit(solution)/shard_map/ppermute | solution.py:272
  30.9 0.8 %collective-permute-start.7 = (bf16[256,128]{1,0:T(8,128)(2,1)S(1)}, bf16[256,128]{1,0:T(8,128)(2,1)S(1)}, u32[]{:S(2)}, u32[]{:S(2)}) collective-permute-start(bf16[256,128]{1,0:T(8,128)(2,1)S(1)} %dynamic-slice_convert_fusion.5), channel_id=1, source_target_pairs={{0,4},{2,6},{4,0},{6,2},{8,12},{10,14},{12,8},{14,10},{16,20},{18,... | collective-permute-start | bytes 196616 | tf_op jit(solution)/shard_map/ppermute | solution.py:272
  31.7 0.8 %collective-permute-done.14 = bf16[512,128]{1,0:T(8,128)(2,1)S(1)} collective-permute-done((bf16[512,128]{1,0:T(8,128)(2,1)S(1)}, bf16[512,128]{1,0:T(8,128)(2,1)S(1)}, u32[]{:S(2)}, u32[]{:S(2)}) %collective-permute-start.14) | collective-permute-done | bytes 131104 | tf_op jit(solution)/shard_map/ppermute | solution.py:272
  32.6 1.0 %collective-permute-start.15 = (bf16[256,128]{1,0:T(8,128)(2,1)S(1)}, bf16[256,128]{1,0:T(8,128)(2,1)S(1)}, u32[]{:S(2)}, u32[]{:S(2)}) collective-permute-start(bf16[256,128]{1,0:T(8,128)(2,1)S(1)} %dynamic-slice_convert_fusion.4), channel_id=1, source_target_pairs={{0,2},{2,0},{4,6},{6,4},{8,10},{10,8},{12,14},{14,12},{16,18},{18,... | collective-permute-start | bytes 196616 | tf_op jit(solution)/shard_map/ppermute | solution.py:272
  33.6 1.1 %collective-permute-start.23 = (bf16[256,128]{1,0:T(8,128)(2,1)S(1)}, bf16[256,128]{1,0:T(8,128)(2,1)S(1)}, u32[]{:S(2)}, u32[]{:S(2)}) collective-permute-start(bf16[256,128]{1,0:T(8,128)(2,1)S(1)} %dynamic-slice_convert_fusion.3), channel_id=1, source_target_pairs={{0,2},{2,0},{4,6},{6,4},{8,10},{10,8},{12,14},{14,12},{16,18},{18,... | collective-permute-start | bytes 196616 | tf_op jit(solution)/shard_map/ppermute | solution.py:272
  35.3 2.7 %collective-permute-start.8 = (bf16[256,128]{1,0:T(8,128)(2,1)S(1)}, bf16[256,128]{1,0:T(8,128)(2,1)S(1)}, u32[]{:S(2)}, u32[]{:S(2)}) collective-permute-start(bf16[256,128]{1,0:T(8,128)(2,1)S(1)} %add_convert_fusion.8), channel_id=1, source_target_pairs={{0,16},{2,18},{4,20},{6,22},{8,24},{10,26},{12,28},{14,30},{16,0},... | collective-permute-start | bytes 196616 | tf_op jit(solution)/shard_map/ppermute | solution.py:272
  38.0 1.5 %collective-permute-start.16 = (bf16[256,128]{1,0:T(8,128)(2,1)S(1)}, bf16[256,128]{1,0:T(8,128)(2,1)S(1)}, u32[]{:S(2)}, u32[]{:S(2)}) collective-permute-start(bf16[256,128]{1,0:T(8,128)(2,1)S(1)} %add_convert_fusion.5), channel_id=1, source_target_pairs={{0,8},{2,10},{4,12},{6,14},{8,0},{10,2},{12,4},{14,6},{16,24},{18,... | collective-permute-start | bytes 196616 | tf_op jit(solution)/shard_map/ppermute | solution.py:272
  39.5 1.5 %collective-permute-start.24 = (bf16[256,128]{1,0:T(8,128)(2,1)S(1)}, bf16[256,128]{1,0:T(8,128)(2,1)S(1)}, u32[]{:S(2)}, u32[]{:S(2)}) collective-permute-start(bf16[256,128]{1,0:T(8,128)(2,1)S(1)} %add_convert_fusion.2), channel_id=1, source_target_pairs={{0,16},{2,18},{4,20},{6,22},{8,24},{10,26},{12,28},{14,30},{16,0},... | collective-permute-start | bytes 196616 | tf_op jit(solution)/shard_map/ppermute | solution.py:272
  41.1 1.7 %collective-permute-start.9 = (bf16[256,128]{1,0:T(8,128)(2,1)S(1)}, bf16[256,128]{1,0:T(8,128)(2,1)S(1)}, u32[]{:S(2)}, u32[]{:S(2)}) collective-permute-start(bf16[256,128]{1,0:T(8,128)(2,1)S(1)} %add_convert_fusion.7), channel_id=1, source_target_pairs={{0,8},{2,10},{4,12},{6,14},{8,0},{10,2},{12,4},{14,6},{16,24},{18,... | collective-permute-start | bytes 196616 | tf_op jit(solution)/shard_map/ppermute | solution.py:272
  42.8 1.5 %collective-permute-done.16 = bf16[256,128]{1,0:T(8,128)(2,1)S(1)} collective-permute-done((bf16[256,128]{1,0:T(8,128)(2,1)S(1)}, bf16[256,128]{1,0:T(8,128)(2,1)S(1)}, u32[]{:S(2)}, u32[]{:S(2)}) %collective-permute-start.16) | collective-permute-done | bytes 65568 | tf_op jit(solution)/shard_map/ppermute | solution.py:272
  44.3 2.0 %collective-permute-start.17 = (bf16[256,128]{1,0:T(8,128)(2,1)S(1)}, bf16[256,128]{1,0:T(8,128)(2,1)S(1)}, u32[]{:S(2)}, u32[]{:S(2)}) collective-permute-start(bf16[256,128]{1,0:T(8,128)(2,1)S(1)} %add_convert_fusion.4), channel_id=1, source_target_pairs={{0,16},{2,18},{4,20},{6,22},{8,24},{10,26},{12,28},{14,30},{16,0},... | collective-permute-start | bytes 196616 | tf_op jit(solution)/shard_map/ppermute | solution.py:272
  46.4 1.3 %collective-permute-start.25 = (bf16[256,128]{1,0:T(8,128)(2,1)S(1)}, bf16[256,128]{1,0:T(8,128)(2,1)S(1)}, u32[]{:S(2)}, u32[]{:S(2)}) collective-permute-start(bf16[256,128]{1,0:T(8,128)(2,1)S(1)} %add_convert_fusion.1), channel_id=1, source_target_pairs={{0,4},{2,6},{4,0},{6,2},{8,12},{10,14},{12,8},{14,10},{16,20},{18,... | collective-permute-start | bytes 196616 | tf_op jit(solution)/shard_map/ppermute | solution.py:272
  47.7 0.9 %collective-permute-start.10 = (bf16[256,128]{1,0:T(8,128)(2,1)S(1)}, bf16[256,128]{1,0:T(8,128)(2,1)S(1)}, u32[]{:S(2)}, u32[]{:S(2)}) collective-permute-start(bf16[256,128]{1,0:T(8,128)(2,1)S(1)} %add_convert_fusion.6), channel_id=1, source_target_pairs={{0,4},{2,6},{4,0},{6,2},{8,12},{10,14},{12,8},{14,10},{16,20},{18,... | collective-permute-start | bytes 196616 | tf_op jit(solution)/shard_map/ppermute | solution.py:272
  48.5 1.2 %collective-permute-done.17 = bf16[256,128]{1,0:T(8,128)(2,1)S(1)} collective-permute-done((bf16[256,128]{1,0:T(8,128)(2,1)S(1)}, bf16[256,128]{1,0:T(8,128)(2,1)S(1)}, u32[]{:S(2)}, u32[]{:S(2)}) %collective-permute-start.17) | collective-permute-done | bytes 65568 | tf_op jit(solution)/shard_map/ppermute | solution.py:272
  50.7 1.2 %collective-permute-start.26 = (bf16[256,128]{1,0:T(8,128)(2,1)S(1)}, bf16[256,128]{1,0:T(8,128)(2,1)S(1)}, u32[]{:S(2)}, u32[]{:S(2)}) collective-permute-start(bf16[256,128]{1,0:T(8,128)(2,1)S(1)} %add_convert_fusion), channel_id=1, source_target_pairs={{0,2},{2,0},{4,6},{6,4},{8,10},{10,8},{12,14},{14,12},{16,18},{18,... | collective-permute-start | bytes 196616 | tf_op jit(solution)/shard_map/ppermute | solution.py:272
  52.1 1.0 %collective-permute-start.11 = (bf16[512,128]{1,0:T(8,128)(2,1)S(1)}, bf16[512,128]{1,0:T(8,128)(2,1)S(1)}, u32[]{:S(2)}, u32[]{:S(2)}) collective-permute-start(bf16[512,128]{1,0:T(8,128)(2,1)S(1)} %maximum_select_fusion.3), channel_id=1, source_target_pairs={{0,2},{2,0},{4,6},{6,4},{8,10},{10,8},{12,14},{14,12},{16,18},{18,... | collective-permute-start | bytes 393224 | tf_op jit(solution)/shard_map/ppermute | solution.py:272
  53.2 0.9 %collective-permute-done.18 = bf16[256,128]{1,0:T(8,128)(2,1)S(1)} collective-permute-done((bf16[256,128]{1,0:T(8,128)(2,1)S(1)}, bf16[256,128]{1,0:T(8,128)(2,1)S(1)}, u32[]{:S(2)}, u32[]{:S(2)}) %collective-permute-start.18) | collective-permute-done | bytes 65568 | tf_op jit(solution)/shard_map/ppermute | solution.py:272
  54.1 1.3 %collective-permute-start.19 = (bf16[512,128]{1,0:T(8,128)(2,1)S(1)}, bf16[512,128]{1,0:T(8,128)(2,1)S(1)}, u32[]{:S(2)}, u32[]{:S(2)}) collective-permute-start(bf16[512,128]{1,0:T(8,128)(2,1)S(1)} %maximum_select_fusion.4), channel_id=1, source_target_pairs={{0,4},{2,6},{4,0},{6,2},{8,12},{10,14},{12,8},{14,10},{16,20},{18,... | collective-permute-start | bytes 393224 | tf_op jit(solution)/shard_map/ppermute | solution.py:272
  56.2 0.9 %collective-permute-done.11 = bf16[512,128]{1,0:T(8,128)(2,1)S(1)} collective-permute-done((bf16[512,128]{1,0:T(8,128)(2,1)S(1)}, bf16[512,128]{1,0:T(8,128)(2,1)S(1)}, u32[]{:S(2)}, u32[]{:S(2)}) %collective-permute-start.11) | collective-permute-done | bytes 131104 | tf_op jit(solution)/shard_map/ppermute | solution.py:272
  57.3 1.8 %collective-permute-done.19 = bf16[512,128]{1,0:T(8,128)(2,1)S(1)} collective-permute-done((bf16[512,128]{1,0:T(8,128)(2,1)S(1)}, bf16[512,128]{1,0:T(8,128)(2,1)S(1)}, u32[]{:S(2)}, u32[]{:S(2)}) %collective-permute-start.19) | collective-permute-done | bytes 131104 | tf_op jit(solution)/shard_map/ppermute | solution.py:272
  59.3 1.2 %collective-permute-done.27 = bf16[512,128]{1,0:T(8,128)(2,1)S(1)} collective-permute-done((bf16[512,128]{1,0:T(8,128)(2,1)S(1)}, bf16[512,128]{1,0:T(8,128)(2,1)S(1)}, u32[]{:S(2)}, u32[]{:S(2)}) %collective-permute-start.27) | collective-permute-done | bytes 131104 | tf_op jit(solution)/shard_map/ppermute | solution.py:272
  60.7 1.4 %shard_map.87._ = f32[27,96,192]{2,1,0:T(8,128)} custom-call(bf16[1024,128]{1,0:T(8,128)(2,1)S(1)} %maximum_select_fusion.own_ref.own_p_ref, bf16[1024,128]{1,0:T(8,128)(2,1)S(1)} %collective-permute-done.12.other_ref.other_p_ref), custom_call_target="tpu_custom_call" | custom-call | flops 100000000 | bytes 4194304 | tf_op jit(solution)/shard_map/pallas_call | solution.py:259
  62.2 2.1 %shard_map.88 = (f32[27,96,96]{2,1,0:T(8,128)}, f32[27,96,192]{2,1,0:T(8,128)}) custom-call(bf16[1024,128]{1,0:T(8,128)(2,1)S(1)} %maximum_select_fusion.own_ref.own_p_ref, bf16[1024,128]{1,0:T(8,128)(2,1)S(1)} %collective-permute-done.12.other_ref.other_p_ref, ...), custom_call_target="tpu_custom_call", output_to_operand_aliasing={{1}: (6, {})} | custom-call | tf_op jit(solution)/shard_map/pallas_call | solution.py:259
  (66 shorter events, 8.1 us)
Async XLA Ops:
  1.7 0.7 %copy-start = (s32[1,512]{1,0:T(1,128)S(1)}, s32[1,512]{1,0:T(1,128)}, u32[]{:S(2)}) copy-start(s32[1,512]{1,0:T(1,128)} %occupancy_ref.1) | copy-start | bytes 6148
  2.3 8.2 %copy-start.2 = (bf16[27,96,192]{2,1,0:T(8,128)(2,1)S(1)}, bf16[27,96,192]{2,1,0:T(8,128)(2,1)}, u32[]{:S(2)}) copy-start(bf16[27,96,192]{2,1,0:T(8,128)(2,1)} %param.8) | copy-start | bytes 2985988
  2.6 11.7 %collective-permute-start = (bf16[512,384]{1,0:T(8,128)(2,1)S(1)}, bf16[512,384]{1,0:T(8,128)(2,1)S(1)}, u32[]{:S(2)}, u32[]{:S(2)}) collective-permute-start(bf16[512,384]{1,0:T(8,128)(2,1)S(1)} %get-tuple-element.19.own_ref), channel_id=1, source_target_pairs={{0,1},{1,0},{2,3},{3,2},{4,5},{5,4},{6,7},{7,6},{8,9},{9,8},{10,11... | collective-permute-start | bytes 1179656 | tf_op jit(solution)/shard_map/ppermute | solution.py:272
  3.1 7.7 %collective-permute-start.2 = (bf16[128,256]{1,0:T(8,128)(2,1)S(1)}, bf16[128,256]{1,0:T(8,128)(2,1)S(1)}, u32[]{:S(2)}, u32[]{:S(2)}) collective-permute-start(bf16[128,256]{1,0:T(8,128)(2,1)S(1)} %get-tuple-element.21), channel_id=1, source_target_pairs={{2,4},{6,8},{10,12},{14,16},{18,20},{22,24},{26,28},{4,2},{8,6},{1... | collective-permute-start | bytes 196616 | tf_op jit(solution)/shard_map/ppermute | solution.py:301
  3.7 9.1 %collective-permute-start.1 = (bf16[128,256]{1,0:T(8,128)(2,1)S(1)}, bf16[128,256]{1,0:T(8,128)(2,1)S(1)}, u32[]{:S(2)}, u32[]{:S(2)}) collective-permute-start(bf16[128,256]{1,0:T(8,128)(2,1)S(1)} %get-tuple-element.20), channel_id=1, source_target_pairs={{0,2},{2,0},{4,6},{6,4},{8,10},{10,8},{12,14},{14,12},{16,18},{18,... | collective-permute-start | bytes 196616 | tf_op jit(solution)/shard_map/ppermute | solution.py:302
  10.5 3.7 %copy-start.1 = (s32[1,27]{1,0:T(1,128)S(1)}, s32[1,27]{1,0:T(1,128)}, u32[]{:S(2)}) copy-start(s32[1,27]{1,0:T(1,128)} %neighbors_ref.1) | copy-start | bytes 328
  12.8 1.3 %collective-permute-start.3 = (bf16[128,256]{1,0:T(8,128)(2,1)S(1)}, bf16[128,256]{1,0:T(8,128)(2,1)S(1)}, u32[]{:S(2)}, u32[]{:S(2)}) collective-permute-start(bf16[128,256]{1,0:T(8,128)(2,1)S(1)} %collective-permute-done.1.first_ref), channel_id=1, source_target_pairs={{0,1},{1,0},{2,3},{3,2},{4,5},{5,4},{6,7},{7,6},{8,9},{9,8},{10,11... | collective-permute-start | bytes 196616 | tf_op jit(solution)/shard_map/ppermute | solution.py:272
  12.8 1.4 %collective-permute-start.4 = (bf16[128,256]{1,0:T(8,128)(2,1)S(1)}, bf16[128,256]{1,0:T(8,128)(2,1)S(1)}, u32[]{:S(2)}, u32[]{:S(2)}) collective-permute-start(bf16[128,256]{1,0:T(8,128)(2,1)S(1)} %collective-permute-done.2.second_ref), channel_id=1, source_target_pairs={{0,1},{1,0},{2,3},{3,2},{4,5},{5,4},{6,7},{7,6},{8,9},{9,8},{10,11... | collective-permute-start | bytes 196616 | tf_op jit(solution)/shard_map/ppermute | solution.py:272
  23.4 1.5 %collective-permute-start.5 = (bf16[1024,128]{1,0:T(8,128)(2,1)S(1)}, bf16[1024,128]{1,0:T(8,128)(2,1)S(1)}, u32[]{:S(2)}, u32[]{:S(2)}) collective-permute-start(bf16[1024,128]{1,0:T(8,128)(2,1)S(1)} %get-tuple-element.28), channel_id=1, source_target_pairs={{0,1},{1,0},{2,3},{3,2},{4,5},{5,4},{6,7},{7,6},{8,9},{9,8},{10,11... | collective-permute-start | bytes 786440 | tf_op jit(solution)/shard_map/ppermute | solution.py:272
  23.7 3.2 %collective-permute-start.13 = (bf16[1024,128]{1,0:T(8,128)(2,1)S(1)}, bf16[1024,128]{1,0:T(8,128)(2,1)S(1)}, u32[]{:S(2)}, u32[]{:S(2)}) collective-permute-start(bf16[1024,128]{1,0:T(8,128)(2,1)S(1)} %get-tuple-element.30), channel_id=1, source_target_pairs={{0,1},{1,0},{2,3},{3,2},{4,5},{5,4},{6,7},{7,6},{8,9},{9,8},{10,11... | collective-permute-start | bytes 786440 | tf_op jit(solution)/shard_map/ppermute | solution.py:272
  23.9 3.9 %collective-permute-start.21 = (bf16[1024,128]{1,0:T(8,128)(2,1)S(1)}, bf16[1024,128]{1,0:T(8,128)(2,1)S(1)}, u32[]{:S(2)}, u32[]{:S(2)}) collective-permute-start(bf16[1024,128]{1,0:T(8,128)(2,1)S(1)} %get-tuple-element.32), channel_id=1, source_target_pairs={{0,1},{1,0},{2,3},{3,2},{4,5},{5,4},{6,7},{7,6},{8,9},{9,8},{10,11... | collective-permute-start | bytes 786440 | tf_op jit(solution)/shard_map/ppermute | solution.py:272
  25.0 5.9 %collective-permute-start.6 = (bf16[512,128]{1,0:T(8,128)(2,1)S(1)}, bf16[512,128]{1,0:T(8,128)(2,1)S(1)}, u32[]{:S(2)}, u32[]{:S(2)}) collective-permute-start(bf16[512,128]{1,0:T(8,128)(2,1)S(1)} %dynamic-slice_convert_fusion.2), channel_id=1, source_target_pairs={{0,2},{2,0},{4,6},{6,4},{8,10},{10,8},{12,14},{14,12},{16,18},{18,... | collective-permute-start | bytes 393224 | tf_op jit(solution)/shard_map/ppermute | solution.py:272
  27.0 5.5 %collective-permute-start.14 = (bf16[512,128]{1,0:T(8,128)(2,1)S(1)}, bf16[512,128]{1,0:T(8,128)(2,1)S(1)}, u32[]{:S(2)}, u32[]{:S(2)}) collective-permute-start(bf16[512,128]{1,0:T(8,128)(2,1)S(1)} %dynamic-slice_convert_fusion.1), channel_id=1, source_target_pairs={{0,4},{2,6},{4,0},{6,2},{8,12},{10,14},{12,8},{14,10},{16,20},{18,... | collective-permute-start | bytes 393224 | tf_op jit(solution)/shard_map/ppermute | solution.py:272
  27.9 5.7 %collective-permute-start.22 = (bf16[512,128]{1,0:T(8,128)(2,1)S(1)}, bf16[512,128]{1,0:T(8,128)(2,1)S(1)}, u32[]{:S(2)}, u32[]{:S(2)}) collective-permute-start(bf16[512,128]{1,0:T(8,128)(2,1)S(1)} %dynamic-slice_convert_fusion), channel_id=1, source_target_pairs={{0,8},{2,10},{4,12},{6,14},{8,0},{10,2},{12,4},{14,6},{16,24},{18,... | collective-permute-start | bytes 393224 | tf_op jit(solution)/shard_map/ppermute | solution.py:272
  30.9 4.3 %collective-permute-start.7 = (bf16[256,128]{1,0:T(8,128)(2,1)S(1)}, bf16[256,128]{1,0:T(8,128)(2,1)S(1)}, u32[]{:S(2)}, u32[]{:S(2)}) collective-permute-start(bf16[256,128]{1,0:T(8,128)(2,1)S(1)} %dynamic-slice_convert_fusion.5), channel_id=1, source_target_pairs={{0,4},{2,6},{4,0},{6,2},{8,12},{10,14},{12,8},{14,10},{16,20},{18,... | collective-permute-start | bytes 196616 | tf_op jit(solution)/shard_map/ppermute | solution.py:272
  32.6 5.4 %collective-permute-start.15 = (bf16[256,128]{1,0:T(8,128)(2,1)S(1)}, bf16[256,128]{1,0:T(8,128)(2,1)S(1)}, u32[]{:S(2)}, u32[]{:S(2)}) collective-permute-start(bf16[256,128]{1,0:T(8,128)(2,1)S(1)} %dynamic-slice_convert_fusion.4), channel_id=1, source_target_pairs={{0,2},{2,0},{4,6},{6,4},{8,10},{10,8},{12,14},{14,12},{16,18},{18,... | collective-permute-start | bytes 196616 | tf_op jit(solution)/shard_map/ppermute | solution.py:272
  33.6 5.9 %collective-permute-start.23 = (bf16[256,128]{1,0:T(8,128)(2,1)S(1)}, bf16[256,128]{1,0:T(8,128)(2,1)S(1)}, u32[]{:S(2)}, u32[]{:S(2)}) collective-permute-start(bf16[256,128]{1,0:T(8,128)(2,1)S(1)} %dynamic-slice_convert_fusion.3), channel_id=1, source_target_pairs={{0,2},{2,0},{4,6},{6,4},{8,10},{10,8},{12,14},{14,12},{16,18},{18,... | collective-permute-start | bytes 196616 | tf_op jit(solution)/shard_map/ppermute | solution.py:272
  35.3 5.8 %collective-permute-start.8 = (bf16[256,128]{1,0:T(8,128)(2,1)S(1)}, bf16[256,128]{1,0:T(8,128)(2,1)S(1)}, u32[]{:S(2)}, u32[]{:S(2)}) collective-permute-start(bf16[256,128]{1,0:T(8,128)(2,1)S(1)} %add_convert_fusion.8), channel_id=1, source_target_pairs={{0,16},{2,18},{4,20},{6,22},{8,24},{10,26},{12,28},{14,30},{16,0},... | collective-permute-start | bytes 196616 | tf_op jit(solution)/shard_map/ppermute | solution.py:272
  38.0 6.3 %collective-permute-start.16 = (bf16[256,128]{1,0:T(8,128)(2,1)S(1)}, bf16[256,128]{1,0:T(8,128)(2,1)S(1)}, u32[]{:S(2)}, u32[]{:S(2)}) collective-permute-start(bf16[256,128]{1,0:T(8,128)(2,1)S(1)} %add_convert_fusion.5), channel_id=1, source_target_pairs={{0,8},{2,10},{4,12},{6,14},{8,0},{10,2},{12,4},{14,6},{16,24},{18,... | collective-permute-start | bytes 196616 | tf_op jit(solution)/shard_map/ppermute | solution.py:272
  39.5 6.8 %collective-permute-start.24 = (bf16[256,128]{1,0:T(8,128)(2,1)S(1)}, bf16[256,128]{1,0:T(8,128)(2,1)S(1)}, u32[]{:S(2)}, u32[]{:S(2)}) collective-permute-start(bf16[256,128]{1,0:T(8,128)(2,1)S(1)} %add_convert_fusion.2), channel_id=1, source_target_pairs={{0,16},{2,18},{4,20},{6,22},{8,24},{10,26},{12,28},{14,30},{16,0},... | collective-permute-start | bytes 196616 | tf_op jit(solution)/shard_map/ppermute | solution.py:272
  41.1 6.6 %collective-permute-start.9 = (bf16[256,128]{1,0:T(8,128)(2,1)S(1)}, bf16[256,128]{1,0:T(8,128)(2,1)S(1)}, u32[]{:S(2)}, u32[]{:S(2)}) collective-permute-start(bf16[256,128]{1,0:T(8,128)(2,1)S(1)} %add_convert_fusion.7), channel_id=1, source_target_pairs={{0,8},{2,10},{4,12},{6,14},{8,0},{10,2},{12,4},{14,6},{16,24},{18,... | collective-permute-start | bytes 196616 | tf_op jit(solution)/shard_map/ppermute | solution.py:272
  44.3 5.4 %collective-permute-start.17 = (bf16[256,128]{1,0:T(8,128)(2,1)S(1)}, bf16[256,128]{1,0:T(8,128)(2,1)S(1)}, u32[]{:S(2)}, u32[]{:S(2)}) collective-permute-start(bf16[256,128]{1,0:T(8,128)(2,1)S(1)} %add_convert_fusion.4), channel_id=1, source_target_pairs={{0,16},{2,18},{4,20},{6,22},{8,24},{10,26},{12,28},{14,30},{16,0},... | collective-permute-start | bytes 196616 | tf_op jit(solution)/shard_map/ppermute | solution.py:272
  46.4 4.3 %collective-permute-start.25 = (bf16[256,128]{1,0:T(8,128)(2,1)S(1)}, bf16[256,128]{1,0:T(8,128)(2,1)S(1)}, u32[]{:S(2)}, u32[]{:S(2)}) collective-permute-start(bf16[256,128]{1,0:T(8,128)(2,1)S(1)} %add_convert_fusion.1), channel_id=1, source_target_pairs={{0,4},{2,6},{4,0},{6,2},{8,12},{10,14},{12,8},{14,10},{16,20},{18,... | collective-permute-start | bytes 196616 | tf_op jit(solution)/shard_map/ppermute | solution.py:272
  47.7 4.4 %collective-permute-start.10 = (bf16[256,128]{1,0:T(8,128)(2,1)S(1)}, bf16[256,128]{1,0:T(8,128)(2,1)S(1)}, u32[]{:S(2)}, u32[]{:S(2)}) collective-permute-start(bf16[256,128]{1,0:T(8,128)(2,1)S(1)} %add_convert_fusion.6), channel_id=1, source_target_pairs={{0,4},{2,6},{4,0},{6,2},{8,12},{10,14},{12,8},{14,10},{16,20},{18,... | collective-permute-start | bytes 196616 | tf_op jit(solution)/shard_map/ppermute | solution.py:272
  49.8 4.3 %collective-permute-start.18 = (bf16[256,128]{1,0:T(8,128)(2,1)S(1)}, bf16[256,128]{1,0:T(8,128)(2,1)S(1)}, u32[]{:S(2)}, u32[]{:S(2)}) collective-permute-start(bf16[256,128]{1,0:T(8,128)(2,1)S(1)} %add_convert_fusion.3), channel_id=1, source_target_pairs={{0,2},{2,0},{4,6},{6,4},{8,10},{10,8},{12,14},{14,12},{16,18},{18,... | collective-permute-start | bytes 196616 | tf_op jit(solution)/shard_map/ppermute | solution.py:272
  50.7 4.8 %collective-permute-start.26 = (bf16[256,128]{1,0:T(8,128)(2,1)S(1)}, bf16[256,128]{1,0:T(8,128)(2,1)S(1)}, u32[]{:S(2)}, u32[]{:S(2)}) collective-permute-start(bf16[256,128]{1,0:T(8,128)(2,1)S(1)} %add_convert_fusion), channel_id=1, source_target_pairs={{0,2},{2,0},{4,6},{6,4},{8,10},{10,8},{12,14},{14,12},{16,18},{18,... | collective-permute-start | bytes 196616 | tf_op jit(solution)/shard_map/ppermute | solution.py:272
  52.1 5.0 %collective-permute-start.11 = (bf16[512,128]{1,0:T(8,128)(2,1)S(1)}, bf16[512,128]{1,0:T(8,128)(2,1)S(1)}, u32[]{:S(2)}, u32[]{:S(2)}) collective-permute-start(bf16[512,128]{1,0:T(8,128)(2,1)S(1)} %maximum_select_fusion.3), channel_id=1, source_target_pairs={{0,2},{2,0},{4,6},{6,4},{8,10},{10,8},{12,14},{14,12},{16,18},{18,... | collective-permute-start | bytes 393224 | tf_op jit(solution)/shard_map/ppermute | solution.py:272
  54.1 5.0 %collective-permute-start.19 = (bf16[512,128]{1,0:T(8,128)(2,1)S(1)}, bf16[512,128]{1,0:T(8,128)(2,1)S(1)}, u32[]{:S(2)}, u32[]{:S(2)}) collective-permute-start(bf16[512,128]{1,0:T(8,128)(2,1)S(1)} %maximum_select_fusion.4), channel_id=1, source_target_pairs={{0,4},{2,6},{4,0},{6,2},{8,12},{10,14},{12,8},{14,10},{16,20},{18,... | collective-permute-start | bytes 393224 | tf_op jit(solution)/shard_map/ppermute | solution.py:272
  55.5 5.0 %collective-permute-start.27 = (bf16[512,128]{1,0:T(8,128)(2,1)S(1)}, bf16[512,128]{1,0:T(8,128)(2,1)S(1)}, u32[]{:S(2)}, u32[]{:S(2)}) collective-permute-start(bf16[512,128]{1,0:T(8,128)(2,1)S(1)} %maximum_select_fusion.5), channel_id=1, source_target_pairs={{0,8},{2,10},{4,12},{6,14},{8,0},{10,2},{12,4},{14,6},{16,24},{18,... | collective-permute-start | bytes 393224 | tf_op jit(solution)/shard_map/ppermute | solution.py:272
  57.3 3.5 %collective-permute-start.12 = (bf16[1024,128]{1,0:T(8,128)(2,1)S(1)}, bf16[1024,128]{1,0:T(8,128)(2,1)S(1)}, u32[]{:S(2)}, u32[]{:S(2)}) collective-permute-start(bf16[1024,128]{1,0:T(8,128)(2,1)S(1)} %maximum_select_fusion.own_ref.own_p_ref), channel_id=1, source_target_pairs={{0,1},{1,0},{2,3},{3,2},{4,5},{5,4},{6,7},{7,6},{8,9},{9,8},{10,11... | collective-permute-start | bytes 786440 | tf_op jit(solution)/shard_map/ppermute | solution.py:272
  59.3 2.9 %collective-permute-start.20 = (bf16[1024,128]{1,0:T(8,128)(2,1)S(1)}, bf16[1024,128]{1,0:T(8,128)(2,1)S(1)}, u32[]{:S(2)}, u32[]{:S(2)}) collective-permute-start(bf16[1024,128]{1,0:T(8,128)(2,1)S(1)} %maximum_select_fusion.1.own_q_ref), channel_id=1, source_target_pairs={{0,1},{1,0},{2,3},{3,2},{4,5},{5,4},{6,7},{7,6},{8,9},{9,8},{10,11... | collective-permute-start | bytes 786440 | tf_op jit(solution)/shard_map/ppermute | solution.py:272
  60.6 1.6 %collective-permute-start.28 = (bf16[1024,128]{1,0:T(8,128)(2,1)S(1)}, bf16[1024,128]{1,0:T(8,128)(2,1)S(1)}, u32[]{:S(2)}, u32[]{:S(2)}) collective-permute-start(bf16[1024,128]{1,0:T(8,128)(2,1)S(1)} %maximum_select_fusion.2.own_r_ref), channel_id=1, source_target_pairs={{0,1},{1,0},{2,3},{3,2},{4,5},{5,4},{6,7},{7,6},{8,9},{9,8},{10,11... | collective-permute-start | bytes 786440 | tf_op jit(solution)/shard_map/ppermute | solution.py:272
